TPU v7x, 32 devices: a whole 2x2x4 slice. The times are simulated.
32 devices in a mesh: pole: 2 (over y), space: 16 (over z, x, core).
Axes of the slice: x: 2, y: 2, z: 4, core: 2. Of those that a mesh axis runs over, the one named last changes fastest.
Arguments:
- conductivity: float32 [32, 64, 128], P('space'), may hold values from 0.1 to 10
- misfit: float32 [32, 64, 128], P('space'), may hold values from -6 to 6
- forward_states: float32 [4, 32, 64, 128], P('pole', 'space'), may hold values from -6 to 6
- pole_shifts: float32 [4], replicated, may hold values from 0.01 to 10
- pole_weights: float32 [4], replicated, may hold values from 0.05 to 1
- pole_order: int32 [4], P('pole'), may hold values from 0 to 3, each once
Outputs:
- adjoint_states: float32 [4, 32, 64, 128], P('pole', 'space')
- gradient: float32 [32, 64, 128], P('space', 'pole')
Inputs may be any that keep to these rules, and one draw needn't show every extreme that they name: `pole_order`: every pole stands in exactly one slot.
All inputs are finite; a program needn't handle non-finite values.
Results may differ from a plain program's by a relative error of at most 0.0001.
Values sent between devices are 32-bit elements; how exact they have to be, the bound alone decides.
No kernel may reach another device: no remote copies, remote signals or barrier semaphores. Data moves between devices by JAX's collectives and lax.ppermute only.
A program may use at most 128 MiB of HBM per device.

v0:
```python
import jax
import jax.numpy as jnp
from jax import lax
from jax.sharding import PartitionSpec as P

ITERS = 2


DAMPING = 0.8


def extended(array, sides, width):
    for axis, dim in sides:
        peers, length = (lax.axis_size(axis), array.shape[dim])
        up = [(i, (i + 1) % peers) for i in range(peers - 1)]
        down = [(j, i) for i, j in up]
        last = lax.slice_in_dim(array, length - width, length, axis=dim)
        leading = lax.slice_in_dim(array, 0, width, axis=dim)
        before = lax.ppermute(last, axis, up)
        after = lax.ppermute(leading, axis, down)
        array = jnp.concatenate([before, array, after], axis=dim)
    return array


def plus_side(field, which_dim):
    extent = field.shape[which_dim]
    inner_part = lax.slice_in_dim(field, 1, extent, axis=which_dim)
    zero_plane = jnp.zeros_like(lax.slice_in_dim(field, 0, 1, axis=which_dim))
    return jnp.concatenate([inner_part, zero_plane], axis=which_dim)


def minus_side(field, which_dim):
    extent = field.shape[which_dim]
    inner_part = lax.slice_in_dim(field, 0, extent - 1, axis=which_dim)
    zero_plane = jnp.zeros_like(lax.slice_in_dim(field, 0, 1, axis=which_dim))
    return jnp.concatenate([zero_plane, inner_part], axis=which_dim)


def coarse_pick(faces, which_dim, offset):
    extent_x, extent_y, extent_z = faces.shape
    blocks = faces.reshape(extent_x // 2, 2, extent_y // 2, 2, extent_z // 2, 2)
    chosen = lax.index_in_dim(blocks, offset, axis=2 * which_dim + 1, keepdims=True)
    return jnp.sum(chosen, axis=(1, 3, 5))


def side_terms(field, plus_faces, minus_faces, widened):
    result = plus_faces[0] * (field - widened[:, 2:]) + minus_faces[0] * (field - widened[:, :-2])
    for which_dim in (1, 2):
        result = result + plus_faces[which_dim] * (field - plus_side(field, which_dim + 1))
        result = result + minus_faces[which_dim] * (field - minus_side(field, which_dim + 1))
    return result


def fine_image(field, plus_faces, minus_faces, shift_value):
    widened = extended(field, (("space", 1),), 1)
    return shift_value * field + side_terms(field, plus_faces, minus_faces, widened)


def coarse_image(field, plus_faces, minus_faces, shift_value):
    widened = extended(field, (("space", 1),), 1)
    return shift_value * field + side_terms(field, plus_faces, minus_faces, widened)


def restrict(field):
    members, extent_x, extent_y, extent_z = field.shape
    shaped = field.reshape(members, extent_x // 2, 2, extent_y // 2, 2, extent_z // 2, 2)
    return jnp.sum(shaped, axis=(2, 4, 6))


def prolong(field):
    return jnp.repeat(jnp.repeat(jnp.repeat(field, 2, axis=1), 2, axis=2), 2, axis=3)


def precondition(residual, fine, coarse):
    plus_faces, minus_faces, shift_value, diagonal = fine
    coarse_plus, coarse_minus, coarse_shift, coarse_diagonal = coarse
    smooth_one = DAMPING * residual / diagonal
    coarse_rhs = restrict(residual - fine_image(smooth_one, plus_faces, minus_faces, shift_value))
    coarse_one = DAMPING * coarse_rhs / coarse_diagonal
    coarse_two = (
        coarse_one
        + DAMPING
        * (coarse_rhs - coarse_image(coarse_one, coarse_plus, coarse_minus, coarse_shift))
        / coarse_diagonal
    )
    corrected = smooth_one + prolong(coarse_two)
    return (
        corrected
        + DAMPING
        * (residual - fine_image(corrected, plus_faces, minus_faces, shift_value))
        / diagonal
    )


def expand(values):
    return values.reshape(-1, 1, 1, 1)


def cell_sums(values):
    return jnp.sum(values, axis=(1, 2, 3))


def norm_sum(residual, precond):
    return lax.psum(cell_sums(residual * precond), "space")


def solve(rhs, fine, coarse):
    plus_faces, minus_faces, shift_value, diagonal = fine
    iterate = jnp.zeros_like(rhs)
    residual = rhs
    precond = precondition(residual, fine, coarse)
    gamma_now = norm_sum(residual, precond)
    search = precond
    for turn_index in range(ITERS):
        image_field = fine_image(search, plus_faces, minus_faces, shift_value)
        curve = lax.psum(cell_sums(search * image_field), "space")
        step_length = gamma_now / curve
        iterate = iterate + expand(step_length) * search
        if turn_index + 1 < ITERS:
            residual = residual - expand(step_length) * image_field
            precond = precondition(residual, fine, coarse)
            gamma_next = norm_sum(residual, precond)
            search = precond + expand(gamma_next / gamma_now) * search
            gamma_now = gamma_next
    return iterate


def per_device(conductivity, misfit, forward_states, pole_shifts, pole_weights, pole_order):
    widened_kappa = extended(conductivity, (("space", 0),), 1)
    plus_faces = [
        0.5 * (conductivity + widened_kappa[2:]),
        0.5 * (conductivity + plus_side(conductivity, 1)),
        0.5 * (conductivity + plus_side(conductivity, 2)),
    ]
    minus_faces = [
        0.5 * (conductivity + widened_kappa[:-2]),
        0.5 * (conductivity + minus_side(conductivity, 1)),
        0.5 * (conductivity + minus_side(conductivity, 2)),
    ]
    base_diagonal = (
        plus_faces[0]
        + plus_faces[1]
        + plus_faces[2]
        + minus_faces[0]
        + minus_faces[1]
        + minus_faces[2]
    )
    coarse_plus = [coarse_pick(plus_faces[which_dim], which_dim, 1) for which_dim in range(3)]
    coarse_minus = [coarse_pick(minus_faces[which_dim], which_dim, 0) for which_dim in range(3)]
    coarse_base = (
        coarse_plus[0]
        + coarse_plus[1]
        + coarse_plus[2]
        + coarse_minus[0]
        + coarse_minus[1]
        + coarse_minus[2]
    )
    pole_index = jnp.arange(pole_shifts.shape[0], dtype=jnp.int32)
    matches = pole_order[:, None] == pole_index[None, :]
    shift_local = jnp.sum(jnp.where(matches, pole_shifts[None, :], 0.0), axis=1)
    weight_local = jnp.sum(jnp.where(matches, pole_weights[None, :], 0.0), axis=1)
    members = forward_states.shape[0]

    def solve_group(shift_part, weight_part):
        shift_value = expand(shift_part)
        fine = (plus_faces, minus_faces, shift_value, base_diagonal[None] + shift_value)
        coarse = (
            coarse_plus,
            coarse_minus,
            8.0 * shift_value,
            coarse_base[None] + 8.0 * shift_value,
        )
        return solve(expand(weight_part) * misfit[None], fine, coarse)

    adjoint_states = jnp.concatenate(
        [
            solve_group(shift_local[member : member + 1], weight_local[member : member + 1])
            for member in range(members)
        ],
        axis=0,
    )
    widened = extended(jnp.stack([adjoint_states, forward_states]), (("space", 2),), 1)
    term = (adjoint_states - widened[0, :, 2:]) * (forward_states - widened[1, :, 2:])
    term = term + (adjoint_states - widened[0, :, :-2]) * (forward_states - widened[1, :, :-2])
    for which_dim in (2, 3):
        term = term + (adjoint_states - plus_side(adjoint_states, which_dim)) * (
            forward_states - plus_side(forward_states, which_dim)
        )
        term = term + (adjoint_states - minus_side(adjoint_states, which_dim)) * (
            forward_states - minus_side(forward_states, which_dim)
        )
    local_term = -0.5 * jnp.sum(term, axis=0)
    gradient = lax.psum_scatter(local_term, "pole", scatter_dimension=1, tiled=True)
    return (adjoint_states, gradient)


def solution(mesh):
    in_specs = (
        P("space", None, None),
        P("space", None, None),
        P("pole", "space", None, None),
        P(),
        P(),
        P("pole"),
    )
    out_specs = (P("pole", "space", None, None), P("space", "pole", None))
    return jax.shard_map(
        per_device, mesh=mesh, in_specs=in_specs, out_specs=out_specs, check_vma=False
    )
```

profile of v0, /device:TPU:0, one launch (start us, length us, event | category | flops | bytes accessed | tf_op | source)
XLA Modules:
  0.0 370.4 jit_solution(15797618333859423636)
XLA Ops:
  9.3 3.0 collective-permute-start.1
  26.4 5.1 %collective-permute-start.3 = (f32[1,1,64,128]{3,2,1,0:T(8,128)S(1)}, f32[1,1,64,128]{3,2,1,0:T(8,128)S(1)}, u32[]{:S(2)}, u32[]{:S(2)}) collective-permute-start(f32[1,1,64,128]{3,2,1,0:T(8,128)S(1)} %get-tuple-element.115), channel_id=1, source_target_pairs={{0,1},{1,2},{2,3},{3,4},{4,5},{5,6},{6,7},{7,8},{8,9},{9,10},{10,1... | collective-permute-start | bytes 98312 | tf_op jit(solution)/shard_map/ppermute | solution.py:19
  31.5 5.5 %reshape.590 = f32[1,2,32,2,64,2]{5,4,3,2,1,0:T(8,128)} reshape(f32[2,64,128]{2,1,0:T(8,128)S(1)} %get-tuple-element.31) | data formatting | bytes 131072 | tf_op jit(solution)/shard_map/reshape | solution.py:41
  39.6 5.5 %reshape.587 = f32[1,2,32,2,64,2]{5,4,3,2,1,0:T(8,128)} reshape(f32[2,64,128]{2,1,0:T(8,128)S(1)} %get-tuple-element.28) | data formatting | bytes 131072 | tf_op jit(solution)/shard_map/reshape | solution.py:41
  45.1 3.6 slice_reduce_fusion.1
  48.8 5.5 %reshape.589 = f32[1,2,32,2,64,2]{5,4,3,2,1,0:T(8,128)} reshape(f32[2,64,128]{2,1,0:T(8,128)S(1)} %get-tuple-element.30) | data formatting | bytes 131072 | tf_op jit(solution)/shard_map/reshape | solution.py:41
  56.2 5.5 %reshape.588 = f32[1,2,32,2,64,2]{5,4,3,2,1,0:T(8,128)} reshape(f32[2,64,128]{2,1,0:T(8,128)S(1)} %get-tuple-element.29) | data formatting | bytes 131072 | tf_op jit(solution)/shard_map/reshape | solution.py:41
  63.7 5.5 %reshape.586 = f32[1,2,32,2,64,2]{5,4,3,2,1,0:T(8,128)} reshape(f32[2,64,128]{2,1,0:T(8,128)S(1)} %get-tuple-element.26) | data formatting | bytes 131072 | tf_op jit(solution)/shard_map/reshape | solution.py:41
  71.2 5.5 %reshape.585 = f32[1,2,32,2,64,2]{5,4,3,2,1,0:T(8,128)} reshape(f32[2,64,128]{2,1,0:T(8,128)S(1)} %get-tuple-element.27) | data formatting | bytes 131072 | tf_op jit(solution)/shard_map/reshape | solution.py:41
  80.0 4.9 %collective-permute-start.19 = (f32[1,1,64,128]{3,2,1,0:T(8,128)}, f32[1,1,64,128]{3,2,1,0:T(8,128)}, u32[]{:S(2)}, u32[]{:S(2)}) collective-permute-start(f32[1,1,64,128]{3,2,1,0:T(8,128)} %get-tuple-element.97), channel_id=1, source_target_pairs={{0,1},{1,2},{2,3},{3,4},{4,5},{5,6},{6,7},{7,8},{8,9},{9,10},{10,1... | collective-permute-start | bytes 98312 | tf_op jit(solution)/shard_map/ppermute | solution.py:19
  90.7 4.5 %collective-permute-start.5 = (f32[1,1,32,64]{3,2,1,0:T(8,128)S(1)}, f32[1,1,32,64]{3,2,1,0:T(8,128)}, u32[]{:S(2)}, u32[]{:S(2)}) collective-permute-start(f32[1,1,32,64]{3,2,1,0:T(8,128)S(1)} %get-tuple-element.22), channel_id=1, source_target_pairs={{0,1},{1,2},{2,3},{3,4},{4,5},{5,6},{6,7},{7,8},{8,9},{9,10},{10,1... | collective-permute-start | bytes 24584 | tf_op jit(solution)/shard_map/ppermute | solution.py:19
  101.9 3.7 collective-permute-start.21
  106.7 2.6 add_bitcast_fusion
  110.8 5.1 %collective-permute-start.7 = (f32[1,1,64,128]{3,2,1,0:T(8,128)S(1)}, f32[1,1,64,128]{3,2,1,0:T(8,128)S(1)}, u32[]{:S(2)}, u32[]{:S(2)}) collective-permute-start(f32[1,1,64,128]{3,2,1,0:T(8,128)S(1)} %get-tuple-element.109), channel_id=1, source_target_pairs={{0,1},{1,2},{2,3},{3,4},{4,5},{5,6},{6,7},{7,8},{8,9},{9,10},{10,1... | collective-permute-start | bytes 98312 | tf_op jit(solution)/shard_map/ppermute | solution.py:19
  117.3 5.1 %collective-permute-start.23 = (f32[1,1,64,128]{3,2,1,0:T(8,128)S(1)}, f32[1,1,64,128]{3,2,1,0:T(8,128)S(1)}, u32[]{:S(2)}, u32[]{:S(2)}) collective-permute-start(f32[1,1,64,128]{3,2,1,0:T(8,128)S(1)} %get-tuple-element.91), channel_id=1, source_target_pairs={{0,1},{1,2},{2,3},{3,4},{4,5},{5,6},{6,7},{7,8},{8,9},{9,10},{10,1... | collective-permute-start | bytes 98312 | tf_op jit(solution)/shard_map/ppermute | solution.py:19
  128.0 5.2 %collective-permute-start.9 = (f32[1,1,64,128]{3,2,1,0:T(8,128)S(1)}, f32[1,1,64,128]{3,2,1,0:T(8,128)S(1)}, u32[]{:S(2)}, u32[]{:S(2)}) collective-permute-start(f32[1,1,64,128]{3,2,1,0:T(8,128)S(1)} %get-tuple-element.99), channel_id=1, source_target_pairs={{0,1},{1,2},{2,3},{3,4},{4,5},{5,6},{6,7},{7,8},{8,9},{9,10},{10,1... | collective-permute-start | bytes 98312 | tf_op jit(solution)/shard_map/ppermute | solution.py:19
  135.1 6.3 %collective-permute-start.25 = (f32[1,1,64,128]{3,2,1,0:T(8,128)}, f32[1,1,64,128]{3,2,1,0:T(8,128)}, u32[]{:S(2)}, u32[]{:S(2)}) collective-permute-start(f32[1,1,64,128]{3,2,1,0:T(8,128)} %get-tuple-element.69), channel_id=1, source_target_pairs={{0,1},{1,2},{2,3},{3,4},{4,5},{5,6},{6,7},{7,8},{8,9},{9,10},{10,1... | collective-permute-start | bytes 98312 | tf_op jit(solution)/shard_map/ppermute | solution.py:19
  143.5 33.8 %all-reduce.79 = (f32[1]{0:T(128)}, f32[1]{0:T(128)}) all-reduce(f32[1]{0:T(128)} %bitcast.25, f32[1]{0:T(128)} %bitcast.26), channel_id=1, replica_groups=mesh['pole'=2,'space'=16] {'space'}, use_global_device_ids=true, to_apply=%region_11.12 | all-reduce | flops 2 | bytes 16 | tf_op jit(solution)/shard_map/psum | solution.py:104
  181.2 3.0 collective-permute-start.11
  190.2 3.0 collective-permute-start.13
  197.1 4.6 %collective-permute-start.15 = (f32[1,1,64,128]{3,2,1,0:T(8,128)S(1)}, f32[1,1,64,128]{3,2,1,0:T(8,128)S(1)}, u32[]{:S(2)}, u32[]{:S(2)}) collective-permute-start(f32[1,1,64,128]{3,2,1,0:T(8,128)S(1)} %get-tuple-element.75), channel_id=1, source_target_pairs={{0,1},{1,2},{2,3},{3,4},{4,5},{5,6},{6,7},{7,8},{8,9},{9,10},{10,1... | collective-permute-start | bytes 98312 | tf_op jit(solution)/shard_map/ppermute | solution.py:19
  202.5 4.3 %multiply_reduce_fusion.2 = (f32[]{:T(128)}, f32[]{:T(128)}, f32[]{:T(128)}, f32[1,2,64,128]{3,2,1,0:T(8,128)S(1)}, f32[1,2,64,128]{3,2,1,0:T(8,128)S(1)}) fusion(f32[1,2,64,128]{3,2,1,0:T(8,128)S(1)} %get-tuple-element.21, f32[]{:T(128)} %bitcast.27, f32[2,64,128]{2,1,0:T(8,128)S(1)} %copy-done, f32[]{:T(128)} %bitcast, f32[1,2,64,128]{3,2,1,0:T(8,128)S(1)} %fusion.77, ...), kind=kLoop, calls=%fused_computation.282 | loop fusion | flops 933885 | bytes 1501216 | tf_op jit(solution)/shard_map/reduce_sum | solution.py:100
  206.8 32.6 %all-reduce.78 = (f32[1]{0:T(128)}, f32[1]{0:T(128)}) all-reduce(f32[1]{0:T(128)} %bitcast.49, f32[1]{0:T(128)} %bitcast.50), channel_id=1, replica_groups=mesh['pole'=2,'space'=16] {'space'}, use_global_device_ids=true, to_apply=%region_23.24 | all-reduce | flops 2 | bytes 16 | tf_op jit(solution)/shard_map/psum | solution.py:104
  243.2 3.0 collective-permute-start.27
  252.4 3.0 collective-permute-start.29
  259.1 4.6 %collective-permute-start.31 = (f32[1,1,64,128]{3,2,1,0:T(8,128)S(1)}, f32[1,1,64,128]{3,2,1,0:T(8,128)S(1)}, u32[]{:S(2)}, u32[]{:S(2)}) collective-permute-start(f32[1,1,64,128]{3,2,1,0:T(8,128)S(1)} %get-tuple-element.57), channel_id=1, source_target_pairs={{0,1},{1,2},{2,3},{3,4},{4,5},{5,6},{6,7},{7,8},{8,9},{9,10},{10,1... | collective-permute-start | bytes 98312 | tf_op jit(solution)/shard_map/ppermute | solution.py:19
  266.5 32.6 %all-reduce.77 = (f32[1]{0:T(128)}, f32[1]{0:T(128)}) all-reduce(f32[1]{0:T(128)} %bitcast.56, f32[1]{0:T(128)} %bitcast.32), channel_id=1, replica_groups=mesh['pole'=2,'space'=16] {'space'}, use_global_device_ids=true, to_apply=%region_29.30 | all-reduce | flops 2 | bytes 16 | tf_op jit(solution)/shard_map/psum | solution.py:104
  303.1 3.0 collective-permute-start.17
  307.4 3.0 collective-permute-start.33
  313.3 31.4 %all-reduce.76 = (f32[1]{0:T(128)}, f32[1]{0:T(128)}) all-reduce(f32[1]{0:T(128)} %bitcast.58, f32[1]{0:T(128)} %bitcast.34), channel_id=1, replica_groups=mesh['pole'=2,'space'=16] {'space'}, use_global_device_ids=true, to_apply=%region_31.32 | all-reduce | flops 2 | bytes 16 | tf_op jit(solution)/shard_map/psum | solution.py:116
  348.6 3.0 collective-permute-start.35
  354.2 9.4 %reduce-scatter.2.cloned.1.call-done = f32[2,32,128]{2,1,0:T(8,128)} async-done(((f32[2,64,128]{2,1,0:T(8,128)}), f32[2,32,128]{2,1,0:T(8,128)}) %reduce-scatter.2.cloned.1.call-update) | async-done | bytes 32784 | tf_op jit(solution)/shard_map/reduce_scatter | solution.py:193
  (180 shorter events, 89.9 us)
Async XLA Ops:
  7.2 356.4 %reduce-scatter.2.cloned.1.call-start = ((), (), s32[]{:S(2)}) async-start(), calls=%async_computation.1 | async-start | bytes 98304 | tf_op jit(solution)/shard_map/reduce_scatter | solution.py:193
  8.0 11.9 %collective-permute-start = (f32[1,64,128]{2,1,0:T(8,128)S(1)}, f32[1,64,128]{2,1,0:T(8,128)S(1)}, u32[]{:S(2)}, u32[]{:S(2)}) collective-permute-start(f32[1,64,128]{2,1,0:T(8,128)S(1)} %get-tuple-element.121), channel_id=1, source_target_pairs={{1,0},{2,1},{3,2},{4,3},{5,4},{6,5},{7,6},{8,7},{9,8},{10,9},{11,1... | collective-permute-start | bytes 98312 | tf_op jit(solution)/shard_map/ppermute | solution.py:20
  9.3 10.6 %collective-permute-start.1 = (f32[1,64,128]{2,1,0:T(8,128)S(1)}, f32[1,64,128]{2,1,0:T(8,128)S(1)}, u32[]{:S(2)}, u32[]{:S(2)}) collective-permute-start(f32[1,64,128]{2,1,0:T(8,128)S(1)} %get-tuple-element.120), channel_id=1, source_target_pairs={{0,1},{1,2},{2,3},{3,4},{4,5},{5,6},{6,7},{7,8},{8,9},{9,10},{10,1... | collective-permute-start | bytes 98312 | tf_op jit(solution)/shard_map/ppermute | solution.py:19
  25.1 59.7 %collective-permute-start.2 = (f32[1,1,64,128]{3,2,1,0:T(8,128)S(1)}, f32[1,1,64,128]{3,2,1,0:T(8,128)S(1)}, u32[]{:S(2)}, u32[]{:S(2)}) collective-permute-start(f32[1,1,64,128]{3,2,1,0:T(8,128)S(1)} %get-tuple-element.114), channel_id=1, source_target_pairs={{1,0},{2,1},{3,2},{4,3},{5,4},{6,5},{7,6},{8,7},{9,8},{10,9},{11,1... | collective-permute-start | bytes 98312 | tf_op jit(solution)/shard_map/ppermute | solution.py:20
  26.4 58.4 %collective-permute-start.3 = (f32[1,1,64,128]{3,2,1,0:T(8,128)S(1)}, f32[1,1,64,128]{3,2,1,0:T(8,128)S(1)}, u32[]{:S(2)}, u32[]{:S(2)}) collective-permute-start(f32[1,1,64,128]{3,2,1,0:T(8,128)S(1)} %get-tuple-element.115), channel_id=1, source_target_pairs={{0,1},{1,2},{2,3},{3,4},{4,5},{5,6},{6,7},{7,8},{8,9},{9,10},{10,1... | collective-permute-start | bytes 98312 | tf_op jit(solution)/shard_map/ppermute | solution.py:19
  78.7 16.5 %collective-permute-start.18 = (f32[1,1,64,128]{3,2,1,0:T(8,128)}, f32[1,1,64,128]{3,2,1,0:T(8,128)}, u32[]{:S(2)}, u32[]{:S(2)}) collective-permute-start(f32[1,1,64,128]{3,2,1,0:T(8,128)} %get-tuple-element.96), channel_id=1, source_target_pairs={{1,0},{2,1},{3,2},{4,3},{5,4},{6,5},{7,6},{8,7},{9,8},{10,9},{11,1... | collective-permute-start | bytes 98312 | tf_op jit(solution)/shard_map/ppermute | solution.py:20
  80.0 15.2 %collective-permute-start.19 = (f32[1,1,64,128]{3,2,1,0:T(8,128)}, f32[1,1,64,128]{3,2,1,0:T(8,128)}, u32[]{:S(2)}, u32[]{:S(2)}) collective-permute-start(f32[1,1,64,128]{3,2,1,0:T(8,128)} %get-tuple-element.97), channel_id=1, source_target_pairs={{0,1},{1,2},{2,3},{3,4},{4,5},{5,6},{6,7},{7,8},{8,9},{9,10},{10,1... | collective-permute-start | bytes 98312 | tf_op jit(solution)/shard_map/ppermute | solution.py:19
  89.4 10.3 %collective-permute-start.4 = (f32[1,1,32,64]{3,2,1,0:T(8,128)S(1)}, f32[1,1,32,64]{3,2,1,0:T(8,128)}, u32[]{:S(2)}, u32[]{:S(2)}) collective-permute-start(f32[1,1,32,64]{3,2,1,0:T(8,128)S(1)} %get-tuple-element.22), channel_id=1, source_target_pairs={{1,0},{2,1},{3,2},{4,3},{5,4},{6,5},{7,6},{8,7},{9,8},{10,9},{11,1... | collective-permute-start | bytes 24584 | tf_op jit(solution)/shard_map/ppermute | solution.py:20
  90.7 9.1 %collective-permute-start.5 = (f32[1,1,32,64]{3,2,1,0:T(8,128)S(1)}, f32[1,1,32,64]{3,2,1,0:T(8,128)}, u32[]{:S(2)}, u32[]{:S(2)}) collective-permute-start(f32[1,1,32,64]{3,2,1,0:T(8,128)S(1)} %get-tuple-element.22), channel_id=1, source_target_pairs={{0,1},{1,2},{2,3},{3,4},{4,5},{5,6},{6,7},{7,8},{8,9},{9,10},{10,1... | collective-permute-start | bytes 24584 | tf_op jit(solution)/shard_map/ppermute | solution.py:19
  100.6 5.3 %collective-permute-start.20 = (f32[1,1,32,64]{3,2,1,0:T(8,128)S(1)}, f32[1,1,32,64]{3,2,1,0:T(8,128)S(1)}, u32[]{:S(2)}, u32[]{:S(2)}) collective-permute-start(f32[1,1,32,64]{3,2,1,0:T(8,128)S(1)} %get-tuple-element.134), channel_id=1, source_target_pairs={{1,0},{2,1},{3,2},{4,3},{5,4},{6,5},{7,6},{8,7},{9,8},{10,9},{11,1... | collective-permute-start | bytes 24584 | tf_op jit(solution)/shard_map/ppermute | solution.py:20
  101.9 4.5 %collective-permute-start.21 = (f32[1,1,32,64]{3,2,1,0:T(8,128)S(1)}, f32[1,1,32,64]{3,2,1,0:T(8,128)S(1)}, u32[]{:S(2)}, u32[]{:S(2)}) collective-permute-start(f32[1,1,32,64]{3,2,1,0:T(8,128)S(1)} %get-tuple-element.134), channel_id=1, source_target_pairs={{0,1},{1,2},{2,3},{3,4},{4,5},{5,6},{6,7},{7,8},{8,9},{9,10},{10,1... | collective-permute-start | bytes 24584 | tf_op jit(solution)/shard_map/ppermute | solution.py:19
  109.5 12.9 %collective-permute-start.6 = (f32[1,1,64,128]{3,2,1,0:T(8,128)S(1)}, f32[1,1,64,128]{3,2,1,0:T(8,128)S(1)}, u32[]{:S(2)}, u32[]{:S(2)}) collective-permute-start(f32[1,1,64,128]{3,2,1,0:T(8,128)S(1)} %get-tuple-element.108), channel_id=1, source_target_pairs={{1,0},{2,1},{3,2},{4,3},{5,4},{6,5},{7,6},{8,7},{9,8},{10,9},{11,1... | collective-permute-start | bytes 98312 | tf_op jit(solution)/shard_map/ppermute | solution.py:20
  110.8 11.6 %collective-permute-start.7 = (f32[1,1,64,128]{3,2,1,0:T(8,128)S(1)}, f32[1,1,64,128]{3,2,1,0:T(8,128)S(1)}, u32[]{:S(2)}, u32[]{:S(2)}) collective-permute-start(f32[1,1,64,128]{3,2,1,0:T(8,128)S(1)} %get-tuple-element.109), channel_id=1, source_target_pairs={{0,1},{1,2},{2,3},{3,4},{4,5},{5,6},{6,7},{7,8},{8,9},{9,10},{10,1... | collective-permute-start | bytes 98312 | tf_op jit(solution)/shard_map/ppermute | solution.py:19
  116.0 8.0 %collective-permute-start.22 = (f32[1,1,64,128]{3,2,1,0:T(8,128)S(1)}, f32[1,1,64,128]{3,2,1,0:T(8,128)S(1)}, u32[]{:S(2)}, u32[]{:S(2)}) collective-permute-start(f32[1,1,64,128]{3,2,1,0:T(8,128)S(1)} %get-tuple-element.90), channel_id=1, source_target_pairs={{1,0},{2,1},{3,2},{4,3},{5,4},{6,5},{7,6},{8,7},{9,8},{10,9},{11,1... | collective-permute-start | bytes 98312 | tf_op jit(solution)/shard_map/ppermute | solution.py:20
  117.3 6.7 %collective-permute-start.23 = (f32[1,1,64,128]{3,2,1,0:T(8,128)S(1)}, f32[1,1,64,128]{3,2,1,0:T(8,128)S(1)}, u32[]{:S(2)}, u32[]{:S(2)}) collective-permute-start(f32[1,1,64,128]{3,2,1,0:T(8,128)S(1)} %get-tuple-element.91), channel_id=1, source_target_pairs={{0,1},{1,2},{2,3},{3,4},{4,5},{5,6},{6,7},{7,8},{8,9},{9,10},{10,1... | collective-permute-start | bytes 98312 | tf_op jit(solution)/shard_map/ppermute | solution.py:19
  126.7 14.7 %collective-permute-start.8 = (f32[1,1,64,128]{3,2,1,0:T(8,128)S(1)}, f32[1,1,64,128]{3,2,1,0:T(8,128)S(1)}, u32[]{:S(2)}, u32[]{:S(2)}) collective-permute-start(f32[1,1,64,128]{3,2,1,0:T(8,128)S(1)} %get-tuple-element.98), channel_id=1, source_target_pairs={{1,0},{2,1},{3,2},{4,3},{5,4},{6,5},{7,6},{8,7},{9,8},{10,9},{11,1... | collective-permute-start | bytes 98312 | tf_op jit(solution)/shard_map/ppermute | solution.py:20
  128.0 13.5 %collective-permute-start.9 = (f32[1,1,64,128]{3,2,1,0:T(8,128)S(1)}, f32[1,1,64,128]{3,2,1,0:T(8,128)S(1)}, u32[]{:S(2)}, u32[]{:S(2)}) collective-permute-start(f32[1,1,64,128]{3,2,1,0:T(8,128)S(1)} %get-tuple-element.99), channel_id=1, source_target_pairs={{0,1},{1,2},{2,3},{3,4},{4,5},{5,6},{6,7},{7,8},{8,9},{9,10},{10,1... | collective-permute-start | bytes 98312 | tf_op jit(solution)/shard_map/ppermute | solution.py:19
  133.8 67.9 %collective-permute-start.24 = (f32[1,1,64,128]{3,2,1,0:T(8,128)}, f32[1,1,64,128]{3,2,1,0:T(8,128)}, u32[]{:S(2)}, u32[]{:S(2)}) collective-permute-start(f32[1,1,64,128]{3,2,1,0:T(8,128)} %get-tuple-element.68), channel_id=1, source_target_pairs={{1,0},{2,1},{3,2},{4,3},{5,4},{6,5},{7,6},{8,7},{9,8},{10,9},{11,1... | collective-permute-start | bytes 98312 | tf_op jit(solution)/shard_map/ppermute | solution.py:20
  135.1 66.6 %collective-permute-start.25 = (f32[1,1,64,128]{3,2,1,0:T(8,128)}, f32[1,1,64,128]{3,2,1,0:T(8,128)}, u32[]{:S(2)}, u32[]{:S(2)}) collective-permute-start(f32[1,1,64,128]{3,2,1,0:T(8,128)} %get-tuple-element.69), channel_id=1, source_target_pairs={{0,1},{1,2},{2,3},{3,4},{4,5},{5,6},{6,7},{7,8},{8,9},{9,10},{10,1... | collective-permute-start | bytes 98312 | tf_op jit(solution)/shard_map/ppermute | solution.py:19
  179.9 4.4 %collective-permute-start.10 = (f32[1,1,64,128]{3,2,1,0:T(8,128)S(1)}, f32[1,1,64,128]{3,2,1,0:T(8,128)S(1)}, u32[]{:S(2)}, u32[]{:S(2)}) collective-permute-start(f32[1,1,64,128]{3,2,1,0:T(8,128)S(1)} %get-tuple-element.84), channel_id=1, source_target_pairs={{1,0},{2,1},{3,2},{4,3},{5,4},{6,5},{7,6},{8,7},{9,8},{10,9},{11,1... | collective-permute-start | bytes 98312 | tf_op jit(solution)/shard_map/ppermute | solution.py:20
  188.9 4.4 %collective-permute-start.12 = (f32[1,1,32,64]{3,2,1,0:T(8,128)S(1)}, f32[1,1,32,64]{3,2,1,0:T(8,128)S(1)}, u32[]{:S(2)}, u32[]{:S(2)}) collective-permute-start(f32[1,1,32,64]{3,2,1,0:T(8,128)S(1)} %fusion.187), channel_id=1, source_target_pairs={{1,0},{2,1},{3,2},{4,3},{5,4},{6,5},{7,6},{8,7},{9,8},{10,9},{11,1... | collective-permute-start | bytes 24584 | tf_op jit(solution)/shard_map/ppermute | solution.py:20
  195.8 6.0 %collective-permute-start.14 = (f32[1,1,64,128]{3,2,1,0:T(8,128)S(1)}, f32[1,1,64,128]{3,2,1,0:T(8,128)S(1)}, u32[]{:S(2)}, u32[]{:S(2)}) collective-permute-start(f32[1,1,64,128]{3,2,1,0:T(8,128)S(1)} %get-tuple-element.74), channel_id=1, source_target_pairs={{1,0},{2,1},{3,2},{4,3},{5,4},{6,5},{7,6},{8,7},{9,8},{10,9},{11,1... | collective-permute-start | bytes 98312 | tf_op jit(solution)/shard_map/ppermute | solution.py:20
  197.1 5.4 %collective-permute-start.15 = (f32[1,1,64,128]{3,2,1,0:T(8,128)S(1)}, f32[1,1,64,128]{3,2,1,0:T(8,128)S(1)}, u32[]{:S(2)}, u32[]{:S(2)}) collective-permute-start(f32[1,1,64,128]{3,2,1,0:T(8,128)S(1)} %get-tuple-element.75), channel_id=1, source_target_pairs={{0,1},{1,2},{2,3},{3,4},{4,5},{5,6},{6,7},{7,8},{8,9},{9,10},{10,1... | collective-permute-start | bytes 98312 | tf_op jit(solution)/shard_map/ppermute | solution.py:19
  241.9 4.4 %collective-permute-start.26 = (f32[1,1,64,128]{3,2,1,0:T(8,128)S(1)}, f32[1,1,64,128]{3,2,1,0:T(8,128)S(1)}, u32[]{:S(2)}, u32[]{:S(2)}) collective-permute-start(f32[1,1,64,128]{3,2,1,0:T(8,128)S(1)} %get-tuple-element.66), channel_id=1, source_target_pairs={{1,0},{2,1},{3,2},{4,3},{5,4},{6,5},{7,6},{8,7},{9,8},{10,9},{11,1... | collective-permute-start | bytes 98312 | tf_op jit(solution)/shard_map/ppermute | solution.py:20
  250.9 4.5 %collective-permute-start.28 = (f32[1,1,32,64]{3,2,1,0:T(8,128)S(1)}, f32[1,1,32,64]{3,2,1,0:T(8,128)S(1)}, u32[]{:S(2)}, u32[]{:S(2)}) collective-permute-start(f32[1,1,32,64]{3,2,1,0:T(8,128)S(1)} %fusion.177), channel_id=1, source_target_pairs={{1,0},{2,1},{3,2},{4,3},{5,4},{6,5},{7,6},{8,7},{9,8},{10,9},{11,1... | collective-permute-start | bytes 24584 | tf_op jit(solution)/shard_map/ppermute | solution.py:20
  257.8 6.0 %collective-permute-start.30 = (f32[1,1,64,128]{3,2,1,0:T(8,128)S(1)}, f32[1,1,64,128]{3,2,1,0:T(8,128)S(1)}, u32[]{:S(2)}, u32[]{:S(2)}) collective-permute-start(f32[1,1,64,128]{3,2,1,0:T(8,128)S(1)} %get-tuple-element.56), channel_id=1, source_target_pairs={{1,0},{2,1},{3,2},{4,3},{5,4},{6,5},{7,6},{8,7},{9,8},{10,9},{11,1... | collective-permute-start | bytes 98312 | tf_op jit(solution)/shard_map/ppermute | solution.py:20
  259.1 5.4 %collective-permute-start.31 = (f32[1,1,64,128]{3,2,1,0:T(8,128)S(1)}, f32[1,1,64,128]{3,2,1,0:T(8,128)S(1)}, u32[]{:S(2)}, u32[]{:S(2)}) collective-permute-start(f32[1,1,64,128]{3,2,1,0:T(8,128)S(1)} %get-tuple-element.57), channel_id=1, source_target_pairs={{0,1},{1,2},{2,3},{3,4},{4,5},{5,6},{6,7},{7,8},{8,9},{9,10},{10,1... | collective-permute-start | bytes 98312 | tf_op jit(solution)/shard_map/ppermute | solution.py:19
  301.8 8.7 %collective-permute-start.16 = (f32[1,1,64,128]{3,2,1,0:T(8,128)S(1)}, f32[1,1,64,128]{3,2,1,0:T(8,128)S(1)}, u32[]{:S(2)}, u32[]{:S(2)}) collective-permute-start(f32[1,1,64,128]{3,2,1,0:T(8,128)S(1)} %get-tuple-element.44), channel_id=1, source_target_pairs={{1,0},{2,1},{3,2},{4,3},{5,4},{6,5},{7,6},{8,7},{9,8},{10,9},{11,1... | collective-permute-start | bytes 98312 | tf_op jit(solution)/shard_map/ppermute | solution.py:20
  303.1 7.4 %collective-permute-start.17 = (f32[1,1,64,128]{3,2,1,0:T(8,128)S(1)}, f32[1,1,64,128]{3,2,1,0:T(8,128)S(1)}, u32[]{:S(2)}, u32[]{:S(2)}) collective-permute-start(f32[1,1,64,128]{3,2,1,0:T(8,128)S(1)} %get-tuple-element.45), channel_id=1, source_target_pairs={{0,1},{1,2},{2,3},{3,4},{4,5},{5,6},{6,7},{7,8},{8,9},{9,10},{10,1... | collective-permute-start | bytes 98312 | tf_op jit(solution)/shard_map/ppermute | solution.py:19
  306.1 5.8 %collective-permute-start.32 = (f32[1,1,64,128]{3,2,1,0:T(8,128)S(1)}, f32[1,1,64,128]{3,2,1,0:T(8,128)S(1)}, u32[]{:S(2)}, u32[]{:S(2)}) collective-permute-start(f32[1,1,64,128]{3,2,1,0:T(8,128)S(1)} %get-tuple-element.50), channel_id=1, source_target_pairs={{1,0},{2,1},{3,2},{4,3},{5,4},{6,5},{7,6},{8,7},{9,8},{10,9},{11,1... | collective-permute-start | bytes 98312 | tf_op jit(solution)/shard_map/ppermute | solution.py:20
  307.4 4.5 %collective-permute-start.33 = (f32[1,1,64,128]{3,2,1,0:T(8,128)S(1)}, f32[1,1,64,128]{3,2,1,0:T(8,128)S(1)}, u32[]{:S(2)}, u32[]{:S(2)}) collective-permute-start(f32[1,1,64,128]{3,2,1,0:T(8,128)S(1)} %get-tuple-element.51), channel_id=1, source_target_pairs={{0,1},{1,2},{2,3},{3,4},{4,5},{5,6},{6,7},{7,8},{8,9},{9,10},{10,1... | collective-permute-start | bytes 98312 | tf_op jit(solution)/shard_map/ppermute | solution.py:19
  347.3 4.5 %collective-permute-start.34 = (f32[2,2,1,64,128]{4,3,2,1,0:T(8,128)S(1)}, f32[2,2,1,64,128]{4,3,2,1,0:T(8,128)S(1)}, u32[]{:S(2)}, u32[]{:S(2)}) collective-permute-start(f32[2,2,1,64,128]{4,3,2,1,0:T(8,128)S(1)} %get-tuple-element.32), channel_id=1, source_target_pairs={{1,0},{2,1},{3,2},{4,3},{5,4},{6,5},{7,6},{8,7},{9,8},{10,9},{11,1... | collective-permute-start | bytes 393224 | tf_op jit(solution)/shard_map/ppermute | solution.py:20
  (10 other events, 238.6 us)
Sparse Core Ops, SparseCore 0:
  353.6 9.9 reduce-scatter.1
where the time goes:
time: 373 us; the launch traced here: 370 us
  blocking collectives  130 us (35%)
  starting transfers between devices  96.6 us (26%)
  local copies, waits for them, and re-layouts  52.8 us (14%)
  other arithmetic  51.5 us (14%)
  between operations  23.8 us (6%)
  waiting for transfers between devices  15.3 us (4%)
    psum x3, blocking collectives, norm_sum(): return lax.psum(cell_sums(residual * precond), 'space')  98.9 us
    ppermute x18, starting transfers between devices, extended(): before = lax.ppermute(last, axis, up)  73.3 us
    reshape x6, local copies, waits for them, and re-layouts, coarse_pick(): blocks = faces.reshape(extent_x // 2, 2, extent_y // 2, 2, extent_z // 2, 2)  33.1 us
    psum x1, blocking collectives, solve(): curve = lax.psum(cell_sums(search * image_field), 'space')  31.4 us
    ppermute x18, starting transfers between devices, extended(): after = lax.ppermute(leading, axis, down)  23.3 us
    reduce_sum x6, other arithmetic, coarse_pick(): return jnp.sum(chosen, axis=(1, 3, 5))  14 us
    reduce_sum x5, other arithmetic, cell_sums(): return jnp.sum(values, axis=(1, 2, 3))  11.1 us
    reduce_scatter x1, waiting for transfers between devices, per_device(): lax.psum_scatter(local_term, 'pole', scatter_dimension=1, tiled=True)  9.4 us
  transfers between devices with their start and end apart: 37, of which 9 were waited for; matrix products, arithmetic and copies ran while one was open for 21% of the time, Pallas kernels for 0%

commit v1 on v0

--- a/solution.py
+++ b/solution.py
@@ -1,12 +1,16 @@
+import functools
+
 import jax
 import jax.numpy as jnp
 from jax import lax
+from jax.experimental import pallas as pl
+from jax.experimental.pallas import tpu as pltpu
 from jax.sharding import PartitionSpec as P
 
 ITERS = 2
-
-
 DAMPING = 0.8
+REPLICATED_CELLS = 32 * 64 * 128
+HALF = 64
 
 
 def extended(array, sides, width):
@@ -20,6 +24,408 @@
         after = lax.ppermute(leading, axis, down)
         array = jnp.concatenate([before, array, after], axis=dim)
     return array
+
+
+def lane_index(shape):
+    return lax.broadcasted_iota(jnp.int32, shape, len(shape) - 1)
+
+
+def row_index(shape):
+    return lax.broadcasted_iota(jnp.int32, shape, len(shape) - 2)
+
+
+def roll(block, shift, axis):
+    return pltpu.roll(block, shift % block.shape[axis], axis)
+
+
+def eights(block):
+    rows = block.shape[0]
+    total = block[0:8]
+    for start in range(8, rows, 8):
+        total = total + block[start : start + 8]
+    return total
+
+
+def slot_totals(acc):
+    line = jnp.sum(acc, axis=0, keepdims=True)
+    lane = lane_index(line.shape)
+    first = jnp.sum(jnp.where(lane < HALF, line, 0.0), axis=1, keepdims=True)
+    second = jnp.sum(jnp.where(lane < HALF, 0.0, line), axis=1, keepdims=True)
+    return jnp.where(lane < HALF, first, second)
+
+
+def solve_kernel(
+    place_ref,
+    shifts_ref,
+    weights_ref,
+    order_ref,
+    kappa_ref,
+    misfit_ref,
+    before_ref,
+    state_ref,
+    after_ref,
+    adjoint_ref,
+    share_ref,
+    half_kappa,
+    inner,
+    outer_x,
+    outer_y,
+    outer_z,
+    inner_sum,
+    diagonal,
+    damped,
+    coarse_off,
+    coarse_damped,
+    residual,
+    scaled,
+    partial,
+    first_dir,
+    second_dir,
+    image,
+    coarse_one,
+    coarse_two,
+    planes,
+):
+    coarse_x = kappa_ref.shape[0] // 2
+    rows = kappa_ref.shape[1] // 2
+    shape = (rows, 2 * HALF)
+    lane = lane_index(shape)
+    row = row_index(shape)
+    slot0 = lane_index((1, 2 * HALF)) < HALF
+
+    def pick(ref):
+        return jnp.where(slot0, ref[order_ref[0]], ref[order_ref[1]])
+
+    shift = pick(shifts_ref)
+    weight = pick(weights_ref)
+
+    def cls(a, b, c):
+        return 4 * a + 2 * b + c
+
+    classes = [(a, b, c) for a in (0, 1) for b in (0, 1) for c in (0, 1)]
+
+    zero = jnp.zeros(shape, jnp.float32)
+    for ref in (half_kappa, scaled, first_dir, second_dir):
+        for k in range(8):
+            ref[k, 0] = zero
+            ref[k, coarse_x + 1] = zero
+    for ref in (coarse_one, coarse_two):
+        ref[0] = zero
+        ref[coarse_x + 1] = zero
+
+    even_lane = 2 * (lane % HALF)
+
+    def split(ref, x, b):
+        block = ref[x, pl.ds(b, rows, stride=2), :]
+        even = jnp.take_along_axis(block, even_lane, axis=1)
+        odd = jnp.take_along_axis(block, even_lane + 1, axis=1)
+        return even, odd
+
+    def arrange(i, carry):
+        for a in (0, 1):
+            for b in (0, 1):
+                for c, value in enumerate(split(kappa_ref, 2 * i + a, b)):
+                    half_kappa[cls(a, b, c), i + 1] = 0.5 * value
+                for c, value in enumerate(split(misfit_ref, 2 * i + a, b)):
+                    residual[cls(a, b, c), i] = weight * value
+        return carry
+
+    lax.fori_loop(0, coarse_x, arrange, 0)
+
+    y_low = jnp.where(row > 0, 1.0, 0.0)
+    y_high = jnp.where(row < rows - 1, 1.0, 0.0)
+    z_low = jnp.where(lane % HALF > 0, 1.0, 0.0)
+    z_high = jnp.where(lane % HALF < HALF - 1, 1.0, 0.0)
+
+    def coefficients(i, carry):
+        x_low = jnp.where(i > 0, 1.0, 0.0)
+        kap = [half_kappa[k, i + 1] for k in range(8)]
+        total = [shift + zero for _ in range(8)]
+        inside = [zero for _ in range(8)]
+        coarse_total = 8.0 * shift + zero
+        cx = zero
+        cy = [zero, zero]
+        cz = [zero, zero]
+        for p in (0, 1):
+            for q in (0, 1):
+                for kind, low, high in (
+                    (0, cls(0, p, q), cls(1, p, q)),
+                    (1, cls(p, 0, q), cls(p, 1, q)),
+                    (2, cls(p, q, 0), cls(p, q, 1)),
+                ):
+                    face = kap[low] + kap[high]
+                    inner[4 * kind + 2 * p + q, i] = face
+                    inside[low] = inside[low] + face
+                    inside[high] = inside[high] + face
+                low, high = cls(0, p, q), cls(1, p, q)
+                minus = kap[low] + half_kappa[high, i]
+                plus = kap[high] + half_kappa[low, i + 2]
+                total[low] = total[low] + minus
+                total[high] = total[high] + plus
+                coarse_total = coarse_total + minus + plus
+                outer_x[2 * p + q, i] = x_low * minus
+                cx = cx + x_low * minus
+                low, high = cls(p, 0, q), cls(p, 1, q)
+                minus = kap[low] + y_low * roll(kap[high], 1, 0)
+                plus = kap[high] + y_high * roll(kap[low], -1, 0)
+                total[low] = total[low] + minus
+                total[high] = total[high] + plus
+                coarse_total = coarse_total + minus + plus
+                minus, plus = y_low * minus, y_high * plus
+                outer_y[2 * p + q, i] = minus
+                outer_y[4 + 2 * p + q, i] = plus
+                cy = [cy[0] + minus, cy[1] + plus]
+                low, high = cls(p, q, 0), cls(p, q, 1)
+                minus = kap[low] + z_low * roll(kap[high], 1, 1)
+                plus = kap[high] + z_high * roll(kap[low], -1, 1)
+                total[low] = total[low] + minus
+                total[high] = total[high] + plus
+                coarse_total = coarse_total + minus + plus
+                minus, plus = z_low * minus, z_high * plus
+                outer_z[2 * p + q, i] = minus
+                outer_z[4 + 2 * p + q, i] = plus
+                cz = [cz[0] + minus, cz[1] + plus]
+        for k in range(8):
+            inner_sum[k, i] = inside[k]
+            diag = total[k] + inside[k]
+            diagonal[k, i] = diag
+            inverse = DAMPING / diag
+            damped[k, i] = inverse
+            scaled[k, i + 1] = inverse * residual[k, i]
+        coarse_off[0, i] = cx
+        coarse_off[1, i] = cy[0]
+        coarse_off[2, i] = cy[1]
+        coarse_off[3, i] = cz[0]
+        coarse_off[4, i] = cz[1]
+        coarse_damped[i] = DAMPING / coarse_total
+        return carry
+
+    lax.fori_loop(0, coarse_x, coefficients, 0)
+    for k in range(4):
+        outer_x[k, coarse_x] = zero
+    coarse_off[0, coarse_x] = zero
+
+    def neighbours(field, a, b, c, i):
+        k = cls(a, b, c)
+        out = inner[2 * b + c, i] * field[cls(1 - a, b, c), i + 1]
+        out = out + inner[4 + 2 * a + c, i] * field[cls(a, 1 - b, c), i + 1]
+        out = out + inner[8 + 2 * a + b, i] * field[cls(a, b, 1 - c), i + 1]
+        out = out + outer_x[2 * b + c, i + a] * field[cls(1 - a, b, c), i + 2 * a]
+        out = out + outer_y[4 * b + 2 * a + c, i] * roll(
+            field[cls(a, 1 - b, c), i + 1], 1 - 2 * b, 0
+        )
+        out = out + outer_z[4 * c + 2 * a + b, i] * roll(
+            field[cls(a, b, 1 - c), i + 1], 1 - 2 * c, 1
+        )
+        return out
+
+    def coarse_neighbours(field, i):
+        here = field[i + 1]
+        out = coarse_off[0, i] * field[i]
+        out = out + coarse_off[0, i + 1] * field[i + 2]
+        out = out + coarse_off[1, i] * roll(here, 1, 0)
+        out = out + coarse_off[2, i] * roll(here, -1, 0)
+        out = out + coarse_off[3, i] * roll(here, 1, 1)
+        out = out + coarse_off[4, i] * roll(here, -1, 1)
+        return out
+
+    def precondition(result):
+        def down(i, carry):
+            rhs = zero
+            for a, b, c in classes:
+                k = cls(a, b, c)
+                res = residual[k, i]
+                part = res + neighbours(scaled, a, b, c, i)
+                partial[k, i] = part
+                rhs = rhs + (part - DAMPING * res)
+            coarse_one[i + 1] = coarse_damped[i] * rhs
+            return carry
+
+        lax.fori_loop(0, coarse_x, down, 0)
+
+        def smooth(i, carry):
+            coarse_two[i + 1] = (2.0 - DAMPING) * coarse_one[
+                i + 1
+            ] + coarse_damped[i] * coarse_neighbours(coarse_one, i)
+            return carry
+
+        lax.fori_loop(0, coarse_x, smooth, 0)
+
+        def up(i, acc):
+            here = coarse_two[i + 1]
+            sides = (
+                (coarse_two[i], coarse_two[i + 2]),
+                (roll(here, 1, 0), roll(here, -1, 0)),
+                (roll(here, 1, 1), roll(here, -1, 1)),
+            )
+            for a, b, c in classes:
+                k = cls(a, b, c)
+                value = partial[k, i] + inner_sum[k, i] * here
+                value = value + outer_x[2 * b + c, i + a] * sides[0][a]
+                value = value + outer_y[4 * b + 2 * a + c, i] * sides[1][b]
+                value = value + outer_z[4 * c + 2 * a + b, i] * sides[2][c]
+                new = (1.0 - DAMPING) * (scaled[k, i + 1] + here) + damped[k, i] * value
+                result[k, i + 1] = new
+                acc = acc + eights(residual[k, i] * new)
+            return acc
+
+        return lax.fori_loop(0, coarse_x, up, jnp.zeros((8, 2 * HALF), jnp.float32))
+
+    def curvature(field, keep):
+        def step(i, acc):
+            for a, b, c in classes:
+                k = cls(a, b, c)
+                here = field[k, i + 1]
+                value = diagonal[k, i] * here - neighbours(field, a, b, c, i)
+                if keep:
+                    image[k, i] = value
+                acc = acc + eights(here * value)
+            return acc
+
+        return lax.fori_loop(0, coarse_x, step, jnp.zeros((8, 2 * HALF), jnp.float32))
+
+    gamma = slot_totals(precondition(first_dir))
+    step_one = gamma / slot_totals(curvature(first_dir, True))
+
+    def update(i, carry):
+        for k in range(8):
+            new = residual[k, i] - step_one * image[k, i]
+            residual[k, i] = new
+            scaled[k, i + 1] = damped[k, i] * new
+        return carry
+
+    lax.fori_loop(0, coarse_x, update, 0)
+
+    gamma_next = slot_totals(precondition(second_dir))
+    ratio = gamma_next / gamma
+
+    def turn(i, carry):
+        for k in range(8):
+            second_dir[k, i + 1] = second_dir[k, i + 1] + ratio * first_dir[k, i + 1]
+        return carry
+
+    lax.fori_loop(0, coarse_x, turn, 0)
+    step_two = gamma_next / slot_totals(curvature(second_dir, False))
+
+    own = adjoint_ref.shape[1]
+    start = place_ref[0] * (own // 2)
+    even = lane % 2 == 0
+    for j in range(own + 2):
+        a = (j + 1) % 2
+        spot = start + (j + 1) // 2
+        for b in (0, 1):
+            pair = []
+            for c in (0, 1):
+                k = cls(a, b, c)
+                pair.append(
+                    step_one * first_dir[k, spot] + step_two * second_dir[k, spot]
+                )
+            for slot in (0, 1):
+                source = lane // 2 + HALF * slot
+                value = jnp.where(
+                    even,
+                    jnp.take_along_axis(pair[0], source, axis=1),
+                    jnp.take_along_axis(pair[1], source, axis=1),
+                )
+                planes[slot, j, pl.ds(b, rows, stride=2), :] = value
+
+    full = (2 * rows, 2 * HALF)
+    y_at = row_index(full)
+    z_at = lane_index(full)
+
+    def drop(value, axis, up):
+        moved = roll(value, -1 if up else 1, axis)
+        at = (y_at, z_at)[axis]
+        edge = full[axis] - 1 if up else 0
+        return value - jnp.where(at == edge, 0.0, moved)
+
+    groups = share_ref.shape[0]
+    chunk = share_ref.shape[2]
+    for j in range(own):
+        term = jnp.zeros(full, jnp.float32)
+        for slot in (0, 1):
+            here = planes[slot, j + 1]
+            adjoint_ref[slot, j] = here
+            f = state_ref[slot, j]
+            f_low = state_ref[slot, j - 1] if j else before_ref[slot, 0]
+            f_high = state_ref[slot, j + 1] if j + 1 < own else after_ref[slot, 0]
+            term = term + (here - planes[slot, j + 2]) * (f - f_high)
+            term = term + (here - planes[slot, j]) * (f - f_low)
+            for axis in (0, 1):
+                for up in (True, False):
+                    term = term + drop(here, axis, up) * drop(f, axis, up)
+        planes[0, j] = -0.5 * term
+        for k in range(groups):
+            at = lax.rem(place_ref[1] + k, groups) * chunk
+            share_ref[k, j] = planes[0, j, pl.ds(pl.multiple_of(at, chunk), chunk), :]
+
+
+def whole_grid(conductivity, misfit, forward_states, pole_shifts, pole_weights, pole_order):
+    members, own, ny, nz = forward_states.shape
+    groups = lax.axis_size("pole")
+    place = jnp.stack([lax.axis_index("space"), lax.axis_index("pole")]).astype(jnp.int32)
+    peers = lax.axis_size("space")
+    up = [(i, i + 1) for i in range(peers - 1)]
+    down = [(i + 1, i) for i in range(peers - 1)]
+    before = lax.ppermute(forward_states[:, own - 1 :], "space", up)
+    after = lax.ppermute(forward_states[:, :1], "space", down)
+    kappa = lax.all_gather(conductivity, "space", axis=0, tiled=True)
+    source = lax.all_gather(misfit, "space", axis=0, tiled=True)
+    coarse_x, rows = kappa.shape[0] // 2, ny // 2
+    lanes = 2 * HALF
+
+    def scratch(count, extent):
+        return pltpu.VMEM((count, extent, rows, lanes), jnp.float32)
+
+    smem = pl.BlockSpec(memory_space=pltpu.SMEM)
+    vmem = pl.BlockSpec(memory_space=pltpu.VMEM)
+    adjoint, share = pl.pallas_call(
+        solve_kernel,
+        out_shape=(
+            jax.ShapeDtypeStruct(forward_states.shape, jnp.float32),
+            jax.ShapeDtypeStruct((groups, own, ny // groups, nz), jnp.float32),
+        ),
+        in_specs=[smem] * 4 + [vmem] * 5,
+        out_specs=(vmem, vmem),
+        scratch_shapes=[
+            scratch(8, coarse_x + 2),
+            scratch(12, coarse_x),
+            scratch(4, coarse_x + 1),
+            scratch(8, coarse_x),
+            scratch(8, coarse_x),
+            scratch(8, coarse_x),
+            scratch(8, coarse_x),
+            scratch(8, coarse_x),
+            scratch(5, coarse_x + 1),
+            pltpu.VMEM((coarse_x, rows, lanes), jnp.float32),
+            scratch(8, coarse_x),
+            scratch(8, coarse_x + 2),
+            scratch(8, coarse_x),
+            scratch(8, coarse_x + 2),
+            scratch(8, coarse_x + 2),
+            scratch(8, coarse_x),
+            pltpu.VMEM((coarse_x + 2, rows, lanes), jnp.float32),
+            pltpu.VMEM((coarse_x + 2, rows, lanes), jnp.float32),
+            pltpu.VMEM((members, own + 2, ny, nz), jnp.float32),
+        ],
+        compiler_params=pltpu.CompilerParams(vmem_limit_bytes=48 * 1024 * 1024),
+        name="solve",
+    )(
+        place,
+        pole_shifts,
+        pole_weights,
+        pole_order,
+        kappa,
+        source,
+        before,
+        forward_states,
+        after,
+    )
+    gradient = share[0]
+    for k in range(1, groups):
+        ring = [(i, (i + k) % groups) for i in range(groups)]
+        gradient = gradient + lax.ppermute(share[k], "pole", ring)
+    return adjoint, gradient
 
 
 def plus_side(field, which_dim):
@@ -125,7 +531,7 @@
     return iterate
 
 
-def per_device(conductivity, misfit, forward_states, pole_shifts, pole_weights, pole_order):
+def divided(conductivity, misfit, forward_states, pole_shifts, pole_weights, pole_order):
     widened_kappa = extended(conductivity, (("space", 0),), 1)
     plus_faces = [
         0.5 * (conductivity + widened_kappa[2:]),
@@ -204,6 +610,15 @@
         P("pole"),
     )
     out_specs = (P("pole", "space", None, None), P("space", "pole", None))
+
+    def body(conductivity, misfit, forward_states, *poles):
+        nx = conductivity.shape[0] * lax.axis_size("space")
+        _, ny, nz = conductivity.shape
+        small = nx * ny * nz <= REPLICATED_CELLS
+        if small and forward_states.shape[0] == 2 and nz == 2 * HALF:
+            return whole_grid(conductivity, misfit, forward_states, *poles)
+        return divided(conductivity, misfit, forward_states, *poles)
+
     return jax.shard_map(
-        per_device, mesh=mesh, in_specs=in_specs, out_specs=out_specs, check_vma=False
-    )
+        body, mesh=mesh, in_specs=in_specs, out_specs=out_specs, check_vma=False
+    )

time: 373 us -> 125 us (0.34)
  blocking collectives: 130 us -> 0 us
  starting transfers between devices: 96.6 us -> 5.88 us
  waiting for transfers between devices: 15.3 us -> 79.7 us
  other arithmetic: 51.5 us -> 0.7 us
  local copies, waits for them, and re-layouts: 52.8 us -> 3.39 us
  Pallas kernels: 0 us -> 20.9 us
  between operations: 23.8 us -> 14.1 us
    psum x4 -> x0, blocking collectives: 130 us -> none  [the longest x3 98.9 us: norm_sum(): return lax.psum(cell_sums(residual * precond), 'space')]
    ppermute x36 -> x3, starting transfers between devices: 96.6 us -> 5.8 us  [the longest x1 3.03 us: whole_grid(): before = lax.ppermute(forward_states[:, own - 1:], 'space', up)]
    all_gather x0 -> x2, waiting for transfers between devices: none -> 75.1 us  [the longest x1 39 us: whole_grid(): source = lax.all_gather(misfit, 'space', axis=0, tiled=True)]
    reduce_sum x21 -> x0, other arithmetic: 33.9 us -> none  [the longest x6 14 us: coarse_pick(): return jnp.sum(chosen, axis=(1, 3, 5))]
    reshape x6 -> x0, local copies, waits for them, and re-layouts: 33.1 us -> none  [coarse_pick(): blocks = faces.reshape(extent_x // 2, 2, extent_y // 2, 2, extent_z // 2, 2)]
    pallas_call x0 -> x1, Pallas kernels: none -> 20.9 us  [whole_grid(): pl.pallas_call(solve_kernel, out_shape=(jax.ShapeDtypeStruct(forward_stat...]
    slice x50 -> x1, local copies, waits for them, and re-layouts: 10.6 us -> 0.92 us  [whole_grid(): after = lax.ppermute(forward_states[:, :1], 'space', down)]
    reduce_scatter x1 -> x0, waiting for transfers between devices: 9.4 us -> none  [per_device(): lax.psum_scatter(local_term, 'pole', scatter_dimension=1, tiled=True)]
  transfers between devices with their start and end apart: 37 -> 5, of which waited for: 9 -> 4; matrix products, arithmetic and copies ran while one was open for 21% -> 1% of each run, Pallas kernels for 0% -> 0%
where the time goes in v1:
time: 125 us
  waiting for transfers between devices  79.7 us (64%)
  Pallas kernels  20.9 us (17%)
  between operations  14.1 us (11%)
  starting transfers between devices  5.88 us (5%)
  local copies, waits for them, and re-layouts  3.39 us (3%)
    all_gather x1, waiting for transfers between devices, whole_grid(): source = lax.all_gather(misfit, 'space', axis=0, tiled=True)  39 us
    all_gather x1, waiting for transfers between devices, whole_grid(): kappa = lax.all_gather(conductivity, 'space', axis=0, tiled=True)  36 us
    pallas_call x1, Pallas kernels, whole_grid(): pl.pallas_call(solve_kernel, out_shape=(jax.ShapeDtypeStruct(forward_stat...  20.9 us
    ppermute x1, starting transfers between devices, whole_grid(): before = lax.ppermute(forward_states[:, own - 1:], 'space', up)  3.03 us
  transfers between devices with their start and end apart: 5, of which 4 were waited for; matrix products, arithmetic and copies ran while one was open for 1% of the time, Pallas kernels for 0%

profile of v1, /device:TPU:0, one launch (start us, length us, event | category | flops | bytes accessed | tf_op | source)
XLA Modules:
  0.0 124.6 jit_solution(11736161774127001662)
XLA Ops:
  7.2 0.0 all-gather.3.cloned.1.call-start
  7.2 0.7 all-gather.3.cloned.1.call-update
  7.9 0.0 all-gather.5.cloned.1.call-start
  7.9 0.7 all-gather.5.cloned.1.call-update
  8.6 0.0 copy-start.2
  8.7 0.9 fusion
  9.6 1.3 %collective-permute-start.1 = (f32[2,1,64,128]{3,2,1,0:T(8,128)S(1)}, f32[2,1,64,128]{3,2,1,0:T(8,128)S(1)}, u32[]{:S(2)}, u32[]{:S(2)}) collective-permute-start(f32[2,1,64,128]{3,2,1,0:T(8,128)S(1)} %get-tuple-element.6), channel_id=1, source_target_pairs={{1,0},{2,1},{3,2},{4,3},{5,4},{6,5},{7,6},{8,7},{9,8},{10,9},{11,1... | collective-permute-start | bytes 196616 | tf_op jit(solution)/shard_map/ppermute | solution.py:371
  10.9 3.0 %collective-permute-start = (f32[2,1,64,128]{3,2,1,0:T(8,128)S(1)}, f32[2,1,64,128]{3,2,1,0:T(8,128)S(1)}, u32[]{:S(2)}, u32[]{:S(2)}) collective-permute-start(f32[2,1,64,128]{3,2,1,0:T(8,128)S(1)} %get-tuple-element.7), channel_id=1, source_target_pairs={{0,1},{1,2},{2,3},{3,4},{4,5},{5,6},{6,7},{7,8},{8,9},{9,10},{10,1... | collective-permute-start | bytes 196616 | tf_op jit(solution)/shard_map/ppermute | solution.py:370
  13.9 0.0 copy-start.3
  13.9 0.0 copy-start.4
  14.0 0.0 copy-start.5
  14.0 0.1 pad_add_fusion.place_ref
  14.0 0.0 collective-permute-done.1.after_ref
  14.0 0.8 collective-permute-done.before_ref
  14.8 36.0 %all-gather.3.cloned.1.call-done.kappa_ref = f32[32,64,128]{2,1,0:T(8,128)} async-done(((f32[2,64,128]{2,1,0:T(8,128)}), f32[32,64,128]{2,1,0:T(8,128)}) %all-gather.3.cloned.1.call-update) | async-done | bytes 1048592 | tf_op jit(solution)/shard_map/all_gather | solution.py:372
  50.8 39.0 %all-gather.5.cloned.1.call-done.misfit_ref = f32[32,64,128]{2,1,0:T(8,128)} async-done(((f32[2,64,128]{2,1,0:T(8,128)}), f32[32,64,128]{2,1,0:T(8,128)}) %all-gather.5.cloned.1.call-update) | async-done | bytes 1048592 | tf_op jit(solution)/shard_map/all_gather | solution.py:373
  89.9 0.0 copy-done.2
  89.9 0.0 copy-done.3
  89.9 0.0 copy-done.4
  89.9 0.0 copy-done.5
  89.9 0.0 copy-start
  89.9 1.2 copy-done
  91.1 0.0 copy-start.1
  91.1 1.2 copy-done.1
  92.3 20.9 %solve.1 = (f32[2,2,64,128]{3,2,1,0:T(8,128)}, f32[2,2,32,128]{3,2,1,0:T(8,128)S(1)}) custom-call(s32[2]{0:T(128)S(1)} %pad_add_fusion.place_ref, f32[4]{0:T(128)S(1)} %copy-done.3, f32[4]{0:T(128)S(1)} %copy-done.4, s32[2]{0:T(128)S(1)} %copy-done.5, f32[32,64,128]{2,1,0:T(8,128)S(1)} %copy-done, f32[32,64,128]{2,1,0:T(8,128)S(1)} %copy-done.1, ...), custom_call_target="tpu_custom_call" | custom-call | tf_op jit(solution)/shard_map/solve/pallas_call | solution.py:382
  113.2 1.5 %collective-permute-start.2 = (f32[2,32,128]{2,1,0:T(8,128)S(1)}, f32[2,32,128]{2,1,0:T(8,128)S(1)}, u32[]{:S(2)}, u32[]{:S(2)}) collective-permute-start(f32[2,32,128]{2,1,0:T(8,128)S(1)} %slice_bitcast_fusion), channel_id=1, source_target_pairs={{0,16},{16,0},{1,17},{17,1},{2,18},{18,2},{3,19},{19,3},{4,20},{20... | collective-permute-start | bytes 98312 | tf_op jit(solution)/shard_map/ppermute | solution.py:427
  114.7 2.4 %collective-permute-done.2 = f32[2,32,128]{2,1,0:T(8,128)S(1)} collective-permute-done((f32[2,32,128]{2,1,0:T(8,128)S(1)}, f32[2,32,128]{2,1,0:T(8,128)S(1)}, u32[]{:S(2)}, u32[]{:S(2)}) %collective-permute-start.2) | collective-permute-done | bytes 32800 | tf_op jit(solution)/shard_map/ppermute | solution.py:427
  117.2 0.6 bitcast_add_fusion
  (1 shorter events, 0.0 us)
Async XLA Ops:
  7.2 43.7 %all-gather.3.cloned.1.call-start = ((), (), s32[]{:S(2)}) async-start(), calls=%async_computation | async-start | bytes 1114112 | tf_op jit(solution)/shard_map/all_gather | solution.py:372
  7.9 82.0 %all-gather.5.cloned.1.call-start = ((), (), s32[]{:S(2)}) async-start(), calls=%async_computation.1 | async-start | bytes 1114112 | tf_op jit(solution)/shard_map/all_gather | solution.py:373
  8.6 81.2 %copy-start.2 = (f32[2,2,64,128]{3,2,1,0:T(8,128)S(1)}, f32[2,2,64,128]{3,2,1,0:T(8,128)}, u32[]{:S(2)}) copy-start(f32[2,2,64,128]{3,2,1,0:T(8,128)} %state_ref.1) | copy-start | bytes 393220
  9.6 4.5 %collective-permute-start.1 = (f32[2,1,64,128]{3,2,1,0:T(8,128)S(1)}, f32[2,1,64,128]{3,2,1,0:T(8,128)S(1)}, u32[]{:S(2)}, u32[]{:S(2)}) collective-permute-start(f32[2,1,64,128]{3,2,1,0:T(8,128)S(1)} %get-tuple-element.6), channel_id=1, source_target_pairs={{1,0},{2,1},{3,2},{4,3},{5,4},{6,5},{7,6},{8,7},{9,8},{10,9},{11,1... | collective-permute-start | bytes 196616 | tf_op jit(solution)/shard_map/ppermute | solution.py:371
  10.9 3.9 %collective-permute-start = (f32[2,1,64,128]{3,2,1,0:T(8,128)S(1)}, f32[2,1,64,128]{3,2,1,0:T(8,128)S(1)}, u32[]{:S(2)}, u32[]{:S(2)}) collective-permute-start(f32[2,1,64,128]{3,2,1,0:T(8,128)S(1)} %get-tuple-element.7), channel_id=1, source_target_pairs={{0,1},{1,2},{2,3},{3,4},{4,5},{5,6},{6,7},{7,8},{8,9},{9,10},{10,1... | collective-permute-start | bytes 196616 | tf_op jit(solution)/shard_map/ppermute | solution.py:370
  13.9 76.0 %copy-start.3 = (f32[4]{0:T(128)S(1)}, f32[4]{0:T(128)}, u32[]{:S(2)}) copy-start(f32[4]{0:T(128)} %shifts_ref.1) | copy-start | bytes 52
  13.9 75.9 %copy-start.4 = (f32[4]{0:T(128)S(1)}, f32[4]{0:T(128)}, u32[]{:S(2)}) copy-start(f32[4]{0:T(128)} %weights_ref.1) | copy-start | bytes 52
  14.0 75.9 %copy-start.5 = (s32[2]{0:T(128)S(1)}, s32[2]{0:T(128)}, u32[]{:S(2)}) copy-start(s32[2]{0:T(128)} %order_ref.1) | copy-start | bytes 28
  89.9 1.2 copy-start
  91.1 1.2 copy-start.1
  113.2 3.9 %collective-permute-start.2 = (f32[2,32,128]{2,1,0:T(8,128)S(1)}, f32[2,32,128]{2,1,0:T(8,128)S(1)}, u32[]{:S(2)}, u32[]{:S(2)}) collective-permute-start(f32[2,32,128]{2,1,0:T(8,128)S(1)} %slice_bitcast_fusion), channel_id=1, source_target_pairs={{0,16},{16,0},{1,17},{17,1},{2,18},{18,2},{3,19},{19,3},{4,20},{20... | collective-permute-start | bytes 98312 | tf_op jit(solution)/shard_map/ppermute | solution.py:427
Sparse Core Ops, SparseCore 0:
  10.2 40.6 all-gather.2
  53.0 36.8 all-gather.4

commit v2 on v1

--- a/solution.py
+++ b/solution.py
@@ -54,13 +54,41 @@
     return jnp.where(lane < HALF, first, second)
 
 
+def swap_masks(peers):
+    even = []
+    mask = peers // 2
+    while mask > 1:
+        even.append(mask)
+        mask //= 2
+    odd = even[-1:] + even[:-1]
+    return even, odd
+
+
+def offset_of(t, parity, peers):
+    even, odd = swap_masks(peers)
+    offset = jnp.int32(0)
+    for step, (mask_even, mask_odd) in enumerate(zip(even, odd)):
+        mask = jnp.where(parity == 0, mask_even, mask_odd)
+        offset = offset ^ (((t >> step) & 1) * mask)
+    return offset
+
+
+def gather_blocks(block, axis):
+    peers = lax.axis_size(axis)
+    held = block[None]
+    for masks in zip(*swap_masks(peers)):
+        pairs = [(i, i ^ masks[i % 2]) for i in range(peers)]
+        held = jnp.concatenate([held, lax.ppermute(held, axis, pairs)], axis=0)
+    return held, lax.ppermute(held, axis, [(i, i ^ 1) for i in range(peers)])
+
+
 def solve_kernel(
     place_ref,
     shifts_ref,
     weights_ref,
     order_ref,
-    kappa_ref,
-    misfit_ref,
+    mine_ref,
+    theirs_ref,
     before_ref,
     state_ref,
     after_ref,
@@ -86,8 +114,9 @@
     coarse_two,
     planes,
 ):
-    coarse_x = kappa_ref.shape[0] // 2
-    rows = kappa_ref.shape[1] // 2
+    blocks, _, own, rows, _ = mine_ref.shape
+    coarse_x = blocks * own
+    rows = rows // 2
     shape = (rows, 2 * HALF)
     lane = lane_index(shape)
     row = row_index(shape)
@@ -115,22 +144,26 @@
 
     even_lane = 2 * (lane % HALF)
 
-    def split(ref, x, b):
-        block = ref[x, pl.ds(b, rows, stride=2), :]
+    def split(ref, t, field, x, b):
+        block = ref[t, field, x, pl.ds(b, rows, stride=2), :]
         even = jnp.take_along_axis(block, even_lane, axis=1)
         odd = jnp.take_along_axis(block, even_lane + 1, axis=1)
         return even, odd
 
-    def arrange(i, carry):
-        for a in (0, 1):
-            for b in (0, 1):
-                for c, value in enumerate(split(kappa_ref, 2 * i + a, b)):
-                    half_kappa[cls(a, b, c), i + 1] = 0.5 * value
-                for c, value in enumerate(split(misfit_ref, 2 * i + a, b)):
-                    residual[cls(a, b, c), i] = weight * value
+    def arrange(t, carry):
+        for ref, holder in ((mine_ref, place_ref[0]), (theirs_ref, place_ref[0] ^ 1)):
+            home = holder ^ offset_of(t, holder % 2, 2 * blocks)
+            for x in range(own):
+                a = x % 2
+                spot = home * (own // 2) + x // 2
+                for b in (0, 1):
+                    for c, value in enumerate(split(ref, t, 0, x, b)):
+                        half_kappa[cls(a, b, c), spot + 1] = 0.5 * value
+                    for c, value in enumerate(split(ref, t, 1, x, b)):
+                        residual[cls(a, b, c), spot] = weight * value
         return carry
 
-    lax.fori_loop(0, coarse_x, arrange, 0)
+    lax.fori_loop(0, blocks, arrange, 0)
 
     y_low = jnp.where(row > 0, 1.0, 0.0)
     y_high = jnp.where(row < rows - 1, 1.0, 0.0)
@@ -369,9 +402,8 @@
     down = [(i + 1, i) for i in range(peers - 1)]
     before = lax.ppermute(forward_states[:, own - 1 :], "space", up)
     after = lax.ppermute(forward_states[:, :1], "space", down)
-    kappa = lax.all_gather(conductivity, "space", axis=0, tiled=True)
-    source = lax.all_gather(misfit, "space", axis=0, tiled=True)
-    coarse_x, rows = kappa.shape[0] // 2, ny // 2
+    mine, theirs = gather_blocks(jnp.stack([conductivity, misfit]), "space")
+    coarse_x, rows = peers * own // 2, ny // 2
     lanes = 2 * HALF
 
     def scratch(count, extent):
@@ -415,8 +447,8 @@
         pole_shifts,
         pole_weights,
         pole_order,
-        kappa,
-        source,
+        mine,
+        theirs,
         before,
         forward_states,
         after,
@@ -614,8 +646,9 @@
     def body(conductivity, misfit, forward_states, *poles):
         nx = conductivity.shape[0] * lax.axis_size("space")
         _, ny, nz = conductivity.shape
-        small = nx * ny * nz <= REPLICATED_CELLS
-        if small and forward_states.shape[0] == 2 and nz == 2 * HALF:
+        peers = lax.axis_size("space")
+        small = nx * ny * nz <= REPLICATED_CELLS and forward_states.shape[0] == 2
+        if small and nz == 2 * HALF and peers > 2 and peers & (peers - 1) == 0:
             return whole_grid(conductivity, misfit, forward_states, *poles)
         return divided(conductivity, misfit, forward_states, *poles)
 

time: 125 us -> 61.6 us (0.49)
  the two profiles are of different devices: /device:TPU:0 before, /device:TPU:12 now
where the time goes in v2:
time: 61.6 us; the launch traced here: 61.4 us
  waiting for transfers between devices  24.9 us (40%)
  Pallas kernels  20.4 us (33%)
  starting transfers between devices  13.5 us (22%)
  other arithmetic  1.74 us (3%)
  between operations  0.75 us (1%)
    pallas_call x1, Pallas kernels, whole_grid(): pl.pallas_call(solve_kernel, out_shape=(jax.ShapeDtypeStruct(forward_stat...  20.4 us
    ppermute x3, waiting for transfers between devices, gather_blocks(): held = jnp.concatenate([held, lax.ppermute(held, axis, pairs)], axis=0)  17.1 us
    ppermute x3, starting transfers between devices, gather_blocks(): held = jnp.concatenate([held, lax.ppermute(held, axis, pairs)], axis=0)  5.63 us
    ppermute x1, starting transfers between devices, whole_grid(): after = lax.ppermute(forward_states[:, :1], 'space', down)  5.41 us
    ppermute x1, waiting for transfers between devices, whole_grid(): before = lax.ppermute(forward_states[:, own - 1:], 'space', up)  4.44 us
    ppermute x1, waiting for transfers between devices, whole_grid(): gradient = gradient + lax.ppermute(share[k], 'pole', ring)  3.41 us
    ppermute x1, starting transfers between devices, whole_grid(): before = lax.ppermute(forward_states[:, own - 1:], 'space', up)  1.92 us
  transfers between devices with their start and end apart: 7, of which 5 were waited for; matrix products, arithmetic and copies ran while one was open for 0% of the time, Pallas kernels for 0%

profile of v2, /device:TPU:12, one launch (start us, length us, event | category | flops | bytes accessed | tf_op | source)
XLA Modules:
  0.0 61.4 jit_solution(10009334196099830014)
XLA Ops:
  0.6 0.9 %maximum_bitcast_fusion = f32[1,2,2,64,128]{4,3,2,1,0:T(8,128)S(1)} fusion(f32[1,2,64,128]{3,2,1,0:T(8,128)} %bitcast.10, f32[1,2,64,128]{3,2,1,0:T(8,128)} %bitcast.11), kind=kLoop, calls=%fused_computation.3 | loop fusion | flops 32768 | bytes 262144 | tf_op jit(solution)/shard_map/broadcast_in_dim | solution.py:78
  1.5 2.7 %collective-permute-start = (f32[1,2,2,64,128]{4,3,2,1,0:T(8,128)S(1)}, f32[1,2,2,64,128]{4,3,2,1,0:T(8,128)S(1)}, u32[]{:S(2)}, u32[]{:S(2)}) collective-permute-start(f32[1,2,2,64,128]{4,3,2,1,0:T(8,128)S(1)} %maximum_bitcast_fusion), channel_id=1, source_target_pairs={{0,8},{1,3},{2,10},{3,1},{4,12},{5,7},{6,14},{7,5},{8,0},{9,11},{1... | collective-permute-start | bytes 393224 | tf_op jit(solution)/shard_map/ppermute | solution.py:81
  4.2 3.8 %collective-permute-done = f32[1,2,2,64,128]{4,3,2,1,0:T(8,128)S(1)} collective-permute-done((f32[1,2,2,64,128]{4,3,2,1,0:T(8,128)S(1)}, f32[1,2,2,64,128]{4,3,2,1,0:T(8,128)S(1)}, u32[]{:S(2)}, u32[]{:S(2)}) %collective-permute-start) | collective-permute-done | bytes 131104 | tf_op jit(solution)/shard_map/ppermute | solution.py:81
  8.0 1.4 %collective-permute-start.1 = (f32[2,2,2,64,128]{4,3,2,1,0:T(8,128)S(1)}, f32[2,2,2,64,128]{4,3,2,1,0:T(8,128)S(1)}, u32[]{:S(2)}, u32[]{:S(2)}) collective-permute-start(f32[2,2,2,64,128]{4,3,2,1,0:T(8,128)S(1)} %pad_maximum_fusion.2), channel_id=1, source_target_pairs={{0,4},{1,9},{2,6},{3,11},{4,0},{5,13},{6,2},{7,15},{8,12},{9,1},{1... | collective-permute-start | bytes 786440 | tf_op jit(solution)/shard_map/ppermute | solution.py:81
  9.4 5.6 %collective-permute-done.1 = f32[2,2,2,64,128]{4,3,2,1,0:T(8,128)S(1)} collective-permute-done((f32[2,2,2,64,128]{4,3,2,1,0:T(8,128)S(1)}, f32[2,2,2,64,128]{4,3,2,1,0:T(8,128)S(1)}, u32[]{:S(2)}, u32[]{:S(2)}) %collective-permute-start.1) | collective-permute-done | bytes 262176 | tf_op jit(solution)/shard_map/ppermute | solution.py:81
  15.1 0.0 copy-start
  15.1 1.6 %collective-permute-start.2 = (f32[4,2,2,64,128]{4,3,2,1,0:T(8,128)S(1)}, f32[4,2,2,64,128]{4,3,2,1,0:T(8,128)S(1)}, u32[]{:S(2)}, u32[]{:S(2)}) collective-permute-start(f32[4,2,2,64,128]{4,3,2,1,0:T(8,128)S(1)} %pad_maximum_fusion.1), channel_id=1, source_target_pairs={{0,2},{1,5},{2,0},{3,7},{4,6},{5,1},{6,4},{7,3},{8,10},{9,13},{10,... | collective-permute-start | bytes 1572872 | tf_op jit(solution)/shard_map/ppermute | solution.py:81
  16.6 7.7 %collective-permute-done.2 = f32[4,2,2,64,128]{4,3,2,1,0:T(8,128)S(1)} collective-permute-done((f32[4,2,2,64,128]{4,3,2,1,0:T(8,128)S(1)}, f32[4,2,2,64,128]{4,3,2,1,0:T(8,128)S(1)}, u32[]{:S(2)}, u32[]{:S(2)}) %collective-permute-start.2) | collective-permute-done | bytes 524320 | tf_op jit(solution)/shard_map/ppermute | solution.py:81
  24.3 0.1 pad_maximum_fusion.mine_ref
  24.4 0.1 collective-permute-start.3
  24.5 0.0 copy-done
  24.5 5.4 %collective-permute-start.5 = (f32[2,1,64,128]{3,2,1,0:T(8,128)S(1)}, f32[2,1,64,128]{3,2,1,0:T(8,128)S(1)}, u32[]{:S(2)}, u32[]{:S(2)}) collective-permute-start(f32[2,1,64,128]{3,2,1,0:T(8,128)S(1)} %get-tuple-element.6), channel_id=1, source_target_pairs={{1,0},{2,1},{3,2},{4,3},{5,4},{6,5},{7,6},{8,7},{9,8},{10,9},{11,1... | collective-permute-start | bytes 196616 | tf_op jit(solution)/shard_map/ppermute | solution.py:404
  29.9 1.9 %collective-permute-start.4 = (f32[2,1,64,128]{3,2,1,0:T(8,128)S(1)}, f32[2,1,64,128]{3,2,1,0:T(8,128)S(1)}, u32[]{:S(2)}, u32[]{:S(2)}) collective-permute-start(f32[2,1,64,128]{3,2,1,0:T(8,128)S(1)} %get-tuple-element.7), channel_id=1, source_target_pairs={{0,1},{1,2},{2,3},{3,4},{4,5},{5,6},{6,7},{7,8},{8,9},{9,10},{10,1... | collective-permute-start | bytes 196616 | tf_op jit(solution)/shard_map/ppermute | solution.py:403
  31.9 0.0 copy-start.1
  31.9 0.0 copy-start.2
  31.9 0.0 copy-start.3
  31.9 0.1 pad_add_fusion.place_ref
  32.0 0.0 collective-permute-done.5.after_ref
  32.0 4.4 %collective-permute-done.4.before_ref = f32[2,1,64,128]{3,2,1,0:T(8,128)S(1)} collective-permute-done((f32[2,1,64,128]{3,2,1,0:T(8,128)S(1)}, f32[2,1,64,128]{3,2,1,0:T(8,128)S(1)}, u32[]{:S(2)}, u32[]{:S(2)}) %collective-permute-start.4) | collective-permute-done | bytes 65568 | tf_op jit(solution)/shard_map/ppermute | solution.py:403
  36.4 0.0 collective-permute-done.3.theirs_ref
  36.4 0.0 copy-done.1
  36.4 0.0 copy-done.2
  36.4 0.0 copy-done.3
  36.5 20.4 %solve.1 = (f32[2,2,64,128]{3,2,1,0:T(8,128)}, f32[2,2,32,128]{3,2,1,0:T(8,128)S(1)}) custom-call(s32[2]{0:T(128)S(1)} %pad_add_fusion.place_ref, f32[4]{0:T(128)S(1)} %copy-done.1, f32[4]{0:T(128)S(1)} %copy-done.2, s32[2]{0:T(128)S(1)} %copy-done.3, f32[8,2,2,64,128]{4,3,2,1,0:T(8,128)S(1)} %pad_maximum_fusion.mine_ref, ...), custom_call_target="tpu_custom_call" | custom-call | tf_op jit(solution)/shard_map/solve/pallas_call | solution.py:414
  56.8 0.5 collective-permute-start.6
  57.3 3.4 %collective-permute-done.6 = f32[2,32,128]{2,1,0:T(8,128)S(1)} collective-permute-done((f32[2,32,128]{2,1,0:T(8,128)S(1)}, f32[2,32,128]{2,1,0:T(8,128)S(1)}, u32[]{:S(2)}, u32[]{:S(2)}) %collective-permute-start.6) | collective-permute-done | bytes 32800 | tf_op jit(solution)/shard_map/ppermute | solution.py:459
  60.7 0.6 %bitcast_add_fusion = f32[2,32,128]{2,1,0:T(8,128)} fusion(f32[2,32,128]{2,1,0:T(8,128)S(1)} %collective-permute-done.6, f32[2,2,32,128]{3,2,1,0:T(8,128)S(1)} %get-tuple-element.5), kind=kLoop, calls=%fused_computation.4 | loop fusion | flops 8192 | bytes 98304 | tf_op jit(solution)/shard_map/add | solution.py:459
  (4 shorter events, 0.1 us)
Async XLA Ops:
  1.5 6.4 %collective-permute-start = (f32[1,2,2,64,128]{4,3,2,1,0:T(8,128)S(1)}, f32[1,2,2,64,128]{4,3,2,1,0:T(8,128)S(1)}, u32[]{:S(2)}, u32[]{:S(2)}) collective-permute-start(f32[1,2,2,64,128]{4,3,2,1,0:T(8,128)S(1)} %maximum_bitcast_fusion), channel_id=1, source_target_pairs={{0,8},{1,3},{2,10},{3,1},{4,12},{5,7},{6,14},{7,5},{8,0},{9,11},{1... | collective-permute-start | bytes 393224 | tf_op jit(solution)/shard_map/ppermute | solution.py:81
  8.0 7.0 %collective-permute-start.1 = (f32[2,2,2,64,128]{4,3,2,1,0:T(8,128)S(1)}, f32[2,2,2,64,128]{4,3,2,1,0:T(8,128)S(1)}, u32[]{:S(2)}, u32[]{:S(2)}) collective-permute-start(f32[2,2,2,64,128]{4,3,2,1,0:T(8,128)S(1)} %pad_maximum_fusion.2), channel_id=1, source_target_pairs={{0,4},{1,9},{2,6},{3,11},{4,0},{5,13},{6,2},{7,15},{8,12},{9,1},{1... | collective-permute-start | bytes 786440 | tf_op jit(solution)/shard_map/ppermute | solution.py:81
  15.1 9.4 %copy-start = (f32[2,2,64,128]{3,2,1,0:T(8,128)S(1)}, f32[2,2,64,128]{3,2,1,0:T(8,128)}, u32[]{:S(2)}) copy-start(f32[2,2,64,128]{3,2,1,0:T(8,128)} %state_ref.1) | copy-start | bytes 393220
  15.1 9.2 %collective-permute-start.2 = (f32[4,2,2,64,128]{4,3,2,1,0:T(8,128)S(1)}, f32[4,2,2,64,128]{4,3,2,1,0:T(8,128)S(1)}, u32[]{:S(2)}, u32[]{:S(2)}) collective-permute-start(f32[4,2,2,64,128]{4,3,2,1,0:T(8,128)S(1)} %pad_maximum_fusion.1), channel_id=1, source_target_pairs={{0,2},{1,5},{2,0},{3,7},{4,6},{5,1},{6,4},{7,3},{8,10},{9,13},{10,... | collective-permute-start | bytes 1572872 | tf_op jit(solution)/shard_map/ppermute | solution.py:81
  24.4 12.0 %collective-permute-start.3 = (f32[8,2,2,64,128]{4,3,2,1,0:T(8,128)S(1)}, f32[8,2,2,64,128]{4,3,2,1,0:T(8,128)S(1)}, u32[]{:S(2)}, u32[]{:S(2)}) collective-permute-start(f32[8,2,2,64,128]{4,3,2,1,0:T(8,128)S(1)} %pad_maximum_fusion.mine_ref), channel_id=1, source_target_pairs={{0,1},{1,0},{2,3},{3,2},{4,5},{5,4},{6,7},{7,6},{8,9},{9,8},{10,11... | collective-permute-start | bytes 3145736 | tf_op jit(solution)/shard_map/ppermute | solution.py:82
  24.5 7.5 %collective-permute-start.5 = (f32[2,1,64,128]{3,2,1,0:T(8,128)S(1)}, f32[2,1,64,128]{3,2,1,0:T(8,128)S(1)}, u32[]{:S(2)}, u32[]{:S(2)}) collective-permute-start(f32[2,1,64,128]{3,2,1,0:T(8,128)S(1)} %get-tuple-element.6), channel_id=1, source_target_pairs={{1,0},{2,1},{3,2},{4,3},{5,4},{6,5},{7,6},{8,7},{9,8},{10,9},{11,1... | collective-permute-start | bytes 196616 | tf_op jit(solution)/shard_map/ppermute | solution.py:404
  29.9 6.5 %collective-permute-start.4 = (f32[2,1,64,128]{3,2,1,0:T(8,128)S(1)}, f32[2,1,64,128]{3,2,1,0:T(8,128)S(1)}, u32[]{:S(2)}, u32[]{:S(2)}) collective-permute-start(f32[2,1,64,128]{3,2,1,0:T(8,128)S(1)} %get-tuple-element.7), channel_id=1, source_target_pairs={{0,1},{1,2},{2,3},{3,4},{4,5},{5,6},{6,7},{7,8},{8,9},{9,10},{10,1... | collective-permute-start | bytes 196616 | tf_op jit(solution)/shard_map/ppermute | solution.py:403
  31.9 4.6 %copy-start.1 = (f32[4]{0:T(128)S(1)}, f32[4]{0:T(128)}, u32[]{:S(2)}) copy-start(f32[4]{0:T(128)} %shifts_ref.1) | copy-start | bytes 52
  31.9 4.5 %copy-start.2 = (f32[4]{0:T(128)S(1)}, f32[4]{0:T(128)}, u32[]{:S(2)}) copy-start(f32[4]{0:T(128)} %weights_ref.1) | copy-start | bytes 52
  31.9 4.5 %copy-start.3 = (s32[2]{0:T(128)S(1)}, s32[2]{0:T(128)}, u32[]{:S(2)}) copy-start(s32[2]{0:T(128)} %order_ref.1) | copy-start | bytes 28
  56.8 3.9 %collective-permute-start.6 = (f32[2,32,128]{2,1,0:T(8,128)S(1)}, f32[2,32,128]{2,1,0:T(8,128)S(1)}, u32[]{:S(2)}, u32[]{:S(2)}) collective-permute-start(f32[2,32,128]{2,1,0:T(8,128)S(1)} %slice_bitcast_fusion), channel_id=1, source_target_pairs={{0,16},{16,0},{1,17},{17,1},{2,18},{18,2},{3,19},{19,3},{4,20},{20... | collective-permute-start | bytes 98312 | tf_op jit(solution)/shard_map/ppermute | solution.py:459

commit v3 on v2

--- a/solution.py
+++ b/solution.py
@@ -11,6 +11,7 @@
 DAMPING = 0.8
 REPLICATED_CELLS = 32 * 64 * 128
 HALF = 64
+TILE = 8
 
 
 def extended(array, sides, width):
@@ -38,12 +39,10 @@
     return pltpu.roll(block, shift % block.shape[axis], axis)
 
 
-def eights(block):
-    rows = block.shape[0]
-    total = block[0:8]
-    for start in range(8, rows, 8):
-        total = total + block[start : start + 8]
-    return total
+def tree_sum(values):
+    while len(values) > 1:
+        values = [sum(values[at : at + 2]) for at in range(0, len(values), 2)]
+    return values[0]
 
 
 def slot_totals(acc):
@@ -117,35 +116,51 @@
     blocks, _, own, rows, _ = mine_ref.shape
     coarse_x = blocks * own
     rows = rows // 2
-    shape = (rows, 2 * HALF)
+    tiles = rows // TILE
+    shape = (TILE, 2 * HALF)
     lane = lane_index(shape)
     row = row_index(shape)
     slot0 = lane_index((1, 2 * HALF)) < HALF
+    zero = jnp.zeros(shape, jnp.float32)
+
+    def tile(j):
+        return pl.ds(TILE * j, TILE)
+
+    def every(b, j):
+        return pl.ds(b + 2 * j, TILE, stride=2 * tiles)
 
     def pick(ref):
         return jnp.where(slot0, ref[order_ref[0]], ref[order_ref[1]])
 
-    shift = pick(shifts_ref)
-    weight = pick(weights_ref)
+    shift = pick(shifts_ref) + zero
+    weight = pick(weights_ref) + zero
 
     def cls(a, b, c):
         return 4 * a + 2 * b + c
 
-    classes = [(a, b, c) for a in (0, 1) for b in (0, 1) for c in (0, 1)]
-
-    zero = jnp.zeros(shape, jnp.float32)
-    for ref in (half_kappa, scaled, first_dir, second_dir):
-        for k in range(8):
-            ref[k, 0] = zero
-            ref[k, coarse_x + 1] = zero
-    for ref in (coarse_one, coarse_two):
-        ref[0] = zero
-        ref[coarse_x + 1] = zero
+    pairs = [(p, q) for p in (0, 1) for q in (0, 1)]
+
+    def before_row(load, j):
+        return load(j - 1) if j else roll(load(tiles - 1), 1, 0)
+
+    def after_row(load, j):
+        return load(j + 1) if j + 1 < tiles else roll(load(0), -1, 0)
+
+    for j in range(tiles):
+        for ref in (half_kappa, scaled, first_dir, second_dir):
+            for k in range(8):
+                ref[k, 0, tile(j)] = zero
+                ref[k, coarse_x + 1, tile(j)] = zero
+        for ref in (coarse_one, coarse_two):
+            ref[0, tile(j)] = zero
+            ref[coarse_x + 1, tile(j)] = zero
+        for k in range(4):
+            outer_x[k, coarse_x, tile(j)] = zero
+        coarse_off[0, coarse_x, tile(j)] = zero
 
     even_lane = 2 * (lane % HALF)
 
-    def split(ref, t, field, x, b):
-        block = ref[t, field, x, pl.ds(b, rows, stride=2), :]
+    def split(block):
         even = jnp.take_along_axis(block, even_lane, axis=1)
         odd = jnp.take_along_axis(block, even_lane + 1, axis=1)
         return even, odd
@@ -157,210 +172,252 @@
                 a = x % 2
                 spot = home * (own // 2) + x // 2
                 for b in (0, 1):
-                    for c, value in enumerate(split(ref, t, 0, x, b)):
-                        half_kappa[cls(a, b, c), spot + 1] = 0.5 * value
-                    for c, value in enumerate(split(ref, t, 1, x, b)):
-                        residual[cls(a, b, c), spot] = weight * value
+                    for j in range(tiles):
+                        block = ref[t, 0, x, every(b, j), :]
+                        for c, value in enumerate(split(block)):
+                            half_kappa[cls(a, b, c), spot + 1, tile(j)] = 0.5 * value
+                        block = ref[t, 1, x, every(b, j), :]
+                        for c, value in enumerate(split(block)):
+                            residual[cls(a, b, c), spot, tile(j)] = weight * value
         return carry
 
     lax.fori_loop(0, blocks, arrange, 0)
 
-    y_low = jnp.where(row > 0, 1.0, 0.0)
-    y_high = jnp.where(row < rows - 1, 1.0, 0.0)
     z_low = jnp.where(lane % HALF > 0, 1.0, 0.0)
     z_high = jnp.where(lane % HALF < HALF - 1, 1.0, 0.0)
+    y_low = [jnp.where(row > 0, 1.0, 0.0)] + [None] * (tiles - 1)
+    y_high = [None] * (tiles - 1) + [jnp.where(row < TILE - 1, 1.0, 0.0)]
+
+    def masked(mask, value):
+        return value if mask is None else mask * value
 
     def coefficients(i, carry):
         x_low = jnp.where(i > 0, 1.0, 0.0)
-        kap = [half_kappa[k, i + 1] for k in range(8)]
-        total = [shift + zero for _ in range(8)]
-        inside = [zero for _ in range(8)]
-        coarse_total = 8.0 * shift + zero
-        cx = zero
-        cy = [zero, zero]
-        cz = [zero, zero]
-        for p in (0, 1):
-            for q in (0, 1):
+        for j in range(tiles):
+            kap = [half_kappa[k, i + 1, tile(j)] for k in range(8)]
+            total = [shift for _ in range(8)]
+            inside = [[] for _ in range(8)]
+            outside = []
+            cx, cy, cz = [], ([], []), ([], [])
+            for p, q in pairs:
                 for kind, low, high in (
                     (0, cls(0, p, q), cls(1, p, q)),
                     (1, cls(p, 0, q), cls(p, 1, q)),
                     (2, cls(p, q, 0), cls(p, q, 1)),
                 ):
                     face = kap[low] + kap[high]
-                    inner[4 * kind + 2 * p + q, i] = face
-                    inside[low] = inside[low] + face
-                    inside[high] = inside[high] + face
+                    inner[4 * kind + 2 * p + q, i, tile(j)] = face
+                    inside[low].append(face)
+                    inside[high].append(face)
+
                 low, high = cls(0, p, q), cls(1, p, q)
-                minus = kap[low] + half_kappa[high, i]
-                plus = kap[high] + half_kappa[low, i + 2]
+                minus = kap[low] + half_kappa[high, i, tile(j)]
+                plus = kap[high] + half_kappa[low, i + 2, tile(j)]
                 total[low] = total[low] + minus
                 total[high] = total[high] + plus
-                coarse_total = coarse_total + minus + plus
-                outer_x[2 * p + q, i] = x_low * minus
-                cx = cx + x_low * minus
+                outside.append(minus + plus)
+                minus = x_low * minus
+                outer_x[2 * p + q, i, tile(j)] = minus
+                cx.append(minus)
+
                 low, high = cls(p, 0, q), cls(p, 1, q)
-                minus = kap[low] + y_low * roll(kap[high], 1, 0)
-                plus = kap[high] + y_high * roll(kap[low], -1, 0)
+                minus = kap[low] + masked(
+                    y_low[j],
+                    before_row(lambda r: half_kappa[high, i + 1, tile(r)], j),
+                )
+                plus = kap[high] + masked(
+                    y_high[j],
+                    after_row(lambda r: half_kappa[low, i + 1, tile(r)], j),
+                )
                 total[low] = total[low] + minus
                 total[high] = total[high] + plus
-                coarse_total = coarse_total + minus + plus
-                minus, plus = y_low * minus, y_high * plus
-                outer_y[2 * p + q, i] = minus
-                outer_y[4 + 2 * p + q, i] = plus
-                cy = [cy[0] + minus, cy[1] + plus]
+                outside.append(minus + plus)
+                minus, plus = masked(y_low[j], minus), masked(y_high[j], plus)
+                outer_y[2 * p + q, i, tile(j)] = minus
+                outer_y[4 + 2 * p + q, i, tile(j)] = plus
+                cy[0].append(minus)
+                cy[1].append(plus)
+
                 low, high = cls(p, q, 0), cls(p, q, 1)
                 minus = kap[low] + z_low * roll(kap[high], 1, 1)
                 plus = kap[high] + z_high * roll(kap[low], -1, 1)
                 total[low] = total[low] + minus
                 total[high] = total[high] + plus
-                coarse_total = coarse_total + minus + plus
+                outside.append(minus + plus)
                 minus, plus = z_low * minus, z_high * plus
-                outer_z[2 * p + q, i] = minus
-                outer_z[4 + 2 * p + q, i] = plus
-                cz = [cz[0] + minus, cz[1] + plus]
-        for k in range(8):
-            inner_sum[k, i] = inside[k]
-            diag = total[k] + inside[k]
-            diagonal[k, i] = diag
-            inverse = DAMPING / diag
-            damped[k, i] = inverse
-            scaled[k, i + 1] = inverse * residual[k, i]
-        coarse_off[0, i] = cx
-        coarse_off[1, i] = cy[0]
-        coarse_off[2, i] = cy[1]
-        coarse_off[3, i] = cz[0]
-        coarse_off[4, i] = cz[1]
-        coarse_damped[i] = DAMPING / coarse_total
+                outer_z[2 * p + q, i, tile(j)] = minus
+                outer_z[4 + 2 * p + q, i, tile(j)] = plus
+                cz[0].append(minus)
+                cz[1].append(plus)
+            for k in range(8):
+                within = sum(inside[k])
+                inner_sum[k, i, tile(j)] = within
+                diag = total[k] + within
+                diagonal[k, i, tile(j)] = diag
+                inverse = DAMPING / diag
+                damped[k, i, tile(j)] = inverse
+                scaled[k, i + 1, tile(j)] = inverse * residual[k, i, tile(j)]
+            for at, part in enumerate((cx, cy[0], cy[1], cz[0], cz[1])):
+                coarse_off[at, i, tile(j)] = tree_sum(part)
+            coarse_damped[i, tile(j)] = DAMPING / (8.0 * shift + tree_sum(outside))
         return carry
 
     lax.fori_loop(0, coarse_x, coefficients, 0)
-    for k in range(4):
-        outer_x[k, coarse_x] = zero
-    coarse_off[0, coarse_x] = zero
-
-    def neighbours(field, a, b, c, i):
-        k = cls(a, b, c)
-        out = inner[2 * b + c, i] * field[cls(1 - a, b, c), i + 1]
-        out = out + inner[4 + 2 * a + c, i] * field[cls(a, 1 - b, c), i + 1]
-        out = out + inner[8 + 2 * a + b, i] * field[cls(a, b, 1 - c), i + 1]
-        out = out + outer_x[2 * b + c, i + a] * field[cls(1 - a, b, c), i + 2 * a]
-        out = out + outer_y[4 * b + 2 * a + c, i] * roll(
-            field[cls(a, 1 - b, c), i + 1], 1 - 2 * b, 0
+
+    def stencil(field, i, j):
+        here = [field[k, i + 1, tile(j)] for k in range(8)]
+        terms = [[] for _ in range(8)]
+        for p, q in pairs:
+            for kind, low, high in (
+                (0, cls(0, p, q), cls(1, p, q)),
+                (1, cls(p, 0, q), cls(p, 1, q)),
+                (2, cls(p, q, 0), cls(p, q, 1)),
+            ):
+                face = inner[4 * kind + 2 * p + q, i, tile(j)]
+                terms[low].append(face * here[high])
+                terms[high].append(face * here[low])
+            at = 2 * p + q
+            low, high = cls(0, p, q), cls(1, p, q)
+            terms[low].append(outer_x[at, i, tile(j)] * field[high, i, tile(j)])
+            terms[high].append(outer_x[at, i + 1, tile(j)] * field[low, i + 2, tile(j)])
+            low, high = cls(p, 0, q), cls(p, 1, q)
+            side = before_row(lambda r: field[high, i + 1, tile(r)], j)
+            terms[low].append(outer_y[at, i, tile(j)] * side)
+            side = after_row(lambda r: field[low, i + 1, tile(r)], j)
+            terms[high].append(outer_y[4 + at, i, tile(j)] * side)
+            low, high = cls(p, q, 0), cls(p, q, 1)
+            terms[low].append(outer_z[at, i, tile(j)] * roll(here[high], 1, 1))
+            terms[high].append(outer_z[4 + at, i, tile(j)] * roll(here[low], -1, 1))
+        return here, [tree_sum(part) for part in terms]
+
+    def coarse_sides(field, i, j):
+        here = field[i + 1, tile(j)]
+        return here, (
+            (field[i, tile(j)], field[i + 2, tile(j)]),
+            (
+                before_row(lambda r: field[i + 1, tile(r)], j),
+                after_row(lambda r: field[i + 1, tile(r)], j),
+            ),
+            (roll(here, 1, 1), roll(here, -1, 1)),
         )
-        out = out + outer_z[4 * c + 2 * a + b, i] * roll(
-            field[cls(a, b, 1 - c), i + 1], 1 - 2 * c, 1
-        )
-        return out
-
-    def coarse_neighbours(field, i):
-        here = field[i + 1]
-        out = coarse_off[0, i] * field[i]
-        out = out + coarse_off[0, i + 1] * field[i + 2]
-        out = out + coarse_off[1, i] * roll(here, 1, 0)
-        out = out + coarse_off[2, i] * roll(here, -1, 0)
-        out = out + coarse_off[3, i] * roll(here, 1, 1)
-        out = out + coarse_off[4, i] * roll(here, -1, 1)
-        return out
-
-    def precondition(result):
+
+    def precondition(result, other):
         def down(i, carry):
-            rhs = zero
-            for a, b, c in classes:
-                k = cls(a, b, c)
-                res = residual[k, i]
-                part = res + neighbours(scaled, a, b, c, i)
-                partial[k, i] = part
-                rhs = rhs + (part - DAMPING * res)
-            coarse_one[i + 1] = coarse_damped[i] * rhs
+            for j in range(tiles):
+                res = [residual[k, i, tile(j)] for k in range(8)]
+                _, sums = stencil(scaled, i, j)
+                parts = [(2.0 - DAMPING) * res[k] + sums[k] for k in range(8)]
+                for k in range(8):
+                    partial[k, i, tile(j)] = parts[k]
+                rhs = tree_sum(parts) - tree_sum(res)
+                coarse_one[i + 1, tile(j)] = coarse_damped[i, tile(j)] * rhs
             return carry
 
-        lax.fori_loop(0, coarse_x, down, 0)
+        lax.fori_loop(0, coarse_x, down, 0, unroll=2)
 
         def smooth(i, carry):
-            coarse_two[i + 1] = (2.0 - DAMPING) * coarse_one[
-                i + 1
-            ] + coarse_damped[i] * coarse_neighbours(coarse_one, i)
+            for j in range(tiles):
+                here, sides = coarse_sides(coarse_one, i, j)
+                total = coarse_off[0, i, tile(j)] * sides[0][0]
+                total = total + coarse_off[0, i + 1, tile(j)] * sides[0][1]
+                total = total + coarse_off[1, i, tile(j)] * sides[1][0]
+                total = total + coarse_off[2, i, tile(j)] * sides[1][1]
+                total = total + coarse_off[3, i, tile(j)] * sides[2][0]
+                total = total + coarse_off[4, i, tile(j)] * sides[2][1]
+                coarse_two[i + 1, tile(j)] = (2.0 - DAMPING) * here + coarse_damped[
+                    i, tile(j)
+                ] * total
             return carry
 
-        lax.fori_loop(0, coarse_x, smooth, 0)
-
-        def up(i, acc):
-            here = coarse_two[i + 1]
-            sides = (
-                (coarse_two[i], coarse_two[i + 2]),
-                (roll(here, 1, 0), roll(here, -1, 0)),
-                (roll(here, 1, 1), roll(here, -1, 1)),
-            )
-            for a, b, c in classes:
-                k = cls(a, b, c)
-                value = partial[k, i] + inner_sum[k, i] * here
-                value = value + outer_x[2 * b + c, i + a] * sides[0][a]
-                value = value + outer_y[4 * b + 2 * a + c, i] * sides[1][b]
-                value = value + outer_z[4 * c + 2 * a + b, i] * sides[2][c]
-                new = (1.0 - DAMPING) * (scaled[k, i + 1] + here) + damped[k, i] * value
-                result[k, i + 1] = new
-                acc = acc + eights(residual[k, i] * new)
-            return acc
-
-        return lax.fori_loop(0, coarse_x, up, jnp.zeros((8, 2 * HALF), jnp.float32))
+        lax.fori_loop(0, coarse_x, smooth, 0, unroll=8)
+
+        def up(i, carry):
+            gamma, cross = carry
+            for j in range(tiles):
+                here, sides = coarse_sides(coarse_two, i, j)
+                kept = (1.0 - DAMPING) * here
+                dots, crosses = [], []
+                for a in (0, 1):
+                    for b in (0, 1):
+                        for c in (0, 1):
+                            k = cls(a, b, c)
+                            value = tree_sum(
+                                [
+                                    partial[k, i, tile(j)],
+                                    inner_sum[k, i, tile(j)] * here,
+                                    outer_x[2 * b + c, i + a, tile(j)] * sides[0][a],
+                                    outer_y[4 * b + 2 * a + c, i, tile(j)] * sides[1][b],
+                                    outer_z[4 * c + 2 * a + b, i, tile(j)] * sides[2][c],
+                                ]
+                            )
+                            new = kept + damped[k, i, tile(j)] * value
+                            result[k, i + 1, tile(j)] = new
+                            dots.append(residual[k, i, tile(j)] * new)
+                            if other is not None:
+                                crosses.append(other[k, i, tile(j)] * new)
+                gamma = gamma + tree_sum(dots)
+                if other is not None:
+                    cross = cross + tree_sum(crosses)
+            return gamma, cross
+
+        sums = lax.fori_loop(0, coarse_x, up, (zero, zero), unroll=2)
+        return [slot_totals(part) for part in sums]
 
     def curvature(field, keep):
         def step(i, acc):
-            for a, b, c in classes:
-                k = cls(a, b, c)
-                here = field[k, i + 1]
-                value = diagonal[k, i] * here - neighbours(field, a, b, c, i)
-                if keep:
-                    image[k, i] = value
-                acc = acc + eights(here * value)
+            for j in range(tiles):
+                here, sums = stencil(field, i, j)
+                dots = []
+                for k in range(8):
+                    value = diagonal[k, i, tile(j)] * here[k] - sums[k]
+                    if keep:
+                        image[k, i, tile(j)] = value
+                    dots.append(here[k] * value)
+                acc = acc + tree_sum(dots)
             return acc
 
-        return lax.fori_loop(0, coarse_x, step, jnp.zeros((8, 2 * HALF), jnp.float32))
-
-    gamma = slot_totals(precondition(first_dir))
-    step_one = gamma / slot_totals(curvature(first_dir, True))
+        return slot_totals(lax.fori_loop(0, coarse_x, step, zero, unroll=2))
+
+    gamma, _ = precondition(first_dir, None)
+    curve = curvature(first_dir, True)
+    step_one = gamma / curve
 
     def update(i, carry):
-        for k in range(8):
-            new = residual[k, i] - step_one * image[k, i]
-            residual[k, i] = new
-            scaled[k, i + 1] = damped[k, i] * new
+        for j in range(tiles):
+            for k in range(8):
+                new = residual[k, i, tile(j)] - step_one * image[k, i, tile(j)]
+                residual[k, i, tile(j)] = new
+                scaled[k, i + 1, tile(j)] = damped[k, i, tile(j)] * new
         return carry
 
-    lax.fori_loop(0, coarse_x, update, 0)
-
-    gamma_next = slot_totals(precondition(second_dir))
+    lax.fori_loop(0, coarse_x, update, 0, unroll=2)
+
+    gamma_next, cross = precondition(second_dir, image)
     ratio = gamma_next / gamma
-
-    def turn(i, carry):
-        for k in range(8):
-            second_dir[k, i + 1] = second_dir[k, i + 1] + ratio * first_dir[k, i + 1]
-        return carry
-
-    lax.fori_loop(0, coarse_x, turn, 0)
-    step_two = gamma_next / slot_totals(curvature(second_dir, False))
-
-    own = adjoint_ref.shape[1]
+    step_two = gamma_next / (
+        curvature(second_dir, False) + ratio * (2.0 * cross + ratio * curve)
+    )
+    step_first = step_one + step_two * ratio
+
     start = place_ref[0] * (own // 2)
     even = lane % 2 == 0
-    for j in range(own + 2):
-        a = (j + 1) % 2
-        spot = start + (j + 1) // 2
+    for at in range(own + 2):
+        a = (at + 1) % 2
+        spot = start + (at + 1) // 2
         for b in (0, 1):
-            pair = []
-            for c in (0, 1):
-                k = cls(a, b, c)
-                pair.append(
-                    step_one * first_dir[k, spot] + step_two * second_dir[k, spot]
-                )
-            for slot in (0, 1):
-                source = lane // 2 + HALF * slot
-                value = jnp.where(
-                    even,
-                    jnp.take_along_axis(pair[0], source, axis=1),
-                    jnp.take_along_axis(pair[1], source, axis=1),
-                )
-                planes[slot, j, pl.ds(b, rows, stride=2), :] = value
+            for j in range(tiles):
+                both = [
+                    step_first * first_dir[cls(a, b, c), spot, tile(j)]
+                    + step_two * second_dir[cls(a, b, c), spot, tile(j)]
+                    for c in (0, 1)
+                ]
+                for slot in (0, 1):
+                    source = lane // 2 + HALF * slot
+                    planes[slot, at, every(b, j), :] = jnp.where(
+                        even,
+                        jnp.take_along_axis(both[0], source, axis=1),
+                        jnp.take_along_axis(both[1], source, axis=1),
+                    )
 
     full = (2 * rows, 2 * HALF)
     y_at = row_index(full)

time: 61.6 us -> 58.3 us (0.946)
  Pallas kernels: 20.4 us -> 17.1 us
    pallas_call x1, Pallas kernels: 20.4 us -> 17.1 us  [whole_grid(): pl.pallas_call(solve_kernel, out_shape=(jax.ShapeDtypeStruct(forward_stat...]
where the time goes in v3:
time: 58.3 us; the launch traced here: 58.1 us
  waiting for transfers between devices  24.9 us (43%)
  Pallas kernels  17.1 us (29%)
  starting transfers between devices  13.5 us (23%)
  other arithmetic  1.74 us (3%)
  between operations  0.75 us (1%)
    pallas_call x1, Pallas kernels, whole_grid(): pl.pallas_call(solve_kernel, out_shape=(jax.ShapeDtypeStruct(forward_stat...  17.1 us
    ppermute x3, waiting for transfers between devices, gather_blocks(): held = jnp.concatenate([held, lax.ppermute(held, axis, pairs)], axis=0)  17.1 us
    ppermute x3, starting transfers between devices, gather_blocks(): held = jnp.concatenate([held, lax.ppermute(held, axis, pairs)], axis=0)  5.63 us
    ppermute x1, starting transfers between devices, whole_grid(): after = lax.ppermute(forward_states[:, :1], 'space', down)  5.41 us
    ppermute x1, waiting for transfers between devices, whole_grid(): before = lax.ppermute(forward_states[:, own - 1:], 'space', up)  4.44 us
    ppermute x1, waiting for transfers between devices, whole_grid(): gradient = gradient + lax.ppermute(share[k], 'pole', ring)  3.41 us
    ppermute x1, starting transfers between devices, whole_grid(): before = lax.ppermute(forward_states[:, own - 1:], 'space', up)  1.92 us
  transfers between devices with their start and end apart: 7, of which 5 were waited for; matrix products, arithmetic and copies ran while one was open for 0% of the time, Pallas kernels for 0%

profile of v3, /device:TPU:12, one launch (start us, length us, event | category | flops | bytes accessed | tf_op | source)
XLA Modules:
  0.0 58.1 jit_solution(7553272378365273126)
XLA Ops:
  0.6 0.9 %maximum_bitcast_fusion = f32[1,2,2,64,128]{4,3,2,1,0:T(8,128)S(1)} fusion(f32[1,2,64,128]{3,2,1,0:T(8,128)} %bitcast.10, f32[1,2,64,128]{3,2,1,0:T(8,128)} %bitcast.11), kind=kLoop, calls=%fused_computation.3 | loop fusion | flops 32768 | bytes 262144 | tf_op jit(solution)/shard_map/broadcast_in_dim | solution.py:77
  1.5 2.7 %collective-permute-start = (f32[1,2,2,64,128]{4,3,2,1,0:T(8,128)S(1)}, f32[1,2,2,64,128]{4,3,2,1,0:T(8,128)S(1)}, u32[]{:S(2)}, u32[]{:S(2)}) collective-permute-start(f32[1,2,2,64,128]{4,3,2,1,0:T(8,128)S(1)} %maximum_bitcast_fusion), channel_id=1, source_target_pairs={{0,8},{1,3},{2,10},{3,1},{4,12},{5,7},{6,14},{7,5},{8,0},{9,11},{1... | collective-permute-start | bytes 393224 | tf_op jit(solution)/shard_map/ppermute | solution.py:80
  4.2 3.8 %collective-permute-done = f32[1,2,2,64,128]{4,3,2,1,0:T(8,128)S(1)} collective-permute-done((f32[1,2,2,64,128]{4,3,2,1,0:T(8,128)S(1)}, f32[1,2,2,64,128]{4,3,2,1,0:T(8,128)S(1)}, u32[]{:S(2)}, u32[]{:S(2)}) %collective-permute-start) | collective-permute-done | bytes 131104 | tf_op jit(solution)/shard_map/ppermute | solution.py:80
  8.0 1.4 %collective-permute-start.1 = (f32[2,2,2,64,128]{4,3,2,1,0:T(8,128)S(1)}, f32[2,2,2,64,128]{4,3,2,1,0:T(8,128)S(1)}, u32[]{:S(2)}, u32[]{:S(2)}) collective-permute-start(f32[2,2,2,64,128]{4,3,2,1,0:T(8,128)S(1)} %pad_maximum_fusion.2), channel_id=1, source_target_pairs={{0,4},{1,9},{2,6},{3,11},{4,0},{5,13},{6,2},{7,15},{8,12},{9,1},{1... | collective-permute-start | bytes 786440 | tf_op jit(solution)/shard_map/ppermute | solution.py:80
  9.4 5.6 %collective-permute-done.1 = f32[2,2,2,64,128]{4,3,2,1,0:T(8,128)S(1)} collective-permute-done((f32[2,2,2,64,128]{4,3,2,1,0:T(8,128)S(1)}, f32[2,2,2,64,128]{4,3,2,1,0:T(8,128)S(1)}, u32[]{:S(2)}, u32[]{:S(2)}) %collective-permute-start.1) | collective-permute-done | bytes 262176 | tf_op jit(solution)/shard_map/ppermute | solution.py:80
  15.1 0.0 copy-start
  15.1 1.6 %collective-permute-start.2 = (f32[4,2,2,64,128]{4,3,2,1,0:T(8,128)S(1)}, f32[4,2,2,64,128]{4,3,2,1,0:T(8,128)S(1)}, u32[]{:S(2)}, u32[]{:S(2)}) collective-permute-start(f32[4,2,2,64,128]{4,3,2,1,0:T(8,128)S(1)} %pad_maximum_fusion.1), channel_id=1, source_target_pairs={{0,2},{1,5},{2,0},{3,7},{4,6},{5,1},{6,4},{7,3},{8,10},{9,13},{10,... | collective-permute-start | bytes 1572872 | tf_op jit(solution)/shard_map/ppermute | solution.py:80
  16.6 7.7 %collective-permute-done.2 = f32[4,2,2,64,128]{4,3,2,1,0:T(8,128)S(1)} collective-permute-done((f32[4,2,2,64,128]{4,3,2,1,0:T(8,128)S(1)}, f32[4,2,2,64,128]{4,3,2,1,0:T(8,128)S(1)}, u32[]{:S(2)}, u32[]{:S(2)}) %collective-permute-start.2) | collective-permute-done | bytes 524320 | tf_op jit(solution)/shard_map/ppermute | solution.py:80
  24.3 0.1 pad_maximum_fusion.mine_ref
  24.4 0.1 collective-permute-start.3
  24.5 0.0 copy-done
  24.5 5.4 %collective-permute-start.5 = (f32[2,1,64,128]{3,2,1,0:T(8,128)S(1)}, f32[2,1,64,128]{3,2,1,0:T(8,128)S(1)}, u32[]{:S(2)}, u32[]{:S(2)}) collective-permute-start(f32[2,1,64,128]{3,2,1,0:T(8,128)S(1)} %get-tuple-element.6), channel_id=1, source_target_pairs={{1,0},{2,1},{3,2},{4,3},{5,4},{6,5},{7,6},{8,7},{9,8},{10,9},{11,1... | collective-permute-start | bytes 196616 | tf_op jit(solution)/shard_map/ppermute | solution.py:461
  29.9 1.9 %collective-permute-start.4 = (f32[2,1,64,128]{3,2,1,0:T(8,128)S(1)}, f32[2,1,64,128]{3,2,1,0:T(8,128)S(1)}, u32[]{:S(2)}, u32[]{:S(2)}) collective-permute-start(f32[2,1,64,128]{3,2,1,0:T(8,128)S(1)} %get-tuple-element.7), channel_id=1, source_target_pairs={{0,1},{1,2},{2,3},{3,4},{4,5},{5,6},{6,7},{7,8},{8,9},{9,10},{10,1... | collective-permute-start | bytes 196616 | tf_op jit(solution)/shard_map/ppermute | solution.py:460
  31.9 0.0 copy-start.1
  31.9 0.0 copy-start.2
  31.9 0.0 copy-start.3
  31.9 0.1 pad_add_fusion.place_ref
  32.0 0.0 collective-permute-done.5.after_ref
  32.0 4.4 %collective-permute-done.4.before_ref = f32[2,1,64,128]{3,2,1,0:T(8,128)S(1)} collective-permute-done((f32[2,1,64,128]{3,2,1,0:T(8,128)S(1)}, f32[2,1,64,128]{3,2,1,0:T(8,128)S(1)}, u32[]{:S(2)}, u32[]{:S(2)}) %collective-permute-start.4) | collective-permute-done | bytes 65568 | tf_op jit(solution)/shard_map/ppermute | solution.py:460
  36.4 0.0 collective-permute-done.3.theirs_ref
  36.4 0.0 copy-done.1
  36.4 0.0 copy-done.2
  36.4 0.0 copy-done.3
  36.5 17.1 %solve.1 = (f32[2,2,64,128]{3,2,1,0:T(8,128)}, f32[2,2,32,128]{3,2,1,0:T(8,128)S(1)}) custom-call(s32[2]{0:T(128)S(1)} %pad_add_fusion.place_ref, f32[4]{0:T(128)S(1)} %copy-done.1, f32[4]{0:T(128)S(1)} %copy-done.2, s32[2]{0:T(128)S(1)} %copy-done.3, f32[8,2,2,64,128]{4,3,2,1,0:T(8,128)S(1)} %pad_maximum_fusion.mine_ref, ...), custom_call_target="tpu_custom_call" | custom-call | tf_op jit(solution)/shard_map/solve/pallas_call | solution.py:471
  53.6 0.5 collective-permute-start.6
  54.1 3.4 %collective-permute-done.6 = f32[2,32,128]{2,1,0:T(8,128)S(1)} collective-permute-done((f32[2,32,128]{2,1,0:T(8,128)S(1)}, f32[2,32,128]{2,1,0:T(8,128)S(1)}, u32[]{:S(2)}, u32[]{:S(2)}) %collective-permute-start.6) | collective-permute-done | bytes 32800 | tf_op jit(solution)/shard_map/ppermute | solution.py:516
  57.5 0.6 %bitcast_add_fusion = f32[2,32,128]{2,1,0:T(8,128)} fusion(f32[2,32,128]{2,1,0:T(8,128)S(1)} %collective-permute-done.6, f32[2,2,32,128]{3,2,1,0:T(8,128)S(1)} %get-tuple-element.5), kind=kLoop, calls=%fused_computation.4 | loop fusion | flops 8192 | bytes 98304 | tf_op jit(solution)/shard_map/add | solution.py:516
  (4 shorter events, 0.1 us)
Async XLA Ops:
  1.5 6.4 %collective-permute-start = (f32[1,2,2,64,128]{4,3,2,1,0:T(8,128)S(1)}, f32[1,2,2,64,128]{4,3,2,1,0:T(8,128)S(1)}, u32[]{:S(2)}, u32[]{:S(2)}) collective-permute-start(f32[1,2,2,64,128]{4,3,2,1,0:T(8,128)S(1)} %maximum_bitcast_fusion), channel_id=1, source_target_pairs={{0,8},{1,3},{2,10},{3,1},{4,12},{5,7},{6,14},{7,5},{8,0},{9,11},{1... | collective-permute-start | bytes 393224 | tf_op jit(solution)/shard_map/ppermute | solution.py:80
  8.0 7.0 %collective-permute-start.1 = (f32[2,2,2,64,128]{4,3,2,1,0:T(8,128)S(1)}, f32[2,2,2,64,128]{4,3,2,1,0:T(8,128)S(1)}, u32[]{:S(2)}, u32[]{:S(2)}) collective-permute-start(f32[2,2,2,64,128]{4,3,2,1,0:T(8,128)S(1)} %pad_maximum_fusion.2), channel_id=1, source_target_pairs={{0,4},{1,9},{2,6},{3,11},{4,0},{5,13},{6,2},{7,15},{8,12},{9,1},{1... | collective-permute-start | bytes 786440 | tf_op jit(solution)/shard_map/ppermute | solution.py:80
  15.1 9.4 %copy-start = (f32[2,2,64,128]{3,2,1,0:T(8,128)S(1)}, f32[2,2,64,128]{3,2,1,0:T(8,128)}, u32[]{:S(2)}) copy-start(f32[2,2,64,128]{3,2,1,0:T(8,128)} %state_ref.1) | copy-start | bytes 393220
  15.1 9.2 %collective-permute-start.2 = (f32[4,2,2,64,128]{4,3,2,1,0:T(8,128)S(1)}, f32[4,2,2,64,128]{4,3,2,1,0:T(8,128)S(1)}, u32[]{:S(2)}, u32[]{:S(2)}) collective-permute-start(f32[4,2,2,64,128]{4,3,2,1,0:T(8,128)S(1)} %pad_maximum_fusion.1), channel_id=1, source_target_pairs={{0,2},{1,5},{2,0},{3,7},{4,6},{5,1},{6,4},{7,3},{8,10},{9,13},{10,... | collective-permute-start | bytes 1572872 | tf_op jit(solution)/shard_map/ppermute | solution.py:80
  24.4 12.0 %collective-permute-start.3 = (f32[8,2,2,64,128]{4,3,2,1,0:T(8,128)S(1)}, f32[8,2,2,64,128]{4,3,2,1,0:T(8,128)S(1)}, u32[]{:S(2)}, u32[]{:S(2)}) collective-permute-start(f32[8,2,2,64,128]{4,3,2,1,0:T(8,128)S(1)} %pad_maximum_fusion.mine_ref), channel_id=1, source_target_pairs={{0,1},{1,0},{2,3},{3,2},{4,5},{5,4},{6,7},{7,6},{8,9},{9,8},{10,11... | collective-permute-start | bytes 3145736 | tf_op jit(solution)/shard_map/ppermute | solution.py:81
  24.5 7.5 %collective-permute-start.5 = (f32[2,1,64,128]{3,2,1,0:T(8,128)S(1)}, f32[2,1,64,128]{3,2,1,0:T(8,128)S(1)}, u32[]{:S(2)}, u32[]{:S(2)}) collective-permute-start(f32[2,1,64,128]{3,2,1,0:T(8,128)S(1)} %get-tuple-element.6), channel_id=1, source_target_pairs={{1,0},{2,1},{3,2},{4,3},{5,4},{6,5},{7,6},{8,7},{9,8},{10,9},{11,1... | collective-permute-start | bytes 196616 | tf_op jit(solution)/shard_map/ppermute | solution.py:461
  29.9 6.5 %collective-permute-start.4 = (f32[2,1,64,128]{3,2,1,0:T(8,128)S(1)}, f32[2,1,64,128]{3,2,1,0:T(8,128)S(1)}, u32[]{:S(2)}, u32[]{:S(2)}) collective-permute-start(f32[2,1,64,128]{3,2,1,0:T(8,128)S(1)} %get-tuple-element.7), channel_id=1, source_target_pairs={{0,1},{1,2},{2,3},{3,4},{4,5},{5,6},{6,7},{7,8},{8,9},{9,10},{10,1... | collective-permute-start | bytes 196616 | tf_op jit(solution)/shard_map/ppermute | solution.py:460
  31.9 4.6 %copy-start.1 = (f32[4]{0:T(128)S(1)}, f32[4]{0:T(128)}, u32[]{:S(2)}) copy-start(f32[4]{0:T(128)} %shifts_ref.1) | copy-start | bytes 52
  31.9 4.5 %copy-start.2 = (f32[4]{0:T(128)S(1)}, f32[4]{0:T(128)}, u32[]{:S(2)}) copy-start(f32[4]{0:T(128)} %weights_ref.1) | copy-start | bytes 52
  31.9 4.5 %copy-start.3 = (s32[2]{0:T(128)S(1)}, s32[2]{0:T(128)}, u32[]{:S(2)}) copy-start(s32[2]{0:T(128)} %order_ref.1) | copy-start | bytes 28
  53.6 3.9 %collective-permute-start.6 = (f32[2,32,128]{2,1,0:T(8,128)S(1)}, f32[2,32,128]{2,1,0:T(8,128)S(1)}, u32[]{:S(2)}, u32[]{:S(2)}) collective-permute-start(f32[2,32,128]{2,1,0:T(8,128)S(1)} %slice_bitcast_fusion), channel_id=1, source_target_pairs={{0,16},{16,0},{1,17},{17,1},{2,18},{18,2},{3,19},{19,3},{4,20},{20... | collective-permute-start | bytes 98312 | tf_op jit(solution)/shard_map/ppermute | solution.py:516

commit v4 on v3

--- a/solution.py
+++ b/solution.py
@@ -53,18 +53,18 @@
     return jnp.where(lane < HALF, first, second)
 
 
-def swap_masks(peers):
+def swap_masks(peers, flip):
     even = []
     mask = peers // 2
     while mask > 1:
         even.append(mask)
         mask //= 2
     odd = even[-1:] + even[:-1]
-    return even, odd
-
-
-def offset_of(t, parity, peers):
-    even, odd = swap_masks(peers)
+    return (odd, even) if flip else (even, odd)
+
+
+def offset_of(t, parity, peers, flip):
+    even, odd = swap_masks(peers, flip)
     offset = jnp.int32(0)
     for step, (mask_even, mask_odd) in enumerate(zip(even, odd)):
         mask = jnp.where(parity == 0, mask_even, mask_odd)
@@ -72,13 +72,22 @@
     return offset
 
 
-def gather_blocks(block, axis):
+def gather_blocks(blocks, halos, axis):
     peers = lax.axis_size(axis)
-    held = block[None]
-    for masks in zip(*swap_masks(peers)):
-        pairs = [(i, i ^ masks[i % 2]) for i in range(peers)]
-        held = jnp.concatenate([held, lax.ppermute(held, axis, pairs)], axis=0)
-    return held, lax.ppermute(held, axis, [(i, i ^ 1) for i in range(peers)])
+    held = [block[None] for block in blocks]
+    swaps = [list(zip(*swap_masks(peers, flip))) for flip in (False, True)]
+    steps = len(swaps[0])
+    for step in range(steps):
+        if step == steps - 1:
+            held[0], arrays = lax.optimization_barrier((held[0], [array for array, _ in halos]))
+            halos = [lax.ppermute(array, axis, pairs) for array, (_, pairs) in zip(arrays, halos)]
+        for at in (0, 1):
+            masks = swaps[at][step]
+            pairs = [(i, i ^ masks[i % 2]) for i in range(peers)]
+            held[at] = jnp.concatenate([held[at], lax.ppermute(held[at], axis, pairs)], axis=0)
+    held[0], halos = lax.optimization_barrier((held[0], halos))
+    other = [lax.ppermute(part, axis, [(i, i ^ 1) for i in range(peers)]) for part in held]
+    return held, other, halos
 
 
 def solve_kernel(
@@ -86,8 +95,10 @@
     shifts_ref,
     weights_ref,
     order_ref,
-    mine_ref,
-    theirs_ref,
+    kappa_mine_ref,
+    misfit_mine_ref,
+    kappa_theirs_ref,
+    misfit_theirs_ref,
     before_ref,
     state_ref,
     after_ref,
@@ -113,7 +124,7 @@
     coarse_two,
     planes,
 ):
-    blocks, _, own, rows, _ = mine_ref.shape
+    blocks, own, rows, _ = kappa_mine_ref.shape
     coarse_x = blocks * own
     rows = rows // 2
     tiles = rows // TILE
@@ -166,19 +177,24 @@
         return even, odd
 
     def arrange(t, carry):
-        for ref, holder in ((mine_ref, place_ref[0]), (theirs_ref, place_ref[0] ^ 1)):
-            home = holder ^ offset_of(t, holder % 2, 2 * blocks)
+        for flip, ref, holder in (
+            (False, kappa_mine_ref, place_ref[0]),
+            (False, kappa_theirs_ref, place_ref[0] ^ 1),
+            (True, misfit_mine_ref, place_ref[0]),
+            (True, misfit_theirs_ref, place_ref[0] ^ 1),
+        ):
+            home = holder ^ offset_of(t, holder % 2, 2 * blocks, flip)
             for x in range(own):
                 a = x % 2
                 spot = home * (own // 2) + x // 2
                 for b in (0, 1):
                     for j in range(tiles):
-                        block = ref[t, 0, x, every(b, j), :]
-                        for c, value in enumerate(split(block)):
-                            half_kappa[cls(a, b, c), spot + 1, tile(j)] = 0.5 * value
-                        block = ref[t, 1, x, every(b, j), :]
-                        for c, value in enumerate(split(block)):
-                            residual[cls(a, b, c), spot, tile(j)] = weight * value
+                        for c, value in enumerate(split(ref[t, x, every(b, j), :])):
+                            k = cls(a, b, c)
+                            if flip:
+                                residual[k, spot, tile(j)] = weight * value
+                            else:
+                                half_kappa[k, spot + 1, tile(j)] = 0.5 * value
         return carry
 
     lax.fori_loop(0, blocks, arrange, 0)
@@ -457,9 +473,9 @@
     peers = lax.axis_size("space")
     up = [(i, i + 1) for i in range(peers - 1)]
     down = [(i + 1, i) for i in range(peers - 1)]
-    before = lax.ppermute(forward_states[:, own - 1 :], "space", up)
-    after = lax.ppermute(forward_states[:, :1], "space", down)
-    mine, theirs = gather_blocks(jnp.stack([conductivity, misfit]), "space")
+    halos = [(forward_states[:, own - 1 :], up), (forward_states[:, :1], down)]
+    mine, theirs, halos = gather_blocks([conductivity, misfit], halos, "space")
+    before, after = halos
     coarse_x, rows = peers * own // 2, ny // 2
     lanes = 2 * HALF
 
@@ -474,7 +490,7 @@
             jax.ShapeDtypeStruct(forward_states.shape, jnp.float32),
             jax.ShapeDtypeStruct((groups, own, ny // groups, nz), jnp.float32),
         ),
-        in_specs=[smem] * 4 + [vmem] * 5,
+        in_specs=[smem] * 4 + [vmem] * 7,
         out_specs=(vmem, vmem),
         scratch_shapes=[
             scratch(8, coarse_x + 2),
@@ -504,8 +520,8 @@
         pole_shifts,
         pole_weights,
         pole_order,
-        mine,
-        theirs,
+        *mine,
+        *theirs,
         before,
         forward_states,
         after,

time: 58.3 us -> 53.4 us (0.916)
  the two profiles are of different devices: /device:TPU:12 before, /device:TPU:14 now
where the time goes in v4:
time: 53.4 us; the launch traced here: 53.2 us
  starting transfers between devices  19.9 us (37%)
  Pallas kernels  17.1 us (32%)
  waiting for transfers between devices  13.7 us (26%)
  other arithmetic  1.67 us (3%)
  between operations  0.76 us (1%)
    pallas_call x1, Pallas kernels, whole_grid(): pl.pallas_call(solve_kernel, out_shape=(jax.ShapeDtypeStruct(forward_stat...  17.1 us
    ppermute x6, starting transfers between devices, gather_blocks(): lax.ppermute(held[at], axis, pairs)  9.9 us
    ppermute x6, waiting for transfers between devices, gather_blocks(): lax.ppermute(held[at], axis, pairs)  5.89 us
    ppermute x2, starting transfers between devices, gather_blocks(): lax.ppermute(array, axis, pairs)  5.55 us
    ppermute x2, starting transfers between devices, gather_blocks(): lax.ppermute(part, axis, [(i, i ^ 1) for i in range(peers)])  3.9 us
    ppermute x1, waiting for transfers between devices, whole_grid(): gradient = gradient + lax.ppermute(share[k], 'pole', ring)  3.41 us
    ppermute x2, waiting for transfers between devices, gather_blocks(): lax.ppermute(array, axis, pairs)  2.41 us
    ppermute x2, waiting for transfers between devices, gather_blocks(): lax.ppermute(part, axis, [(i, i ^ 1) for i in range(peers)])  2.04 us
  transfers between devices with their start and end apart: 11, of which 7 were waited for; matrix products, arithmetic and copies ran while one was open for 2% of the time, Pallas kernels for 0%

profile of v4, /device:TPU:14, one launch (start us, length us, event | category | flops | bytes accessed | tf_op | source)
XLA Modules:
  0.0 53.2 jit_solution(7183828255576213364)
XLA Ops:
  0.6 2.7 %collective-permute-start = (f32[1,2,64,128]{3,2,1,0:T(8,128)}, f32[1,2,64,128]{3,2,1,0:T(8,128)S(1)}, u32[]{:S(2)}, u32[]{:S(2)}) collective-permute-start(f32[1,2,64,128]{3,2,1,0:T(8,128)} %bitcast.12), channel_id=1, source_target_pairs={{0,8},{1,3},{2,10},{3,1},{4,12},{5,7},{6,14},{7,5},{8,0},{9,11},{1... | collective-permute-start | bytes 196616 | tf_op jit(solution)/shard_map/ppermute | solution.py:87
  3.3 0.5 %collective-permute-start.5 = (f32[1,2,64,128]{3,2,1,0:T(8,128)}, f32[1,2,64,128]{3,2,1,0:T(8,128)S(1)}, u32[]{:S(2)}, u32[]{:S(2)}) collective-permute-start(f32[1,2,64,128]{3,2,1,0:T(8,128)} %bitcast.8), channel_id=1, source_target_pairs={{0,2},{1,9},{2,0},{3,11},{4,6},{5,13},{6,4},{7,15},{8,10},{9,1},{1... | collective-permute-start | bytes 196616 | tf_op jit(solution)/shard_map/ppermute | solution.py:87
  3.8 2.7 %collective-permute-done = f32[1,2,64,128]{3,2,1,0:T(8,128)S(1)} collective-permute-done((f32[1,2,64,128]{3,2,1,0:T(8,128)}, f32[1,2,64,128]{3,2,1,0:T(8,128)S(1)}, u32[]{:S(2)}, u32[]{:S(2)}) %collective-permute-start) | collective-permute-done | bytes 65568 | tf_op jit(solution)/shard_map/ppermute | solution.py:87
  6.5 0.8 %pad_maximum_fusion.4 = f32[2,2,64,128]{3,2,1,0:T(8,128)S(1)} fusion(f32[1,2,64,128]{3,2,1,0:T(8,128)S(1)} %collective-permute-done, f32[1,2,64,128]{3,2,1,0:T(8,128)} %bitcast.13), kind=kLoop, calls=%fused_computation.4 | loop fusion | flops 32768 | bytes 262144 | tf_op jit(solution)/shard_map/concatenate | solution.py:87
  7.4 0.0 copy-start
  7.4 1.5 %collective-permute-start.1 = (f32[2,2,64,128]{3,2,1,0:T(8,128)S(1)}, f32[2,2,64,128]{3,2,1,0:T(8,128)S(1)}, u32[]{:S(2)}, u32[]{:S(2)}) collective-permute-start(f32[2,2,64,128]{3,2,1,0:T(8,128)S(1)} %pad_maximum_fusion.4), channel_id=1, source_target_pairs={{0,4},{1,9},{2,6},{3,11},{4,0},{5,13},{6,2},{7,15},{8,12},{9,1},{1... | collective-permute-start | bytes 393224 | tf_op jit(solution)/shard_map/ppermute | solution.py:87
  8.9 0.0 collective-permute-done.5
  8.9 0.0 copy-start.5
  8.9 1.9 %collective-permute-start.6 = (f32[2,2,64,128]{3,2,1,0:T(8,128)S(1)}, f32[2,2,64,128]{3,2,1,0:T(8,128)S(1)}, u32[]{:S(2)}, u32[]{:S(2)}) collective-permute-start(f32[2,2,64,128]{3,2,1,0:T(8,128)S(1)} %pad_maximum_fusion.5), channel_id=1, source_target_pairs={{0,8},{1,5},{2,10},{3,7},{4,12},{5,1},{6,14},{7,3},{8,0},{9,13},{1... | collective-permute-start | bytes 393224 | tf_op jit(solution)/shard_map/ppermute | solution.py:87
  10.8 1.8 %collective-permute-done.1 = f32[2,2,64,128]{3,2,1,0:T(8,128)S(1)} collective-permute-done((f32[2,2,64,128]{3,2,1,0:T(8,128)S(1)}, f32[2,2,64,128]{3,2,1,0:T(8,128)S(1)}, u32[]{:S(2)}, u32[]{:S(2)}) %collective-permute-start.1) | collective-permute-done | bytes 131104 | tf_op jit(solution)/shard_map/ppermute | solution.py:87
  12.6 1.5 %collective-permute-start.2 = (f32[4,2,64,128]{3,2,1,0:T(8,128)S(1)}, f32[4,2,64,128]{3,2,1,0:T(8,128)S(1)}, u32[]{:S(2)}, u32[]{:S(2)}) collective-permute-start(f32[4,2,64,128]{3,2,1,0:T(8,128)S(1)} %pad_maximum_fusion.2), channel_id=1, source_target_pairs={{0,2},{1,5},{2,0},{3,7},{4,6},{5,1},{6,4},{7,3},{8,10},{9,13},{10,... | collective-permute-start | bytes 786440 | tf_op jit(solution)/shard_map/ppermute | solution.py:87
  14.2 1.4 %collective-permute-done.6 = f32[2,2,64,128]{3,2,1,0:T(8,128)S(1)} collective-permute-done((f32[2,2,64,128]{3,2,1,0:T(8,128)S(1)}, f32[2,2,64,128]{3,2,1,0:T(8,128)S(1)}, u32[]{:S(2)}, u32[]{:S(2)}) %collective-permute-start.6) | collective-permute-done | bytes 131104 | tf_op jit(solution)/shard_map/ppermute | solution.py:87
  15.6 1.7 %collective-permute-start.7 = (f32[4,2,64,128]{3,2,1,0:T(8,128)S(1)}, f32[4,2,64,128]{3,2,1,0:T(8,128)S(1)}, u32[]{:S(2)}, u32[]{:S(2)}) collective-permute-start(f32[4,2,64,128]{3,2,1,0:T(8,128)S(1)} %pad_maximum_fusion.3), channel_id=1, source_target_pairs={{0,4},{1,3},{2,6},{3,1},{4,0},{5,7},{6,2},{7,5},{8,12},{9,11},{10,... | collective-permute-start | bytes 786440 | tf_op jit(solution)/shard_map/ppermute | solution.py:87
  17.4 1.9 %collective-permute-start.3 = (f32[2,1,64,128]{3,2,1,0:T(8,128)S(1)}, f32[2,1,64,128]{3,2,1,0:T(8,128)S(1)}, u32[]{:S(2)}, u32[]{:S(2)}) collective-permute-start(f32[2,1,64,128]{3,2,1,0:T(8,128)S(1)} %get-tuple-element.11), channel_id=1, source_target_pairs={{0,1},{1,2},{2,3},{3,4},{4,5},{5,6},{6,7},{7,8},{8,9},{9,10},{10,1... | collective-permute-start | bytes 196616 | tf_op jit(solution)/shard_map/ppermute | solution.py:83
  19.3 3.6 %collective-permute-start.4 = (f32[2,1,64,128]{3,2,1,0:T(8,128)S(1)}, f32[2,1,64,128]{3,2,1,0:T(8,128)S(1)}, u32[]{:S(2)}, u32[]{:S(2)}) collective-permute-start(f32[2,1,64,128]{3,2,1,0:T(8,128)S(1)} %get-tuple-element.12), channel_id=1, source_target_pairs={{1,0},{2,1},{3,2},{4,3},{5,4},{6,5},{7,6},{8,7},{9,8},{10,9},{11,1... | collective-permute-start | bytes 196616 | tf_op jit(solution)/shard_map/ppermute | solution.py:83
  22.9 0.0 collective-permute-done.2
  23.0 0.0 collective-permute-done.3.before_ref
  23.0 2.4 %collective-permute-done.4.after_ref = f32[2,1,64,128]{3,2,1,0:T(8,128)S(1)} collective-permute-done((f32[2,1,64,128]{3,2,1,0:T(8,128)S(1)}, f32[2,1,64,128]{3,2,1,0:T(8,128)S(1)}, u32[]{:S(2)}, u32[]{:S(2)}) %collective-permute-start.4) | collective-permute-done | bytes 65568 | tf_op jit(solution)/shard_map/ppermute | solution.py:83
  25.4 3.8 %collective-permute-start.8 = (f32[8,2,64,128]{3,2,1,0:T(8,128)S(1)}, f32[8,2,64,128]{3,2,1,0:T(8,128)S(1)}, u32[]{:S(2)}, u32[]{:S(2)}) collective-permute-start(f32[8,2,64,128]{3,2,1,0:T(8,128)S(1)} %pad_maximum_fusion.kappa_mine_ref), channel_id=1, source_target_pairs={{0,1},{1,0},{2,3},{3,2},{4,5},{5,4},{6,7},{7,6},{8,9},{9,8},{10,11... | collective-permute-start | bytes 1572872 | tf_op jit(solution)/shard_map/ppermute | solution.py:89
  29.3 0.0 collective-permute-done.7
  29.3 0.1 collective-permute-start.9
  29.4 0.0 copy-start.1
  29.4 0.0 copy-start.2
  29.4 0.0 copy-start.3
  29.4 0.1 pad_add_fusion.place_ref
  29.5 1.3 %collective-permute-done.8.kappa_theirs_ref = f32[8,2,64,128]{3,2,1,0:T(8,128)S(1)} collective-permute-done((f32[8,2,64,128]{3,2,1,0:T(8,128)S(1)}, f32[8,2,64,128]{3,2,1,0:T(8,128)S(1)}, u32[]{:S(2)}, u32[]{:S(2)}) %collective-permute-start.8) | collective-permute-done | bytes 524320 | tf_op jit(solution)/shard_map/ppermute | solution.py:89
  30.8 0.7 %collective-permute-done.9.misfit_theirs_ref = f32[8,2,64,128]{3,2,1,0:T(8,128)S(1)} collective-permute-done((f32[8,2,64,128]{3,2,1,0:T(8,128)S(1)}, f32[8,2,64,128]{3,2,1,0:T(8,128)S(1)}, u32[]{:S(2)}, u32[]{:S(2)}) %collective-permute-start.9) | collective-permute-done | bytes 524320 | tf_op jit(solution)/shard_map/ppermute | solution.py:89
  31.5 0.0 copy-done.1
  31.6 17.1 %solve.1 = (f32[2,2,64,128]{3,2,1,0:T(8,128)}, f32[2,2,32,128]{3,2,1,0:T(8,128)S(1)}) custom-call(s32[2]{0:T(128)S(1)} %pad_add_fusion.place_ref, f32[4]{0:T(128)S(1)} %copy-done.1, f32[4]{0:T(128)S(1)} %copy-done.2, s32[2]{0:T(128)S(1)} %copy-done.3, f32[8,2,64,128]{3,2,1,0:T(8,128)S(1)} %pad_maximum_fusion.kappa_mine_ref, ...), custom_call_target="tpu_custom_call" | custom-call | tf_op jit(solution)/shard_map/solve/pallas_call | solution.py:487
  48.7 0.5 collective-permute-start.10
  49.2 3.4 %collective-permute-done.10 = f32[2,32,128]{2,1,0:T(8,128)S(1)} collective-permute-done((f32[2,32,128]{2,1,0:T(8,128)S(1)}, f32[2,32,128]{2,1,0:T(8,128)S(1)}, u32[]{:S(2)}, u32[]{:S(2)}) %collective-permute-start.10) | collective-permute-done | bytes 32800 | tf_op jit(solution)/shard_map/ppermute | solution.py:532
  52.6 0.6 %bitcast_add_fusion = f32[2,32,128]{2,1,0:T(8,128)} fusion(f32[2,32,128]{2,1,0:T(8,128)S(1)} %collective-permute-done.10, f32[2,2,32,128]{3,2,1,0:T(8,128)S(1)} %get-tuple-element.17), kind=kLoop, calls=%fused_computation.6 | loop fusion | flops 8192 | bytes 98304 | tf_op jit(solution)/shard_map/add | solution.py:532
  (13 shorter events, 0.2 us)
Async XLA Ops:
  0.6 5.9 %collective-permute-start = (f32[1,2,64,128]{3,2,1,0:T(8,128)}, f32[1,2,64,128]{3,2,1,0:T(8,128)S(1)}, u32[]{:S(2)}, u32[]{:S(2)}) collective-permute-start(f32[1,2,64,128]{3,2,1,0:T(8,128)} %bitcast.12), channel_id=1, source_target_pairs={{0,8},{1,3},{2,10},{3,1},{4,12},{5,7},{6,14},{7,5},{8,0},{9,11},{1... | collective-permute-start | bytes 196616 | tf_op jit(solution)/shard_map/ppermute | solution.py:87
  3.3 5.6 %copy-start.4 = (f32[2,64,128]{2,1,0:T(8,128)S(1)}, f32[2,64,128]{2,1,0:T(8,128)}, u32[]{:S(2)}) copy-start(f32[2,64,128]{2,1,0:T(8,128)} %param.7) | copy-start | bytes 196612
  3.3 5.6 %collective-permute-start.5 = (f32[1,2,64,128]{3,2,1,0:T(8,128)}, f32[1,2,64,128]{3,2,1,0:T(8,128)S(1)}, u32[]{:S(2)}, u32[]{:S(2)}) collective-permute-start(f32[1,2,64,128]{3,2,1,0:T(8,128)} %bitcast.8), channel_id=1, source_target_pairs={{0,2},{1,9},{2,0},{3,11},{4,6},{5,13},{6,4},{7,15},{8,10},{9,1},{1... | collective-permute-start | bytes 196616 | tf_op jit(solution)/shard_map/ppermute | solution.py:87
  7.4 3.5 %copy-start = (f32[2,2,64,128]{3,2,1,0:T(8,128)S(1)}, f32[2,2,64,128]{3,2,1,0:T(8,128)}, u32[]{:S(2)}) copy-start(f32[2,2,64,128]{3,2,1,0:T(8,128)} %state_ref.1) | copy-start | bytes 393220
  7.4 5.2 %collective-permute-start.1 = (f32[2,2,64,128]{3,2,1,0:T(8,128)S(1)}, f32[2,2,64,128]{3,2,1,0:T(8,128)S(1)}, u32[]{:S(2)}, u32[]{:S(2)}) collective-permute-start(f32[2,2,64,128]{3,2,1,0:T(8,128)S(1)} %pad_maximum_fusion.4), channel_id=1, source_target_pairs={{0,4},{1,9},{2,6},{3,11},{4,0},{5,13},{6,2},{7,15},{8,12},{9,1},{1... | collective-permute-start | bytes 393224 | tf_op jit(solution)/shard_map/ppermute | solution.py:87
  8.9 3.7 %copy-start.5 = (f32[2,64,128]{2,1,0:T(8,128)S(1)}, f32[2,64,128]{2,1,0:T(8,128)}, u32[]{:S(2)}) copy-start(f32[2,64,128]{2,1,0:T(8,128)} %param.6) | copy-start | bytes 196612
  8.9 6.7 %collective-permute-start.6 = (f32[2,2,64,128]{3,2,1,0:T(8,128)S(1)}, f32[2,2,64,128]{3,2,1,0:T(8,128)S(1)}, u32[]{:S(2)}, u32[]{:S(2)}) collective-permute-start(f32[2,2,64,128]{3,2,1,0:T(8,128)S(1)} %pad_maximum_fusion.5), channel_id=1, source_target_pairs={{0,8},{1,5},{2,10},{3,7},{4,12},{5,1},{6,14},{7,3},{8,0},{9,13},{1... | collective-permute-start | bytes 393224 | tf_op jit(solution)/shard_map/ppermute | solution.py:87
  12.6 10.3 %collective-permute-start.2 = (f32[4,2,64,128]{3,2,1,0:T(8,128)S(1)}, f32[4,2,64,128]{3,2,1,0:T(8,128)S(1)}, u32[]{:S(2)}, u32[]{:S(2)}) collective-permute-start(f32[4,2,64,128]{3,2,1,0:T(8,128)S(1)} %pad_maximum_fusion.2), channel_id=1, source_target_pairs={{0,2},{1,5},{2,0},{3,7},{4,6},{5,1},{6,4},{7,3},{8,10},{9,13},{10,... | collective-permute-start | bytes 786440 | tf_op jit(solution)/shard_map/ppermute | solution.py:87
  15.6 13.6 %collective-permute-start.7 = (f32[4,2,64,128]{3,2,1,0:T(8,128)S(1)}, f32[4,2,64,128]{3,2,1,0:T(8,128)S(1)}, u32[]{:S(2)}, u32[]{:S(2)}) collective-permute-start(f32[4,2,64,128]{3,2,1,0:T(8,128)S(1)} %pad_maximum_fusion.3), channel_id=1, source_target_pairs={{0,4},{1,3},{2,6},{3,1},{4,0},{5,7},{6,2},{7,5},{8,12},{9,11},{10,... | collective-permute-start | bytes 786440 | tf_op jit(solution)/shard_map/ppermute | solution.py:87
  17.4 5.6 %collective-permute-start.3 = (f32[2,1,64,128]{3,2,1,0:T(8,128)S(1)}, f32[2,1,64,128]{3,2,1,0:T(8,128)S(1)}, u32[]{:S(2)}, u32[]{:S(2)}) collective-permute-start(f32[2,1,64,128]{3,2,1,0:T(8,128)S(1)} %get-tuple-element.11), channel_id=1, source_target_pairs={{0,1},{1,2},{2,3},{3,4},{4,5},{5,6},{6,7},{7,8},{8,9},{9,10},{10,1... | collective-permute-start | bytes 196616 | tf_op jit(solution)/shard_map/ppermute | solution.py:83
  19.3 6.1 %collective-permute-start.4 = (f32[2,1,64,128]{3,2,1,0:T(8,128)S(1)}, f32[2,1,64,128]{3,2,1,0:T(8,128)S(1)}, u32[]{:S(2)}, u32[]{:S(2)}) collective-permute-start(f32[2,1,64,128]{3,2,1,0:T(8,128)S(1)} %get-tuple-element.12), channel_id=1, source_target_pairs={{1,0},{2,1},{3,2},{4,3},{5,4},{6,5},{7,6},{8,7},{9,8},{10,9},{11,1... | collective-permute-start | bytes 196616 | tf_op jit(solution)/shard_map/ppermute | solution.py:83
  25.4 5.4 %collective-permute-start.8 = (f32[8,2,64,128]{3,2,1,0:T(8,128)S(1)}, f32[8,2,64,128]{3,2,1,0:T(8,128)S(1)}, u32[]{:S(2)}, u32[]{:S(2)}) collective-permute-start(f32[8,2,64,128]{3,2,1,0:T(8,128)S(1)} %pad_maximum_fusion.kappa_mine_ref), channel_id=1, source_target_pairs={{0,1},{1,0},{2,3},{3,2},{4,5},{5,4},{6,7},{7,6},{8,9},{9,8},{10,11... | collective-permute-start | bytes 1572872 | tf_op jit(solution)/shard_map/ppermute | solution.py:89
  29.3 2.2 %collective-permute-start.9 = (f32[8,2,64,128]{3,2,1,0:T(8,128)S(1)}, f32[8,2,64,128]{3,2,1,0:T(8,128)S(1)}, u32[]{:S(2)}, u32[]{:S(2)}) collective-permute-start(f32[8,2,64,128]{3,2,1,0:T(8,128)S(1)} %pad_maximum_fusion.1.misfit_mine_ref), channel_id=1, source_target_pairs={{0,1},{1,0},{2,3},{3,2},{4,5},{5,4},{6,7},{7,6},{8,9},{9,8},{10,11... | collective-permute-start | bytes 1572872 | tf_op jit(solution)/shard_map/ppermute | solution.py:89
  29.4 2.2 %copy-start.1 = (f32[4]{0:T(128)S(1)}, f32[4]{0:T(128)}, u32[]{:S(2)}) copy-start(f32[4]{0:T(128)} %shifts_ref.1) | copy-start | bytes 52
  29.4 2.1 %copy-start.2 = (f32[4]{0:T(128)S(1)}, f32[4]{0:T(128)}, u32[]{:S(2)}) copy-start(f32[4]{0:T(128)} %weights_ref.1) | copy-start | bytes 52
  29.4 2.1 %copy-start.3 = (s32[2]{0:T(128)S(1)}, s32[2]{0:T(128)}, u32[]{:S(2)}) copy-start(s32[2]{0:T(128)} %order_ref.1) | copy-start | bytes 28
  48.7 3.9 %collective-permute-start.10 = (f32[2,32,128]{2,1,0:T(8,128)S(1)}, f32[2,32,128]{2,1,0:T(8,128)S(1)}, u32[]{:S(2)}, u32[]{:S(2)}) collective-permute-start(f32[2,32,128]{2,1,0:T(8,128)S(1)} %slice_bitcast_fusion), channel_id=1, source_target_pairs={{0,16},{16,0},{1,17},{17,1},{2,18},{18,2},{3,19},{19,3},{4,20},{20... | collective-permute-start | bytes 98312 | tf_op jit(solution)/shard_map/ppermute | solution.py:532

commit v5 on v4

--- a/solution.py
+++ b/solution.py
@@ -85,7 +85,6 @@
             masks = swaps[at][step]
             pairs = [(i, i ^ masks[i % 2]) for i in range(peers)]
             held[at] = jnp.concatenate([held[at], lax.ppermute(held[at], axis, pairs)], axis=0)
-    held[0], halos = lax.optimization_barrier((held[0], halos))
     other = [lax.ppermute(part, axis, [(i, i ^ 1) for i in range(peers)]) for part in held]
     return held, other, halos
 
@@ -99,9 +98,9 @@
     misfit_mine_ref,
     kappa_theirs_ref,
     misfit_theirs_ref,
-    before_ref,
     state_ref,
-    after_ref,
+    far_ref,
+    near_ref,
     adjoint_ref,
     share_ref,
     half_kappa,
@@ -445,6 +444,7 @@
         edge = full[axis] - 1 if up else 0
         return value - jnp.where(at == edge, 0.0, moved)
 
+    is_even = place_ref[0] % 2 == 0
     groups = share_ref.shape[0]
     chunk = share_ref.shape[2]
     for j in range(own):
@@ -453,8 +453,8 @@
             here = planes[slot, j + 1]
             adjoint_ref[slot, j] = here
             f = state_ref[slot, j]
-            f_low = state_ref[slot, j - 1] if j else before_ref[slot, 0]
-            f_high = state_ref[slot, j + 1] if j + 1 < own else after_ref[slot, 0]
+            f_low = state_ref[slot, j - 1] if j else jnp.where(is_even, far_ref[slot, 0], near_ref[slot, 0])
+            f_high = state_ref[slot, j + 1] if j + 1 < own else jnp.where(is_even, near_ref[slot, 0], far_ref[slot, 0])
             term = term + (here - planes[slot, j + 2]) * (f - f_high)
             term = term + (here - planes[slot, j]) * (f - f_low)
             for axis in (0, 1):
@@ -471,11 +471,13 @@
     groups = lax.axis_size("pole")
     place = jnp.stack([lax.axis_index("space"), lax.axis_index("pole")]).astype(jnp.int32)
     peers = lax.axis_size("space")
-    up = [(i, i + 1) for i in range(peers - 1)]
-    down = [(i + 1, i) for i in range(peers - 1)]
-    halos = [(forward_states[:, own - 1 :], up), (forward_states[:, :1], down)]
+    even = place[0] % 2 == 0
+    first, last = forward_states[:, :1], forward_states[:, own - 1 :]
+    near = [(i, i ^ 1) for i in range(peers)]
+    far = [(i, i + 1 if i % 2 else i - 1) for i in range(1, peers - 1)]
+    halos = [(jnp.where(even, first, last), far), (jnp.where(even, last, first), near)]
     mine, theirs, halos = gather_blocks([conductivity, misfit], halos, "space")
-    before, after = halos
+    far, near = halos
     coarse_x, rows = peers * own // 2, ny // 2
     lanes = 2 * HALF
 
@@ -522,9 +524,9 @@
         pole_order,
         *mine,
         *theirs,
-        before,
         forward_states,
-        after,
+        far,
+        near,
     )
     gradient = share[0]
     for k in range(1, groups):

time: 53.4 us -> 52.5 us (0.983)
  the two profiles are of different devices: /device:TPU:14 before, /device:TPU:28 now
where the time goes in v5:
time: 52.5 us; the launch traced here: 52.3 us
  waiting for transfers between devices  24.3 us (46%)
  Pallas kernels  17 us (32%)
  starting transfers between devices  8.48 us (16%)
  other arithmetic  1.65 us (3%)
  between operations  0.8 us (2%)
    ppermute x6, waiting for transfers between devices, gather_blocks(): lax.ppermute(held[at], axis, pairs)  17.4 us
    pallas_call x1, Pallas kernels, whole_grid(): pl.pallas_call(solve_kernel, out_shape=(jax.ShapeDtypeStruct(forward_stat...  17 us
    ppermute x6, starting transfers between devices, gather_blocks(): lax.ppermute(held[at], axis, pairs)  4.85 us
    ppermute x2, waiting for transfers between devices, gather_blocks(): lax.ppermute(array, axis, pairs)  3.47 us
    ppermute x1, waiting for transfers between devices, whole_grid(): gradient = gradient + lax.ppermute(share[k], 'pole', ring)  3.41 us
    ppermute x2, starting transfers between devices, gather_blocks(): lax.ppermute(array, axis, pairs)  2.99 us
  transfers between devices with their start and end apart: 11, of which 6 were waited for; matrix products, arithmetic and copies ran while one was open for 2% of the time, Pallas kernels for 0%

profile of v5, /device:TPU:28, one launch (start us, length us, event | category | flops | bytes accessed | tf_op | source)
XLA Modules:
  0.0 52.3 jit_solution(12375346299055547574)
XLA Ops:
  0.6 0.4 collective-permute-start
  1.0 1.5 %collective-permute-start.3 = (f32[1,2,64,128]{3,2,1,0:T(8,128)}, f32[1,2,64,128]{3,2,1,0:T(8,128)S(1)}, u32[]{:S(2)}, u32[]{:S(2)}) collective-permute-start(f32[1,2,64,128]{3,2,1,0:T(8,128)} %bitcast.8), channel_id=1, source_target_pairs={{0,2},{1,9},{2,0},{3,11},{4,6},{5,13},{6,4},{7,15},{8,10},{9,1},{1... | collective-permute-start | bytes 196616 | tf_op jit(solution)/shard_map/ppermute | solution.py:87
  2.5 5.5 %collective-permute-done = f32[1,2,64,128]{3,2,1,0:T(8,128)S(1)} collective-permute-done((f32[1,2,64,128]{3,2,1,0:T(8,128)}, f32[1,2,64,128]{3,2,1,0:T(8,128)S(1)}, u32[]{:S(2)}, u32[]{:S(2)}) %collective-permute-start) | collective-permute-done | bytes 65568 | tf_op jit(solution)/shard_map/ppermute | solution.py:87
  8.1 0.8 %pad_maximum_fusion.3 = f32[2,2,64,128]{3,2,1,0:T(8,128)S(1)} fusion(f32[1,2,64,128]{3,2,1,0:T(8,128)S(1)} %collective-permute-done, f32[1,2,64,128]{3,2,1,0:T(8,128)} %bitcast.13), kind=kLoop, calls=%fused_computation.3 | loop fusion | flops 32768 | bytes 262144 | tf_op jit(solution)/shard_map/concatenate | solution.py:87
  8.9 0.0 copy-start
  8.9 0.1 collective-permute-start.1
  9.0 0.0 collective-permute-done.3
  9.0 0.0 copy-done.4
  9.0 0.0 copy-start.5
  9.1 0.9 %collective-permute-start.4 = (f32[2,2,64,128]{3,2,1,0:T(8,128)S(1)}, f32[2,2,64,128]{3,2,1,0:T(8,128)S(1)}, u32[]{:S(2)}, u32[]{:S(2)}) collective-permute-start(f32[2,2,64,128]{3,2,1,0:T(8,128)S(1)} %pad_maximum_fusion.4), channel_id=1, source_target_pairs={{0,8},{1,5},{2,10},{3,7},{4,12},{5,1},{6,14},{7,3},{8,0},{9,13},{1... | collective-permute-start | bytes 393224 | tf_op jit(solution)/shard_map/ppermute | solution.py:87
  9.9 5.9 %collective-permute-done.1 = f32[2,2,64,128]{3,2,1,0:T(8,128)S(1)} collective-permute-done((f32[2,2,64,128]{3,2,1,0:T(8,128)S(1)}, f32[2,2,64,128]{3,2,1,0:T(8,128)S(1)}, u32[]{:S(2)}, u32[]{:S(2)}) %collective-permute-start.1) | collective-permute-done | bytes 131104 | tf_op jit(solution)/shard_map/ppermute | solution.py:87
  15.9 1.7 %collective-permute-start.2 = (f32[4,2,64,128]{3,2,1,0:T(8,128)S(1)}, f32[4,2,64,128]{3,2,1,0:T(8,128)S(1)}, u32[]{:S(2)}, u32[]{:S(2)}) collective-permute-start(f32[4,2,64,128]{3,2,1,0:T(8,128)S(1)} %pad_maximum_fusion.1), channel_id=1, source_target_pairs={{0,2},{1,5},{2,0},{3,7},{4,6},{5,1},{6,4},{7,3},{8,10},{9,13},{10,... | collective-permute-start | bytes 786440 | tf_op jit(solution)/shard_map/ppermute | solution.py:87
  17.5 0.0 collective-permute-done.4
  17.6 0.3 collective-permute-start.5
  17.9 4.7 %collective-permute-done.2 = f32[4,2,64,128]{3,2,1,0:T(8,128)S(1)} collective-permute-done((f32[4,2,64,128]{3,2,1,0:T(8,128)S(1)}, f32[4,2,64,128]{3,2,1,0:T(8,128)S(1)}, u32[]{:S(2)}, u32[]{:S(2)}) %collective-permute-start.2) | collective-permute-done | bytes 262176 | tf_op jit(solution)/shard_map/ppermute | solution.py:87
  22.6 0.1 collective-permute-start.6
  22.7 1.3 %collective-permute-done.5 = f32[4,2,64,128]{3,2,1,0:T(8,128)S(1)} collective-permute-done((f32[4,2,64,128]{3,2,1,0:T(8,128)S(1)}, f32[4,2,64,128]{3,2,1,0:T(8,128)S(1)}, u32[]{:S(2)}, u32[]{:S(2)}) %collective-permute-start.5) | collective-permute-done | bytes 262176 | tf_op jit(solution)/shard_map/ppermute | solution.py:87
  24.0 0.1 collective-permute-start.7
  24.1 2.9 %collective-permute-start.8 = (f32[2,1,64,128]{3,2,1,0:T(8,128)S(1)}, f32[2,1,64,128]{3,2,1,0:T(8,128)S(1)}, u32[]{:S(2)}, u32[]{:S(2)}) collective-permute-start(f32[2,1,64,128]{3,2,1,0:T(8,128)S(1)} %get-tuple-element.8), channel_id=1, source_target_pairs={{1,2},{2,1},{3,4},{4,3},{5,6},{6,5},{7,8},{8,7},{9,10},{10,9},{11,... | collective-permute-start | bytes 196616 | tf_op jit(solution)/shard_map/ppermute | solution.py:83
  27.1 0.1 collective-permute-start.9
  27.1 0.0 copy-start.1
  27.1 0.0 copy-start.2
  27.2 0.0 copy-start.3
  27.2 0.1 pad_add_fusion.place_ref
  27.2 3.5 %collective-permute-done.8.far_ref = f32[2,1,64,128]{3,2,1,0:T(8,128)S(1)} collective-permute-done((f32[2,1,64,128]{3,2,1,0:T(8,128)S(1)}, f32[2,1,64,128]{3,2,1,0:T(8,128)S(1)}, u32[]{:S(2)}, u32[]{:S(2)}) %collective-permute-start.8) | collective-permute-done | bytes 65568 | tf_op jit(solution)/shard_map/ppermute | solution.py:83
  30.7 0.0 collective-permute-done.9.near_ref
  30.7 0.0 collective-permute-done.6.kappa_theirs_ref
  30.7 0.0 collective-permute-done.7.misfit_theirs_ref
  30.8 17.0 %solve.1 = (f32[2,2,64,128]{3,2,1,0:T(8,128)}, f32[2,2,32,128]{3,2,1,0:T(8,128)S(1)}) custom-call(s32[2]{0:T(128)S(1)} %pad_add_fusion.place_ref, f32[4]{0:T(128)S(1)} %copy-done.1, f32[4]{0:T(128)S(1)} %copy-done.2, s32[2]{0:T(128)S(1)} %copy-done.3, f32[8,2,64,128]{3,2,1,0:T(8,128)S(1)} %constant_dynamic-update-slice_fusion.kappa_mine_ref, ...), custom_call_target="tpu_custom_call" | custom-call | tf_op jit(solution)/shard_map/solve/pallas_call | solution.py:489
  47.8 0.5 collective-permute-start.10
  48.3 3.4 %collective-permute-done.10 = f32[2,32,128]{2,1,0:T(8,128)S(1)} collective-permute-done((f32[2,32,128]{2,1,0:T(8,128)S(1)}, f32[2,32,128]{2,1,0:T(8,128)S(1)}, u32[]{:S(2)}, u32[]{:S(2)}) %collective-permute-start.10) | collective-permute-done | bytes 32800 | tf_op jit(solution)/shard_map/ppermute | solution.py:534
  51.7 0.6 %bitcast_add_fusion = f32[2,32,128]{2,1,0:T(8,128)} fusion(f32[2,32,128]{2,1,0:T(8,128)S(1)} %collective-permute-done.10, f32[2,2,32,128]{3,2,1,0:T(8,128)S(1)} %get-tuple-element.11), kind=kLoop, calls=%fused_computation.7 | loop fusion | flops 8192 | bytes 98304 | tf_op jit(solution)/shard_map/add | solution.py:534
  (14 shorter events, 0.1 us)
Async XLA Ops:
  0.6 7.4 %collective-permute-start = (f32[1,2,64,128]{3,2,1,0:T(8,128)}, f32[1,2,64,128]{3,2,1,0:T(8,128)S(1)}, u32[]{:S(2)}, u32[]{:S(2)}) collective-permute-start(f32[1,2,64,128]{3,2,1,0:T(8,128)} %bitcast.12), channel_id=1, source_target_pairs={{0,8},{1,3},{2,10},{3,1},{4,12},{5,7},{6,14},{7,5},{8,0},{9,11},{1... | collective-permute-start | bytes 196616 | tf_op jit(solution)/shard_map/ppermute | solution.py:87
  1.0 8.0 %collective-permute-start.3 = (f32[1,2,64,128]{3,2,1,0:T(8,128)}, f32[1,2,64,128]{3,2,1,0:T(8,128)S(1)}, u32[]{:S(2)}, u32[]{:S(2)}) collective-permute-start(f32[1,2,64,128]{3,2,1,0:T(8,128)} %bitcast.8), channel_id=1, source_target_pairs={{0,2},{1,9},{2,0},{3,11},{4,6},{5,13},{6,4},{7,15},{8,10},{9,1},{1... | collective-permute-start | bytes 196616 | tf_op jit(solution)/shard_map/ppermute | solution.py:87
  2.5 6.5 %copy-start.4 = (f32[2,64,128]{2,1,0:T(8,128)S(1)}, f32[2,64,128]{2,1,0:T(8,128)}, u32[]{:S(2)}) copy-start(f32[2,64,128]{2,1,0:T(8,128)} %param.7) | copy-start | bytes 196612
  8.9 1.0 %copy-start = (f32[2,2,64,128]{3,2,1,0:T(8,128)S(1)}, f32[2,2,64,128]{3,2,1,0:T(8,128)}, u32[]{:S(2)}) copy-start(f32[2,2,64,128]{3,2,1,0:T(8,128)} %state_ref.1) | copy-start | bytes 393220
  8.9 6.9 %collective-permute-start.1 = (f32[2,2,64,128]{3,2,1,0:T(8,128)S(1)}, f32[2,2,64,128]{3,2,1,0:T(8,128)S(1)}, u32[]{:S(2)}, u32[]{:S(2)}) collective-permute-start(f32[2,2,64,128]{3,2,1,0:T(8,128)S(1)} %pad_maximum_fusion.3), channel_id=1, source_target_pairs={{0,4},{1,9},{2,6},{3,11},{4,0},{5,13},{6,2},{7,15},{8,12},{9,1},{1... | collective-permute-start | bytes 393224 | tf_op jit(solution)/shard_map/ppermute | solution.py:87
  9.0 6.8 %copy-start.5 = (f32[2,64,128]{2,1,0:T(8,128)S(1)}, f32[2,64,128]{2,1,0:T(8,128)}, u32[]{:S(2)}) copy-start(f32[2,64,128]{2,1,0:T(8,128)} %param.6) | copy-start | bytes 196612
  9.1 8.5 %collective-permute-start.4 = (f32[2,2,64,128]{3,2,1,0:T(8,128)S(1)}, f32[2,2,64,128]{3,2,1,0:T(8,128)S(1)}, u32[]{:S(2)}, u32[]{:S(2)}) collective-permute-start(f32[2,2,64,128]{3,2,1,0:T(8,128)S(1)} %pad_maximum_fusion.4), channel_id=1, source_target_pairs={{0,8},{1,5},{2,10},{3,7},{4,12},{5,1},{6,14},{7,3},{8,0},{9,13},{1... | collective-permute-start | bytes 393224 | tf_op jit(solution)/shard_map/ppermute | solution.py:87
  15.9 6.7 %collective-permute-start.2 = (f32[4,2,64,128]{3,2,1,0:T(8,128)S(1)}, f32[4,2,64,128]{3,2,1,0:T(8,128)S(1)}, u32[]{:S(2)}, u32[]{:S(2)}) collective-permute-start(f32[4,2,64,128]{3,2,1,0:T(8,128)S(1)} %pad_maximum_fusion.1), channel_id=1, source_target_pairs={{0,2},{1,5},{2,0},{3,7},{4,6},{5,1},{6,4},{7,3},{8,10},{9,13},{10,... | collective-permute-start | bytes 786440 | tf_op jit(solution)/shard_map/ppermute | solution.py:87
  17.6 6.4 %collective-permute-start.5 = (f32[4,2,64,128]{3,2,1,0:T(8,128)S(1)}, f32[4,2,64,128]{3,2,1,0:T(8,128)S(1)}, u32[]{:S(2)}, u32[]{:S(2)}) collective-permute-start(f32[4,2,64,128]{3,2,1,0:T(8,128)S(1)} %pad_maximum_fusion.2), channel_id=1, source_target_pairs={{0,4},{1,3},{2,6},{3,1},{4,0},{5,7},{6,2},{7,5},{8,12},{9,11},{10,... | collective-permute-start | bytes 786440 | tf_op jit(solution)/shard_map/ppermute | solution.py:87
  22.6 8.1 %collective-permute-start.6 = (f32[8,2,64,128]{3,2,1,0:T(8,128)S(1)}, f32[8,2,64,128]{3,2,1,0:T(8,128)S(1)}, u32[]{:S(2)}, u32[]{:S(2)}) collective-permute-start(f32[8,2,64,128]{3,2,1,0:T(8,128)S(1)} %constant_dynamic-update-slice_fusion.kappa_mine_ref), channel_id=1, source_target_pairs={{0,1},{1,0},{2,3},{3,2},{4,5},{5,4},{6,7},{7,6},{8,9},{9,8},{10,11... | collective-permute-start | bytes 1572872 | tf_op jit(solution)/shard_map/ppermute | solution.py:88
  24.0 6.7 %collective-permute-start.7 = (f32[8,2,64,128]{3,2,1,0:T(8,128)S(1)}, f32[8,2,64,128]{3,2,1,0:T(8,128)S(1)}, u32[]{:S(2)}, u32[]{:S(2)}) collective-permute-start(f32[8,2,64,128]{3,2,1,0:T(8,128)S(1)} %pad_maximum_fusion.misfit_mine_ref), channel_id=1, source_target_pairs={{0,1},{1,0},{2,3},{3,2},{4,5},{5,4},{6,7},{7,6},{8,9},{9,8},{10,11... | collective-permute-start | bytes 1572872 | tf_op jit(solution)/shard_map/ppermute | solution.py:88
  24.1 6.6 %collective-permute-start.8 = (f32[2,1,64,128]{3,2,1,0:T(8,128)S(1)}, f32[2,1,64,128]{3,2,1,0:T(8,128)S(1)}, u32[]{:S(2)}, u32[]{:S(2)}) collective-permute-start(f32[2,1,64,128]{3,2,1,0:T(8,128)S(1)} %get-tuple-element.8), channel_id=1, source_target_pairs={{1,2},{2,1},{3,4},{4,3},{5,6},{6,5},{7,8},{8,7},{9,10},{10,9},{11,... | collective-permute-start | bytes 196616 | tf_op jit(solution)/shard_map/ppermute | solution.py:83
  27.1 3.7 %collective-permute-start.9 = (f32[2,1,64,128]{3,2,1,0:T(8,128)S(1)}, f32[2,1,64,128]{3,2,1,0:T(8,128)S(1)}, u32[]{:S(2)}, u32[]{:S(2)}) collective-permute-start(f32[2,1,64,128]{3,2,1,0:T(8,128)S(1)} %get-tuple-element.9), channel_id=1, source_target_pairs={{0,1},{1,0},{2,3},{3,2},{4,5},{5,4},{6,7},{7,6},{8,9},{9,8},{10,11... | collective-permute-start | bytes 196616 | tf_op jit(solution)/shard_map/ppermute | solution.py:83
  27.1 3.6 %copy-start.1 = (f32[4]{0:T(128)S(1)}, f32[4]{0:T(128)}, u32[]{:S(2)}) copy-start(f32[4]{0:T(128)} %shifts_ref.1) | copy-start | bytes 52
  27.1 3.6 %copy-start.2 = (f32[4]{0:T(128)S(1)}, f32[4]{0:T(128)}, u32[]{:S(2)}) copy-start(f32[4]{0:T(128)} %weights_ref.1) | copy-start | bytes 52
  27.2 3.6 %copy-start.3 = (s32[2]{0:T(128)S(1)}, s32[2]{0:T(128)}, u32[]{:S(2)}) copy-start(s32[2]{0:T(128)} %order_ref.1) | copy-start | bytes 28
  47.8 3.9 %collective-permute-start.10 = (f32[2,32,128]{2,1,0:T(8,128)S(1)}, f32[2,32,128]{2,1,0:T(8,128)S(1)}, u32[]{:S(2)}, u32[]{:S(2)}) collective-permute-start(f32[2,32,128]{2,1,0:T(8,128)S(1)} %slice_bitcast_fusion), channel_id=1, source_target_pairs={{0,16},{16,0},{1,17},{17,1},{2,18},{18,2},{3,19},{19,3},{4,20},{20... | collective-permute-start | bytes 98312 | tf_op jit(solution)/shard_map/ppermute | solution.py:534

commit v6 on v5

--- a/solution.py
+++ b/solution.py
@@ -74,17 +74,22 @@
 
 def gather_blocks(blocks, halos, axis):
     peers = lax.axis_size(axis)
+    own_half = lax.optimization_barrier(0.5 * blocks[0][None])
     held = [block[None] for block in blocks]
+    halos = [lax.ppermute(array, axis, pairs) for array, pairs in halos]
     swaps = [list(zip(*swap_masks(peers, flip))) for flip in (False, True)]
     steps = len(swaps[0])
     for step in range(steps):
         if step == steps - 1:
-            held[0], arrays = lax.optimization_barrier((held[0], [array for array, _ in halos]))
-            halos = [lax.ppermute(array, axis, pairs) for array, (_, pairs) in zip(arrays, halos)]
+            held[0], halos[0] = lax.optimization_barrier((held[0], halos[0]))
         for at in (0, 1):
             masks = swaps[at][step]
             pairs = [(i, i ^ masks[i % 2]) for i in range(peers)]
-            held[at] = jnp.concatenate([held[at], lax.ppermute(held[at], axis, pairs)], axis=0)
+            arrived = lax.ppermute(held[at], axis, pairs)
+            if step == 0 and at == 0:
+                held[0], arrived = own_half, 0.5 * arrived
+            held[at] = jnp.concatenate([held[at], arrived], axis=0)
+    held[0], halos[1] = lax.optimization_barrier((held[0], halos[1]))
     other = [lax.ppermute(part, axis, [(i, i ^ 1) for i in range(peers)]) for part in held]
     return held, other, halos
 
@@ -193,7 +198,7 @@
                             if flip:
                                 residual[k, spot, tile(j)] = weight * value
                             else:
-                                half_kappa[k, spot + 1, tile(j)] = 0.5 * value
+                                half_kappa[k, spot + 1, tile(j)] = value
         return carry
 
     lax.fori_loop(0, blocks, arrange, 0)

time: 52.5 us -> 49.4 us (0.941)
  the two profiles are of different devices: /device:TPU:28 before, /device:TPU:0 now
where the time goes in v6:
time: 49.4 us; the launch traced here: 49.3 us
  Pallas kernels  17 us (34%)
  starting transfers between devices  16.4 us (33%)
  waiting for transfers between devices  13.2 us (27%)
  other arithmetic  1.73 us (4%)
  between operations  0.78 us (2%)
    pallas_call x1, Pallas kernels, whole_grid(): pl.pallas_call(solve_kernel, out_shape=(jax.ShapeDtypeStruct(forward_stat...  17 us
    ppermute x6, starting transfers between devices, gather_blocks(): arrived = lax.ppermute(held[at], axis, pairs)  13.9 us
    ppermute x6, waiting for transfers between devices, gather_blocks(): arrived = lax.ppermute(held[at], axis, pairs)  9.07 us
    ppermute x1, waiting for transfers between devices, whole_grid(): gradient = gradient + lax.ppermute(share[k], 'pole', ring)  2.39 us
    ppermute x2, waiting for transfers between devices, gather_blocks(): lax.ppermute(part, axis, [(i, i ^ 1) for i in range(peers)])  1.78 us
    ppermute x1, starting transfers between devices, whole_grid(): gradient = gradient + lax.ppermute(share[k], 'pole', ring)  1.52 us
  transfers between devices with their start and end apart: 11, of which 6 were waited for; matrix products, arithmetic and copies ran while one was open for 2% of the time, Pallas kernels for 0%

profile of v6, /device:TPU:0, one launch (start us, length us, event | category | flops | bytes accessed | tf_op | source)
XLA Modules:
  0.0 49.3 jit_solution(7714709207584656666)
XLA Ops:
  0.6 3.0 %collective-permute-start.5 = (f32[1,2,64,128]{3,2,1,0:T(8,128)}, f32[1,2,64,128]{3,2,1,0:T(8,128)S(1)}, u32[]{:S(2)}, u32[]{:S(2)}) collective-permute-start(f32[1,2,64,128]{3,2,1,0:T(8,128)} %bitcast.10), channel_id=1, source_target_pairs={{0,2},{1,9},{2,0},{3,11},{4,6},{5,13},{6,4},{7,15},{8,10},{9,1},{1... | collective-permute-start | bytes 196616 | tf_op jit(solution)/shard_map/ppermute | solution.py:88
  3.6 2.6 %collective-permute-start = (f32[1,2,64,128]{3,2,1,0:T(8,128)}, f32[1,2,64,128]{3,2,1,0:T(8,128)S(1)}, u32[]{:S(2)}, u32[]{:S(2)}) collective-permute-start(f32[1,2,64,128]{3,2,1,0:T(8,128)} %bitcast.14), channel_id=1, source_target_pairs={{0,8},{1,3},{2,10},{3,1},{4,12},{5,7},{6,14},{7,5},{8,0},{9,11},{1... | collective-permute-start | bytes 196616 | tf_op jit(solution)/shard_map/ppermute | solution.py:88
  6.2 0.9 %multiply_bitcast_fusion = f32[1,2,64,128]{3,2,1,0:T(8,128)S(1)} fusion(f32[2,64,128]{2,1,0:T(8,128)} %param.6), kind=kLoop, calls=%fused_computation.6 | loop fusion | flops 16384 | bytes 131072 | tf_op jit(solution)/shard_map/mul | solution.py:77
  7.1 0.0 collective-permute-done.5
  7.1 0.0 copy-done.4
  7.1 2.2 %collective-permute-start.6 = (f32[2,2,64,128]{3,2,1,0:T(8,128)S(1)}, f32[2,2,64,128]{3,2,1,0:T(8,128)S(1)}, u32[]{:S(2)}, u32[]{:S(2)}) collective-permute-start(f32[2,2,64,128]{3,2,1,0:T(8,128)S(1)} %pad_maximum_fusion.5), channel_id=1, source_target_pairs={{0,8},{1,5},{2,10},{3,7},{4,12},{5,1},{6,14},{7,3},{8,0},{9,13},{1... | collective-permute-start | bytes 393224 | tf_op jit(solution)/shard_map/ppermute | solution.py:88
  9.3 0.0 collective-permute-done
  9.3 0.0 copy-start
  9.3 1.6 %collective-permute-start.1 = (f32[2,2,64,128]{3,2,1,0:T(8,128)S(1)}, f32[2,2,64,128]{3,2,1,0:T(8,128)S(1)}, u32[]{:S(2)}, u32[]{:S(2)}) collective-permute-start(f32[2,2,64,128]{3,2,1,0:T(8,128)S(1)} %pad_maximum_fusion.4), channel_id=1, source_target_pairs={{0,4},{1,9},{2,6},{3,11},{4,0},{5,13},{6,2},{7,15},{8,12},{9,1},{1... | collective-permute-start | bytes 393224 | tf_op jit(solution)/shard_map/ppermute | solution.py:88
  11.0 0.7 %collective-permute-start.2 = (f32[2,1,64,128]{3,2,1,0:T(8,128)S(1)}, f32[2,1,64,128]{3,2,1,0:T(8,128)S(1)}, u32[]{:S(2)}, u32[]{:S(2)}) collective-permute-start(f32[2,1,64,128]{3,2,1,0:T(8,128)S(1)} %get-tuple-element.15), channel_id=1, source_target_pairs={{1,2},{2,1},{3,4},{4,3},{5,6},{6,5},{7,8},{8,7},{9,10},{10,9},{11,... | collective-permute-start | bytes 196616 | tf_op jit(solution)/shard_map/ppermute | solution.py:79
  11.7 3.0 %collective-permute-done.1 = f32[2,2,64,128]{3,2,1,0:T(8,128)S(1)} collective-permute-done((f32[2,2,64,128]{3,2,1,0:T(8,128)S(1)}, f32[2,2,64,128]{3,2,1,0:T(8,128)S(1)}, u32[]{:S(2)}, u32[]{:S(2)}) %collective-permute-start.1) | collective-permute-done | bytes 131104 | tf_op jit(solution)/shard_map/ppermute | solution.py:88
  14.7 0.0 collective-permute-done.2.far_ref
  14.7 3.4 %collective-permute-start.3 = (f32[4,2,64,128]{3,2,1,0:T(8,128)S(1)}, f32[4,2,64,128]{3,2,1,0:T(8,128)S(1)}, u32[]{:S(2)}, u32[]{:S(2)}) collective-permute-start(f32[4,2,64,128]{3,2,1,0:T(8,128)S(1)} %pad_maximum_fusion.2), channel_id=1, source_target_pairs={{0,2},{1,5},{2,0},{3,7},{4,6},{5,1},{6,4},{7,3},{8,10},{9,13},{10,... | collective-permute-start | bytes 786440 | tf_op jit(solution)/shard_map/ppermute | solution.py:88
  18.1 0.0 collective-permute-done.6
  18.1 1.1 %collective-permute-start.7 = (f32[4,2,64,128]{3,2,1,0:T(8,128)S(1)}, f32[4,2,64,128]{3,2,1,0:T(8,128)S(1)}, u32[]{:S(2)}, u32[]{:S(2)}) collective-permute-start(f32[4,2,64,128]{3,2,1,0:T(8,128)S(1)} %pad_maximum_fusion.3), channel_id=1, source_target_pairs={{0,4},{1,3},{2,6},{3,1},{4,0},{5,7},{6,2},{7,5},{8,12},{9,11},{10,... | collective-permute-start | bytes 786440 | tf_op jit(solution)/shard_map/ppermute | solution.py:88
  19.2 0.2 collective-permute-start.4
  19.4 4.9 %collective-permute-done.3 = f32[4,2,64,128]{3,2,1,0:T(8,128)S(1)} collective-permute-done((f32[4,2,64,128]{3,2,1,0:T(8,128)S(1)}, f32[4,2,64,128]{3,2,1,0:T(8,128)S(1)}, u32[]{:S(2)}, u32[]{:S(2)}) %collective-permute-start.3) | collective-permute-done | bytes 262176 | tf_op jit(solution)/shard_map/ppermute | solution.py:88
  24.3 0.0 collective-permute-done.4.near_ref
  24.4 0.1 collective-permute-start.8
  24.4 1.2 %collective-permute-done.7 = f32[4,2,64,128]{3,2,1,0:T(8,128)S(1)} collective-permute-done((f32[4,2,64,128]{3,2,1,0:T(8,128)S(1)}, f32[4,2,64,128]{3,2,1,0:T(8,128)S(1)}, u32[]{:S(2)}, u32[]{:S(2)}) %collective-permute-start.7) | collective-permute-done | bytes 262176 | tf_op jit(solution)/shard_map/ppermute | solution.py:88
  25.7 0.1 collective-permute-start.9
  25.8 0.0 copy-start.1
  25.8 0.0 copy-start.2
  25.8 0.0 copy-start.3
  25.8 0.1 pad_add_fusion.place_ref
  25.9 0.4 collective-permute-done.8.kappa_theirs_ref
  26.3 1.3 %collective-permute-done.9.misfit_theirs_ref = f32[8,2,64,128]{3,2,1,0:T(8,128)S(1)} collective-permute-done((f32[8,2,64,128]{3,2,1,0:T(8,128)S(1)}, f32[8,2,64,128]{3,2,1,0:T(8,128)S(1)}, u32[]{:S(2)}, u32[]{:S(2)}) %collective-permute-start.9) | collective-permute-done | bytes 524320 | tf_op jit(solution)/shard_map/ppermute | solution.py:93
  27.7 0.0 copy-done.3
  27.7 17.0 %solve.1 = (f32[2,2,64,128]{3,2,1,0:T(8,128)}, f32[2,2,32,128]{3,2,1,0:T(8,128)S(1)}) custom-call(s32[2]{0:T(128)S(1)} %pad_add_fusion.place_ref, f32[4]{0:T(128)S(1)} %copy-done.1, f32[4]{0:T(128)S(1)} %copy-done.2, s32[2]{0:T(128)S(1)} %copy-done.3, f32[8,2,64,128]{3,2,1,0:T(8,128)S(1)} %pad_maximum_fusion.kappa_mine_ref, ...), custom_call_target="tpu_custom_call" | custom-call | tf_op jit(solution)/shard_map/solve/pallas_call | solution.py:494
  44.7 1.5 %collective-permute-start.10 = (f32[2,32,128]{2,1,0:T(8,128)S(1)}, f32[2,32,128]{2,1,0:T(8,128)S(1)}, u32[]{:S(2)}, u32[]{:S(2)}) collective-permute-start(f32[2,32,128]{2,1,0:T(8,128)S(1)} %slice_bitcast_fusion), channel_id=1, source_target_pairs={{0,16},{16,0},{1,17},{17,1},{2,18},{18,2},{3,19},{19,3},{4,20},{20... | collective-permute-start | bytes 98312 | tf_op jit(solution)/shard_map/ppermute | solution.py:539
  46.3 2.4 %collective-permute-done.10 = f32[2,32,128]{2,1,0:T(8,128)S(1)} collective-permute-done((f32[2,32,128]{2,1,0:T(8,128)S(1)}, f32[2,32,128]{2,1,0:T(8,128)S(1)}, u32[]{:S(2)}, u32[]{:S(2)}) %collective-permute-start.10) | collective-permute-done | bytes 32800 | tf_op jit(solution)/shard_map/ppermute | solution.py:539
  48.7 0.6 %bitcast_add_fusion = f32[2,32,128]{2,1,0:T(8,128)} fusion(f32[2,32,128]{2,1,0:T(8,128)S(1)} %collective-permute-done.10, f32[2,2,32,128]{3,2,1,0:T(8,128)S(1)} %get-tuple-element.13), kind=kLoop, calls=%fused_computation.9 | loop fusion | flops 8192 | bytes 98304 | tf_op jit(solution)/shard_map/add | solution.py:539
  (13 shorter events, 0.2 us)
Async XLA Ops:
  0.6 6.5 %collective-permute-start.5 = (f32[1,2,64,128]{3,2,1,0:T(8,128)}, f32[1,2,64,128]{3,2,1,0:T(8,128)S(1)}, u32[]{:S(2)}, u32[]{:S(2)}) collective-permute-start(f32[1,2,64,128]{3,2,1,0:T(8,128)} %bitcast.10), channel_id=1, source_target_pairs={{0,2},{1,9},{2,0},{3,11},{4,6},{5,13},{6,4},{7,15},{8,10},{9,1},{1... | collective-permute-start | bytes 196616 | tf_op jit(solution)/shard_map/ppermute | solution.py:88
  3.6 3.5 %copy-start.4 = (f32[2,64,128]{2,1,0:T(8,128)S(1)}, f32[2,64,128]{2,1,0:T(8,128)}, u32[]{:S(2)}) copy-start(f32[2,64,128]{2,1,0:T(8,128)} %param.7) | copy-start | bytes 196612
  3.6 5.7 %collective-permute-start = (f32[1,2,64,128]{3,2,1,0:T(8,128)}, f32[1,2,64,128]{3,2,1,0:T(8,128)S(1)}, u32[]{:S(2)}, u32[]{:S(2)}) collective-permute-start(f32[1,2,64,128]{3,2,1,0:T(8,128)} %bitcast.14), channel_id=1, source_target_pairs={{0,8},{1,3},{2,10},{3,1},{4,12},{5,7},{6,14},{7,5},{8,0},{9,11},{1... | collective-permute-start | bytes 196616 | tf_op jit(solution)/shard_map/ppermute | solution.py:88
  7.1 10.9 %collective-permute-start.6 = (f32[2,2,64,128]{3,2,1,0:T(8,128)S(1)}, f32[2,2,64,128]{3,2,1,0:T(8,128)S(1)}, u32[]{:S(2)}, u32[]{:S(2)}) collective-permute-start(f32[2,2,64,128]{3,2,1,0:T(8,128)S(1)} %pad_maximum_fusion.5), channel_id=1, source_target_pairs={{0,8},{1,5},{2,10},{3,7},{4,12},{5,1},{6,14},{7,3},{8,0},{9,13},{1... | collective-permute-start | bytes 393224 | tf_op jit(solution)/shard_map/ppermute | solution.py:88
  9.3 1.7 %copy-start = (f32[2,2,64,128]{3,2,1,0:T(8,128)S(1)}, f32[2,2,64,128]{3,2,1,0:T(8,128)}, u32[]{:S(2)}) copy-start(f32[2,2,64,128]{3,2,1,0:T(8,128)} %state_ref.1) | copy-start | bytes 393220
  9.3 5.3 %collective-permute-start.1 = (f32[2,2,64,128]{3,2,1,0:T(8,128)S(1)}, f32[2,2,64,128]{3,2,1,0:T(8,128)S(1)}, u32[]{:S(2)}, u32[]{:S(2)}) collective-permute-start(f32[2,2,64,128]{3,2,1,0:T(8,128)S(1)} %pad_maximum_fusion.4), channel_id=1, source_target_pairs={{0,4},{1,9},{2,6},{3,11},{4,0},{5,13},{6,2},{7,15},{8,12},{9,1},{1... | collective-permute-start | bytes 393224 | tf_op jit(solution)/shard_map/ppermute | solution.py:88
  11.0 3.7 %collective-permute-start.2 = (f32[2,1,64,128]{3,2,1,0:T(8,128)S(1)}, f32[2,1,64,128]{3,2,1,0:T(8,128)S(1)}, u32[]{:S(2)}, u32[]{:S(2)}) collective-permute-start(f32[2,1,64,128]{3,2,1,0:T(8,128)S(1)} %get-tuple-element.15), channel_id=1, source_target_pairs={{1,2},{2,1},{3,4},{4,3},{5,6},{6,5},{7,8},{8,7},{9,10},{10,9},{11,... | collective-permute-start | bytes 196616 | tf_op jit(solution)/shard_map/ppermute | solution.py:79
  14.7 9.6 %collective-permute-start.3 = (f32[4,2,64,128]{3,2,1,0:T(8,128)S(1)}, f32[4,2,64,128]{3,2,1,0:T(8,128)S(1)}, u32[]{:S(2)}, u32[]{:S(2)}) collective-permute-start(f32[4,2,64,128]{3,2,1,0:T(8,128)S(1)} %pad_maximum_fusion.2), channel_id=1, source_target_pairs={{0,2},{1,5},{2,0},{3,7},{4,6},{5,1},{6,4},{7,3},{8,10},{9,13},{10,... | collective-permute-start | bytes 786440 | tf_op jit(solution)/shard_map/ppermute | solution.py:88
  18.1 7.6 %collective-permute-start.7 = (f32[4,2,64,128]{3,2,1,0:T(8,128)S(1)}, f32[4,2,64,128]{3,2,1,0:T(8,128)S(1)}, u32[]{:S(2)}, u32[]{:S(2)}) collective-permute-start(f32[4,2,64,128]{3,2,1,0:T(8,128)S(1)} %pad_maximum_fusion.3), channel_id=1, source_target_pairs={{0,4},{1,3},{2,6},{3,1},{4,0},{5,7},{6,2},{7,5},{8,12},{9,11},{10,... | collective-permute-start | bytes 786440 | tf_op jit(solution)/shard_map/ppermute | solution.py:88
  19.2 5.2 %collective-permute-start.4 = (f32[2,1,64,128]{3,2,1,0:T(8,128)S(1)}, f32[2,1,64,128]{3,2,1,0:T(8,128)S(1)}, u32[]{:S(2)}, u32[]{:S(2)}) collective-permute-start(f32[2,1,64,128]{3,2,1,0:T(8,128)S(1)} %get-tuple-element.14), channel_id=1, source_target_pairs={{0,1},{1,0},{2,3},{3,2},{4,5},{5,4},{6,7},{7,6},{8,9},{9,8},{10,11... | collective-permute-start | bytes 196616 | tf_op jit(solution)/shard_map/ppermute | solution.py:79
  24.4 2.0 %collective-permute-start.8 = (f32[8,2,64,128]{3,2,1,0:T(8,128)S(1)}, f32[8,2,64,128]{3,2,1,0:T(8,128)S(1)}, u32[]{:S(2)}, u32[]{:S(2)}) collective-permute-start(f32[8,2,64,128]{3,2,1,0:T(8,128)S(1)} %pad_maximum_fusion.kappa_mine_ref), channel_id=1, source_target_pairs={{0,1},{1,0},{2,3},{3,2},{4,5},{5,4},{6,7},{7,6},{8,9},{9,8},{10,11... | collective-permute-start | bytes 1572872 | tf_op jit(solution)/shard_map/ppermute | solution.py:93
  25.7 2.0 %collective-permute-start.9 = (f32[8,2,64,128]{3,2,1,0:T(8,128)S(1)}, f32[8,2,64,128]{3,2,1,0:T(8,128)S(1)}, u32[]{:S(2)}, u32[]{:S(2)}) collective-permute-start(f32[8,2,64,128]{3,2,1,0:T(8,128)S(1)} %pad_maximum_fusion.1.misfit_mine_ref), channel_id=1, source_target_pairs={{0,1},{1,0},{2,3},{3,2},{4,5},{5,4},{6,7},{7,6},{8,9},{9,8},{10,11... | collective-permute-start | bytes 1572872 | tf_op jit(solution)/shard_map/ppermute | solution.py:93
  25.8 1.9 %copy-start.1 = (f32[4]{0:T(128)S(1)}, f32[4]{0:T(128)}, u32[]{:S(2)}) copy-start(f32[4]{0:T(128)} %shifts_ref.1) | copy-start | bytes 52
  25.8 1.9 %copy-start.2 = (f32[4]{0:T(128)S(1)}, f32[4]{0:T(128)}, u32[]{:S(2)}) copy-start(f32[4]{0:T(128)} %weights_ref.1) | copy-start | bytes 52
  25.8 1.9 %copy-start.3 = (s32[2]{0:T(128)S(1)}, s32[2]{0:T(128)}, u32[]{:S(2)}) copy-start(s32[2]{0:T(128)} %order_ref.1) | copy-start | bytes 28
  44.7 3.9 %collective-permute-start.10 = (f32[2,32,128]{2,1,0:T(8,128)S(1)}, f32[2,32,128]{2,1,0:T(8,128)S(1)}, u32[]{:S(2)}, u32[]{:S(2)}) collective-permute-start(f32[2,32,128]{2,1,0:T(8,128)S(1)} %slice_bitcast_fusion), channel_id=1, source_target_pairs={{0,16},{16,0},{1,17},{17,1},{2,18},{18,2},{3,19},{19,3},{4,20},{20... | collective-permute-start | bytes 98312 | tf_op jit(solution)/shard_map/ppermute | solution.py:539

commit v7 on v0

--- a/solution.py
+++ b/solution.py
@@ -1,12 +1,17 @@
+import functools
+
 import jax
 import jax.numpy as jnp
 from jax import lax
+from jax.experimental import pallas as pl
+from jax.experimental.pallas import tpu as pltpu
 from jax.sharding import PartitionSpec as P
 
 ITERS = 2
-
-
 DAMPING = 0.8
+REPLICATED_CELLS = 32 * 64 * 128
+HALF = 64
+TILE = 8
 
 
 def extended(array, sides, width):
@@ -20,6 +25,615 @@
         after = lax.ppermute(leading, axis, down)
         array = jnp.concatenate([before, array, after], axis=dim)
     return array
+
+
+def lane_index(shape):
+    return lax.broadcasted_iota(jnp.int32, shape, len(shape) - 1)
+
+
+def row_index(shape):
+    return lax.broadcasted_iota(jnp.int32, shape, len(shape) - 2)
+
+
+def roll(block, shift, axis):
+    return pltpu.roll(block, shift % block.shape[axis], axis)
+
+
+def tree_sum(values):
+    while len(values) > 1:
+        values = [sum(values[at : at + 2]) for at in range(0, len(values), 2)]
+    return values[0]
+
+
+def grand_total(acc):
+    line = jnp.sum(acc, axis=0, keepdims=True)
+    return jnp.broadcast_to(jnp.sum(line, axis=1, keepdims=True), acc.shape)
+
+
+def swap_masks(peers, flip):
+    even = []
+    mask = peers // 2
+    while mask > 1:
+        even.append(mask)
+        mask //= 2
+    odd = even[-1:] + even[:-1]
+    return (odd, even) if flip else (even, odd)
+
+
+def block_pair(u, holder, peers, flip):
+    even, odd = swap_masks(peers, flip)
+    parity = holder % 2
+    top = jnp.where(parity == 0, even.index(peers // 2), odd.index(peers // 2))
+    below = u & ((1 << top) - 1)
+    base = ((u >> top) << (top + 1)) | below
+    upper = jnp.where(holder >= peers // 2, 1, 0)
+    first = base | (upper << top)
+    second = base | ((1 - upper) << top)
+    home = holder
+    for step, (mask_even, mask_odd) in enumerate(zip(even, odd)):
+        mask = jnp.where(parity == 0, mask_even, mask_odd)
+        home = home ^ (((first >> step) & 1) * mask)
+    return first, second, home
+
+
+def gather_blocks(blocks, halos, axis):
+    peers = lax.axis_size(axis)
+    own_half = lax.optimization_barrier(0.5 * blocks[0][None])
+    held = [block[None] for block in blocks]
+    halos = [lax.ppermute(array, axis, pairs) for array, pairs in halos]
+    swaps = [list(zip(*swap_masks(peers, flip))) for flip in (False, True)]
+    steps = len(swaps[0])
+    for step in range(steps):
+        if step == steps - 1:
+            held[0], halos[0] = lax.optimization_barrier((held[0], halos[0]))
+        for at in (0, 1):
+            masks = swaps[at][step]
+            pairs = [(i, i ^ masks[i % 2]) for i in range(peers)]
+            arrived = lax.ppermute(held[at], axis, pairs)
+            if step == 0 and at == 0:
+                held[0], arrived = own_half, 0.5 * arrived
+            held[at] = jnp.concatenate([held[at], arrived], axis=0)
+    held[0], halos[1] = lax.optimization_barrier((held[0], halos[1]))
+    other = [lax.ppermute(part, axis, [(i, i ^ 1) for i in range(peers)]) for part in held]
+    return held, other, halos
+
+
+CLASSES = [(a, b, c) for a in (0, 1) for b in (0, 1) for c in (0, 1)]
+PAIRS = [(p, q) for p in (0, 1) for q in (0, 1)]
+
+
+def cls(a, b, c):
+    return 4 * a + 2 * b + c
+
+
+def inner_faces(p, q):
+    return (
+        (2 * p + q, cls(0, p, q), cls(1, p, q)),
+        (4 + 2 * p + q, cls(p, 0, q), cls(p, 1, q)),
+        (8 + 2 * p + q, cls(p, q, 0), cls(p, q, 1)),
+    )
+
+
+class Layout:
+    def __init__(self, rows):
+        self.tiles = rows // TILE
+        self.lane = lane_index((TILE, 2 * HALF))
+        self.row = row_index((TILE, 2 * HALF))
+        self.left = self.lane < HALF
+        self.zero = jnp.zeros((TILE, 2 * HALF), jnp.float32)
+
+    def tile(self, j):
+        return pl.ds(TILE * j, TILE)
+
+    def every(self, b, j):
+        return pl.ds(b + 2 * j, TILE, stride=2 * self.tiles)
+
+    def row_before(self, load, j):
+        return load(j - 1) if j else roll(load(self.tiles - 1), 1, 0)
+
+    def row_after(self, load, j):
+        return load(j + 1) if j + 1 < self.tiles else roll(load(0), -1, 0)
+
+    def seam(self, ref, low, high):
+        last = ref.shape[1] - 1
+        for j in range(self.tiles):
+            for k in low:
+                moved = roll(ref[k, last - 1, self.tile(j)], HALF, 1)
+                ref[k, 0, self.tile(j)] = jnp.where(self.left, 0.0, moved)
+            for k in high:
+                moved = roll(ref[k, 1, self.tile(j)], HALF, 1)
+                ref[k, last, self.tile(j)] = jnp.where(self.left, moved, 0.0)
+
+    def seam_fine(self, ref):
+        count = ref.shape[0]
+        self.seam(
+            ref,
+            [k for k in range(count) if k % 8 >= 4],
+            [k for k in range(count) if k % 8 < 4],
+        )
+
+    def arrange(self, mine_ref, theirs_ref, place, flip, store):
+        blocks, own, rows, _ = mine_ref.shape
+        column = self.lane % HALF
+        even_odd = 2 * column + jnp.where(self.left, 0, 1)
+        odd_even = 2 * column + jnp.where(self.left, 1, 0)
+
+        def pair(u, carry):
+            for ref, holder in ((mine_ref, place), (theirs_ref, place ^ 1)):
+                first, second, home = block_pair(u, holder, 2 * blocks, flip)
+                for x in range(own):
+                    spot = home * (own // 2) + x // 2
+                    for b in (0, 1):
+                        for j in range(self.tiles):
+                            one = jnp.take_along_axis(
+                                ref[first, x, self.every(b, j), :], even_odd, axis=1
+                            )
+                            two = jnp.take_along_axis(
+                                ref[second, x, self.every(b, j), :], odd_even, axis=1
+                            )
+                            store(cls(x % 2, b, 0), spot, j, jnp.where(self.left, one, two))
+                            odd = roll(jnp.where(self.left, two, one), HALF, 1)
+                            store(cls(x % 2, b, 1), spot, j, odd)
+            return carry
+
+        lax.fori_loop(0, blocks // 2, pair, 0)
+
+
+def setup_kernel(
+    place_ref,
+    shifts_ref,
+    order_ref,
+    mine_ref,
+    theirs_ref,
+    inner,
+    outer_x,
+    outer_y,
+    outer_z,
+    inner_sum,
+    diagonal,
+    damped,
+    coarse_off,
+    coarse_damped,
+    half_kappa,
+):
+    half = inner.shape[1]
+    at_ = Layout(inner.shape[2])
+    tile, tiles = at_.tile, at_.tiles
+    members = coarse_damped.shape[0]
+    shifts = [shifts_ref[order_ref[slot]] for slot in range(members)]
+
+    def keep(k, spot, j, value):
+        half_kappa[k, spot + 1, tile(j)] = value
+
+    at_.arrange(mine_ref, theirs_ref, place_ref[0], False, keep)
+    at_.seam_fine(half_kappa)
+
+    z_low = jnp.where(at_.lane % HALF > 0, 1.0, 0.0)
+    z_high = jnp.where(at_.lane % HALF < HALF - 1, 1.0, 0.0)
+    y_low = [jnp.where(at_.row > 0, 1.0, 0.0)] + [None] * (tiles - 1)
+    y_high = [None] * (tiles - 1) + [jnp.where(at_.row < TILE - 1, 1.0, 0.0)]
+
+    def masked(mask, value):
+        return value if mask is None else mask * value
+
+    def plane(i, carry):
+        for j in range(tiles):
+            kap = [half_kappa[k, i + 1, tile(j)] for k in range(8)]
+            inside = [[] for _ in range(8)]
+            outside = [[] for _ in range(8)]
+            off = [[] for _ in range(5)]
+            for p, q in PAIRS:
+                for face_at, low, high in inner_faces(p, q):
+                    face = kap[low] + kap[high]
+                    inner[face_at, i, tile(j)] = face
+                    inside[low].append(face)
+                    inside[high].append(face)
+                at = 2 * p + q
+
+                low, high = cls(0, p, q), cls(1, p, q)
+                minus = kap[low] + half_kappa[high, i, tile(j)]
+                plus = kap[high] + half_kappa[low, i + 2, tile(j)]
+                outside[low].append(minus)
+                outside[high].append(plus)
+                outer_x[at, i, tile(j)] = minus
+                off[0].append(minus)
+
+                low, high = cls(p, 0, q), cls(p, 1, q)
+                side = at_.row_before(lambda r: half_kappa[high, i + 1, tile(r)], j)
+                minus = kap[low] + masked(y_low[j], side)
+                side = at_.row_after(lambda r: half_kappa[low, i + 1, tile(r)], j)
+                plus = kap[high] + masked(y_high[j], side)
+                outside[low].append(minus)
+                outside[high].append(plus)
+                minus, plus = masked(y_low[j], minus), masked(y_high[j], plus)
+                outer_y[at, i, tile(j)] = minus
+                outer_y[4 + at, i, tile(j)] = plus
+                off[1].append(minus)
+                off[2].append(plus)
+
+                low, high = cls(p, q, 0), cls(p, q, 1)
+                minus = kap[low] + z_low * roll(kap[high], 1, 1)
+                plus = kap[high] + z_high * roll(kap[low], -1, 1)
+                outside[low].append(minus)
+                outside[high].append(plus)
+                minus, plus = z_low * minus, z_high * plus
+                outer_z[at, i, tile(j)] = minus
+                outer_z[4 + at, i, tile(j)] = plus
+                off[3].append(minus)
+                off[4].append(plus)
+            coarse_total = []
+            for k in range(8):
+                within, without = tree_sum(inside[k]), tree_sum(outside[k])
+                inner_sum[k, i, tile(j)] = within
+                base = within + without
+                diagonal[k, i, tile(j)] = base
+                coarse_total.append(without)
+                for slot in range(members):
+                    damped[8 * slot + k, i, tile(j)] = DAMPING / (base + shifts[slot])
+            for at, part in enumerate(off):
+                coarse_off[at, i, tile(j)] = tree_sum(part)
+            total = tree_sum(coarse_total)
+            for slot in range(members):
+                coarse_damped[slot, i, tile(j)] = DAMPING / (total + 8.0 * shifts[slot])
+        return carry
+
+    lax.fori_loop(0, half, plane, 0)
+    for j in range(tiles):
+        part = []
+        for p, q in PAIRS:
+            face = half_kappa[cls(0, p, q), half + 1, tile(j)]
+            face = face + half_kappa[cls(1, p, q), half, tile(j)]
+            outer_x[2 * p + q, half, tile(j)] = face
+            part.append(face)
+        coarse_off[0, half, tile(j)] = tree_sum(part)
+
+
+def solve_kernel(
+    place_ref,
+    shifts_ref,
+    weights_ref,
+    order_ref,
+    mine_ref,
+    theirs_ref,
+    state_ref,
+    far_ref,
+    near_ref,
+    inner,
+    outer_x,
+    outer_y,
+    outer_z,
+    inner_sum,
+    diagonal,
+    damped,
+    coarse_off,
+    coarse_damped,
+    adjoint_ref,
+    share_ref,
+    residual,
+    scaled,
+    partial,
+    first_dir,
+    second_dir,
+    image,
+    coarse_one,
+    coarse_two,
+    planes,
+):
+    half, rows = inner.shape[1:3]
+    at_ = Layout(rows)
+    tile, tiles, zero = at_.tile, at_.tiles, at_.zero
+    members = coarse_damped.shape[0]
+    slots = range(members)
+    shifts = [shifts_ref[order_ref[slot]] for slot in slots]
+    weights = [weights_ref[order_ref[slot]] for slot in slots]
+
+    def begin(k, spot, j, value):
+        for slot in slots:
+            at = 8 * slot + k
+            res = weights[slot] * value
+            residual[at, spot, tile(j)] = res
+            scaled[at, spot + 1, tile(j)] = damped[at, spot, tile(j)] * res
+
+    at_.arrange(mine_ref, theirs_ref, place_ref[0], True, begin)
+    at_.seam_fine(scaled)
+
+    def stencil(field, i, j):
+        here = [[field[8 * s + k, i + 1, tile(j)] for k in range(8)] for s in slots]
+        sums = [[None] * 8 for _ in slots]
+
+        def add(s, k, value):
+            sums[s][k] = value if sums[s][k] is None else sums[s][k] + value
+
+        for p, q in PAIRS:
+            at = 2 * p + q
+            for face_at, low, high in inner_faces(p, q):
+                face = inner[face_at, i, tile(j)]
+                for s in slots:
+                    add(s, low, face * here[s][high])
+                    add(s, high, face * here[s][low])
+            low, high = cls(0, p, q), cls(1, p, q)
+            minus, plus = outer_x[at, i, tile(j)], outer_x[at, i + 1, tile(j)]
+            for s in slots:
+                add(s, low, minus * field[8 * s + high, i, tile(j)])
+                add(s, high, plus * field[8 * s + low, i + 2, tile(j)])
+            low, high = cls(p, 0, q), cls(p, 1, q)
+            minus, plus = outer_y[at, i, tile(j)], outer_y[4 + at, i, tile(j)]
+            for s in slots:
+                side = at_.row_before(lambda r: field[8 * s + high, i + 1, tile(r)], j)
+                add(s, low, minus * side)
+                side = at_.row_after(lambda r: field[8 * s + low, i + 1, tile(r)], j)
+                add(s, high, plus * side)
+            low, high = cls(p, q, 0), cls(p, q, 1)
+            minus, plus = outer_z[at, i, tile(j)], outer_z[4 + at, i, tile(j)]
+            for s in slots:
+                add(s, low, minus * roll(here[s][high], 1, 1))
+                add(s, high, plus * roll(here[s][low], -1, 1))
+        return here, sums
+
+    def coarse_sides(field, s, i, j):
+        here = field[s, i + 1, tile(j)]
+        return here, (
+            (field[s, i, tile(j)], field[s, i + 2, tile(j)]),
+            (
+                at_.row_before(lambda r: field[s, i + 1, tile(r)], j),
+                at_.row_after(lambda r: field[s, i + 1, tile(r)], j),
+            ),
+            (roll(here, 1, 1), roll(here, -1, 1)),
+        )
+
+    def precondition(result, other):
+        def down(i, carry):
+            for j in range(tiles):
+                _, sums = stencil(scaled, i, j)
+                for s in slots:
+                    rhs = None
+                    for k in range(8):
+                        res = residual[8 * s + k, i, tile(j)]
+                        part = (2.0 - DAMPING) * res + sums[s][k]
+                        partial[8 * s + k, i, tile(j)] = part
+                        rhs = part - res if rhs is None else rhs + (part - res)
+                    coarse_one[s, i + 1, tile(j)] = coarse_damped[s, i, tile(j)] * rhs
+            return carry
+
+        lax.fori_loop(0, half, down, 0)
+        at_.seam(coarse_one, slots, slots)
+
+        def smooth(i, carry):
+            for j in range(tiles):
+                faces = [coarse_off[0, i + 1, tile(j)]]
+                faces += [coarse_off[at, i, tile(j)] for at in range(5)]
+                for s in slots:
+                    here, sides = coarse_sides(coarse_one, s, i, j)
+                    total = faces[1] * sides[0][0] + faces[0] * sides[0][1]
+                    total = total + (faces[2] * sides[1][0] + faces[3] * sides[1][1])
+                    total = total + (faces[4] * sides[2][0] + faces[5] * sides[2][1])
+                    coarse_two[s, i + 1, tile(j)] = (2.0 - DAMPING) * here + coarse_damped[
+                        s, i, tile(j)
+                    ] * total
+            return carry
+
+        lax.fori_loop(0, half, smooth, 0, unroll=4)
+        at_.seam(coarse_two, slots, slots)
+
+        def up(i, carry):
+            carry = list(carry)
+            for j in range(tiles):
+                around = [coarse_sides(coarse_two, s, i, j) for s in slots]
+                kept = [(1.0 - DAMPING) * around[s][0] for s in slots]
+                for a, b, c in CLASSES:
+                    k = cls(a, b, c)
+                    faces = (
+                        inner_sum[k, i, tile(j)],
+                        outer_x[2 * b + c, i + a, tile(j)],
+                        outer_y[4 * b + 2 * a + c, i, tile(j)],
+                        outer_z[4 * c + 2 * a + b, i, tile(j)],
+                    )
+                    for s in slots:
+                        at = 8 * s + k
+                        here, sides = around[s]
+                        value = partial[at, i, tile(j)] + faces[0] * here
+                        value = value + (faces[1] * sides[0][a] + faces[2] * sides[1][b])
+                        value = value + faces[3] * sides[2][c]
+                        new = kept[s] + damped[at, i, tile(j)] * value
+                        result[at, i + 1, tile(j)] = new
+                        carry[s] = carry[s] + residual[at, i, tile(j)] * new
+                        if other is not None:
+                            into = members + s
+                            carry[into] = carry[into] + other[at, i, tile(j)] * new
+            return tuple(carry)
+
+        count = members if other is None else 2 * members
+        sums = lax.fori_loop(0, half, up, (zero,) * count)
+        at_.seam_fine(result)
+        return [grand_total(part) for part in sums]
+
+    def curvature(field, keep):
+        def step(i, carry):
+            carry = list(carry)
+            for j in range(tiles):
+                here, sums = stencil(field, i, j)
+                for k in range(8):
+                    base = diagonal[k, i, tile(j)]
+                    for s in slots:
+                        value = (base + shifts[s]) * here[s][k] - sums[s][k]
+                        if keep:
+                            image[8 * s + k, i, tile(j)] = value
+                        carry[s] = carry[s] + here[s][k] * value
+            return tuple(carry)
+
+        sums = lax.fori_loop(0, half, step, (zero,) * members)
+        return [grand_total(part) for part in sums]
+
+    gamma = precondition(first_dir, None)
+    curve = curvature(first_dir, True)
+    step_one = [gamma[s] / curve[s] for s in slots]
+
+    def update(i, carry):
+        for j in range(tiles):
+            for s in slots:
+                for k in range(8):
+                    at = 8 * s + k
+                    new = residual[at, i, tile(j)] - step_one[s] * image[at, i, tile(j)]
+                    residual[at, i, tile(j)] = new
+                    scaled[at, i + 1, tile(j)] = damped[at, i, tile(j)] * new
+        return carry
+
+    lax.fori_loop(0, half, update, 0)
+    at_.seam_fine(scaled)
+
+    sums = precondition(second_dir, image)
+    gamma_next, cross = sums[:members], sums[members:]
+    bend = curvature(second_dir, False)
+    ratio = [gamma_next[s] / gamma[s] for s in slots]
+    step_two = [
+        gamma_next[s] / (bend[s] + ratio[s] * (2.0 * cross[s] + ratio[s] * curve[s]))
+        for s in slots
+    ]
+    step_first = [step_one[s] + step_two[s] * ratio[s] for s in slots]
+
+    own = adjoint_ref.shape[1]
+    start = place_ref[0] * (own // 2)
+    upper = jnp.where(start >= half, 1, 0)
+    start = start - half * upper
+    even = at_.lane % 2 == 0
+    source = at_.lane // 2 + HALF * upper
+    for at in range(own + 2):
+        a = (at + 1) % 2
+        spot = start + (at + 1) // 2
+        for b in (0, 1):
+            for j in range(tiles):
+                for s in slots:
+                    both = []
+                    for c in (0, 1):
+                        k = 8 * s + cls(a, b, c)
+                        both.append(
+                            step_first[s] * first_dir[k, spot, tile(j)]
+                            + step_two[s] * second_dir[k, spot, tile(j)]
+                        )
+                    planes[s, at, at_.every(b, j), :] = jnp.where(
+                        even,
+                        jnp.take_along_axis(both[0], source, axis=1),
+                        jnp.take_along_axis(both[1], source, axis=1),
+                    )
+
+    full = (2 * rows, 2 * HALF)
+    y_at = row_index(full)
+    z_at = lane_index(full)
+
+    def drop(value, axis, up):
+        moved = roll(value, -1 if up else 1, axis)
+        at = (y_at, z_at)[axis]
+        edge = full[axis] - 1 if up else 0
+        return value - jnp.where(at == edge, 0.0, moved)
+
+    is_even = place_ref[0] % 2 == 0
+    groups = share_ref.shape[0]
+    chunk = share_ref.shape[2]
+    for j in range(own):
+        term = jnp.zeros(full, jnp.float32)
+        for s in slots:
+            here = planes[s, j + 1]
+            adjoint_ref[s, j] = here
+            f = state_ref[s, j]
+            if j:
+                f_low = state_ref[s, j - 1]
+            else:
+                f_low = jnp.where(is_even, far_ref[s, 0], near_ref[s, 0])
+            if j + 1 < own:
+                f_high = state_ref[s, j + 1]
+            else:
+                f_high = jnp.where(is_even, near_ref[s, 0], far_ref[s, 0])
+            term = term + (here - planes[s, j + 2]) * (f - f_high)
+            term = term + (here - planes[s, j]) * (f - f_low)
+            for axis in (0, 1):
+                for up in (True, False):
+                    term = term + drop(here, axis, up) * drop(f, axis, up)
+        planes[0, j] = -0.5 * term
+        for k in range(groups):
+            at = lax.rem(place_ref[1] + k, groups) * chunk
+            share_ref[k, j] = planes[0, j, pl.ds(pl.multiple_of(at, chunk), chunk), :]
+
+
+def whole_grid(conductivity, misfit, forward_states, pole_shifts, pole_weights, pole_order):
+    members, own, ny, nz = forward_states.shape
+    groups = lax.axis_size("pole")
+    place = jnp.stack([lax.axis_index("space"), lax.axis_index("pole")]).astype(jnp.int32)
+    peers = lax.axis_size("space")
+    even = place[0] % 2 == 0
+    first, last = forward_states[:, :1], forward_states[:, own - 1 :]
+    near = [(i, i ^ 1) for i in range(peers)]
+    far = [(i, i + 1 if i % 2 else i - 1) for i in range(1, peers - 1)]
+    halos = [(jnp.where(even, first, last), far), (jnp.where(even, last, first), near)]
+    mine, theirs, halos = gather_blocks([conductivity, misfit], halos, "space")
+    far, near = halos
+    half, rows = peers * own // 4, ny // 2
+
+    def field(count, extent):
+        return (count, extent, rows, 2 * HALF)
+
+    def held(*shape):
+        return pltpu.VMEM(shape, jnp.float32)
+
+    smem = pl.BlockSpec(memory_space=pltpu.SMEM)
+    vmem = pl.BlockSpec(memory_space=pltpu.VMEM)
+    shapes = [
+        field(12, half),
+        field(4, half + 1),
+        field(8, half),
+        field(8, half),
+        field(8, half),
+        field(8, half),
+        field(8 * members, half),
+        field(5, half + 1),
+        field(members, half),
+    ]
+    coefficients = pl.pallas_call(
+        setup_kernel,
+        out_shape=[jax.ShapeDtypeStruct(shape, jnp.float32) for shape in shapes],
+        in_specs=[smem] * 3 + [vmem] * 2,
+        out_specs=[vmem] * len(shapes),
+        scratch_shapes=[held(*field(8, half + 2))],
+        compiler_params=pltpu.CompilerParams(vmem_limit_bytes=20 * 1024 * 1024),
+        name="setup",
+    )(place, pole_shifts, pole_order, mine[0], theirs[0])
+    adjoint, share = pl.pallas_call(
+        solve_kernel,
+        out_shape=(
+            jax.ShapeDtypeStruct(forward_states.shape, jnp.float32),
+            jax.ShapeDtypeStruct((groups, own, ny // groups, nz), jnp.float32),
+        ),
+        in_specs=[smem] * 4 + [vmem] * (5 + len(shapes)),
+        out_specs=(vmem, vmem),
+        scratch_shapes=[
+            held(*field(8 * members, half)),
+            held(*field(8 * members, half + 2)),
+            held(*field(8 * members, half)),
+            held(*field(8 * members, half + 2)),
+            held(*field(8 * members, half + 2)),
+            held(*field(8 * members, half)),
+            held(*field(members, half + 2)),
+            held(*field(members, half + 2)),
+            held(members, own + 2, ny, nz),
+        ],
+        compiler_params=pltpu.CompilerParams(vmem_limit_bytes=36 * 1024 * 1024),
+        name="solve",
+    )(
+        place,
+        pole_shifts,
+        pole_weights,
+        pole_order,
+        mine[1],
+        theirs[1],
+        forward_states,
+        far,
+        near,
+        *coefficients,
+    )
+    gradient = share[0]
+    for k in range(1, groups):
+        ring = [(i, (i + k) % groups) for i in range(groups)]
+        gradient = gradient + lax.ppermute(share[k], "pole", ring)
+    return adjoint, gradient
 
 
 def plus_side(field, which_dim):
@@ -125,7 +739,7 @@
     return iterate
 
 
-def per_device(conductivity, misfit, forward_states, pole_shifts, pole_weights, pole_order):
+def divided(conductivity, misfit, forward_states, pole_shifts, pole_weights, pole_order):
     widened_kappa = extended(conductivity, (("space", 0),), 1)
     plus_faces = [
         0.5 * (conductivity + widened_kappa[2:]),
@@ -204,6 +818,16 @@
         P("pole"),
     )
     out_specs = (P("pole", "space", None, None), P("space", "pole", None))
+
+    def body(conductivity, misfit, forward_states, *poles):
+        nx = conductivity.shape[0] * lax.axis_size("space")
+        _, ny, nz = conductivity.shape
+        peers = lax.axis_size("space")
+        small = nx * ny * nz <= REPLICATED_CELLS and conductivity.shape[0] % 2 == 0
+        if small and nz == 2 * HALF and peers > 2 and peers & (peers - 1) == 0:
+            return whole_grid(conductivity, misfit, forward_states, *poles)
+        return divided(conductivity, misfit, forward_states, *poles)
+
     return jax.shard_map(
-        per_device, mesh=mesh, in_specs=in_specs, out_specs=out_specs, check_vma=False
+        body, mesh=mesh, in_specs=in_specs, out_specs=out_specs, check_vma=False
     )

time: 373 us -> 53.3 us (0.14)
  the two profiles are of different devices: /device:TPU:0 before, /device:TPU:8 now
where the time goes in v7:
time: 53.3 us; the launch traced here: 53 us
  waiting for transfers between devices  17.9 us (34%)
  Pallas kernels  17.6 us (33%)
  starting transfers between devices  12.4 us (23%)
  other arithmetic  4.25 us (8%)
  between operations  0.79 us (1%)
    pallas_call x1, Pallas kernels, whole_grid(): pl.pallas_call(solve_kernel, out_shape=(jax.ShapeDtypeStruct(forward_stat...  14.6 us
    ppermute x6, waiting for transfers between devices, gather_blocks(): arrived = lax.ppermute(held[at], axis, pairs)  9.77 us
    ppermute x6, starting transfers between devices, gather_blocks(): arrived = lax.ppermute(held[at], axis, pairs)  8.08 us
    ppermute x2, waiting for transfers between devices, gather_blocks(): halos = [lax.ppermute(array, axis, pairs) for array, pairs in halos]  4.52 us
    pallas_call x1, Pallas kernels, whole_grid(): pl.pallas_call(setup_kernel, out_shape=[jax.ShapeDtypeStruct(shape, jnp.f...  3.05 us
    ppermute x1, waiting for transfers between devices, whole_grid(): gradient = gradient + lax.ppermute(share[k], 'pole', ring)  2.39 us
    ppermute x2, starting transfers between devices, gather_blocks(): halos = [lax.ppermute(array, axis, pairs) for array, pairs in halos]  2.14 us
    concatenate x6, other arithmetic, gather_blocks(): held[at] = jnp.concatenate([held[at], arrived], axis=0)  1.82 us
  transfers between devices with their start and end apart: 11, of which 5 were waited for; matrix products, arithmetic and copies ran while one was open for 7% of the time, Pallas kernels for 6%

profile of v7, /device:TPU:8, one launch (start us, length us, event | category | flops | bytes accessed | tf_op | source)
XLA Modules:
  0.0 53.0 jit_solution(14734356858782275143)
XLA Ops:
  0.6 0.0 copy-start.4
  0.6 2.7 %collective-permute-start.4 = (f32[1,2,64,128]{3,2,1,0:T(8,128)}, f32[1,2,64,128]{3,2,1,0:T(8,128)S(1)}, u32[]{:S(2)}, u32[]{:S(2)}) collective-permute-start(f32[1,2,64,128]{3,2,1,0:T(8,128)} %bitcast.14), channel_id=1, source_target_pairs={{0,8},{1,3},{2,10},{3,1},{4,12},{5,7},{6,14},{7,5},{8,0},{9,11},{1... | collective-permute-start | bytes 196616 | tf_op jit(solution)/shard_map/ppermute | solution.py:92
  3.3 1.5 %collective-permute-start = (f32[1,2,64,128]{3,2,1,0:T(8,128)}, f32[1,2,64,128]{3,2,1,0:T(8,128)S(1)}, u32[]{:S(2)}, u32[]{:S(2)}) collective-permute-start(f32[1,2,64,128]{3,2,1,0:T(8,128)} %bitcast.10), channel_id=1, source_target_pairs={{0,2},{1,9},{2,0},{3,11},{4,6},{5,13},{6,4},{7,15},{8,10},{9,1},{1... | collective-permute-start | bytes 196616 | tf_op jit(solution)/shard_map/ppermute | solution.py:92
  4.8 0.8 %multiply_bitcast_fusion = f32[1,2,64,128]{3,2,1,0:T(8,128)S(1)} fusion(f32[2,64,128]{2,1,0:T(8,128)} %param.6), kind=kLoop, calls=%fused_computation.6 | loop fusion | flops 16384 | bytes 131072 | tf_op jit(solution)/shard_map/mul | solution.py:81
  5.6 3.0 %collective-permute-done.4 = f32[1,2,64,128]{3,2,1,0:T(8,128)S(1)} collective-permute-done((f32[1,2,64,128]{3,2,1,0:T(8,128)}, f32[1,2,64,128]{3,2,1,0:T(8,128)S(1)}, u32[]{:S(2)}, u32[]{:S(2)}) %collective-permute-start.4) | collective-permute-done | bytes 65568 | tf_op jit(solution)/shard_map/ppermute | solution.py:92
  8.7 0.1 collective-permute-start.5
  8.7 0.0 collective-permute-done
  8.8 0.9 %pad_maximum_fusion.4 = f32[2,2,64,128]{3,2,1,0:T(8,128)S(1)} fusion(f32[1,2,64,128]{3,2,1,0:T(8,128)S(1)} %collective-permute-done, f32[1,2,64,128]{3,2,1,0:T(8,128)} %bitcast.11), kind=kLoop, calls=%fused_computation.4 | loop fusion | flops 32768 | bytes 262144 | tf_op jit(solution)/shard_map/concatenate | solution.py:95
  9.6 3.5 %collective-permute-start.1 = (f32[2,2,64,128]{3,2,1,0:T(8,128)S(1)}, f32[2,2,64,128]{3,2,1,0:T(8,128)S(1)}, u32[]{:S(2)}, u32[]{:S(2)}) collective-permute-start(f32[2,2,64,128]{3,2,1,0:T(8,128)S(1)} %pad_maximum_fusion.4), channel_id=1, source_target_pairs={{0,8},{1,5},{2,10},{3,7},{4,12},{5,1},{6,14},{7,3},{8,0},{9,13},{1... | collective-permute-start | bytes 393224 | tf_op jit(solution)/shard_map/ppermute | solution.py:92
  13.1 0.9 %slice_select_fusion = (f32[2,1,64,128]{3,2,1,0:T(8,128)S(1)}, f32[2,1,64,128]{3,2,1,0:T(8,128)S(1)}) fusion(f32[2,2,64,128]{3,2,1,0:T(8,128)} %state_ref.1, pred[]{:T(512)S(6)} %eq.5), kind=kLoop, calls=%fused_computation.7 | loop fusion | flops 32768 | bytes 262145 | tf_op jit(solution)/shard_map/jit(_where)/select_n | solution.py:566
  14.0 0.0 copy-start
  14.0 0.0 copy-start.3
  14.0 2.1 %collective-permute-start.6 = (f32[2,1,64,128]{3,2,1,0:T(8,128)S(1)}, f32[2,1,64,128]{3,2,1,0:T(8,128)S(1)}, u32[]{:S(2)}, u32[]{:S(2)}) collective-permute-start(f32[2,1,64,128]{3,2,1,0:T(8,128)S(1)} %get-tuple-element.33), channel_id=1, source_target_pairs={{1,2},{2,1},{3,4},{4,3},{5,6},{6,5},{7,8},{8,7},{9,10},{10,9},{11,... | collective-permute-start | bytes 196616 | tf_op jit(solution)/shard_map/ppermute | solution.py:83
  16.1 0.0 collective-permute-done.5
  16.1 4.5 %collective-permute-done.6.far_ref = f32[2,1,64,128]{3,2,1,0:T(8,128)S(1)} collective-permute-done((f32[2,1,64,128]{3,2,1,0:T(8,128)S(1)}, f32[2,1,64,128]{3,2,1,0:T(8,128)S(1)}, u32[]{:S(2)}, u32[]{:S(2)}) %collective-permute-start.6) | collective-permute-done | bytes 65568 | tf_op jit(solution)/shard_map/ppermute | solution.py:83
  20.6 0.0 collective-permute-start.7
  20.6 0.0 collective-permute-done.1
  20.6 0.9 %pad_maximum_fusion.2 = f32[4,2,64,128]{3,2,1,0:T(8,128)S(1)} fusion(f32[2,2,64,128]{3,2,1,0:T(8,128)S(1)} %collective-permute-done.1, f32[1,2,64,128]{3,2,1,0:T(8,128)S(1)} %collective-permute-done, f32[1,2,64,128]{3,2,1,0:T(8,128)} %bitcast.12), kind=kLoop, calls=%fused_computation.2 | loop fusion | flops 131072 | bytes 524288 | tf_op jit(solution)/shard_map/concatenate | solution.py:95
  21.5 0.4 collective-permute-start.2
  21.9 0.1 collective-permute-start.8
  22.0 6.8 %collective-permute-done.7 = f32[4,2,64,128]{3,2,1,0:T(8,128)S(1)} collective-permute-done((f32[4,2,64,128]{3,2,1,0:T(8,128)S(1)}, f32[4,2,64,128]{3,2,1,0:T(8,128)S(1)}, u32[]{:S(2)}, u32[]{:S(2)}) %collective-permute-start.7) | collective-permute-done | bytes 262176 | tf_op jit(solution)/shard_map/ppermute | solution.py:92
  28.8 0.0 collective-permute-done.8.near_ref
  28.8 0.1 collective-permute-start.9
  28.9 0.0 collective-permute-done.2
  28.9 0.5 %collective-permute-start.3 = (f32[8,2,64,128]{3,2,1,0:T(8,128)S(1)}, f32[8,2,64,128]{3,2,1,0:T(8,128)S(1)}, u32[]{:S(2)}, u32[]{:S(2)}) collective-permute-start(f32[8,2,64,128]{3,2,1,0:T(8,128)S(1)} %pad_maximum_fusion.mine_ref), channel_id=1, source_target_pairs={{0,1},{1,0},{2,3},{3,2},{4,5},{5,4},{6,7},{7,6},{8,9},{9,8},{10,11... | collective-permute-start | bytes 1572872 | tf_op jit(solution)/shard_map/ppermute | solution.py:97
  29.5 0.1 pad_add_fusion.place_ref
  29.5 1.2 %collective-permute-done.9.theirs_ref = f32[8,2,64,128]{3,2,1,0:T(8,128)S(1)} collective-permute-done((f32[8,2,64,128]{3,2,1,0:T(8,128)S(1)}, f32[8,2,64,128]{3,2,1,0:T(8,128)S(1)}, u32[]{:S(2)}, u32[]{:S(2)}) %collective-permute-start.9) | collective-permute-done | bytes 524320 | tf_op jit(solution)/shard_map/ppermute | solution.py:97
  30.8 3.1 %setup.1 = (f32[12,8,32,128]{3,2,1,0:T(8,128)S(1)}, f32[4,9,32,128]{3,2,1,0:T(8,128)S(1)}, f32[8,8,32,128]{3,2,1,0:T(8,128)S(1)}, f32[8,8,32,128]{3,2,1,0:T(8,12...) custom-call(s32[2]{0:T(128)S(1)} %pad_add_fusion.place_ref, ...), custom_call_target="tpu_custom_call" | custom-call | tf_op jit(solution)/shard_map/setup/pallas_call | solution.py:590
  33.8 14.6 %solve.1 = (f32[2,2,64,128]{3,2,1,0:T(8,128)}, f32[2,2,32,128]{3,2,1,0:T(8,128)S(1)}) custom-call(s32[2]{0:T(128)S(1)} %pad_add_fusion.place_ref, f32[4]{0:T(128)S(1)} %copy-done.1, f32[4]{0:T(128)S(1)} %copy-done.3, s32[2]{0:T(128)S(1)} %copy-done.2, f32[8,2,64,128]{3,2,1,0:T(8,128)S(1)} %pad_maximum_fusion.mine_ref, ...), custom_call_target="tpu_custom_call" | custom-call | tf_op jit(solution)/shard_map/solve/pallas_call | solution.py:599
  48.4 1.5 %collective-permute-start.10 = (f32[2,32,128]{2,1,0:T(8,128)S(1)}, f32[2,32,128]{2,1,0:T(8,128)S(1)}, u32[]{:S(2)}, u32[]{:S(2)}) collective-permute-start(f32[2,32,128]{2,1,0:T(8,128)S(1)} %slice_bitcast_fusion), channel_id=1, source_target_pairs={{0,16},{16,0},{1,17},{17,1},{2,18},{18,2},{3,19},{19,3},{4,20},{20... | collective-permute-start | bytes 98312 | tf_op jit(solution)/shard_map/ppermute | solution.py:635
  49.9 2.4 %collective-permute-done.10 = f32[2,32,128]{2,1,0:T(8,128)S(1)} collective-permute-done((f32[2,32,128]{2,1,0:T(8,128)S(1)}, f32[2,32,128]{2,1,0:T(8,128)S(1)}, u32[]{:S(2)}, u32[]{:S(2)}) %collective-permute-start.10) | collective-permute-done | bytes 32800 | tf_op jit(solution)/shard_map/ppermute | solution.py:635
  52.3 0.6 %bitcast_add_fusion = f32[2,32,128]{2,1,0:T(8,128)} fusion(f32[2,32,128]{2,1,0:T(8,128)S(1)} %collective-permute-done.10, f32[2,2,32,128]{3,2,1,0:T(8,128)S(1)} %get-tuple-element.31), kind=kLoop, calls=%fused_computation.9 | loop fusion | flops 8192 | bytes 98304 | tf_op jit(solution)/shard_map/add | solution.py:635
  (14 shorter events, 0.1 us)
Async XLA Ops:
  0.6 28.2 %copy-start.4 = (f32[2,64,128]{2,1,0:T(8,128)S(1)}, f32[2,64,128]{2,1,0:T(8,128)}, u32[]{:S(2)}) copy-start(f32[2,64,128]{2,1,0:T(8,128)} %param.7) | copy-start | bytes 196612
  0.6 8.0 %collective-permute-start.4 = (f32[1,2,64,128]{3,2,1,0:T(8,128)}, f32[1,2,64,128]{3,2,1,0:T(8,128)S(1)}, u32[]{:S(2)}, u32[]{:S(2)}) collective-permute-start(f32[1,2,64,128]{3,2,1,0:T(8,128)} %bitcast.14), channel_id=1, source_target_pairs={{0,8},{1,3},{2,10},{3,1},{4,12},{5,7},{6,14},{7,5},{8,0},{9,11},{1... | collective-permute-start | bytes 196616 | tf_op jit(solution)/shard_map/ppermute | solution.py:92
  3.3 27.5 %copy-start.1 = (f32[4]{0:T(128)S(1)}, f32[4]{0:T(128)}, u32[]{:S(2)}) copy-start(f32[4]{0:T(128)} %shifts_ref.3) | copy-start | bytes 52
  3.3 27.5 %copy-start.2 = (s32[2]{0:T(128)S(1)}, s32[2]{0:T(128)}, u32[]{:S(2)}) copy-start(s32[2]{0:T(128)} %order_ref.3) | copy-start | bytes 28
  3.3 5.4 %collective-permute-start = (f32[1,2,64,128]{3,2,1,0:T(8,128)}, f32[1,2,64,128]{3,2,1,0:T(8,128)S(1)}, u32[]{:S(2)}, u32[]{:S(2)}) collective-permute-start(f32[1,2,64,128]{3,2,1,0:T(8,128)} %bitcast.10), channel_id=1, source_target_pairs={{0,2},{1,9},{2,0},{3,11},{4,6},{5,13},{6,4},{7,15},{8,10},{9,1},{1... | collective-permute-start | bytes 196616 | tf_op jit(solution)/shard_map/ppermute | solution.py:92
  8.7 7.4 %collective-permute-start.5 = (f32[2,2,64,128]{3,2,1,0:T(8,128)S(1)}, f32[2,2,64,128]{3,2,1,0:T(8,128)S(1)}, u32[]{:S(2)}, u32[]{:S(2)}) collective-permute-start(f32[2,2,64,128]{3,2,1,0:T(8,128)S(1)} %pad_maximum_fusion.5), channel_id=1, source_target_pairs={{0,4},{1,9},{2,6},{3,11},{4,0},{5,13},{6,2},{7,15},{8,12},{9,1},{1... | collective-permute-start | bytes 393224 | tf_op jit(solution)/shard_map/ppermute | solution.py:92
  9.6 11.0 %collective-permute-start.1 = (f32[2,2,64,128]{3,2,1,0:T(8,128)S(1)}, f32[2,2,64,128]{3,2,1,0:T(8,128)S(1)}, u32[]{:S(2)}, u32[]{:S(2)}) collective-permute-start(f32[2,2,64,128]{3,2,1,0:T(8,128)S(1)} %pad_maximum_fusion.4), channel_id=1, source_target_pairs={{0,8},{1,5},{2,10},{3,7},{4,12},{5,1},{6,14},{7,3},{8,0},{9,13},{1... | collective-permute-start | bytes 393224 | tf_op jit(solution)/shard_map/ppermute | solution.py:92
  14.0 19.8 %copy-start = (f32[2,2,64,128]{3,2,1,0:T(8,128)S(1)}, f32[2,2,64,128]{3,2,1,0:T(8,128)}, u32[]{:S(2)}) copy-start(f32[2,2,64,128]{3,2,1,0:T(8,128)} %state_ref.1) | copy-start | bytes 393220
  14.0 19.8 %copy-start.3 = (f32[4]{0:T(128)S(1)}, f32[4]{0:T(128)}, u32[]{:S(2)}) copy-start(f32[4]{0:T(128)} %weights_ref.1) | copy-start | bytes 52
  14.0 6.6 %collective-permute-start.6 = (f32[2,1,64,128]{3,2,1,0:T(8,128)S(1)}, f32[2,1,64,128]{3,2,1,0:T(8,128)S(1)}, u32[]{:S(2)}, u32[]{:S(2)}) collective-permute-start(f32[2,1,64,128]{3,2,1,0:T(8,128)S(1)} %get-tuple-element.33), channel_id=1, source_target_pairs={{1,2},{2,1},{3,4},{4,3},{5,6},{6,5},{7,8},{8,7},{9,10},{10,9},{11,... | collective-permute-start | bytes 196616 | tf_op jit(solution)/shard_map/ppermute | solution.py:83
  20.6 8.1 %collective-permute-start.7 = (f32[4,2,64,128]{3,2,1,0:T(8,128)S(1)}, f32[4,2,64,128]{3,2,1,0:T(8,128)S(1)}, u32[]{:S(2)}, u32[]{:S(2)}) collective-permute-start(f32[4,2,64,128]{3,2,1,0:T(8,128)S(1)} %pad_maximum_fusion.3), channel_id=1, source_target_pairs={{0,2},{1,5},{2,0},{3,7},{4,6},{5,1},{6,4},{7,3},{8,10},{9,13},{10,... | collective-permute-start | bytes 786440 | tf_op jit(solution)/shard_map/ppermute | solution.py:92
  21.5 7.4 %collective-permute-start.2 = (f32[4,2,64,128]{3,2,1,0:T(8,128)S(1)}, f32[4,2,64,128]{3,2,1,0:T(8,128)S(1)}, u32[]{:S(2)}, u32[]{:S(2)}) collective-permute-start(f32[4,2,64,128]{3,2,1,0:T(8,128)S(1)} %pad_maximum_fusion.2), channel_id=1, source_target_pairs={{0,4},{1,3},{2,6},{3,1},{4,0},{5,7},{6,2},{7,5},{8,12},{9,11},{10,... | collective-permute-start | bytes 786440 | tf_op jit(solution)/shard_map/ppermute | solution.py:92
  21.9 6.9 %collective-permute-start.8 = (f32[2,1,64,128]{3,2,1,0:T(8,128)S(1)}, f32[2,1,64,128]{3,2,1,0:T(8,128)S(1)}, u32[]{:S(2)}, u32[]{:S(2)}) collective-permute-start(f32[2,1,64,128]{3,2,1,0:T(8,128)S(1)} %get-tuple-element.32), channel_id=1, source_target_pairs={{0,1},{1,0},{2,3},{3,2},{4,5},{5,4},{6,7},{7,6},{8,9},{9,8},{10,11... | collective-permute-start | bytes 196616 | tf_op jit(solution)/shard_map/ppermute | solution.py:83
  28.8 2.0 %collective-permute-start.9 = (f32[8,2,64,128]{3,2,1,0:T(8,128)S(1)}, f32[8,2,64,128]{3,2,1,0:T(8,128)S(1)}, u32[]{:S(2)}, u32[]{:S(2)}) collective-permute-start(f32[8,2,64,128]{3,2,1,0:T(8,128)S(1)} %pad_maximum_fusion.1.mine_ref), channel_id=1, source_target_pairs={{0,1},{1,0},{2,3},{3,2},{4,5},{5,4},{6,7},{7,6},{8,9},{9,8},{10,11... | collective-permute-start | bytes 1572872 | tf_op jit(solution)/shard_map/ppermute | solution.py:97
  28.9 4.9 %collective-permute-start.3 = (f32[8,2,64,128]{3,2,1,0:T(8,128)S(1)}, f32[8,2,64,128]{3,2,1,0:T(8,128)S(1)}, u32[]{:S(2)}, u32[]{:S(2)}) collective-permute-start(f32[8,2,64,128]{3,2,1,0:T(8,128)S(1)} %pad_maximum_fusion.mine_ref), channel_id=1, source_target_pairs={{0,1},{1,0},{2,3},{3,2},{4,5},{5,4},{6,7},{7,6},{8,9},{9,8},{10,11... | collective-permute-start | bytes 1572872 | tf_op jit(solution)/shard_map/ppermute | solution.py:97
  48.4 3.9 %collective-permute-start.10 = (f32[2,32,128]{2,1,0:T(8,128)S(1)}, f32[2,32,128]{2,1,0:T(8,128)S(1)}, u32[]{:S(2)}, u32[]{:S(2)}) collective-permute-start(f32[2,32,128]{2,1,0:T(8,128)S(1)} %slice_bitcast_fusion), channel_id=1, source_target_pairs={{0,16},{16,0},{1,17},{17,1},{2,18},{18,2},{3,19},{19,3},{4,20},{20... | collective-permute-start | bytes 98312 | tf_op jit(solution)/shard_map/ppermute | solution.py:635

commit v8 on v7

--- a/solution.py
+++ b/solution.py
@@ -76,16 +76,22 @@
     return first, second, home
 
 
-def gather_blocks(blocks, halos, axis):
+def gather_blocks(blocks, states, axis):
     peers = lax.axis_size(axis)
+    even = lax.axis_index(axis) % 2 == 0
+    swap = [(i, i ^ 1) for i in range(peers)]
     own_half = lax.optimization_barrier(0.5 * blocks[0][None])
     held = [block[None] for block in blocks]
-    halos = [lax.ppermute(array, axis, pairs) for array, pairs in halos]
+    edge = jnp.where(even, states[:, :1], states[:, -1:])
+    over = [(i, i + 1 if i % 2 else i - 1) for i in range(1, peers - 1)]
+    far = lax.ppermute(edge, axis, over)
     swaps = [list(zip(*swap_masks(peers, flip))) for flip in (False, True)]
     steps = len(swaps[0])
     for step in range(steps):
         if step == steps - 1:
-            held[0], halos[0] = lax.optimization_barrier((held[0], halos[0]))
+            held[0], far = lax.optimization_barrier((held[0], far))
+            given = jnp.concatenate([states, far], axis=1)
+            near = lax.ppermute(jnp.where(even, given[1], given[0]), axis, swap)
         for at in (0, 1):
             masks = swaps[at][step]
             pairs = [(i, i ^ masks[i % 2]) for i in range(peers)]
@@ -93,9 +99,9 @@
             if step == 0 and at == 0:
                 held[0], arrived = own_half, 0.5 * arrived
             held[at] = jnp.concatenate([held[at], arrived], axis=0)
-    held[0], halos[1] = lax.optimization_barrier((held[0], halos[1]))
-    other = [lax.ppermute(part, axis, [(i, i ^ 1) for i in range(peers)]) for part in held]
-    return held, other, halos
+    held[0], near = lax.optimization_barrier((held[0], near))
+    other = [lax.ppermute(part, axis, swap) for part in held]
+    return held, other, far, near
 
 
 CLASSES = [(a, b, c) for a in (0, 1) for b in (0, 1) for c in (0, 1)]
@@ -199,8 +205,7 @@
     half = inner.shape[1]
     at_ = Layout(inner.shape[2])
     tile, tiles = at_.tile, at_.tiles
-    members = coarse_damped.shape[0]
-    shifts = [shifts_ref[order_ref[slot]] for slot in range(members)]
+    shift = shifts_ref[order_ref[place_ref[0] % 2]]
 
     def keep(k, spot, j, value):
         half_kappa[k, spot + 1, tile(j)] = value
@@ -265,16 +270,13 @@
             for k in range(8):
                 within, without = tree_sum(inside[k]), tree_sum(outside[k])
                 inner_sum[k, i, tile(j)] = within
-                base = within + without
+                base = within + without + shift
                 diagonal[k, i, tile(j)] = base
                 coarse_total.append(without)
-                for slot in range(members):
-                    damped[8 * slot + k, i, tile(j)] = DAMPING / (base + shifts[slot])
+                damped[k, i, tile(j)] = DAMPING / base
             for at, part in enumerate(off):
                 coarse_off[at, i, tile(j)] = tree_sum(part)
-            total = tree_sum(coarse_total)
-            for slot in range(members):
-                coarse_damped[slot, i, tile(j)] = DAMPING / (total + 8.0 * shifts[slot])
+            coarse_damped[i, tile(j)] = DAMPING / (tree_sum(coarse_total) + 8.0 * shift)
         return carry
 
     lax.fori_loop(0, half, plane, 0)
@@ -290,7 +292,6 @@
 
 def solve_kernel(
     place_ref,
-    shifts_ref,
     weights_ref,
     order_ref,
     mine_ref,
@@ -322,61 +323,51 @@
     half, rows = inner.shape[1:3]
     at_ = Layout(rows)
     tile, tiles, zero = at_.tile, at_.tiles, at_.zero
-    members = coarse_damped.shape[0]
-    slots = range(members)
-    shifts = [shifts_ref[order_ref[slot]] for slot in slots]
-    weights = [weights_ref[order_ref[slot]] for slot in slots]
+    core = place_ref[0] % 2
+    weight = weights_ref[order_ref[core]]
 
     def begin(k, spot, j, value):
-        for slot in slots:
-            at = 8 * slot + k
-            res = weights[slot] * value
-            residual[at, spot, tile(j)] = res
-            scaled[at, spot + 1, tile(j)] = damped[at, spot, tile(j)] * res
+        res = weight * value
+        residual[k, spot, tile(j)] = res
+        scaled[k, spot + 1, tile(j)] = damped[k, spot, tile(j)] * res
 
     at_.arrange(mine_ref, theirs_ref, place_ref[0], True, begin)
     at_.seam_fine(scaled)
 
-    def stencil(field, i, j):
-        here = [[field[8 * s + k, i + 1, tile(j)] for k in range(8)] for s in slots]
-        sums = [[None] * 8 for _ in slots]
-
-        def add(s, k, value):
-            sums[s][k] = value if sums[s][k] is None else sums[s][k] + value
-
+    def stencil(field, i, j, both):
+        here = [field[k, i + 1, tile(j)] for k in range(8)]
+        terms = [[] for _ in range(8)]
         for p, q in PAIRS:
             at = 2 * p + q
             for face_at, low, high in inner_faces(p, q):
                 face = inner[face_at, i, tile(j)]
-                for s in slots:
-                    add(s, low, face * here[s][high])
-                    add(s, high, face * here[s][low])
+                terms[low].append(face * here[high])
+                if both:
+                    terms[high].append(face * here[low])
             low, high = cls(0, p, q), cls(1, p, q)
-            minus, plus = outer_x[at, i, tile(j)], outer_x[at, i + 1, tile(j)]
-            for s in slots:
-                add(s, low, minus * field[8 * s + high, i, tile(j)])
-                add(s, high, plus * field[8 * s + low, i + 2, tile(j)])
+            terms[low].append(outer_x[at, i, tile(j)] * field[high, i, tile(j)])
+            if both:
+                side = field[low, i + 2, tile(j)]
+                terms[high].append(outer_x[at, i + 1, tile(j)] * side)
             low, high = cls(p, 0, q), cls(p, 1, q)
-            minus, plus = outer_y[at, i, tile(j)], outer_y[4 + at, i, tile(j)]
-            for s in slots:
-                side = at_.row_before(lambda r: field[8 * s + high, i + 1, tile(r)], j)
-                add(s, low, minus * side)
-                side = at_.row_after(lambda r: field[8 * s + low, i + 1, tile(r)], j)
-                add(s, high, plus * side)
+            side = at_.row_before(lambda r: field[high, i + 1, tile(r)], j)
+            terms[low].append(outer_y[at, i, tile(j)] * side)
+            if both:
+                side = at_.row_after(lambda r: field[low, i + 1, tile(r)], j)
+                terms[high].append(outer_y[4 + at, i, tile(j)] * side)
             low, high = cls(p, q, 0), cls(p, q, 1)
-            minus, plus = outer_z[at, i, tile(j)], outer_z[4 + at, i, tile(j)]
-            for s in slots:
-                add(s, low, minus * roll(here[s][high], 1, 1))
-                add(s, high, plus * roll(here[s][low], -1, 1))
-        return here, sums
-
-    def coarse_sides(field, s, i, j):
-        here = field[s, i + 1, tile(j)]
+            terms[low].append(outer_z[at, i, tile(j)] * roll(here[high], 1, 1))
+            if both:
+                terms[high].append(outer_z[4 + at, i, tile(j)] * roll(here[low], -1, 1))
+        return here, [tree_sum(part) if part else None for part in terms]
+
+    def coarse_sides(field, i, j):
+        here = field[0, i + 1, tile(j)]
         return here, (
-            (field[s, i, tile(j)], field[s, i + 2, tile(j)]),
+            (field[0, i, tile(j)], field[0, i + 2, tile(j)]),
             (
-                at_.row_before(lambda r: field[s, i + 1, tile(r)], j),
-                at_.row_after(lambda r: field[s, i + 1, tile(r)], j),
+                at_.row_before(lambda r: field[0, i + 1, tile(r)], j),
+                at_.row_after(lambda r: field[0, i + 1, tile(r)], j),
             ),
             (roll(here, 1, 1), roll(here, -1, 1)),
         )
@@ -384,139 +375,134 @@
     def precondition(result, other):
         def down(i, carry):
             for j in range(tiles):
-                _, sums = stencil(scaled, i, j)
-                for s in slots:
-                    rhs = None
-                    for k in range(8):
-                        res = residual[8 * s + k, i, tile(j)]
-                        part = (2.0 - DAMPING) * res + sums[s][k]
-                        partial[8 * s + k, i, tile(j)] = part
-                        rhs = part - res if rhs is None else rhs + (part - res)
-                    coarse_one[s, i + 1, tile(j)] = coarse_damped[s, i, tile(j)] * rhs
+                res = [residual[k, i, tile(j)] for k in range(8)]
+                _, sums = stencil(scaled, i, j, True)
+                parts = [(2.0 - DAMPING) * res[k] + sums[k] for k in range(8)]
+                for k in range(8):
+                    partial[k, i, tile(j)] = parts[k]
+                rhs = tree_sum(parts) - tree_sum(res)
+                coarse_one[0, i + 1, tile(j)] = coarse_damped[i, tile(j)] * rhs
             return carry
 
-        lax.fori_loop(0, half, down, 0)
-        at_.seam(coarse_one, slots, slots)
+        lax.fori_loop(0, half, down, 0, unroll=2)
+        at_.seam(coarse_one, [0], [0])
 
         def smooth(i, carry):
             for j in range(tiles):
-                faces = [coarse_off[0, i + 1, tile(j)]]
-                faces += [coarse_off[at, i, tile(j)] for at in range(5)]
-                for s in slots:
-                    here, sides = coarse_sides(coarse_one, s, i, j)
-                    total = faces[1] * sides[0][0] + faces[0] * sides[0][1]
-                    total = total + (faces[2] * sides[1][0] + faces[3] * sides[1][1])
-                    total = total + (faces[4] * sides[2][0] + faces[5] * sides[2][1])
-                    coarse_two[s, i + 1, tile(j)] = (2.0 - DAMPING) * here + coarse_damped[
-                        s, i, tile(j)
-                    ] * total
+                here, sides = coarse_sides(coarse_one, i, j)
+                total = coarse_off[0, i, tile(j)] * sides[0][0]
+                total = total + coarse_off[0, i + 1, tile(j)] * sides[0][1]
+                more = coarse_off[1, i, tile(j)] * sides[1][0]
+                more = more + coarse_off[2, i, tile(j)] * sides[1][1]
+                most = coarse_off[3, i, tile(j)] * sides[2][0]
+                most = most + coarse_off[4, i, tile(j)] * sides[2][1]
+                coarse_two[0, i + 1, tile(j)] = (2.0 - DAMPING) * here + coarse_damped[
+                    i, tile(j)
+                ] * (total + more + most)
             return carry
 
-        lax.fori_loop(0, half, smooth, 0, unroll=4)
-        at_.seam(coarse_two, slots, slots)
+        lax.fori_loop(0, half, smooth, 0, unroll=8)
+        at_.seam(coarse_two, [0], [0])
 
         def up(i, carry):
-            carry = list(carry)
+            gamma, cross = carry
             for j in range(tiles):
-                around = [coarse_sides(coarse_two, s, i, j) for s in slots]
-                kept = [(1.0 - DAMPING) * around[s][0] for s in slots]
+                here, sides = coarse_sides(coarse_two, i, j)
+                kept = (1.0 - DAMPING) * here
+                dots, crosses = [], []
                 for a, b, c in CLASSES:
                     k = cls(a, b, c)
-                    faces = (
-                        inner_sum[k, i, tile(j)],
-                        outer_x[2 * b + c, i + a, tile(j)],
-                        outer_y[4 * b + 2 * a + c, i, tile(j)],
-                        outer_z[4 * c + 2 * a + b, i, tile(j)],
+                    value = tree_sum(
+                        [
+                            partial[k, i, tile(j)],
+                            inner_sum[k, i, tile(j)] * here,
+                            outer_x[2 * b + c, i + a, tile(j)] * sides[0][a],
+                            outer_y[4 * b + 2 * a + c, i, tile(j)] * sides[1][b],
+                            outer_z[4 * c + 2 * a + b, i, tile(j)] * sides[2][c],
+                        ]
                     )
-                    for s in slots:
-                        at = 8 * s + k
-                        here, sides = around[s]
-                        value = partial[at, i, tile(j)] + faces[0] * here
-                        value = value + (faces[1] * sides[0][a] + faces[2] * sides[1][b])
-                        value = value + faces[3] * sides[2][c]
-                        new = kept[s] + damped[at, i, tile(j)] * value
-                        result[at, i + 1, tile(j)] = new
-                        carry[s] = carry[s] + residual[at, i, tile(j)] * new
-                        if other is not None:
-                            into = members + s
-                            carry[into] = carry[into] + other[at, i, tile(j)] * new
-            return tuple(carry)
-
-        count = members if other is None else 2 * members
-        sums = lax.fori_loop(0, half, up, (zero,) * count)
+                    new = kept + damped[k, i, tile(j)] * value
+                    result[k, i + 1, tile(j)] = new
+                    dots.append(residual[k, i, tile(j)] * new)
+                    if other is not None:
+                        crosses.append(other[k, i, tile(j)] * new)
+                gamma = gamma + tree_sum(dots)
+                if other is not None:
+                    cross = cross + tree_sum(crosses)
+            return gamma, cross
+
+        sums = lax.fori_loop(0, half, up, (zero, zero), unroll=2)
         at_.seam_fine(result)
         return [grand_total(part) for part in sums]
 
-    def curvature(field, keep):
-        def step(i, carry):
-            carry = list(carry)
-            for j in range(tiles):
-                here, sums = stencil(field, i, j)
-                for k in range(8):
-                    base = diagonal[k, i, tile(j)]
-                    for s in slots:
-                        value = (base + shifts[s]) * here[s][k] - sums[s][k]
-                        if keep:
-                            image[8 * s + k, i, tile(j)] = value
-                        carry[s] = carry[s] + here[s][k] * value
-            return tuple(carry)
-
-        sums = lax.fori_loop(0, half, step, (zero,) * members)
-        return [grand_total(part) for part in sums]
-
-    gamma = precondition(first_dir, None)
-    curve = curvature(first_dir, True)
-    step_one = [gamma[s] / curve[s] for s in slots]
+    gamma, _ = precondition(first_dir, None)
+
+    def apply(i, acc):
+        for j in range(tiles):
+            here, sums = stencil(first_dir, i, j, True)
+            dots = []
+            for k in range(8):
+                value = diagonal[k, i, tile(j)] * here[k] - sums[k]
+                image[k, i, tile(j)] = value
+                dots.append(here[k] * value)
+            acc = acc + tree_sum(dots)
+        return acc
+
+    curve = grand_total(lax.fori_loop(0, half, apply, zero, unroll=2))
+    step_one = gamma / curve
 
     def update(i, carry):
         for j in range(tiles):
-            for s in slots:
-                for k in range(8):
-                    at = 8 * s + k
-                    new = residual[at, i, tile(j)] - step_one[s] * image[at, i, tile(j)]
-                    residual[at, i, tile(j)] = new
-                    scaled[at, i + 1, tile(j)] = damped[at, i, tile(j)] * new
+            for k in range(8):
+                new = residual[k, i, tile(j)] - step_one * image[k, i, tile(j)]
+                residual[k, i, tile(j)] = new
+                scaled[k, i + 1, tile(j)] = damped[k, i, tile(j)] * new
         return carry
 
-    lax.fori_loop(0, half, update, 0)
+    lax.fori_loop(0, half, update, 0, unroll=2)
     at_.seam_fine(scaled)
 
-    sums = precondition(second_dir, image)
-    gamma_next, cross = sums[:members], sums[members:]
-    bend = curvature(second_dir, False)
-    ratio = [gamma_next[s] / gamma[s] for s in slots]
-    step_two = [
-        gamma_next[s] / (bend[s] + ratio[s] * (2.0 * cross[s] + ratio[s] * curve[s]))
-        for s in slots
-    ]
-    step_first = [step_one[s] + step_two[s] * ratio[s] for s in slots]
-
-    own = adjoint_ref.shape[1]
-    start = place_ref[0] * (own // 2)
+    gamma_next, cross = precondition(second_dir, image)
+
+    def bend(i, carry):
+        own_part, face_part = carry
+        for j in range(tiles):
+            here, sums = stencil(second_dir, i, j, False)
+            own_part = own_part + tree_sum(
+                [here[k] * (diagonal[k, i, tile(j)] * here[k]) for k in range(8)]
+            )
+            face_part = face_part + tree_sum([here[k] * sums[k] for k in range(7)])
+        return own_part, face_part
+
+    own_part, face_part = lax.fori_loop(0, half, bend, (zero, zero), unroll=2)
+    ratio = gamma_next / gamma
+    curve_next = grand_total(own_part - 2.0 * face_part)
+    step_two = gamma_next / (curve_next + ratio * (2.0 * cross + ratio * curve))
+    step_first = step_one + step_two * ratio
+
+    _, own, ny, nz = adjoint_ref.shape
+    start = (place_ref[0] - core) * (own // 2)
     upper = jnp.where(start >= half, 1, 0)
     start = start - half * upper
     even = at_.lane % 2 == 0
     source = at_.lane // 2 + HALF * upper
-    for at in range(own + 2):
+    for at in range(2 * own + 2):
         a = (at + 1) % 2
         spot = start + (at + 1) // 2
         for b in (0, 1):
             for j in range(tiles):
-                for s in slots:
-                    both = []
-                    for c in (0, 1):
-                        k = 8 * s + cls(a, b, c)
-                        both.append(
-                            step_first[s] * first_dir[k, spot, tile(j)]
-                            + step_two[s] * second_dir[k, spot, tile(j)]
-                        )
-                    planes[s, at, at_.every(b, j), :] = jnp.where(
-                        even,
-                        jnp.take_along_axis(both[0], source, axis=1),
-                        jnp.take_along_axis(both[1], source, axis=1),
-                    )
-
-    full = (2 * rows, 2 * HALF)
+                both = [
+                    step_first * first_dir[cls(a, b, c), spot, tile(j)]
+                    + step_two * second_dir[cls(a, b, c), spot, tile(j)]
+                    for c in (0, 1)
+                ]
+                planes[at, at_.every(b, j), :] = jnp.where(
+                    even,
+                    jnp.take_along_axis(both[0], source, axis=1),
+                    jnp.take_along_axis(both[1], source, axis=1),
+                )
+
+    full = (ny, nz)
     y_at = row_index(full)
     z_at = lane_index(full)
 
@@ -526,32 +512,28 @@
         edge = full[axis] - 1 if up else 0
         return value - jnp.where(at == edge, 0.0, moved)
 
-    is_even = place_ref[0] % 2 == 0
+    is_even = core == 0
+    state = [jnp.where(is_even, far_ref[core, 0], near_ref[own])]
+    state += [jnp.where(is_even, state_ref[core, x], near_ref[x]) for x in range(own)]
+    state += [jnp.where(is_even, near_ref[x], state_ref[core, x]) for x in range(own)]
+    state += [jnp.where(is_even, near_ref[own], far_ref[core, 0])]
     groups = share_ref.shape[0]
-    chunk = share_ref.shape[2]
-    for j in range(own):
-        term = jnp.zeros(full, jnp.float32)
-        for s in slots:
-            here = planes[s, j + 1]
-            adjoint_ref[s, j] = here
-            f = state_ref[s, j]
-            if j:
-                f_low = state_ref[s, j - 1]
-            else:
-                f_low = jnp.where(is_even, far_ref[s, 0], near_ref[s, 0])
-            if j + 1 < own:
-                f_high = state_ref[s, j + 1]
-            else:
-                f_high = jnp.where(is_even, near_ref[s, 0], far_ref[s, 0])
-            term = term + (here - planes[s, j + 2]) * (f - f_high)
-            term = term + (here - planes[s, j]) * (f - f_low)
+    chunk = share_ref.shape[3]
+    for owner in (0, 1):
+        target = jnp.where(core == owner, 0, 1)
+        for x in range(own):
+            j = owner * own + x + 1
+            here, f = planes[j], state[j]
+            adjoint_ref[target, x] = here
+            term = (here - planes[j + 1]) * (f - state[j + 1])
+            term = term + (here - planes[j - 1]) * (f - state[j - 1])
             for axis in (0, 1):
                 for up in (True, False):
                     term = term + drop(here, axis, up) * drop(f, axis, up)
-        planes[0, j] = -0.5 * term
-        for k in range(groups):
-            at = lax.rem(place_ref[1] + k, groups) * chunk
-            share_ref[k, j] = planes[0, j, pl.ds(pl.multiple_of(at, chunk), chunk), :]
+            planes[2 * own + 2 + x] = -0.5 * term
+            for k in range(groups):
+                at = pl.multiple_of(lax.rem(place_ref[1] + k, groups) * chunk, chunk)
+                share_ref[k, target, x] = planes[2 * own + 2 + x, pl.ds(at, chunk), :]
 
 
 def whole_grid(conductivity, misfit, forward_states, pole_shifts, pole_weights, pole_order):
@@ -559,13 +541,7 @@
     groups = lax.axis_size("pole")
     place = jnp.stack([lax.axis_index("space"), lax.axis_index("pole")]).astype(jnp.int32)
     peers = lax.axis_size("space")
-    even = place[0] % 2 == 0
-    first, last = forward_states[:, :1], forward_states[:, own - 1 :]
-    near = [(i, i ^ 1) for i in range(peers)]
-    far = [(i, i + 1 if i % 2 else i - 1) for i in range(1, peers - 1)]
-    halos = [(jnp.where(even, first, last), far), (jnp.where(even, last, first), near)]
-    mine, theirs, halos = gather_blocks([conductivity, misfit], halos, "space")
-    far, near = halos
+    mine, theirs, far, near = gather_blocks([conductivity, misfit], forward_states, "space")
     half, rows = peers * own // 4, ny // 2
 
     def field(count, extent):
@@ -583,9 +559,9 @@
         field(8, half),
         field(8, half),
         field(8, half),
-        field(8 * members, half),
+        field(8, half),
         field(5, half + 1),
-        field(members, half),
+        (half, rows, 2 * HALF),
     ]
     coefficients = pl.pallas_call(
         setup_kernel,
@@ -593,33 +569,32 @@
         in_specs=[smem] * 3 + [vmem] * 2,
         out_specs=[vmem] * len(shapes),
         scratch_shapes=[held(*field(8, half + 2))],
-        compiler_params=pltpu.CompilerParams(vmem_limit_bytes=20 * 1024 * 1024),
+        compiler_params=pltpu.CompilerParams(vmem_limit_bytes=6 * 1024 * 1024),
         name="setup",
     )(place, pole_shifts, pole_order, mine[0], theirs[0])
     adjoint, share = pl.pallas_call(
         solve_kernel,
         out_shape=(
-            jax.ShapeDtypeStruct(forward_states.shape, jnp.float32),
-            jax.ShapeDtypeStruct((groups, own, ny // groups, nz), jnp.float32),
+            jax.ShapeDtypeStruct((2, own, ny, nz), jnp.float32),
+            jax.ShapeDtypeStruct((groups, 2, own, ny // groups, nz), jnp.float32),
         ),
-        in_specs=[smem] * 4 + [vmem] * (5 + len(shapes)),
+        in_specs=[smem] * 3 + [vmem] * (5 + len(shapes)),
         out_specs=(vmem, vmem),
         scratch_shapes=[
-            held(*field(8 * members, half)),
-            held(*field(8 * members, half + 2)),
-            held(*field(8 * members, half)),
-            held(*field(8 * members, half + 2)),
-            held(*field(8 * members, half + 2)),
-            held(*field(8 * members, half)),
-            held(*field(members, half + 2)),
-            held(*field(members, half + 2)),
-            held(members, own + 2, ny, nz),
+            held(*field(8, half)),
+            held(*field(8, half + 2)),
+            held(*field(8, half)),
+            held(*field(8, half + 2)),
+            held(*field(8, half + 2)),
+            held(*field(8, half)),
+            held(*field(1, half + 2)),
+            held(*field(1, half + 2)),
+            held(3 * own + 2, ny, nz),
         ],
-        compiler_params=pltpu.CompilerParams(vmem_limit_bytes=36 * 1024 * 1024),
+        compiler_params=pltpu.CompilerParams(vmem_limit_bytes=12 * 1024 * 1024),
         name="solve",
     )(
         place,
-        pole_shifts,
         pole_weights,
         pole_order,
         mine[1],
@@ -629,11 +604,24 @@
         near,
         *coefficients,
     )
-    gradient = share[0]
-    for k in range(1, groups):
-        ring = [(i, (i + k) % groups) for i in range(groups)]
-        gradient = gradient + lax.ppermute(share[k], "pole", ring)
-    return adjoint, gradient
+
+    gradient = share[0, 0]
+    for k in range(groups):
+        for side in (0, 1):
+            if k or side:
+                pairs = [
+                    (i * peers + j, (i + k) % groups * peers + (j ^ side))
+                    for i in range(groups)
+                    for j in range(peers)
+                ]
+                gradient = gradient + lax.ppermute(share[k, side], ("pole", "space"), pairs)
+    swap = [(i, i ^ 1) for i in range(peers)]
+    partner = lax.ppermute(adjoint[1], "space", swap)
+    even = place[0] % 2 == 0
+    adjoint_states = jnp.stack(
+        [jnp.where(even, adjoint[0], partner), jnp.where(even, partner, adjoint[0])]
+    )
+    return adjoint_states, gradient
 
 
 def plus_side(field, which_dim):
@@ -823,7 +811,7 @@
         nx = conductivity.shape[0] * lax.axis_size("space")
         _, ny, nz = conductivity.shape
         peers = lax.axis_size("space")
-        small = nx * ny * nz <= REPLICATED_CELLS and conductivity.shape[0] % 2 == 0
+        small = nx * ny * nz <= REPLICATED_CELLS and forward_states.shape[:2] == (2, 2)
         if small and nz == 2 * HALF and peers > 2 and peers & (peers - 1) == 0:
             return whole_grid(conductivity, misfit, forward_states, *poles)
         return divided(conductivity, misfit, forward_states, *poles)

time: 53.3 us -> 49 us (0.919)
  the two profiles are of different devices: /device:TPU:8 before, /device:TPU:25 now
where the time goes in v8:
time: 49 us; the launch traced here: 48.7 us
  starting transfers between devices  15.6 us (32%)
  waiting for transfers between devices  15.6 us (32%)
  Pallas kernels  11.7 us (24%)
  other arithmetic  4.14 us (8%)
  local copies, waits for them, and re-layouts  0.97 us (2%)
  between operations  0.85 us (2%)
    ppermute x6, waiting for transfers between devices, gather_blocks(): arrived = lax.ppermute(held[at], axis, pairs)  10.5 us
    pallas_call x1, Pallas kernels, whole_grid(): pl.pallas_call(solve_kernel, out_shape=(jax.ShapeDtypeStruct((2, own, ny,...  8.72 us
    ppermute x2, starting transfers between devices, gather_blocks(): other = [lax.ppermute(part, axis, swap) for part in held]  5.22 us
    ppermute x1, starting transfers between devices, gather_blocks(): far = lax.ppermute(edge, axis, over)  3.68 us
    pallas_call x1, Pallas kernels, whole_grid(): pl.pallas_call(setup_kernel, out_shape=[jax.ShapeDtypeStruct(shape, jnp.f...  2.93 us
    ppermute x3, waiting for transfers between devices, whole_grid(): gradient = gradient + lax.ppermute(share[k, side], ('pole', 'space'), pairs)  2.83 us
    ppermute x1, starting transfers between devices, gather_blocks(): near = lax.ppermute(jnp.where(even, given[1], given[0]), axis, swap)  2.69 us
    ppermute x3, starting transfers between devices, whole_grid(): gradient = gradient + lax.ppermute(share[k, side], ('pole', 'space'), pairs)  2.22 us
  transfers between devices with their start and end apart: 14, of which 8 were waited for; matrix products, arithmetic and copies ran while one was open for 7% of the time, Pallas kernels for 6%

profile of v8, /device:TPU:25, one launch (start us, length us, event | category | flops | bytes accessed | tf_op | source)
XLA Modules:
  0.0 48.7 jit_solution(5838066051815678180)
XLA Ops:
  0.6 0.0 copy-start.4
  0.7 0.9 %slice_select_fusion.1 = f32[2,1,64,128]{3,2,1,0:T(8,128)S(1)} fusion(f32[2,2,64,128]{3,2,1,0:T(8,128)} %state_ref.1, pred[]{:T(512)S(6)} %eq.7), kind=kLoop, calls=%fused_computation.14 | loop fusion | flops 16384 | bytes 196609 | tf_op jit(solution)/shard_map/jit(_where)/select_n | solution.py:85
  1.6 3.7 %collective-permute-start.6 = (f32[2,1,64,128]{3,2,1,0:T(8,128)S(1)}, f32[2,1,64,128]{3,2,1,0:T(8,128)S(1)}, u32[]{:S(2)}, u32[]{:S(2)}) collective-permute-start(f32[2,1,64,128]{3,2,1,0:T(8,128)S(1)} %slice_select_fusion.1), channel_id=1, source_target_pairs={{1,2},{2,1},{3,4},{4,3},{5,6},{6,5},{7,8},{8,7},{9,10},{10,9},{11,... | collective-permute-start | bytes 196616 | tf_op jit(solution)/shard_map/ppermute | solution.py:87
  5.3 0.1 collective-permute-start.4
  5.3 1.3 %collective-permute-start = (f32[1,2,64,128]{3,2,1,0:T(8,128)}, f32[1,2,64,128]{3,2,1,0:T(8,128)S(1)}, u32[]{:S(2)}, u32[]{:S(2)}) collective-permute-start(f32[1,2,64,128]{3,2,1,0:T(8,128)} %bitcast.33), channel_id=1, source_target_pairs={{0,2},{1,9},{2,0},{3,11},{4,6},{5,13},{6,4},{7,15},{8,10},{9,1},{1... | collective-permute-start | bytes 196616 | tf_op jit(solution)/shard_map/ppermute | solution.py:98
  6.7 0.8 %multiply_bitcast_fusion = f32[1,2,64,128]{3,2,1,0:T(8,128)S(1)} fusion(f32[2,64,128]{2,1,0:T(8,128)} %param.6), kind=kLoop, calls=%fused_computation.15 | loop fusion | flops 16384 | bytes 131072 | tf_op jit(solution)/shard_map/mul | solution.py:83
  7.5 1.9 %collective-permute-done.4 = f32[1,2,64,128]{3,2,1,0:T(8,128)S(1)} collective-permute-done((f32[1,2,64,128]{3,2,1,0:T(8,128)}, f32[1,2,64,128]{3,2,1,0:T(8,128)S(1)}, u32[]{:S(2)}, u32[]{:S(2)}) %collective-permute-start.4) | collective-permute-done | bytes 65568 | tf_op jit(solution)/shard_map/ppermute | solution.py:98
  9.4 0.1 collective-permute-start.5
  9.5 2.5 %collective-permute-done = f32[1,2,64,128]{3,2,1,0:T(8,128)S(1)} collective-permute-done((f32[1,2,64,128]{3,2,1,0:T(8,128)}, f32[1,2,64,128]{3,2,1,0:T(8,128)S(1)}, u32[]{:S(2)}, u32[]{:S(2)}) %collective-permute-start) | collective-permute-done | bytes 65568 | tf_op jit(solution)/shard_map/ppermute | solution.py:98
  12.0 0.8 %pad_maximum_fusion.4 = f32[2,2,64,128]{3,2,1,0:T(8,128)S(1)} fusion(f32[1,2,64,128]{3,2,1,0:T(8,128)S(1)} %collective-permute-done, f32[1,2,64,128]{3,2,1,0:T(8,128)} %bitcast.34), kind=kLoop, calls=%fused_computation.4 | loop fusion | flops 32768 | bytes 262144 | tf_op jit(solution)/shard_map/concatenate | solution.py:101
  12.9 0.1 collective-permute-start.1
  12.9 0.9 %constant_dynamic-update-slice_fusion.1 = f32[2,3,64,128]{3,2,1,0:T(8,128)S(1)} fusion(f32[2,2,64,128]{3,2,1,0:T(8,128)} %state_ref.1), kind=kLoop, calls=%fused_computation.24 | loop fusion | bytes 262144
  13.9 1.8 %collective-permute-done.5 = f32[2,2,64,128]{3,2,1,0:T(8,128)S(1)} collective-permute-done((f32[2,2,64,128]{3,2,1,0:T(8,128)S(1)}, f32[2,2,64,128]{3,2,1,0:T(8,128)S(1)}, u32[]{:S(2)}, u32[]{:S(2)}) %collective-permute-start.5) | collective-permute-done | bytes 131104 | tf_op jit(solution)/shard_map/ppermute | solution.py:98
  15.7 0.1 collective-permute-start.7
  15.8 4.3 %collective-permute-done.1 = f32[2,2,64,128]{3,2,1,0:T(8,128)S(1)} collective-permute-done((f32[2,2,64,128]{3,2,1,0:T(8,128)S(1)}, f32[2,2,64,128]{3,2,1,0:T(8,128)S(1)}, u32[]{:S(2)}, u32[]{:S(2)}) %collective-permute-start.1) | collective-permute-done | bytes 131104 | tf_op jit(solution)/shard_map/ppermute | solution.py:98
  20.1 0.1 collective-permute-start.2
  20.3 2.7 %collective-permute-start.8 = (f32[3,64,128]{2,1,0:T(8,128)S(1)}, f32[3,64,128]{2,1,0:T(8,128)S(1)}, u32[]{:S(2)}, u32[]{:S(2)}) collective-permute-start(f32[3,64,128]{2,1,0:T(8,128)S(1)} %fusion), channel_id=1, source_target_pairs={{0,1},{1,0},{2,3},{3,2},{4,5},{5,4},{6,7},{7,6},{8,9},{9,8},{10,11... | collective-permute-start | bytes 294920 | tf_op jit(solution)/shard_map/ppermute | solution.py:94
  23.0 0.9 %collective-permute-done.8.near_ref = f32[3,64,128]{2,1,0:T(8,128)S(1)} collective-permute-done((f32[3,64,128]{2,1,0:T(8,128)S(1)}, f32[3,64,128]{2,1,0:T(8,128)S(1)}, u32[]{:S(2)}, u32[]{:S(2)}) %collective-permute-start.8) | collective-permute-done | bytes 98336 | tf_op jit(solution)/shard_map/ppermute | solution.py:94
  23.9 5.1 %collective-permute-start.9 = (f32[8,2,64,128]{3,2,1,0:T(8,128)S(1)}, f32[8,2,64,128]{3,2,1,0:T(8,128)S(1)}, u32[]{:S(2)}, u32[]{:S(2)}) collective-permute-start(f32[8,2,64,128]{3,2,1,0:T(8,128)S(1)} %pad_maximum_fusion.1.mine_ref), channel_id=1, source_target_pairs={{0,1},{1,0},{2,3},{3,2},{4,5},{5,4},{6,7},{7,6},{8,9},{9,8},{10,11... | collective-permute-start | bytes 1572872 | tf_op jit(solution)/shard_map/ppermute | solution.py:103
  29.1 0.1 collective-permute-start.3
  29.2 0.1 pad_add_fusion.place_ref
  29.2 1.3 %collective-permute-done.9.theirs_ref = f32[8,2,64,128]{3,2,1,0:T(8,128)S(1)} collective-permute-done((f32[8,2,64,128]{3,2,1,0:T(8,128)S(1)}, f32[8,2,64,128]{3,2,1,0:T(8,128)S(1)}, u32[]{:S(2)}, u32[]{:S(2)}) %collective-permute-start.9) | collective-permute-done | bytes 524320 | tf_op jit(solution)/shard_map/ppermute | solution.py:103
  30.6 2.9 %setup.1 = (f32[12,8,32,128]{3,2,1,0:T(8,128)S(1)}, f32[4,9,32,128]{3,2,1,0:T(8,128)S(1)}, f32[8,8,32,128]{3,2,1,0:T(8,128)S(1)}, f32[8,8,32,128]{3,2,1,0:T(8,12...) custom-call(s32[2]{0:T(128)S(1)} %pad_add_fusion.place_ref, ...), custom_call_target="tpu_custom_call" | custom-call | tf_op jit(solution)/shard_map/setup/pallas_call | solution.py:566
  33.5 8.7 %solve.1 = (f32[2,2,64,128]{3,2,1,0:T(8,128)S(1)}, f32[2,2,2,32,128]{4,3,2,1,0:T(8,128)S(1)}) custom-call(s32[2]{0:T(128)S(1)} %pad_add_fusion.place_ref, f32[4]{0:T(128)S(1)} %copy-done.3, s32[2]{0:T(128)S(1)} %copy-done.1, f32[8,2,64,128]{3,2,1,0:T(8,128)S(1)} %pad_maximum_fusion.mine_ref, f32[8,2,64,128]{3,2,1,0:T(8,128)S(1)} %collective-permute-done.3.theirs_ref, ...), custom_call_target="tpu_custom_call" | custom-call | tf_op jit(solution)/shard_map/solve/pallas_call | solution.py:575
  42.3 0.4 collective-permute-start.11
  42.7 1.2 %collective-permute-start.12 = (f32[2,32,128]{2,1,0:T(8,128)S(1)}, f32[2,32,128]{2,1,0:T(8,128)S(1)}, u32[]{:S(2)}, u32[]{:S(2)}) collective-permute-start(f32[2,32,128]{2,1,0:T(8,128)S(1)} %get-tuple-element.36), channel_id=1, source_target_pairs={{0,16},{1,17},{2,18},{3,19},{4,20},{5,21},{6,22},{7,23},{8,24},{9,... | collective-permute-start | bytes 98312 | tf_op jit(solution)/shard_map/ppermute | solution.py:617
  44.0 0.5 %collective-permute-start.13 = (f32[2,32,128]{2,1,0:T(8,128)S(1)}, f32[2,32,128]{2,1,0:T(8,128)S(1)}, u32[]{:S(2)}, u32[]{:S(2)}) collective-permute-start(f32[2,32,128]{2,1,0:T(8,128)S(1)} %get-tuple-element.35), channel_id=1, source_target_pairs={{0,17},{1,16},{2,19},{3,18},{4,21},{5,20},{6,23},{7,22},{8,25},{9,... | collective-permute-start | bytes 98312 | tf_op jit(solution)/shard_map/ppermute | solution.py:617
  44.5 0.1 collective-permute-start.10
  44.6 0.9 %collective-permute-done.12 = f32[2,32,128]{2,1,0:T(8,128)S(1)} collective-permute-done((f32[2,32,128]{2,1,0:T(8,128)S(1)}, f32[2,32,128]{2,1,0:T(8,128)S(1)}, u32[]{:S(2)}, u32[]{:S(2)}) %collective-permute-start.12) | collective-permute-done | bytes 32800 | tf_op jit(solution)/shard_map/ppermute | solution.py:617
  45.5 1.9 %collective-permute-done.13 = f32[2,32,128]{2,1,0:T(8,128)S(1)} collective-permute-done((f32[2,32,128]{2,1,0:T(8,128)S(1)}, f32[2,32,128]{2,1,0:T(8,128)S(1)}, u32[]{:S(2)}, u32[]{:S(2)}) %collective-permute-start.13) | collective-permute-done | bytes 32800 | tf_op jit(solution)/shard_map/ppermute | solution.py:617
  47.4 0.6 %fusion.4 = f32[2,32,128]{2,1,0:T(8,128)} fusion(f32[2,32,128]{2,1,0:T(8,128)S(1)} %collective-permute-done.13, f32[2,32,128]{2,1,0:T(8,128)S(1)} %collective-permute-done.12, f32[2,32,128]{2,1,0:T(8,128)S(1)} %collective-permute-done.11, f32[2,2,2,32,128]{4,3,2,1,0:T(8,128)S(1)} %get-tuple-element.31), kind=kLoop, calls=%fused_computation.18 | loop fusion | flops 24576 | bytes 163840 | tf_op jit(solution)/shard_map/add | solution.py:617
  48.1 0.7 %pad_maximum_fusion.6 = f32[2,2,64,128]{3,2,1,0:T(8,128)} fusion(f32[1,2,64,128]{3,2,1,0:T(8,128)S(1)} %get-tuple-element.33, f32[1,2,64,128]{3,2,1,0:T(8,128)S(1)} %get-tuple-element.32), kind=kLoop, calls=%fused_computation.6 | loop fusion | flops 32768 | bytes 262144 | tf_op jit(solution)/shard_map/stack | solution.py:621
  (26 shorter events, 0.2 us)
Async XLA Ops:
  0.6 19.5 %copy-start.4 = (f32[2,64,128]{2,1,0:T(8,128)S(1)}, f32[2,64,128]{2,1,0:T(8,128)}, u32[]{:S(2)}) copy-start(f32[2,64,128]{2,1,0:T(8,128)} %param.7) | copy-start | bytes 196612
  1.6 14.1 %collective-permute-start.6 = (f32[2,1,64,128]{3,2,1,0:T(8,128)S(1)}, f32[2,1,64,128]{3,2,1,0:T(8,128)S(1)}, u32[]{:S(2)}, u32[]{:S(2)}) collective-permute-start(f32[2,1,64,128]{3,2,1,0:T(8,128)S(1)} %slice_select_fusion.1), channel_id=1, source_target_pairs={{1,2},{2,1},{3,4},{4,3},{5,6},{6,5},{7,8},{8,7},{9,10},{10,9},{11,... | collective-permute-start | bytes 196616 | tf_op jit(solution)/shard_map/ppermute | solution.py:87
  5.3 4.1 %collective-permute-start.4 = (f32[1,2,64,128]{3,2,1,0:T(8,128)}, f32[1,2,64,128]{3,2,1,0:T(8,128)S(1)}, u32[]{:S(2)}, u32[]{:S(2)}) collective-permute-start(f32[1,2,64,128]{3,2,1,0:T(8,128)} %bitcast.37), channel_id=1, source_target_pairs={{0,8},{1,3},{2,10},{3,1},{4,12},{5,7},{6,14},{7,5},{8,0},{9,11},{1... | collective-permute-start | bytes 196616 | tf_op jit(solution)/shard_map/ppermute | solution.py:98
  5.3 6.7 %collective-permute-start = (f32[1,2,64,128]{3,2,1,0:T(8,128)}, f32[1,2,64,128]{3,2,1,0:T(8,128)S(1)}, u32[]{:S(2)}, u32[]{:S(2)}) collective-permute-start(f32[1,2,64,128]{3,2,1,0:T(8,128)} %bitcast.33), channel_id=1, source_target_pairs={{0,2},{1,9},{2,0},{3,11},{4,6},{5,13},{6,4},{7,15},{8,10},{9,1},{1... | collective-permute-start | bytes 196616 | tf_op jit(solution)/shard_map/ppermute | solution.py:98
  9.4 6.2 %collective-permute-start.5 = (f32[2,2,64,128]{3,2,1,0:T(8,128)S(1)}, f32[2,2,64,128]{3,2,1,0:T(8,128)S(1)}, u32[]{:S(2)}, u32[]{:S(2)}) collective-permute-start(f32[2,2,64,128]{3,2,1,0:T(8,128)S(1)} %pad_maximum_fusion.5), channel_id=1, source_target_pairs={{0,4},{1,9},{2,6},{3,11},{4,0},{5,13},{6,2},{7,15},{8,12},{9,1},{1... | collective-permute-start | bytes 393224 | tf_op jit(solution)/shard_map/ppermute | solution.py:98
  12.9 7.2 %collective-permute-start.1 = (f32[2,2,64,128]{3,2,1,0:T(8,128)S(1)}, f32[2,2,64,128]{3,2,1,0:T(8,128)S(1)}, u32[]{:S(2)}, u32[]{:S(2)}) collective-permute-start(f32[2,2,64,128]{3,2,1,0:T(8,128)S(1)} %pad_maximum_fusion.4), channel_id=1, source_target_pairs={{0,8},{1,5},{2,10},{3,7},{4,12},{5,1},{6,14},{7,3},{8,0},{9,13},{1... | collective-permute-start | bytes 393224 | tf_op jit(solution)/shard_map/ppermute | solution.py:98
  15.6 14.9 %copy-start.1 = (s32[2]{0:T(128)S(1)}, s32[2]{0:T(128)}, u32[]{:S(2)}) copy-start(s32[2]{0:T(128)} %order_ref.3) | copy-start | bytes 28
  15.6 14.9 %copy-start.2 = (f32[4]{0:T(128)S(1)}, f32[4]{0:T(128)}, u32[]{:S(2)}) copy-start(f32[4]{0:T(128)} %shifts_ref.1) | copy-start | bytes 52
  15.7 7.3 %collective-permute-start.7 = (f32[4,2,64,128]{3,2,1,0:T(8,128)S(1)}, f32[4,2,64,128]{3,2,1,0:T(8,128)S(1)}, u32[]{:S(2)}, u32[]{:S(2)}) collective-permute-start(f32[4,2,64,128]{3,2,1,0:T(8,128)S(1)} %pad_maximum_fusion.3), channel_id=1, source_target_pairs={{0,2},{1,5},{2,0},{3,7},{4,6},{5,1},{6,4},{7,3},{8,10},{9,13},{10,... | collective-permute-start | bytes 786440 | tf_op jit(solution)/shard_map/ppermute | solution.py:98
  20.1 8.9 %collective-permute-start.2 = (f32[4,2,64,128]{3,2,1,0:T(8,128)S(1)}, f32[4,2,64,128]{3,2,1,0:T(8,128)S(1)}, u32[]{:S(2)}, u32[]{:S(2)}) collective-permute-start(f32[4,2,64,128]{3,2,1,0:T(8,128)S(1)} %pad_maximum_fusion.2), channel_id=1, source_target_pairs={{0,4},{1,3},{2,6},{3,1},{4,0},{5,7},{6,2},{7,5},{8,12},{9,11},{10,... | collective-permute-start | bytes 786440 | tf_op jit(solution)/shard_map/ppermute | solution.py:98
  20.2 13.3 %copy-start = (f32[2,2,64,128]{3,2,1,0:T(8,128)S(1)}, f32[2,2,64,128]{3,2,1,0:T(8,128)}, u32[]{:S(2)}) copy-start(f32[2,2,64,128]{3,2,1,0:T(8,128)} %state_ref.1) | copy-start | bytes 393220
  20.3 13.3 %copy-start.3 = (f32[4]{0:T(128)S(1)}, f32[4]{0:T(128)}, u32[]{:S(2)}) copy-start(f32[4]{0:T(128)} %weights_ref.1) | copy-start | bytes 52
  20.3 3.6 %collective-permute-start.8 = (f32[3,64,128]{2,1,0:T(8,128)S(1)}, f32[3,64,128]{2,1,0:T(8,128)S(1)}, u32[]{:S(2)}, u32[]{:S(2)}) collective-permute-start(f32[3,64,128]{2,1,0:T(8,128)S(1)} %fusion), channel_id=1, source_target_pairs={{0,1},{1,0},{2,3},{3,2},{4,5},{5,4},{6,7},{7,6},{8,9},{9,8},{10,11... | collective-permute-start | bytes 294920 | tf_op jit(solution)/shard_map/ppermute | solution.py:94
  23.9 6.7 %collective-permute-start.9 = (f32[8,2,64,128]{3,2,1,0:T(8,128)S(1)}, f32[8,2,64,128]{3,2,1,0:T(8,128)S(1)}, u32[]{:S(2)}, u32[]{:S(2)}) collective-permute-start(f32[8,2,64,128]{3,2,1,0:T(8,128)S(1)} %pad_maximum_fusion.1.mine_ref), channel_id=1, source_target_pairs={{0,1},{1,0},{2,3},{3,2},{4,5},{5,4},{6,7},{7,6},{8,9},{9,8},{10,11... | collective-permute-start | bytes 1572872 | tf_op jit(solution)/shard_map/ppermute | solution.py:103
  29.1 4.4 %collective-permute-start.3 = (f32[8,2,64,128]{3,2,1,0:T(8,128)S(1)}, f32[8,2,64,128]{3,2,1,0:T(8,128)S(1)}, u32[]{:S(2)}, u32[]{:S(2)}) collective-permute-start(f32[8,2,64,128]{3,2,1,0:T(8,128)S(1)} %pad_maximum_fusion.mine_ref), channel_id=1, source_target_pairs={{0,1},{1,0},{2,3},{3,2},{4,5},{5,4},{6,7},{7,6},{8,9},{9,8},{10,11... | collective-permute-start | bytes 1572872 | tf_op jit(solution)/shard_map/ppermute | solution.py:103
  42.3 2.3 %collective-permute-start.11 = (f32[2,32,128]{2,1,0:T(8,128)S(1)}, f32[2,32,128]{2,1,0:T(8,128)S(1)}, u32[]{:S(2)}, u32[]{:S(2)}) collective-permute-start(f32[2,32,128]{2,1,0:T(8,128)S(1)} %get-tuple-element.34), channel_id=1, source_target_pairs={{0,1},{1,0},{2,3},{3,2},{4,5},{5,4},{6,7},{7,6},{8,9},{9,8},{10,11... | collective-permute-start | bytes 98312 | tf_op jit(solution)/shard_map/ppermute | solution.py:617
  42.7 2.8 %collective-permute-start.12 = (f32[2,32,128]{2,1,0:T(8,128)S(1)}, f32[2,32,128]{2,1,0:T(8,128)S(1)}, u32[]{:S(2)}, u32[]{:S(2)}) collective-permute-start(f32[2,32,128]{2,1,0:T(8,128)S(1)} %get-tuple-element.36), channel_id=1, source_target_pairs={{0,16},{1,17},{2,18},{3,19},{4,20},{5,21},{6,22},{7,23},{8,24},{9,... | collective-permute-start | bytes 98312 | tf_op jit(solution)/shard_map/ppermute | solution.py:617
  44.0 3.5 %collective-permute-start.13 = (f32[2,32,128]{2,1,0:T(8,128)S(1)}, f32[2,32,128]{2,1,0:T(8,128)S(1)}, u32[]{:S(2)}, u32[]{:S(2)}) collective-permute-start(f32[2,32,128]{2,1,0:T(8,128)S(1)} %get-tuple-element.35), channel_id=1, source_target_pairs={{0,17},{1,16},{2,19},{3,18},{4,21},{5,20},{6,23},{7,22},{8,25},{9,... | collective-permute-start | bytes 98312 | tf_op jit(solution)/shard_map/ppermute | solution.py:617
  44.5 3.5 %collective-permute-start.10 = (f32[2,64,128]{2,1,0:T(8,128)S(1)}, f32[2,64,128]{2,1,0:T(8,128)S(1)}, u32[]{:S(2)}, u32[]{:S(2)}) collective-permute-start(f32[2,64,128]{2,1,0:T(8,128)S(1)} %slice_bitcast_fusion), channel_id=1, source_target_pairs={{0,1},{1,0},{2,3},{3,2},{4,5},{5,4},{6,7},{7,6},{8,9},{9,8},{10,11... | collective-permute-start | bytes 196616 | tf_op jit(solution)/shard_map/ppermute | solution.py:619

commit v9 on v8

--- a/solution.py
+++ b/solution.py
@@ -12,6 +12,7 @@
 REPLICATED_CELLS = 32 * 64 * 128
 HALF = 64
 TILE = 8
+UNROLL = 8
 
 
 def extended(array, sides, width):
@@ -37,6 +38,11 @@
 
 def roll(block, shift, axis):
     return pltpu.roll(block, shift % block.shape[axis], axis)
+
+
+def inverse(value):
+    guess = pl.reciprocal(value, approx=True)
+    return guess * (2.0 - value * guess)
 
 
 def tree_sum(values):
@@ -76,17 +82,36 @@
     return first, second, home
 
 
-def gather_blocks(blocks, states, axis):
+def prepare_kernel(place_ref, kappa_ref, misfit_ref, state_ref, half_ref, own_ref, held_ref, edge_ref):
+    half_ref[0] = 0.5 * kappa_ref[...]
+    own_ref[0] = misfit_ref[...]
+    held_ref[...] = state_ref[...]
+    even = place_ref[0] % 2 == 0
+    last = state_ref.shape[1] - 1
+    for slot in (0, 1):
+        edge_ref[slot, 0] = jnp.where(even, state_ref[slot, 0], state_ref[slot, last])
+
+
+def gather_blocks(place, kappa, misfit, states, axis):
     peers = lax.axis_size(axis)
-    even = lax.axis_index(axis) % 2 == 0
+    even = place[0] % 2 == 0
     swap = [(i, i ^ 1) for i in range(peers)]
-    own_half = lax.optimization_barrier(0.5 * blocks[0][None])
-    held = [block[None] for block in blocks]
-    edge = jnp.where(even, states[:, :1], states[:, -1:])
+    smem = pl.BlockSpec(memory_space=pltpu.SMEM)
+    vmem = pl.BlockSpec(memory_space=pltpu.VMEM)
+    shapes = [(1, *kappa.shape), (1, *misfit.shape), states.shape, (2, 1, *states.shape[2:])]
+    half, own, states, edge = pl.pallas_call(
+        prepare_kernel,
+        out_shape=[jax.ShapeDtypeStruct(shape, jnp.float32) for shape in shapes],
+        in_specs=[smem] + [vmem] * 3,
+        out_specs=[vmem] * 4,
+        compiler_params=pltpu.CompilerParams(vmem_limit_bytes=2 * 1024 * 1024),
+        name="prepare",
+    )(place, kappa, misfit, states)
     over = [(i, i + 1 if i % 2 else i - 1) for i in range(1, peers - 1)]
     far = lax.ppermute(edge, axis, over)
     swaps = [list(zip(*swap_masks(peers, flip))) for flip in (False, True)]
     steps = len(swaps[0])
+    held = [kappa[None], misfit[None]]
     for step in range(steps):
         if step == steps - 1:
             held[0], far = lax.optimization_barrier((held[0], far))
@@ -96,12 +121,13 @@
             masks = swaps[at][step]
             pairs = [(i, i ^ masks[i % 2]) for i in range(peers)]
             arrived = lax.ppermute(held[at], axis, pairs)
-            if step == 0 and at == 0:
-                held[0], arrived = own_half, 0.5 * arrived
+            if step == 0:
+                held[at] = (half, own)[at]
+                arrived = (0.5, 1.0)[at] * arrived
             held[at] = jnp.concatenate([held[at], arrived], axis=0)
     held[0], near = lax.optimization_barrier((held[0], near))
     other = [lax.ppermute(part, axis, swap) for part in held]
-    return held, other, far, near
+    return held, other, states, far, near
 
 
 CLASSES = [(a, b, c) for a in (0, 1) for b in (0, 1) for c in (0, 1)]
@@ -273,10 +299,10 @@
                 base = within + without + shift
                 diagonal[k, i, tile(j)] = base
                 coarse_total.append(without)
-                damped[k, i, tile(j)] = DAMPING / base
+                damped[k, i, tile(j)] = DAMPING * inverse(base)
             for at, part in enumerate(off):
                 coarse_off[at, i, tile(j)] = tree_sum(part)
-            coarse_damped[i, tile(j)] = DAMPING / (tree_sum(coarse_total) + 8.0 * shift)
+            coarse_damped[i, tile(j)] = DAMPING * inverse(tree_sum(coarse_total) + 8.0 * shift)
         return carry
 
     lax.fori_loop(0, half, plane, 0)
@@ -309,7 +335,9 @@
     coarse_off,
     coarse_damped,
     adjoint_ref,
-    share_ref,
+    keep_ref,
+    partner_ref,
+    send_ref,
     residual,
     scaled,
     partial,
@@ -384,7 +412,7 @@
                 coarse_one[0, i + 1, tile(j)] = coarse_damped[i, tile(j)] * rhs
             return carry
 
-        lax.fori_loop(0, half, down, 0, unroll=2)
+        lax.fori_loop(0, half, down, 0, unroll=UNROLL)
         at_.seam(coarse_one, [0], [0])
 
         def smooth(i, carry):
@@ -401,7 +429,7 @@
                 ] * (total + more + most)
             return carry
 
-        lax.fori_loop(0, half, smooth, 0, unroll=8)
+        lax.fori_loop(0, half, smooth, 0, unroll=UNROLL)
         at_.seam(coarse_two, [0], [0])
 
         def up(i, carry):
@@ -431,7 +459,7 @@
                     cross = cross + tree_sum(crosses)
             return gamma, cross
 
-        sums = lax.fori_loop(0, half, up, (zero, zero), unroll=2)
+        sums = lax.fori_loop(0, half, up, (zero, zero), unroll=UNROLL)
         at_.seam_fine(result)
         return [grand_total(part) for part in sums]
 
@@ -448,7 +476,7 @@
             acc = acc + tree_sum(dots)
         return acc
 
-    curve = grand_total(lax.fori_loop(0, half, apply, zero, unroll=2))
+    curve = grand_total(lax.fori_loop(0, half, apply, zero, unroll=UNROLL))
     step_one = gamma / curve
 
     def update(i, carry):
@@ -459,7 +487,7 @@
                 scaled[k, i + 1, tile(j)] = damped[k, i, tile(j)] * new
         return carry
 
-    lax.fori_loop(0, half, update, 0, unroll=2)
+    lax.fori_loop(0, half, update, 0, unroll=UNROLL)
     at_.seam_fine(scaled)
 
     gamma_next, cross = precondition(second_dir, image)
@@ -474,13 +502,13 @@
             face_part = face_part + tree_sum([here[k] * sums[k] for k in range(7)])
         return own_part, face_part
 
-    own_part, face_part = lax.fori_loop(0, half, bend, (zero, zero), unroll=2)
+    own_part, face_part = lax.fori_loop(0, half, bend, (zero, zero), unroll=UNROLL)
     ratio = gamma_next / gamma
     curve_next = grand_total(own_part - 2.0 * face_part)
     step_two = gamma_next / (curve_next + ratio * (2.0 * cross + ratio * curve))
     step_first = step_one + step_two * ratio
 
-    _, own, ny, nz = adjoint_ref.shape
+    own, ny, nz = adjoint_ref.shape
     start = (place_ref[0] - core) * (own // 2)
     upper = jnp.where(start >= half, 1, 0)
     start = start - half * upper
@@ -517,23 +545,32 @@
     state += [jnp.where(is_even, state_ref[core, x], near_ref[x]) for x in range(own)]
     state += [jnp.where(is_even, near_ref[x], state_ref[core, x]) for x in range(own)]
     state += [jnp.where(is_even, near_ref[own], far_ref[core, 0])]
-    groups = share_ref.shape[0]
-    chunk = share_ref.shape[3]
-    for owner in (0, 1):
-        target = jnp.where(core == owner, 0, 1)
-        for x in range(own):
-            j = owner * own + x + 1
-            here, f = planes[j], state[j]
-            adjoint_ref[target, x] = here
-            term = (here - planes[j + 1]) * (f - state[j + 1])
-            term = term + (here - planes[j - 1]) * (f - state[j - 1])
-            for axis in (0, 1):
-                for up in (True, False):
-                    term = term + drop(here, axis, up) * drop(f, axis, up)
-            planes[2 * own + 2 + x] = -0.5 * term
-            for k in range(groups):
-                at = pl.multiple_of(lax.rem(place_ref[1] + k, groups) * chunk, chunk)
-                share_ref[k, target, x] = planes[2 * own + 2 + x, pl.ds(at, chunk), :]
+    terms = 2 * own + 2
+    for x in range(2 * own):
+        here, f = planes[x + 1], state[x + 1]
+        term = (here - planes[x + 2]) * (f - state[x + 2])
+        term = term + (here - planes[x]) * (f - state[x])
+        for axis in (0, 1):
+            for up in (True, False):
+                term = term + drop(here, axis, up) * drop(f, axis, up)
+        planes[terms + x] = -0.5 * term
+
+    groups = send_ref.shape[0] + 1
+    chunk = keep_ref.shape[1]
+    for x in range(own):
+        mine, other = core * own + x, (1 - core) * own + x
+        adjoint_ref[x] = planes[1 + mine]
+        partner_ref[x, :ny] = planes[1 + other]
+        for k in range(groups):
+            at = pl.multiple_of(lax.rem(place_ref[1] + k, groups) * chunk, chunk)
+            for side, plane in enumerate((mine, other)):
+                share = planes[terms + plane, pl.ds(at, chunk), :]
+                if k:
+                    send_ref[k - 1, side, x] = share
+                elif side:
+                    partner_ref[x, ny:] = share
+                else:
+                    keep_ref[x] = share
 
 
 def whole_grid(conductivity, misfit, forward_states, pole_shifts, pole_weights, pole_order):
@@ -541,7 +578,9 @@
     groups = lax.axis_size("pole")
     place = jnp.stack([lax.axis_index("space"), lax.axis_index("pole")]).astype(jnp.int32)
     peers = lax.axis_size("space")
-    mine, theirs, far, near = gather_blocks([conductivity, misfit], forward_states, "space")
+    mine, theirs, states, far, near = gather_blocks(
+        place, conductivity, misfit, forward_states, "space"
+    )
     half, rows = peers * own // 4, ny // 2
 
     def field(count, extent):
@@ -572,14 +611,17 @@
         compiler_params=pltpu.CompilerParams(vmem_limit_bytes=6 * 1024 * 1024),
         name="setup",
     )(place, pole_shifts, pole_order, mine[0], theirs[0])
-    adjoint, share = pl.pallas_call(
+    chunk = ny // groups
+    adjoint, gradient, partner, send = pl.pallas_call(
         solve_kernel,
-        out_shape=(
-            jax.ShapeDtypeStruct((2, own, ny, nz), jnp.float32),
-            jax.ShapeDtypeStruct((groups, 2, own, ny // groups, nz), jnp.float32),
-        ),
+        out_shape=[
+            jax.ShapeDtypeStruct((own, ny, nz), jnp.float32),
+            jax.ShapeDtypeStruct((own, chunk, nz), jnp.float32),
+            jax.ShapeDtypeStruct((own, ny + chunk, nz), jnp.float32),
+            jax.ShapeDtypeStruct((groups - 1, 2, own, chunk, nz), jnp.float32),
+        ],
         in_specs=[smem] * 3 + [vmem] * (5 + len(shapes)),
-        out_specs=(vmem, vmem),
+        out_specs=[vmem] * 4,
         scratch_shapes=[
             held(*field(8, half)),
             held(*field(8, half + 2)),
@@ -589,7 +631,7 @@
             held(*field(8, half)),
             held(*field(1, half + 2)),
             held(*field(1, half + 2)),
-            held(3 * own + 2, ny, nz),
+            held(4 * own + 2, ny, nz),
         ],
         compiler_params=pltpu.CompilerParams(vmem_limit_bytes=12 * 1024 * 1024),
         name="solve",
@@ -599,29 +641,29 @@
         pole_order,
         mine[1],
         theirs[1],
-        forward_states,
+        states,
         far,
         near,
         *coefficients,
     )
 
-    gradient = share[0, 0]
-    for k in range(groups):
+    arrived = lax.ppermute(partner, "space", [(i, i ^ 1) for i in range(peers)])
+    shares = []
+    for k in range(1, groups):
         for side in (0, 1):
-            if k or side:
-                pairs = [
-                    (i * peers + j, (i + k) % groups * peers + (j ^ side))
-                    for i in range(groups)
-                    for j in range(peers)
-                ]
-                gradient = gradient + lax.ppermute(share[k, side], ("pole", "space"), pairs)
-    swap = [(i, i ^ 1) for i in range(peers)]
-    partner = lax.ppermute(adjoint[1], "space", swap)
+            pairs = [
+                (i * peers + j, (i + k) % groups * peers + (j ^ side))
+                for i in range(groups)
+                for j in range(peers)
+            ]
+            shares.append(lax.ppermute(send[k - 1, side], ("pole", "space"), pairs))
     even = place[0] % 2 == 0
+    theirs = arrived[:, :ny]
     adjoint_states = jnp.stack(
-        [jnp.where(even, adjoint[0], partner), jnp.where(even, partner, adjoint[0])]
-    )
-    return adjoint_states, gradient
+        [jnp.where(even, adjoint, theirs), jnp.where(even, theirs, adjoint)]
+    )
+    adjoint_states, arrived = lax.optimization_barrier((adjoint_states, arrived))
+    return adjoint_states, gradient + arrived[:, ny:] + sum(shares)
 
 
 def plus_side(field, which_dim):

time: 49 us -> 46.5 us (0.949)
  the two profiles are of different devices: /device:TPU:25 before, /device:TPU:0 now
where the time goes in v9:
time: 46.5 us; the launch traced here: 46.2 us
  waiting for transfers between devices  16.1 us (35%)
  starting transfers between devices  13.8 us (30%)
  Pallas kernels  12.3 us (26%)
  local copies, waits for them, and re-layouts  1.82 us (4%)
  other arithmetic  1.5 us (3%)
  between operations  0.83 us (2%)
    ppermute x6, waiting for transfers between devices, gather_blocks(): arrived = lax.ppermute(held[at], axis, pairs)  13 us
    ppermute x6, starting transfers between devices, gather_blocks(): arrived = lax.ppermute(held[at], axis, pairs)  10.7 us
    pallas_call x1, Pallas kernels, whole_grid(): pl.pallas_call(solve_kernel, out_shape=[jax.ShapeDtypeStruct((own, ny, nz...  8.36 us
    pallas_call x1, Pallas kernels, whole_grid(): pl.pallas_call(setup_kernel, out_shape=[jax.ShapeDtypeStruct(shape, jnp.f...  3.05 us
    ppermute x2, waiting for transfers between devices, whole_grid(): shares.append(lax.ppermute(send[k - 1, side], ('pole', 'space'), pairs))  2.99 us
    unnamed x14, local copies, waits for them, and re-layouts  1.79 us
    ppermute x2, starting transfers between devices, whole_grid(): shares.append(lax.ppermute(send[k - 1, side], ('pole', 'space'), pairs))  1.52 us
  transfers between devices with their start and end apart: 13, of which 7 were waited for; matrix products, arithmetic and copies ran while one was open for 2% of the time, Pallas kernels for 8%

profile of v9, /device:TPU:0, one launch (start us, length us, event | category | flops | bytes accessed | tf_op | source)
XLA Modules:
  0.0 46.2 jit_solution(8472443892231852876)
XLA Ops:
  0.6 4.1 %collective-permute-start.4 = (f32[1,2,64,128]{3,2,1,0:T(8,128)}, f32[1,2,64,128]{3,2,1,0:T(8,128)S(1)}, u32[]{:S(2)}, u32[]{:S(2)}) collective-permute-start(f32[1,2,64,128]{3,2,1,0:T(8,128)} %bitcast.14), channel_id=1, source_target_pairs={{0,8},{1,3},{2,10},{3,1},{4,12},{5,7},{6,14},{7,5},{8,0},{9,11},{1... | collective-permute-start | bytes 196616 | tf_op jit(solution)/shard_map/ppermute | solution.py:123
  4.7 0.1 pad_add_fusion.place_ref
  4.8 0.9 %copy-done = f32[2,2,64,128]{3,2,1,0:T(8,128)S(1)} copy-done((f32[2,2,64,128]{3,2,1,0:T(8,128)S(1)}, f32[2,2,64,128]{3,2,1,0:T(8,128)}, u32[]{:S(2)}) %copy-start) | copy-done | bytes 131096
  5.7 0.8 %copy-done.1 = f32[2,64,128]{2,1,0:T(8,128)S(1)} copy-done((f32[2,64,128]{2,1,0:T(8,128)S(1)}, f32[2,64,128]{2,1,0:T(8,128)}, u32[]{:S(2)}) %copy-start.1) | copy-done | bytes 65560
  6.6 0.9 %prepare.1 = (f32[1,2,64,128]{3,2,1,0:T(8,128)S(1)}, f32[1,2,64,128]{3,2,1,0:T(8,128)S(1)}, f32[2,2,64,128]{3,2,1,0:T(8,128)S(1)}, f32[2,1,64,128]{3,2,1,0:T(8,128)S(1)}) custom-call(s32[2]{0:T(128)S(1)} %pad_add_fusion.place_ref, f32[2,64,128]{2,1,0:T(8,128)S(1)} %copy-done.1, f32[2,64,128]{2,1,0:T(8,128)} %misfit_ref.1, f32[2,2,64,128]{3,2,1,0:T(8,128)S(1)} %copy-done), custom_call_target="tpu_custom_call" | custom-call | tf_op jit(solution)/shard_map/prepare/pallas_call | solution.py:102
  7.4 0.7 %collective-permute-start.6 = (f32[2,1,64,128]{3,2,1,0:T(8,128)S(1)}, f32[2,1,64,128]{3,2,1,0:T(8,128)S(1)}, u32[]{:S(2)}, u32[]{:S(2)}) collective-permute-start(f32[2,1,64,128]{3,2,1,0:T(8,128)S(1)} %get-tuple-element.28), channel_id=1, source_target_pairs={{1,2},{2,1},{3,4},{4,3},{5,6},{6,5},{7,8},{8,7},{9,10},{10,9},{11,... | collective-permute-start | bytes 196616 | tf_op jit(solution)/shard_map/ppermute | solution.py:111
  8.1 2.8 %collective-permute-start = (f32[1,2,64,128]{3,2,1,0:T(8,128)}, f32[1,2,64,128]{3,2,1,0:T(8,128)S(1)}, u32[]{:S(2)}, u32[]{:S(2)}) collective-permute-start(f32[1,2,64,128]{3,2,1,0:T(8,128)} %bitcast.2), channel_id=1, source_target_pairs={{0,2},{1,9},{2,0},{3,11},{4,6},{5,13},{6,4},{7,15},{8,10},{9,1},{1... | collective-permute-start | bytes 196616 | tf_op jit(solution)/shard_map/ppermute | solution.py:123
  10.9 0.0 collective-permute-done.4
  11.0 1.6 %collective-permute-start.5 = (f32[2,2,64,128]{3,2,1,0:T(8,128)S(1)}, f32[2,2,64,128]{3,2,1,0:T(8,128)S(1)}, u32[]{:S(2)}, u32[]{:S(2)}) collective-permute-start(f32[2,2,64,128]{3,2,1,0:T(8,128)S(1)} %pad_maximum_fusion.4), channel_id=1, source_target_pairs={{0,4},{1,9},{2,6},{3,11},{4,0},{5,13},{6,2},{7,15},{8,12},{9,1},{1... | collective-permute-start | bytes 393224 | tf_op jit(solution)/shard_map/ppermute | solution.py:123
  12.6 1.1 %collective-permute-done = f32[1,2,64,128]{3,2,1,0:T(8,128)S(1)} collective-permute-done((f32[1,2,64,128]{3,2,1,0:T(8,128)}, f32[1,2,64,128]{3,2,1,0:T(8,128)S(1)}, u32[]{:S(2)}, u32[]{:S(2)}) %collective-permute-start) | collective-permute-done | bytes 65568 | tf_op jit(solution)/shard_map/ppermute | solution.py:123
  13.8 1.6 %collective-permute-start.1 = (f32[2,2,64,128]{3,2,1,0:T(8,128)S(1)}, f32[2,2,64,128]{3,2,1,0:T(8,128)S(1)}, u32[]{:S(2)}, u32[]{:S(2)}) collective-permute-start(f32[2,2,64,128]{3,2,1,0:T(8,128)S(1)} %pad_maximum_fusion.3), channel_id=1, source_target_pairs={{0,8},{1,5},{2,10},{3,7},{4,12},{5,1},{6,14},{7,3},{8,0},{9,13},{1... | collective-permute-start | bytes 393224 | tf_op jit(solution)/shard_map/ppermute | solution.py:123
  15.4 0.0 copy-start.3
  15.4 2.4 %collective-permute-done.5 = f32[2,2,64,128]{3,2,1,0:T(8,128)S(1)} collective-permute-done((f32[2,2,64,128]{3,2,1,0:T(8,128)S(1)}, f32[2,2,64,128]{3,2,1,0:T(8,128)S(1)}, u32[]{:S(2)}, u32[]{:S(2)}) %collective-permute-start.5) | collective-permute-done | bytes 131104 | tf_op jit(solution)/shard_map/ppermute | solution.py:123
  17.9 0.0 collective-permute-done.6.far_ref
  17.9 0.1 collective-permute-start.7
  18.0 3.8 %collective-permute-done.1 = f32[2,2,64,128]{3,2,1,0:T(8,128)S(1)} collective-permute-done((f32[2,2,64,128]{3,2,1,0:T(8,128)S(1)}, f32[2,2,64,128]{3,2,1,0:T(8,128)S(1)}, u32[]{:S(2)}, u32[]{:S(2)}) %collective-permute-start.1) | collective-permute-done | bytes 131104 | tf_op jit(solution)/shard_map/ppermute | solution.py:123
  21.9 0.5 collective-permute-start.2
  22.3 0.1 collective-permute-start.8
  22.4 2.1 %collective-permute-done.7 = f32[4,2,64,128]{3,2,1,0:T(8,128)S(1)} collective-permute-done((f32[4,2,64,128]{3,2,1,0:T(8,128)S(1)}, f32[4,2,64,128]{3,2,1,0:T(8,128)S(1)}, u32[]{:S(2)}, u32[]{:S(2)}) %collective-permute-start.7) | collective-permute-done | bytes 262176 | tf_op jit(solution)/shard_map/ppermute | solution.py:123
  24.6 0.2 collective-permute-start.9
  24.8 3.5 %collective-permute-done.2 = f32[4,2,64,128]{3,2,1,0:T(8,128)S(1)} collective-permute-done((f32[4,2,64,128]{3,2,1,0:T(8,128)S(1)}, f32[4,2,64,128]{3,2,1,0:T(8,128)S(1)}, u32[]{:S(2)}, u32[]{:S(2)}) %collective-permute-start.2) | collective-permute-done | bytes 262176 | tf_op jit(solution)/shard_map/ppermute | solution.py:123
  28.3 0.1 collective-permute-start.3
  28.4 0.0 collective-permute-done.9.theirs_ref
  28.4 3.0 %setup.1 = (f32[12,8,32,128]{3,2,1,0:T(8,128)S(1)}, f32[4,9,32,128]{3,2,1,0:T(8,128)S(1)}, f32[8,8,32,128]{3,2,1,0:T(8,128)S(1)}, f32[8,8,32,128]{3,2,1,0:T(8,12...) custom-call(s32[2]{0:T(128)S(1)} %pad_add_fusion.place_ref, ...), custom_call_target="tpu_custom_call" | custom-call | tf_op jit(solution)/shard_map/setup/pallas_call | solution.py:605
  31.5 8.4 %solve.1 = (f32[2,64,128]{2,1,0:T(8,128)S(1)}, f32[2,32,128]{2,1,0:T(8,128)S(1)}, f32[2,96,128]{2,1,0:T(8,128)S(1)}, f32[1,2,2,32,128]{4,3,2,1,0:T(8,128)S(1)}) custom-call(s32[2]{0:T(128)S(1)} %pad_add_fusion.place_ref, f32[4]{0:T(128)S(1)} %copy-done.4, s32[2]{0:T(128)S(1)} %copy-done.2, f32[8,2,64,128]{3,2,1,0:T(8,128)S(1)} %constant_dynamic-update-slice_fusion.mine_ref, ...), custom_call_target="tpu_custom_call" | custom-call | tf_op jit(solution)/shard_map/solve/pallas_call | solution.py:615
  39.9 0.5 %collective-permute-start.10 = (f32[2,96,128]{2,1,0:T(8,128)S(1)}, f32[2,96,128]{2,1,0:T(8,128)S(1)}, u32[]{:S(2)}, u32[]{:S(2)}) collective-permute-start(f32[2,96,128]{2,1,0:T(8,128)S(1)} %get-tuple-element.43), channel_id=1, source_target_pairs={{0,1},{1,0},{2,3},{3,2},{4,5},{5,4},{6,7},{7,6},{8,9},{9,8},{10,11... | collective-permute-start | bytes 294920 | tf_op jit(solution)/shard_map/ppermute | solution.py:650
  40.4 1.5 %collective-permute-start.11 = (f32[2,32,128]{2,1,0:T(8,128)S(1)}, f32[2,32,128]{2,1,0:T(8,128)S(1)}, u32[]{:S(2)}, u32[]{:S(2)}) collective-permute-start(f32[2,32,128]{2,1,0:T(8,128)S(1)} %get-tuple-element.51), channel_id=1, source_target_pairs={{0,16},{1,17},{2,18},{3,19},{4,20},{5,21},{6,22},{7,23},{8,24},{9,... | collective-permute-start | bytes 98312 | tf_op jit(solution)/shard_map/ppermute | solution.py:659
  41.9 0.0 collective-permute-done.10
  42.0 0.7 %pad_maximum_fusion.5 = f32[2,2,64,128]{3,2,1,0:T(8,128)} fusion(f32[1,2,64,128]{3,2,1,0:T(8,128)S(1)} %get-tuple-element.49, f32[1,2,64,128]{3,2,1,0:T(8,128)S(1)} %get-tuple-element.48), kind=kLoop, calls=%fused_computation.5 | loop fusion | flops 32768 | bytes 262144 | tf_op jit(solution)/shard_map/stack | solution.py:662
  42.6 1.7 %collective-permute-done.11 = f32[2,32,128]{2,1,0:T(8,128)S(1)} collective-permute-done((f32[2,32,128]{2,1,0:T(8,128)S(1)}, f32[2,32,128]{2,1,0:T(8,128)S(1)}, u32[]{:S(2)}, u32[]{:S(2)}) %collective-permute-start.11) | collective-permute-done | bytes 32800 | tf_op jit(solution)/shard_map/ppermute | solution.py:659
  44.3 1.3 %collective-permute-done.12 = f32[2,32,128]{2,1,0:T(8,128)S(1)} collective-permute-done((f32[2,32,128]{2,1,0:T(8,128)S(1)}, f32[2,32,128]{2,1,0:T(8,128)S(1)}, u32[]{:S(2)}, u32[]{:S(2)}) %collective-permute-start.12) | collective-permute-done | bytes 32800 | tf_op jit(solution)/shard_map/ppermute | solution.py:659
  45.6 0.6 %add_add_fusion = f32[2,32,128]{2,1,0:T(8,128)} fusion(f32[2,32,128]{2,1,0:T(8,128)S(1)} %collective-permute-done.11, f32[2,32,128]{2,1,0:T(8,128)S(1)} %collective-permute-done.12, f32[2,32,128]{2,1,0:T(8,128)S(1)} %get-tuple-element.45, f32[2,96,128]{2,1,0:T(8,128)S(1)} %collective-permute-done.10), kind=kLoop, calls=%fused_computation.10 | loop fusion | flops 24576 | bytes 163840 | tf_op jit(solution)/shard_map/add | solution.py:666
  (25 shorter events, 0.2 us)
Async XLA Ops:
  0.6 10.3 %collective-permute-start.4 = (f32[1,2,64,128]{3,2,1,0:T(8,128)}, f32[1,2,64,128]{3,2,1,0:T(8,128)S(1)}, u32[]{:S(2)}, u32[]{:S(2)}) collective-permute-start(f32[1,2,64,128]{3,2,1,0:T(8,128)} %bitcast.14), channel_id=1, source_target_pairs={{0,8},{1,3},{2,10},{3,1},{4,12},{5,7},{6,14},{7,5},{8,0},{9,11},{1... | collective-permute-start | bytes 196616 | tf_op jit(solution)/shard_map/ppermute | solution.py:123
  4.8 0.9 %copy-start = (f32[2,2,64,128]{3,2,1,0:T(8,128)S(1)}, f32[2,2,64,128]{3,2,1,0:T(8,128)}, u32[]{:S(2)}) copy-start(f32[2,2,64,128]{3,2,1,0:T(8,128)} %state_ref.1) | copy-start | bytes 393220
  5.7 0.8 %copy-start.1 = (f32[2,64,128]{2,1,0:T(8,128)S(1)}, f32[2,64,128]{2,1,0:T(8,128)}, u32[]{:S(2)}) copy-start(f32[2,64,128]{2,1,0:T(8,128)} %kappa_ref.1) | copy-start | bytes 196612
  7.4 10.5 %collective-permute-start.6 = (f32[2,1,64,128]{3,2,1,0:T(8,128)S(1)}, f32[2,1,64,128]{3,2,1,0:T(8,128)S(1)}, u32[]{:S(2)}, u32[]{:S(2)}) collective-permute-start(f32[2,1,64,128]{3,2,1,0:T(8,128)S(1)} %get-tuple-element.28), channel_id=1, source_target_pairs={{1,2},{2,1},{3,4},{4,3},{5,6},{6,5},{7,8},{8,7},{9,10},{10,9},{11,... | collective-permute-start | bytes 196616 | tf_op jit(solution)/shard_map/ppermute | solution.py:111
  8.1 5.7 %collective-permute-start = (f32[1,2,64,128]{3,2,1,0:T(8,128)}, f32[1,2,64,128]{3,2,1,0:T(8,128)S(1)}, u32[]{:S(2)}, u32[]{:S(2)}) collective-permute-start(f32[1,2,64,128]{3,2,1,0:T(8,128)} %bitcast.2), channel_id=1, source_target_pairs={{0,2},{1,9},{2,0},{3,11},{4,6},{5,13},{6,4},{7,15},{8,10},{9,1},{1... | collective-permute-start | bytes 196616 | tf_op jit(solution)/shard_map/ppermute | solution.py:123
  11.0 6.9 %collective-permute-start.5 = (f32[2,2,64,128]{3,2,1,0:T(8,128)S(1)}, f32[2,2,64,128]{3,2,1,0:T(8,128)S(1)}, u32[]{:S(2)}, u32[]{:S(2)}) collective-permute-start(f32[2,2,64,128]{3,2,1,0:T(8,128)S(1)} %pad_maximum_fusion.4), channel_id=1, source_target_pairs={{0,4},{1,9},{2,6},{3,11},{4,0},{5,13},{6,2},{7,15},{8,12},{9,1},{1... | collective-permute-start | bytes 393224 | tf_op jit(solution)/shard_map/ppermute | solution.py:123
  13.8 8.1 %collective-permute-start.1 = (f32[2,2,64,128]{3,2,1,0:T(8,128)S(1)}, f32[2,2,64,128]{3,2,1,0:T(8,128)S(1)}, u32[]{:S(2)}, u32[]{:S(2)}) collective-permute-start(f32[2,2,64,128]{3,2,1,0:T(8,128)S(1)} %pad_maximum_fusion.3), channel_id=1, source_target_pairs={{0,8},{1,5},{2,10},{3,7},{4,12},{5,1},{6,14},{7,3},{8,0},{9,13},{1... | collective-permute-start | bytes 393224 | tf_op jit(solution)/shard_map/ppermute | solution.py:123
  15.4 13.0 %copy-start.2 = (s32[2]{0:T(128)S(1)}, s32[2]{0:T(128)}, u32[]{:S(2)}) copy-start(s32[2]{0:T(128)} %order_ref.3) | copy-start | bytes 28
  15.4 13.0 %copy-start.3 = (f32[4]{0:T(128)S(1)}, f32[4]{0:T(128)}, u32[]{:S(2)}) copy-start(f32[4]{0:T(128)} %shifts_ref.1) | copy-start | bytes 52
  17.9 6.7 %collective-permute-start.7 = (f32[4,2,64,128]{3,2,1,0:T(8,128)S(1)}, f32[4,2,64,128]{3,2,1,0:T(8,128)S(1)}, u32[]{:S(2)}, u32[]{:S(2)}) collective-permute-start(f32[4,2,64,128]{3,2,1,0:T(8,128)S(1)} %pad_maximum_fusion.2), channel_id=1, source_target_pairs={{0,2},{1,5},{2,0},{3,7},{4,6},{5,1},{6,4},{7,3},{8,10},{9,13},{10,... | collective-permute-start | bytes 786440 | tf_op jit(solution)/shard_map/ppermute | solution.py:123
  21.9 6.4 %collective-permute-start.2 = (f32[4,2,64,128]{3,2,1,0:T(8,128)S(1)}, f32[4,2,64,128]{3,2,1,0:T(8,128)S(1)}, u32[]{:S(2)}, u32[]{:S(2)}) collective-permute-start(f32[4,2,64,128]{3,2,1,0:T(8,128)S(1)} %pad_maximum_fusion.1), channel_id=1, source_target_pairs={{0,4},{1,3},{2,6},{3,1},{4,0},{5,7},{6,2},{7,5},{8,12},{9,11},{10,... | collective-permute-start | bytes 786440 | tf_op jit(solution)/shard_map/ppermute | solution.py:123
  22.3 9.2 %copy-start.4 = (f32[4]{0:T(128)S(1)}, f32[4]{0:T(128)}, u32[]{:S(2)}) copy-start(f32[4]{0:T(128)} %weights_ref.1) | copy-start | bytes 52
  22.3 2.3 %collective-permute-start.8 = (f32[3,64,128]{2,1,0:T(8,128)S(1)}, f32[3,64,128]{2,1,0:T(8,128)S(1)}, u32[]{:S(2)}, u32[]{:S(2)}) collective-permute-start(f32[3,64,128]{2,1,0:T(8,128)S(1)} %fusion), channel_id=1, source_target_pairs={{0,1},{1,0},{2,3},{3,2},{4,5},{5,4},{6,7},{7,6},{8,9},{9,8},{10,11... | collective-permute-start | bytes 294920 | tf_op jit(solution)/shard_map/ppermute | solution.py:119
  24.6 3.8 %collective-permute-start.9 = (f32[8,2,64,128]{3,2,1,0:T(8,128)S(1)}, f32[8,2,64,128]{3,2,1,0:T(8,128)S(1)}, u32[]{:S(2)}, u32[]{:S(2)}) collective-permute-start(f32[8,2,64,128]{3,2,1,0:T(8,128)S(1)} %pad_maximum_fusion.mine_ref), channel_id=1, source_target_pairs={{0,1},{1,0},{2,3},{3,2},{4,5},{5,4},{6,7},{7,6},{8,9},{9,8},{10,11... | collective-permute-start | bytes 1572872 | tf_op jit(solution)/shard_map/ppermute | solution.py:129
  28.3 3.2 %collective-permute-start.3 = (f32[8,2,64,128]{3,2,1,0:T(8,128)S(1)}, f32[8,2,64,128]{3,2,1,0:T(8,128)S(1)}, u32[]{:S(2)}, u32[]{:S(2)}) collective-permute-start(f32[8,2,64,128]{3,2,1,0:T(8,128)S(1)} %constant_dynamic-update-slice_fusion.mine_ref), channel_id=1, source_target_pairs={{0,1},{1,0},{2,3},{3,2},{4,5},{5,4},{6,7},{7,6},{8,9},{9,8},{10,11... | collective-permute-start | bytes 1572872 | tf_op jit(solution)/shard_map/ppermute | solution.py:129
  39.9 2.1 %collective-permute-start.10 = (f32[2,96,128]{2,1,0:T(8,128)S(1)}, f32[2,96,128]{2,1,0:T(8,128)S(1)}, u32[]{:S(2)}, u32[]{:S(2)}) collective-permute-start(f32[2,96,128]{2,1,0:T(8,128)S(1)} %get-tuple-element.43), channel_id=1, source_target_pairs={{0,1},{1,0},{2,3},{3,2},{4,5},{5,4},{6,7},{7,6},{8,9},{9,8},{10,11... | collective-permute-start | bytes 294920 | tf_op jit(solution)/shard_map/ppermute | solution.py:650
  40.4 3.9 %collective-permute-start.11 = (f32[2,32,128]{2,1,0:T(8,128)S(1)}, f32[2,32,128]{2,1,0:T(8,128)S(1)}, u32[]{:S(2)}, u32[]{:S(2)}) collective-permute-start(f32[2,32,128]{2,1,0:T(8,128)S(1)} %get-tuple-element.51), channel_id=1, source_target_pairs={{0,16},{1,17},{2,18},{3,19},{4,20},{5,21},{6,22},{7,23},{8,24},{9,... | collective-permute-start | bytes 98312 | tf_op jit(solution)/shard_map/ppermute | solution.py:659
  41.9 3.7 %collective-permute-start.12 = (f32[2,32,128]{2,1,0:T(8,128)S(1)}, f32[2,32,128]{2,1,0:T(8,128)S(1)}, u32[]{:S(2)}, u32[]{:S(2)}) collective-permute-start(f32[2,32,128]{2,1,0:T(8,128)S(1)} %get-tuple-element.50), channel_id=1, source_target_pairs={{0,17},{1,16},{2,19},{3,18},{4,21},{5,20},{6,23},{7,22},{8,25},{9,... | collective-permute-start | bytes 98312 | tf_op jit(solution)/shard_map/ppermute | solution.py:659

commit v10 on v9

--- a/solution.py
+++ b/solution.py
@@ -12,7 +12,7 @@
 REPLICATED_CELLS = 32 * 64 * 128
 HALF = 64
 TILE = 8
-UNROLL = 8
+UNROLL = 2
 
 
 def extended(array, sides, width):
@@ -57,13 +57,14 @@
 
 
 def swap_masks(peers, flip):
-    even = []
+    falling = []
     mask = peers // 2
     while mask > 1:
-        even.append(mask)
+        falling.append(mask)
         mask //= 2
-    odd = even[-1:] + even[:-1]
-    return (odd, even) if flip else (even, odd)
+    if flip:
+        return falling[::-1], falling[:1] + falling[:0:-1]
+    return falling, falling[-1:] + falling[:-1]
 
 
 def block_pair(u, holder, peers, flip):
@@ -82,33 +83,25 @@
     return first, second, home
 
 
-def prepare_kernel(place_ref, kappa_ref, misfit_ref, state_ref, half_ref, own_ref, held_ref, edge_ref):
-    half_ref[0] = 0.5 * kappa_ref[...]
-    own_ref[0] = misfit_ref[...]
-    held_ref[...] = state_ref[...]
-    even = place_ref[0] % 2 == 0
-    last = state_ref.shape[1] - 1
-    for slot in (0, 1):
-        edge_ref[slot, 0] = jnp.where(even, state_ref[slot, 0], state_ref[slot, last])
+def prepare_kernel(kappa_ref, misfit_ref, kappa_out, misfit_out):
+    kappa_out[0] = kappa_ref[...]
+    misfit_out[0] = misfit_ref[...]
 
 
 def gather_blocks(place, kappa, misfit, states, axis):
     peers = lax.axis_size(axis)
     even = place[0] % 2 == 0
     swap = [(i, i ^ 1) for i in range(peers)]
-    smem = pl.BlockSpec(memory_space=pltpu.SMEM)
     vmem = pl.BlockSpec(memory_space=pltpu.VMEM)
-    shapes = [(1, *kappa.shape), (1, *misfit.shape), states.shape, (2, 1, *states.shape[2:])]
-    half, own, states, edge = pl.pallas_call(
+    own = pl.pallas_call(
         prepare_kernel,
-        out_shape=[jax.ShapeDtypeStruct(shape, jnp.float32) for shape in shapes],
-        in_specs=[smem] + [vmem] * 3,
-        out_specs=[vmem] * 4,
-        compiler_params=pltpu.CompilerParams(vmem_limit_bytes=2 * 1024 * 1024),
+        out_shape=[jax.ShapeDtypeStruct((1, *kappa.shape), jnp.float32)] * 2,
+        in_specs=[vmem] * 2,
+        out_specs=[vmem] * 2,
+        compiler_params=pltpu.CompilerParams(vmem_limit_bytes=1024 * 1024),
         name="prepare",
-    )(place, kappa, misfit, states)
+    )(kappa, misfit)
     over = [(i, i + 1 if i % 2 else i - 1) for i in range(1, peers - 1)]
-    far = lax.ppermute(edge, axis, over)
     swaps = [list(zip(*swap_masks(peers, flip))) for flip in (False, True)]
     steps = len(swaps[0])
     held = [kappa[None], misfit[None]]
@@ -121,10 +114,12 @@
             masks = swaps[at][step]
             pairs = [(i, i ^ masks[i % 2]) for i in range(peers)]
             arrived = lax.ppermute(held[at], axis, pairs)
-            if step == 0:
-                held[at] = (half, own)[at]
-                arrived = (0.5, 1.0)[at] * arrived
-            held[at] = jnp.concatenate([held[at], arrived], axis=0)
+            mine = held[at] if step else own[at]
+            held[at] = jnp.concatenate([mine, arrived], axis=0)
+        if step == 0:
+            held[1], states = lax.optimization_barrier((held[1], states))
+            edge = jnp.where(even, states[:, :1], states[:, -1:])
+            far = lax.ppermute(edge, axis, over)
     held[0], near = lax.optimization_barrier((held[0], near))
     other = [lax.ppermute(part, axis, swap) for part in held]
     return held, other, states, far, near
@@ -234,7 +229,7 @@
     shift = shifts_ref[order_ref[place_ref[0] % 2]]
 
     def keep(k, spot, j, value):
-        half_kappa[k, spot + 1, tile(j)] = value
+        half_kappa[k, spot + 1, tile(j)] = 0.5 * value
 
     at_.arrange(mine_ref, theirs_ref, place_ref[0], False, keep)
     at_.seam_fine(half_kappa)
@@ -362,8 +357,18 @@
     at_.arrange(mine_ref, theirs_ref, place_ref[0], True, begin)
     at_.seam_fine(scaled)
 
-    def stencil(field, i, j, both):
-        here = [field[k, i + 1, tile(j)] for k in range(8)]
+    def rows_of(field, i):
+        cache = {}
+
+        def load(k, j):
+            if (k, j) not in cache:
+                cache[k, j] = field[k, i + 1, tile(j)]
+            return cache[k, j]
+
+        return load
+
+    def stencil(field, load, i, j, both):
+        here = [load(k, j) for k in range(8)]
         terms = [[] for _ in range(8)]
         for p, q in PAIRS:
             at = 2 * p + q
@@ -378,10 +383,10 @@
                 side = field[low, i + 2, tile(j)]
                 terms[high].append(outer_x[at, i + 1, tile(j)] * side)
             low, high = cls(p, 0, q), cls(p, 1, q)
-            side = at_.row_before(lambda r: field[high, i + 1, tile(r)], j)
+            side = at_.row_before(lambda r: load(high, r), j)
             terms[low].append(outer_y[at, i, tile(j)] * side)
             if both:
-                side = at_.row_after(lambda r: field[low, i + 1, tile(r)], j)
+                side = at_.row_after(lambda r: load(low, r), j)
                 terms[high].append(outer_y[4 + at, i, tile(j)] * side)
             low, high = cls(p, q, 0), cls(p, q, 1)
             terms[low].append(outer_z[at, i, tile(j)] * roll(here[high], 1, 1))
@@ -402,9 +407,10 @@
 
     def precondition(result, other):
         def down(i, carry):
+            load = rows_of(scaled, i)
             for j in range(tiles):
                 res = [residual[k, i, tile(j)] for k in range(8)]
-                _, sums = stencil(scaled, i, j, True)
+                _, sums = stencil(scaled, load, i, j, True)
                 parts = [(2.0 - DAMPING) * res[k] + sums[k] for k in range(8)]
                 for k in range(8):
                     partial[k, i, tile(j)] = parts[k]
@@ -466,8 +472,9 @@
     gamma, _ = precondition(first_dir, None)
 
     def apply(i, acc):
+        load = rows_of(first_dir, i)
         for j in range(tiles):
-            here, sums = stencil(first_dir, i, j, True)
+            here, sums = stencil(first_dir, load, i, j, True)
             dots = []
             for k in range(8):
                 value = diagonal[k, i, tile(j)] * here[k] - sums[k]
@@ -494,8 +501,9 @@
 
     def bend(i, carry):
         own_part, face_part = carry
+        load = rows_of(second_dir, i)
         for j in range(tiles):
-            here, sums = stencil(second_dir, i, j, False)
+            here, sums = stencil(second_dir, load, i, j, False)
             own_part = own_part + tree_sum(
                 [here[k] * (diagonal[k, i, tile(j)] * here[k]) for k in range(8)]
             )

time: 46.5 us -> 48.6 us (1.045)
  the two profiles are of different devices: /device:TPU:0 before, /device:TPU:27 now
where the time goes in v10:
time: 48.6 us; the launch traced here: 48.3 us
  starting transfers between devices  18.4 us (38%)
  Pallas kernels  12.3 us (25%)
  waiting for transfers between devices  11.7 us (24%)
  local copies, waits for them, and re-layouts  2.67 us (5%)
  other arithmetic  2.37 us (5%)
  between operations  0.84 us (2%)
    pallas_call x1, Pallas kernels, whole_grid(): pl.pallas_call(solve_kernel, out_shape=[jax.ShapeDtypeStruct((own, ny, nz...  9.35 us
    ppermute x6, waiting for transfers between devices, gather_blocks(): arrived = lax.ppermute(held[at], axis, pairs)  9.21 us
    ppermute x6, starting transfers between devices, gather_blocks(): arrived = lax.ppermute(held[at], axis, pairs)  8.47 us
    ppermute x2, starting transfers between devices, gather_blocks(): other = [lax.ppermute(part, axis, swap) for part in held]  5.14 us
    pallas_call x1, Pallas kernels, whole_grid(): pl.pallas_call(setup_kernel, out_shape=[jax.ShapeDtypeStruct(shape, jnp.f...  2.95 us
    unnamed x14, local copies, waits for them, and re-layouts  2.64 us
    ppermute x2, waiting for transfers between devices, whole_grid(): shares.append(lax.ppermute(send[k - 1, side], ('pole', 'space'), pairs))  2.47 us
    ppermute x2, starting transfers between devices, whole_grid(): shares.append(lax.ppermute(send[k - 1, side], ('pole', 'space'), pairs))  2.12 us
  transfers between devices with their start and end apart: 13, of which 5 were waited for; matrix products, arithmetic and copies ran while one was open for 6% of the time, Pallas kernels for 6%

profile of v10, /device:TPU:27, one launch (start us, length us, event | category | flops | bytes accessed | tf_op | source)
XLA Modules:
  0.0 48.3 jit_solution(8597718213938613037)
XLA Ops:
  0.6 0.1 collective-permute-start
  0.8 0.3 collective-permute-start.4
  1.0 0.8 %copy-done.1 = f32[2,64,128]{2,1,0:T(8,128)S(1)} copy-done((f32[2,64,128]{2,1,0:T(8,128)S(1)}, f32[2,64,128]{2,1,0:T(8,128)}, u32[]{:S(2)}) %copy-start.1) | copy-done | bytes 65560
  1.9 0.8 %copy-done.2 = f32[2,64,128]{2,1,0:T(8,128)S(1)} copy-done((f32[2,64,128]{2,1,0:T(8,128)S(1)}, f32[2,64,128]{2,1,0:T(8,128)}, u32[]{:S(2)}) %copy-start.2) | copy-done | bytes 65560
  2.7 2.8 %collective-permute-done = f32[1,2,64,128]{3,2,1,0:T(8,128)S(1)} collective-permute-done((f32[1,2,64,128]{3,2,1,0:T(8,128)}, f32[1,2,64,128]{3,2,1,0:T(8,128)S(1)}, u32[]{:S(2)}, u32[]{:S(2)}) %collective-permute-start) | collective-permute-done | bytes 65568 | tf_op jit(solution)/shard_map/ppermute | solution.py:116
  5.5 0.0 collective-permute-done.4
  5.6 1.2 %collective-permute-start.5 = (f32[2,2,64,128]{3,2,1,0:T(8,128)S(1)}, f32[2,2,64,128]{3,2,1,0:T(8,128)S(1)}, u32[]{:S(2)}, u32[]{:S(2)}) collective-permute-start(f32[2,2,64,128]{3,2,1,0:T(8,128)S(1)} %pad_maximum_fusion.4), channel_id=1, source_target_pairs={{0,4},{1,9},{2,6},{3,11},{4,0},{5,13},{6,2},{7,15},{8,12},{9,1},{1... | collective-permute-start | bytes 393224 | tf_op jit(solution)/shard_map/ppermute | solution.py:116
  6.8 0.9 %slice_select_fusion.1 = f32[2,1,64,128]{3,2,1,0:T(8,128)S(1)} fusion(f32[2,2,64,128]{3,2,1,0:T(8,128)} %state_ref, pred[]{:T(512)S(6)} %eq.7), kind=kLoop, calls=%fused_computation.10 | loop fusion | flops 16384 | bytes 196609 | tf_op jit(solution)/shard_map/jit(_where)/select_n | solution.py:121
  7.6 0.9 %constant_dynamic-update-slice_fusion.2 = (f32[8,2,64,128]{3,2,1,0:T(8,128)S(1)}, f32[2,3,64,128]{3,2,1,0:T(8,128)S(1)}) fusion(f32[2,2,64,128]{3,2,1,0:T(8,128)S(1)} %pad_maximum_fusion.3, f32[2,2,64,128]{3,2,1,0:T(8,128)} %state_ref), kind=kLoop, calls=%fused_computation.16 | loop fusion | bytes 524288
  8.6 0.0 copy-start.3
  8.6 0.0 copy-start.4
  8.6 0.7 %collective-permute-start.6 = (f32[2,1,64,128]{3,2,1,0:T(8,128)S(1)}, f32[2,1,64,128]{3,2,1,0:T(8,128)S(1)}, u32[]{:S(2)}, u32[]{:S(2)}) collective-permute-start(f32[2,1,64,128]{3,2,1,0:T(8,128)S(1)} %slice_select_fusion.1), channel_id=1, source_target_pairs={{1,2},{2,1},{3,4},{4,3},{5,6},{6,5},{7,8},{8,7},{9,10},{10,9},{11,... | collective-permute-start | bytes 196616 | tf_op jit(solution)/shard_map/ppermute | solution.py:122
  9.3 1.8 %collective-permute-done.5 = f32[2,2,64,128]{3,2,1,0:T(8,128)S(1)} collective-permute-done((f32[2,2,64,128]{3,2,1,0:T(8,128)S(1)}, f32[2,2,64,128]{3,2,1,0:T(8,128)S(1)}, u32[]{:S(2)}, u32[]{:S(2)}) %collective-permute-start.5) | collective-permute-done | bytes 131104 | tf_op jit(solution)/shard_map/ppermute | solution.py:116
  11.2 6.8 %collective-permute-start.7 = (f32[4,2,64,128]{3,2,1,0:T(8,128)S(1)}, f32[4,2,64,128]{3,2,1,0:T(8,128)S(1)}, u32[]{:S(2)}, u32[]{:S(2)}) collective-permute-start(f32[4,2,64,128]{3,2,1,0:T(8,128)S(1)} %pad_maximum_fusion.2), channel_id=1, source_target_pairs={{0,2},{1,5},{2,0},{3,7},{4,6},{5,1},{6,4},{7,3},{8,10},{9,13},{10,... | collective-permute-start | bytes 786440 | tf_op jit(solution)/shard_map/ppermute | solution.py:116
  18.0 0.1 collective-permute-start.2
  18.1 0.0 copy-start
  18.1 0.0 copy-start.5
  18.1 1.9 %collective-permute-start.8 = (f32[3,64,128]{2,1,0:T(8,128)S(1)}, f32[3,64,128]{2,1,0:T(8,128)S(1)}, u32[]{:S(2)}, u32[]{:S(2)}) collective-permute-start(f32[3,64,128]{2,1,0:T(8,128)S(1)} %fusion), channel_id=1, source_target_pairs={{0,1},{1,0},{2,3},{3,2},{4,5},{5,4},{6,7},{7,6},{8,9},{9,8},{10,11... | collective-permute-start | bytes 294920 | tf_op jit(solution)/shard_map/ppermute | solution.py:112
  20.0 2.0 %collective-permute-done.7 = f32[4,2,64,128]{3,2,1,0:T(8,128)S(1)} collective-permute-done((f32[4,2,64,128]{3,2,1,0:T(8,128)S(1)}, f32[4,2,64,128]{3,2,1,0:T(8,128)S(1)}, u32[]{:S(2)}, u32[]{:S(2)}) %collective-permute-start.7) | collective-permute-done | bytes 262176 | tf_op jit(solution)/shard_map/ppermute | solution.py:116
  22.1 2.2 %collective-permute-start.9 = (f32[8,2,64,128]{3,2,1,0:T(8,128)S(1)}, f32[8,2,64,128]{3,2,1,0:T(8,128)S(1)}, u32[]{:S(2)}, u32[]{:S(2)}) collective-permute-start(f32[8,2,64,128]{3,2,1,0:T(8,128)S(1)} %pad_maximum_fusion.mine_ref), channel_id=1, source_target_pairs={{0,1},{1,0},{2,3},{3,2},{4,5},{5,4},{6,7},{7,6},{8,9},{9,8},{10,11... | collective-permute-start | bytes 1572872 | tf_op jit(solution)/shard_map/ppermute | solution.py:124
  24.3 2.6 %collective-permute-done.2 = f32[4,2,64,128]{3,2,1,0:T(8,128)S(1)} collective-permute-done((f32[4,2,64,128]{3,2,1,0:T(8,128)S(1)}, f32[4,2,64,128]{3,2,1,0:T(8,128)S(1)}, u32[]{:S(2)}, u32[]{:S(2)}) %collective-permute-start.2) | collective-permute-done | bytes 262176 | tf_op jit(solution)/shard_map/ppermute | solution.py:116
  26.9 2.9 %collective-permute-start.3 = (f32[8,2,64,128]{3,2,1,0:T(8,128)S(1)}, f32[8,2,64,128]{3,2,1,0:T(8,128)S(1)}, u32[]{:S(2)}, u32[]{:S(2)}) collective-permute-start(f32[8,2,64,128]{3,2,1,0:T(8,128)S(1)} %constant_dynamic-update-slice_fusion.mine_ref), channel_id=1, source_target_pairs={{0,1},{1,0},{2,3},{3,2},{4,5},{5,4},{6,7},{7,6},{8,9},{9,8},{10,11... | collective-permute-start | bytes 1572872 | tf_op jit(solution)/shard_map/ppermute | solution.py:124
  29.8 0.1 pad_add_fusion.place_ref
  29.9 3.0 %setup.1 = (f32[12,8,32,128]{3,2,1,0:T(8,128)S(1)}, f32[4,9,32,128]{3,2,1,0:T(8,128)S(1)}, f32[8,8,32,128]{3,2,1,0:T(8,128)S(1)}, f32[8,8,32,128]{3,2,1,0:T(8,12...) custom-call(s32[2]{0:T(128)S(1)} %pad_add_fusion.place_ref, ...), custom_call_target="tpu_custom_call" | custom-call | tf_op jit(solution)/shard_map/setup/pallas_call | solution.py:613
  32.9 9.4 %solve.1 = (f32[2,64,128]{2,1,0:T(8,128)S(1)}, f32[2,32,128]{2,1,0:T(8,128)S(1)}, f32[2,96,128]{2,1,0:T(8,128)S(1)}, f32[1,2,2,32,128]{4,3,2,1,0:T(8,128)S(1)}) custom-call(s32[2]{0:T(128)S(1)} %pad_add_fusion.place_ref, f32[4]{0:T(128)S(1)} %copy-done.5, s32[2]{0:T(128)S(1)} %copy-done.3, f32[8,2,64,128]{3,2,1,0:T(8,128)S(1)} %constant_dynamic-update-slice_fusion.mine_ref, ...), custom_call_target="tpu_custom_call" | custom-call | tf_op jit(solution)/shard_map/solve/pallas_call | solution.py:623
  42.3 0.1 collective-permute-start.10
  42.4 1.3 %collective-permute-start.11 = (f32[2,32,128]{2,1,0:T(8,128)S(1)}, f32[2,32,128]{2,1,0:T(8,128)S(1)}, u32[]{:S(2)}, u32[]{:S(2)}) collective-permute-start(f32[2,32,128]{2,1,0:T(8,128)S(1)} %get-tuple-element.51), channel_id=1, source_target_pairs={{0,16},{1,17},{2,18},{3,19},{4,20},{5,21},{6,22},{7,23},{8,24},{9,... | collective-permute-start | bytes 98312 | tf_op jit(solution)/shard_map/ppermute | solution.py:667
  43.7 0.8 %collective-permute-start.12 = (f32[2,32,128]{2,1,0:T(8,128)S(1)}, f32[2,32,128]{2,1,0:T(8,128)S(1)}, u32[]{:S(2)}, u32[]{:S(2)}) collective-permute-start(f32[2,32,128]{2,1,0:T(8,128)S(1)} %get-tuple-element.50), channel_id=1, source_target_pairs={{0,17},{1,16},{2,19},{3,18},{4,21},{5,20},{6,23},{7,22},{8,25},{9,... | collective-permute-start | bytes 98312 | tf_op jit(solution)/shard_map/ppermute | solution.py:667
  44.5 0.7 %pad_maximum_fusion.5 = f32[2,2,64,128]{3,2,1,0:T(8,128)} fusion(f32[1,2,64,128]{3,2,1,0:T(8,128)S(1)} %get-tuple-element.49, f32[1,2,64,128]{3,2,1,0:T(8,128)S(1)} %get-tuple-element.48), kind=kLoop, calls=%fused_computation.5 | loop fusion | flops 32768 | bytes 262144 | tf_op jit(solution)/shard_map/stack | solution.py:670
  45.2 0.0 collective-permute-done.11
  45.2 2.4 %collective-permute-done.12 = f32[2,32,128]{2,1,0:T(8,128)S(1)} collective-permute-done((f32[2,32,128]{2,1,0:T(8,128)S(1)}, f32[2,32,128]{2,1,0:T(8,128)S(1)}, u32[]{:S(2)}, u32[]{:S(2)}) %collective-permute-start.12) | collective-permute-done | bytes 32800 | tf_op jit(solution)/shard_map/ppermute | solution.py:667
  47.6 0.6 %add_add_fusion = f32[2,32,128]{2,1,0:T(8,128)} fusion(f32[2,32,128]{2,1,0:T(8,128)S(1)} %collective-permute-done.11, f32[2,32,128]{2,1,0:T(8,128)S(1)} %collective-permute-done.12, f32[2,32,128]{2,1,0:T(8,128)S(1)} %get-tuple-element.45, f32[2,96,128]{2,1,0:T(8,128)S(1)} %collective-permute-done.10), kind=kLoop, calls=%fused_computation.11 | loop fusion | flops 24576 | bytes 163840 | tf_op jit(solution)/shard_map/add | solution.py:674
  (25 shorter events, 0.2 us)
Async XLA Ops:
  0.6 4.9 %collective-permute-start = (f32[1,2,64,128]{3,2,1,0:T(8,128)}, f32[1,2,64,128]{3,2,1,0:T(8,128)S(1)}, u32[]{:S(2)}, u32[]{:S(2)}) collective-permute-start(f32[1,2,64,128]{3,2,1,0:T(8,128)} %bitcast.14), channel_id=1, source_target_pairs={{0,2},{1,9},{2,0},{3,11},{4,6},{5,13},{6,4},{7,15},{8,10},{9,1},{1... | collective-permute-start | bytes 196616 | tf_op jit(solution)/shard_map/ppermute | solution.py:116
  0.8 4.8 %collective-permute-start.4 = (f32[1,2,64,128]{3,2,1,0:T(8,128)}, f32[1,2,64,128]{3,2,1,0:T(8,128)S(1)}, u32[]{:S(2)}, u32[]{:S(2)}) collective-permute-start(f32[1,2,64,128]{3,2,1,0:T(8,128)} %bitcast.15), channel_id=1, source_target_pairs={{0,8},{1,3},{2,10},{3,1},{4,12},{5,7},{6,14},{7,5},{8,0},{9,11},{1... | collective-permute-start | bytes 196616 | tf_op jit(solution)/shard_map/ppermute | solution.py:116
  1.0 0.8 %copy-start.1 = (f32[2,64,128]{2,1,0:T(8,128)S(1)}, f32[2,64,128]{2,1,0:T(8,128)}, u32[]{:S(2)}) copy-start(f32[2,64,128]{2,1,0:T(8,128)} %misfit_ref.1) | copy-start | bytes 196612
  1.9 0.8 %copy-start.2 = (f32[2,64,128]{2,1,0:T(8,128)S(1)}, f32[2,64,128]{2,1,0:T(8,128)}, u32[]{:S(2)}) copy-start(f32[2,64,128]{2,1,0:T(8,128)} %kappa_ref.1) | copy-start | bytes 196612
  5.6 5.6 %collective-permute-start.5 = (f32[2,2,64,128]{3,2,1,0:T(8,128)S(1)}, f32[2,2,64,128]{3,2,1,0:T(8,128)S(1)}, u32[]{:S(2)}, u32[]{:S(2)}) collective-permute-start(f32[2,2,64,128]{3,2,1,0:T(8,128)S(1)} %pad_maximum_fusion.4), channel_id=1, source_target_pairs={{0,4},{1,9},{2,6},{3,11},{4,0},{5,13},{6,2},{7,15},{8,12},{9,1},{1... | collective-permute-start | bytes 393224 | tf_op jit(solution)/shard_map/ppermute | solution.py:116
  6.8 11.2 %collective-permute-start.1 = (f32[2,2,64,128]{3,2,1,0:T(8,128)S(1)}, f32[2,2,64,128]{3,2,1,0:T(8,128)S(1)}, u32[]{:S(2)}, u32[]{:S(2)}) collective-permute-start(f32[2,2,64,128]{3,2,1,0:T(8,128)S(1)} %pad_maximum_fusion.3), channel_id=1, source_target_pairs={{0,4},{1,3},{2,6},{3,1},{4,0},{5,7},{6,2},{7,5},{8,12},{9,11},{10,... | collective-permute-start | bytes 393224 | tf_op jit(solution)/shard_map/ppermute | solution.py:116
  8.6 21.3 %copy-start.3 = (s32[2]{0:T(128)S(1)}, s32[2]{0:T(128)}, u32[]{:S(2)}) copy-start(s32[2]{0:T(128)} %order_ref.3) | copy-start | bytes 28
  8.6 21.3 %copy-start.4 = (f32[4]{0:T(128)S(1)}, f32[4]{0:T(128)}, u32[]{:S(2)}) copy-start(f32[4]{0:T(128)} %shifts_ref.1) | copy-start | bytes 52
  8.6 2.5 %collective-permute-start.6 = (f32[2,1,64,128]{3,2,1,0:T(8,128)S(1)}, f32[2,1,64,128]{3,2,1,0:T(8,128)S(1)}, u32[]{:S(2)}, u32[]{:S(2)}) collective-permute-start(f32[2,1,64,128]{3,2,1,0:T(8,128)S(1)} %slice_select_fusion.1), channel_id=1, source_target_pairs={{1,2},{2,1},{3,4},{4,3},{5,6},{6,5},{7,8},{8,7},{9,10},{10,9},{11,... | collective-permute-start | bytes 196616 | tf_op jit(solution)/shard_map/ppermute | solution.py:122
  11.2 10.8 %collective-permute-start.7 = (f32[4,2,64,128]{3,2,1,0:T(8,128)S(1)}, f32[4,2,64,128]{3,2,1,0:T(8,128)S(1)}, u32[]{:S(2)}, u32[]{:S(2)}) collective-permute-start(f32[4,2,64,128]{3,2,1,0:T(8,128)S(1)} %pad_maximum_fusion.2), channel_id=1, source_target_pairs={{0,2},{1,5},{2,0},{3,7},{4,6},{5,1},{6,4},{7,3},{8,10},{9,13},{10,... | collective-permute-start | bytes 786440 | tf_op jit(solution)/shard_map/ppermute | solution.py:116
  18.0 8.9 %collective-permute-start.2 = (f32[4,2,64,128]{3,2,1,0:T(8,128)S(1)}, f32[4,2,64,128]{3,2,1,0:T(8,128)S(1)}, u32[]{:S(2)}, u32[]{:S(2)}) collective-permute-start(f32[4,2,64,128]{3,2,1,0:T(8,128)S(1)} %pad_maximum_fusion.1), channel_id=1, source_target_pairs={{0,8},{1,5},{2,10},{3,7},{4,12},{5,1},{6,14},{7,3},{8,0},{9,13},{1... | collective-permute-start | bytes 786440 | tf_op jit(solution)/shard_map/ppermute | solution.py:116
  18.1 14.8 %copy-start = (f32[2,2,64,128]{3,2,1,0:T(8,128)S(1)}, f32[2,2,64,128]{3,2,1,0:T(8,128)}, u32[]{:S(2)}) copy-start(f32[2,2,64,128]{3,2,1,0:T(8,128)} %state_ref) | copy-start | bytes 393220
  18.1 14.8 %copy-start.5 = (f32[4]{0:T(128)S(1)}, f32[4]{0:T(128)}, u32[]{:S(2)}) copy-start(f32[4]{0:T(128)} %weights_ref.1) | copy-start | bytes 52
  18.1 3.9 %collective-permute-start.8 = (f32[3,64,128]{2,1,0:T(8,128)S(1)}, f32[3,64,128]{2,1,0:T(8,128)S(1)}, u32[]{:S(2)}, u32[]{:S(2)}) collective-permute-start(f32[3,64,128]{2,1,0:T(8,128)S(1)} %fusion), channel_id=1, source_target_pairs={{0,1},{1,0},{2,3},{3,2},{4,5},{5,4},{6,7},{7,6},{8,9},{9,8},{10,11... | collective-permute-start | bytes 294920 | tf_op jit(solution)/shard_map/ppermute | solution.py:112
  22.1 7.9 %collective-permute-start.9 = (f32[8,2,64,128]{3,2,1,0:T(8,128)S(1)}, f32[8,2,64,128]{3,2,1,0:T(8,128)S(1)}, u32[]{:S(2)}, u32[]{:S(2)}) collective-permute-start(f32[8,2,64,128]{3,2,1,0:T(8,128)S(1)} %pad_maximum_fusion.mine_ref), channel_id=1, source_target_pairs={{0,1},{1,0},{2,3},{3,2},{4,5},{5,4},{6,7},{7,6},{8,9},{9,8},{10,11... | collective-permute-start | bytes 1572872 | tf_op jit(solution)/shard_map/ppermute | solution.py:124
  26.9 6.0 %collective-permute-start.3 = (f32[8,2,64,128]{3,2,1,0:T(8,128)S(1)}, f32[8,2,64,128]{3,2,1,0:T(8,128)S(1)}, u32[]{:S(2)}, u32[]{:S(2)}) collective-permute-start(f32[8,2,64,128]{3,2,1,0:T(8,128)S(1)} %constant_dynamic-update-slice_fusion.mine_ref), channel_id=1, source_target_pairs={{0,1},{1,0},{2,3},{3,2},{4,5},{5,4},{6,7},{7,6},{8,9},{9,8},{10,11... | collective-permute-start | bytes 1572872 | tf_op jit(solution)/shard_map/ppermute | solution.py:124
  42.3 2.2 %collective-permute-start.10 = (f32[2,96,128]{2,1,0:T(8,128)S(1)}, f32[2,96,128]{2,1,0:T(8,128)S(1)}, u32[]{:S(2)}, u32[]{:S(2)}) collective-permute-start(f32[2,96,128]{2,1,0:T(8,128)S(1)} %get-tuple-element.43), channel_id=1, source_target_pairs={{0,1},{1,0},{2,3},{3,2},{4,5},{5,4},{6,7},{7,6},{8,9},{9,8},{10,11... | collective-permute-start | bytes 294920 | tf_op jit(solution)/shard_map/ppermute | solution.py:658
  42.4 2.8 %collective-permute-start.11 = (f32[2,32,128]{2,1,0:T(8,128)S(1)}, f32[2,32,128]{2,1,0:T(8,128)S(1)}, u32[]{:S(2)}, u32[]{:S(2)}) collective-permute-start(f32[2,32,128]{2,1,0:T(8,128)S(1)} %get-tuple-element.51), channel_id=1, source_target_pairs={{0,16},{1,17},{2,18},{3,19},{4,20},{5,21},{6,22},{7,23},{8,24},{9,... | collective-permute-start | bytes 98312 | tf_op jit(solution)/shard_map/ppermute | solution.py:667
  43.7 4.0 %collective-permute-start.12 = (f32[2,32,128]{2,1,0:T(8,128)S(1)}, f32[2,32,128]{2,1,0:T(8,128)S(1)}, u32[]{:S(2)}, u32[]{:S(2)}) collective-permute-start(f32[2,32,128]{2,1,0:T(8,128)S(1)} %get-tuple-element.50), channel_id=1, source_target_pairs={{0,17},{1,16},{2,19},{3,18},{4,21},{5,20},{6,23},{7,22},{8,25},{9,... | collective-permute-start | bytes 98312 | tf_op jit(solution)/shard_map/ppermute | solution.py:667

commit v11 on v10

--- a/solution.py
+++ b/solution.py
@@ -84,45 +84,62 @@
 
 
 def prepare_kernel(kappa_ref, misfit_ref, kappa_out, misfit_out):
-    kappa_out[0] = kappa_ref[...]
-    misfit_out[0] = misfit_ref[...]
-
-
-def gather_blocks(place, kappa, misfit, states, axis):
+    kappa_out[...] = kappa_ref[...]
+    misfit_out[...] = misfit_ref[...]
+
+
+def join_kernel(place_ref, *refs, masks, peers):
+    place = place_ref[0]
+    at_ = Layout(refs[0].shape[1] // 2)
+    for at, (even, odd) in enumerate(masks):
+        partner = place ^ jnp.where(place % 2 == 0, even, odd)
+        for t, (ref, holder) in enumerate(((refs[at], place), (refs[2 + at], partner))):
+            at_.deal(ref, refs[4 + at].at[t], jnp.where(holder >= peers // 2, 1, 0))
+
+
+def gather_blocks(place, blocks, states, axis):
     peers = lax.axis_size(axis)
     even = place[0] % 2 == 0
     swap = [(i, i ^ 1) for i in range(peers)]
+    over = [(i, i + 1 if i % 2 else i - 1) for i in range(1, peers - 1)]
+    smem = pl.BlockSpec(memory_space=pltpu.SMEM)
     vmem = pl.BlockSpec(memory_space=pltpu.VMEM)
+    swaps = [list(zip(*swap_masks(peers, flip))) for flip in (False, True)]
     own = pl.pallas_call(
         prepare_kernel,
-        out_shape=[jax.ShapeDtypeStruct((1, *kappa.shape), jnp.float32)] * 2,
+        out_shape=[jax.ShapeDtypeStruct(block.shape, jnp.float32) for block in blocks],
         in_specs=[vmem] * 2,
         out_specs=[vmem] * 2,
         compiler_params=pltpu.CompilerParams(vmem_limit_bytes=1024 * 1024),
         name="prepare",
-    )(kappa, misfit)
-    over = [(i, i + 1 if i % 2 else i - 1) for i in range(1, peers - 1)]
-    swaps = [list(zip(*swap_masks(peers, flip))) for flip in (False, True)]
-    steps = len(swaps[0])
-    held = [kappa[None], misfit[None]]
-    for step in range(steps):
-        if step == steps - 1:
-            held[0], far = lax.optimization_barrier((held[0], far))
-            given = jnp.concatenate([states, far], axis=1)
-            near = lax.ppermute(jnp.where(even, given[1], given[0]), axis, swap)
+    )(*blocks)
+    held = list(blocks)
+    for step in range(len(swaps[0])):
+        arrived = []
         for at in (0, 1):
             masks = swaps[at][step]
             pairs = [(i, i ^ masks[i % 2]) for i in range(peers)]
-            arrived = lax.ppermute(held[at], axis, pairs)
-            mine = held[at] if step else own[at]
-            held[at] = jnp.concatenate([mine, arrived], axis=0)
-        if step == 0:
-            held[1], states = lax.optimization_barrier((held[1], states))
-            edge = jnp.where(even, states[:, :1], states[:, -1:])
-            far = lax.ppermute(edge, axis, over)
-    held[0], near = lax.optimization_barrier((held[0], near))
+            arrived.append(lax.ppermute(held[at], axis, pairs))
+        if step:
+            held = [jnp.concatenate(pair, axis=0) for pair in zip(held, arrived)]
+            continue
+        masks = [swaps[at][0] for at in (0, 1)]
+        shape = jax.ShapeDtypeStruct((2, *blocks[0].shape), jnp.float32)
+        held[:] = pl.pallas_call(
+            functools.partial(join_kernel, masks=masks, peers=peers),
+            out_shape=[shape] * 2,
+            in_specs=[smem] + [vmem] * 4,
+            out_specs=[vmem] * 2,
+            compiler_params=pltpu.CompilerParams(vmem_limit_bytes=1024 * 1024),
+            name="join",
+        )(place, *own, *arrived)
+        held[1], states = lax.optimization_barrier((held[1], states))
+        far = lax.ppermute(jnp.where(even, states[:, :1], states[:, -1:]), axis, over)
+    held[1], far = lax.optimization_barrier((held[1], far))
+    given = jnp.concatenate([states, far], axis=1)
+    near = lax.ppermute(jnp.where(even, given[1], given[0]), axis, swap)
     other = [lax.ppermute(part, axis, swap) for part in held]
-    return held, other, states, far, near
+    return held, other, far, near
 
 
 CLASSES = [(a, b, c) for a in (0, 1) for b in (0, 1) for c in (0, 1)]
@@ -179,11 +196,20 @@
             [k for k in range(count) if k % 8 < 4],
         )
 
+    def dealt(self, b, j):
+        return pl.ds(TILE * (self.tiles * b + j), TILE)
+
+    def deal(self, block_ref, out_ref, upper):
+        odd = jnp.where(self.left, upper, 1 - upper)
+        column = 2 * (self.lane % HALF) + odd
+        for x in range(block_ref.shape[0]):
+            for b in (0, 1):
+                for j in range(self.tiles):
+                    rows = block_ref[x, self.every(b, j), :]
+                    out_ref[x, self.dealt(b, j), :] = jnp.take_along_axis(rows, column, axis=1)
+
     def arrange(self, mine_ref, theirs_ref, place, flip, store):
-        blocks, own, rows, _ = mine_ref.shape
-        column = self.lane % HALF
-        even_odd = 2 * column + jnp.where(self.left, 0, 1)
-        odd_even = 2 * column + jnp.where(self.left, 1, 0)
+        blocks, own = mine_ref.shape[:2]
 
         def pair(u, carry):
             for ref, holder in ((mine_ref, place), (theirs_ref, place ^ 1)):
@@ -192,12 +218,8 @@
                     spot = home * (own // 2) + x // 2
                     for b in (0, 1):
                         for j in range(self.tiles):
-                            one = jnp.take_along_axis(
-                                ref[first, x, self.every(b, j), :], even_odd, axis=1
-                            )
-                            two = jnp.take_along_axis(
-                                ref[second, x, self.every(b, j), :], odd_even, axis=1
-                            )
+                            one = ref[first, x, self.dealt(b, j), :]
+                            two = ref[second, x, self.dealt(b, j), :]
                             store(cls(x % 2, b, 0), spot, j, jnp.where(self.left, one, two))
                             odd = roll(jnp.where(self.left, two, one), HALF, 1)
                             store(cls(x % 2, b, 1), spot, j, odd)
@@ -273,7 +295,6 @@
                 outside[high].append(plus)
                 minus, plus = masked(y_low[j], minus), masked(y_high[j], plus)
                 outer_y[at, i, tile(j)] = minus
-                outer_y[4 + at, i, tile(j)] = plus
                 off[1].append(minus)
                 off[2].append(plus)
 
@@ -357,42 +378,54 @@
     at_.arrange(mine_ref, theirs_ref, place_ref[0], True, begin)
     at_.seam_fine(scaled)
 
-    def rows_of(field, i):
+    def rows_of(ref, i):
         cache = {}
 
-        def load(k, j):
+        def load(k, j, step):
+            if abs(j - step) > 1:
+                return ref[k, i, tile(j)]
             if (k, j) not in cache:
-                cache[k, j] = field[k, i + 1, tile(j)]
+                cache[k, j] = ref[k, i, tile(j)]
             return cache[k, j]
 
-        return load
-
-    def stencil(field, load, i, j, both):
-        here = [load(k, j) for k in range(8)]
-        terms = [[] for _ in range(8)]
-        for p, q in PAIRS:
-            at = 2 * p + q
-            for face_at, low, high in inner_faces(p, q):
-                face = inner[face_at, i, tile(j)]
-                terms[low].append(face * here[high])
+        def get(k, j):
+            return load(k, j, j)
+
+        def before(k, j):
+            return at_.row_before(lambda r: load(k, r, j), j)
+
+        def after(k, j):
+            return at_.row_after(lambda r: load(k, r, j), j)
+
+        return get, before, after
+
+    def stencil(field, i, both):
+        get, before, after = rows_of(field, i + 1)
+        face_get, _, face_after = rows_of(outer_y, i)
+        for j in range(tiles):
+            here = [get(k, j) for k in range(8)]
+            terms = [[] for _ in range(8)]
+            for p, q in PAIRS:
+                at = 2 * p + q
+                for face_at, low, high in inner_faces(p, q):
+                    face = inner[face_at, i, tile(j)]
+                    terms[low].append(face * here[high])
+                    if both:
+                        terms[high].append(face * here[low])
+                low, high = cls(0, p, q), cls(1, p, q)
+                terms[low].append(outer_x[at, i, tile(j)] * field[high, i, tile(j)])
                 if both:
-                    terms[high].append(face * here[low])
-            low, high = cls(0, p, q), cls(1, p, q)
-            terms[low].append(outer_x[at, i, tile(j)] * field[high, i, tile(j)])
-            if both:
-                side = field[low, i + 2, tile(j)]
-                terms[high].append(outer_x[at, i + 1, tile(j)] * side)
-            low, high = cls(p, 0, q), cls(p, 1, q)
-            side = at_.row_before(lambda r: load(high, r), j)
-            terms[low].append(outer_y[at, i, tile(j)] * side)
-            if both:
-                side = at_.row_after(lambda r: load(low, r), j)
-                terms[high].append(outer_y[4 + at, i, tile(j)] * side)
-            low, high = cls(p, q, 0), cls(p, q, 1)
-            terms[low].append(outer_z[at, i, tile(j)] * roll(here[high], 1, 1))
-            if both:
-                terms[high].append(outer_z[4 + at, i, tile(j)] * roll(here[low], -1, 1))
-        return here, [tree_sum(part) if part else None for part in terms]
+                    side = field[low, i + 2, tile(j)]
+                    terms[high].append(outer_x[at, i + 1, tile(j)] * side)
+                low, high = cls(p, 0, q), cls(p, 1, q)
+                terms[low].append(face_get(at, j) * before(high, j))
+                if both:
+                    terms[high].append(face_after(at, j) * after(low, j))
+                low, high = cls(p, q, 0), cls(p, q, 1)
+                terms[low].append(outer_z[at, i, tile(j)] * roll(here[high], 1, 1))
+                if both:
+                    terms[high].append(outer_z[4 + at, i, tile(j)] * roll(here[low], -1, 1))
+            yield j, here, [tree_sum(part) if part else None for part in terms]
 
     def coarse_sides(field, i, j):
         here = field[0, i + 1, tile(j)]
@@ -407,10 +440,8 @@
 
     def precondition(result, other):
         def down(i, carry):
-            load = rows_of(scaled, i)
-            for j in range(tiles):
+            for j, _, sums in stencil(scaled, i, True):
                 res = [residual[k, i, tile(j)] for k in range(8)]
-                _, sums = stencil(scaled, load, i, j, True)
                 parts = [(2.0 - DAMPING) * res[k] + sums[k] for k in range(8)]
                 for k in range(8):
                     partial[k, i, tile(j)] = parts[k]
@@ -440,6 +471,7 @@
 
         def up(i, carry):
             gamma, cross = carry
+            face_get, _, face_after = rows_of(outer_y, i)
             for j in range(tiles):
                 here, sides = coarse_sides(coarse_two, i, j)
                 kept = (1.0 - DAMPING) * here
@@ -451,7 +483,7 @@
                             partial[k, i, tile(j)],
                             inner_sum[k, i, tile(j)] * here,
                             outer_x[2 * b + c, i + a, tile(j)] * sides[0][a],
-                            outer_y[4 * b + 2 * a + c, i, tile(j)] * sides[1][b],
+                            (face_after if b else face_get)(2 * a + c, j) * sides[1][b],
                             outer_z[4 * c + 2 * a + b, i, tile(j)] * sides[2][c],
                         ]
                     )
@@ -472,9 +504,7 @@
     gamma, _ = precondition(first_dir, None)
 
     def apply(i, acc):
-        load = rows_of(first_dir, i)
-        for j in range(tiles):
-            here, sums = stencil(first_dir, load, i, j, True)
+        for j, here, sums in stencil(first_dir, i, True):
             dots = []
             for k in range(8):
                 value = diagonal[k, i, tile(j)] * here[k] - sums[k]
@@ -501,9 +531,7 @@
 
     def bend(i, carry):
         own_part, face_part = carry
-        load = rows_of(second_dir, i)
-        for j in range(tiles):
-            here, sums = stencil(second_dir, load, i, j, False)
+        for j, here, sums in stencil(second_dir, i, False):
             own_part = own_part + tree_sum(
                 [here[k] * (diagonal[k, i, tile(j)] * here[k]) for k in range(8)]
             )
@@ -586,8 +614,8 @@
     groups = lax.axis_size("pole")
     place = jnp.stack([lax.axis_index("space"), lax.axis_index("pole")]).astype(jnp.int32)
     peers = lax.axis_size("space")
-    mine, theirs, states, far, near = gather_blocks(
-        place, conductivity, misfit, forward_states, "space"
+    mine, theirs, far, near = gather_blocks(
+        place, [conductivity, misfit], forward_states, "space"
     )
     half, rows = peers * own // 4, ny // 2
 
@@ -602,7 +630,7 @@
     shapes = [
         field(12, half),
         field(4, half + 1),
-        field(8, half),
+        field(4, half),
         field(8, half),
         field(8, half),
         field(8, half),
@@ -649,7 +677,7 @@
         pole_order,
         mine[1],
         theirs[1],
-        states,
+        forward_states,
         far,
         near,
         *coefficients,

time: 48.6 us -> 44.8 us (0.922)
  the two profiles are of different devices: /device:TPU:27 before, /device:TPU:0 now
where the time goes in v11:
time: 44.8 us; the launch traced here: 44.5 us
  starting transfers between devices  17.4 us (39%)
  Pallas kernels  11.2 us (25%)
  waiting for transfers between devices  11 us (25%)
  other arithmetic  2.35 us (5%)
  local copies, waits for them, and re-layouts  1.76 us (4%)
  between operations  0.81 us (2%)
    ppermute x6, starting transfers between devices, gather_blocks(): arrived.append(lax.ppermute(held[at], axis, pairs))  12 us
    ppermute x6, waiting for transfers between devices, gather_blocks(): arrived.append(lax.ppermute(held[at], axis, pairs))  8.35 us
    pallas_call x1, Pallas kernels, whole_grid(): pl.pallas_call(solve_kernel, out_shape=[jax.ShapeDtypeStruct((own, ny, nz...  8.23 us
    ppermute x2, waiting for transfers between devices, whole_grid(): shares.append(lax.ppermute(send[k - 1, side], ('pole', 'space'), pairs))  2.59 us
    ppermute x2, starting transfers between devices, gather_blocks(): other = [lax.ppermute(part, axis, swap) for part in held]  2.29 us
    pallas_call x1, Pallas kernels, whole_grid(): pl.pallas_call(setup_kernel, out_shape=[jax.ShapeDtypeStruct(shape, jnp.f...  2.24 us
    ppermute x2, starting transfers between devices, whole_grid(): shares.append(lax.ppermute(send[k - 1, side], ('pole', 'space'), pairs))  1.84 us
    unnamed x15, local copies, waits for them, and re-layouts  1.73 us
  transfers between devices with their start and end apart: 13, of which 7 were waited for; matrix products, arithmetic and copies ran while one was open for 4% of the time, Pallas kernels for 5%

profile of v11, /device:TPU:0, one launch (start us, length us, event | category | flops | bytes accessed | tf_op | source)
XLA Modules:
  0.0 44.5 jit_solution(16224432531795883792)
XLA Ops:
  0.6 4.1 %collective-permute-start = (f32[2,64,128]{2,1,0:T(8,128)}, f32[2,64,128]{2,1,0:T(8,128)S(1)}, u32[]{:S(2)}, u32[]{:S(2)}) collective-permute-start(f32[2,64,128]{2,1,0:T(8,128)} %kappa_ref.1), channel_id=1, source_target_pairs={{0,8},{1,3},{2,10},{3,1},{4,12},{5,7},{6,14},{7,5},{8,0},{9,11},{1... | collective-permute-start | bytes 196616 | tf_op jit(solution)/shard_map/ppermute | solution.py:122
  4.7 1.5 %collective-permute-start.1 = (f32[2,64,128]{2,1,0:T(8,128)}, f32[2,64,128]{2,1,0:T(8,128)S(1)}, u32[]{:S(2)}, u32[]{:S(2)}) collective-permute-start(f32[2,64,128]{2,1,0:T(8,128)} %misfit_ref.1), channel_id=1, source_target_pairs={{0,2},{1,9},{2,0},{3,11},{4,6},{5,13},{6,4},{7,15},{8,10},{9,1},{1... | collective-permute-start | bytes 196616 | tf_op jit(solution)/shard_map/ppermute | solution.py:122
  6.2 0.8 %copy-done.1 = f32[2,64,128]{2,1,0:T(8,128)S(1)} copy-done((f32[2,64,128]{2,1,0:T(8,128)S(1)}, f32[2,64,128]{2,1,0:T(8,128)}, u32[]{:S(2)}) %copy-start.1) | copy-done | bytes 65560
  7.1 0.8 %copy-done.2 = f32[2,64,128]{2,1,0:T(8,128)S(1)} copy-done((f32[2,64,128]{2,1,0:T(8,128)S(1)}, f32[2,64,128]{2,1,0:T(8,128)}, u32[]{:S(2)}) %copy-start.2) | copy-done | bytes 65560
  7.9 0.1 pad_add_fusion.place_ref
  8.0 1.2 %collective-permute-done.1.refs_3_ = f32[2,64,128]{2,1,0:T(8,128)S(1)} collective-permute-done((f32[2,64,128]{2,1,0:T(8,128)}, f32[2,64,128]{2,1,0:T(8,128)S(1)}, u32[]{:S(2)}, u32[]{:S(2)}) %collective-permute-start.1) | collective-permute-done | bytes 65568 | tf_op jit(solution)/shard_map/ppermute | solution.py:122
  9.2 0.7 %join.1 = (f32[2,2,64,128]{3,2,1,0:T(8,128)S(1)}, f32[2,2,64,128]{3,2,1,0:T(8,128)S(1)}) custom-call(s32[2]{0:T(128)S(1)} %pad_add_fusion.place_ref, f32[2,64,128]{2,1,0:T(8,128)S(1)} %get-tuple-element.25.refs_0_, f32[2,64,128]{2,1,0:T(8,128)S(1)} %get-tuple-element.26.refs_1_, f32[2,64,128]{2,1,0:T(8,128)S(1)} %collective-permute-done.refs_2_, ...), custom_call_target="tpu_custom_call" | custom-call | tf_op jit(solution)/shard_map/join/pallas_call | solution.py:128
  9.9 1.6 %collective-permute-start.7 = (f32[2,2,64,128]{3,2,1,0:T(8,128)S(1)}, f32[2,2,64,128]{3,2,1,0:T(8,128)S(1)}, u32[]{:S(2)}, u32[]{:S(2)}) collective-permute-start(f32[2,2,64,128]{3,2,1,0:T(8,128)S(1)} %get-tuple-element.32), channel_id=1, source_target_pairs={{0,4},{1,9},{2,6},{3,11},{4,0},{5,13},{6,2},{7,15},{8,12},{9,1},{1... | collective-permute-start | bytes 393224 | tf_op jit(solution)/shard_map/ppermute | solution.py:122
  11.5 0.4 %collective-permute-start.2 = (f32[2,2,64,128]{3,2,1,0:T(8,128)S(1)}, f32[2,2,64,128]{3,2,1,0:T(8,128)S(1)}, u32[]{:S(2)}, u32[]{:S(2)}) collective-permute-start(f32[2,2,64,128]{3,2,1,0:T(8,128)S(1)} %get-tuple-element.28), channel_id=1, source_target_pairs={{0,4},{1,3},{2,6},{3,1},{4,0},{5,7},{6,2},{7,5},{8,12},{9,11},{10,... | collective-permute-start | bytes 393224 | tf_op jit(solution)/shard_map/ppermute | solution.py:122
  12.0 0.9 %slice_select_fusion.1 = f32[2,1,64,128]{3,2,1,0:T(8,128)S(1)} fusion(f32[2,2,64,128]{3,2,1,0:T(8,128)} %state_ref.1, pred[]{:T(512)S(6)} %eq.7), kind=kLoop, calls=%fused_computation.8 | loop fusion | flops 16384 | bytes 196609 | tf_op jit(solution)/shard_map/jit(_where)/select_n | solution.py:137
  12.9 2.4 %collective-permute-done.7 = f32[2,2,64,128]{3,2,1,0:T(8,128)S(1)} collective-permute-done((f32[2,2,64,128]{3,2,1,0:T(8,128)S(1)}, f32[2,2,64,128]{3,2,1,0:T(8,128)S(1)}, u32[]{:S(2)}, u32[]{:S(2)}) %collective-permute-start.7) | collective-permute-done | bytes 131104 | tf_op jit(solution)/shard_map/ppermute | solution.py:122
  15.3 0.0 copy-start.3
  15.3 0.0 copy-start.4
  15.3 1.2 %collective-permute-start.8 = (f32[4,2,64,128]{3,2,1,0:T(8,128)S(1)}, f32[4,2,64,128]{3,2,1,0:T(8,128)S(1)}, u32[]{:S(2)}, u32[]{:S(2)}) collective-permute-start(f32[4,2,64,128]{3,2,1,0:T(8,128)S(1)} %pad_maximum_fusion.2), channel_id=1, source_target_pairs={{0,2},{1,5},{2,0},{3,7},{4,6},{5,1},{6,4},{7,3},{8,10},{9,13},{10,... | collective-permute-start | bytes 786440 | tf_op jit(solution)/shard_map/ppermute | solution.py:122
  16.5 0.1 collective-permute-done.2
  16.7 3.1 %collective-permute-start.3 = (f32[4,2,64,128]{3,2,1,0:T(8,128)S(1)}, f32[4,2,64,128]{3,2,1,0:T(8,128)S(1)}, u32[]{:S(2)}, u32[]{:S(2)}) collective-permute-start(f32[4,2,64,128]{3,2,1,0:T(8,128)S(1)} %pad_maximum_fusion.1), channel_id=1, source_target_pairs={{0,8},{1,5},{2,10},{3,7},{4,12},{5,1},{6,14},{7,3},{8,0},{9,13},{1... | collective-permute-start | bytes 786440 | tf_op jit(solution)/shard_map/ppermute | solution.py:122
  19.8 0.7 %collective-permute-start.4 = (f32[2,1,64,128]{3,2,1,0:T(8,128)S(1)}, f32[2,1,64,128]{3,2,1,0:T(8,128)S(1)}, u32[]{:S(2)}, u32[]{:S(2)}) collective-permute-start(f32[2,1,64,128]{3,2,1,0:T(8,128)S(1)} %slice_select_fusion.1), channel_id=1, source_target_pairs={{1,2},{2,1},{3,4},{4,3},{5,6},{6,5},{7,8},{8,7},{9,10},{10,9},{11,... | collective-permute-start | bytes 196616 | tf_op jit(solution)/shard_map/ppermute | solution.py:137
  20.5 0.0 copy-start.5
  20.5 1.2 %collective-permute-done.8 = f32[4,2,64,128]{3,2,1,0:T(8,128)S(1)} collective-permute-done((f32[4,2,64,128]{3,2,1,0:T(8,128)S(1)}, f32[4,2,64,128]{3,2,1,0:T(8,128)S(1)}, u32[]{:S(2)}, u32[]{:S(2)}) %collective-permute-start.8) | collective-permute-done | bytes 262176 | tf_op jit(solution)/shard_map/ppermute | solution.py:122
  21.8 1.0 %collective-permute-start.9 = (f32[8,2,64,128]{3,2,1,0:T(8,128)S(1)}, f32[8,2,64,128]{3,2,1,0:T(8,128)S(1)}, u32[]{:S(2)}, u32[]{:S(2)}) collective-permute-start(f32[8,2,64,128]{3,2,1,0:T(8,128)S(1)} %constant_dynamic-update-slice_fusion.2.mine_ref), channel_id=1, source_target_pairs={{0,1},{1,0},{2,3},{3,2},{4,5},{5,4},{6,7},{7,6},{8,9},{9,8},{10,11... | collective-permute-start | bytes 1572872 | tf_op jit(solution)/shard_map/ppermute | solution.py:141
  22.7 3.4 %collective-permute-done.3 = f32[4,2,64,128]{3,2,1,0:T(8,128)S(1)} collective-permute-done((f32[4,2,64,128]{3,2,1,0:T(8,128)S(1)}, f32[4,2,64,128]{3,2,1,0:T(8,128)S(1)}, u32[]{:S(2)}, u32[]{:S(2)}) %collective-permute-start.3) | collective-permute-done | bytes 262176 | tf_op jit(solution)/shard_map/ppermute | solution.py:122
  26.2 1.3 %collective-permute-start.5 = (f32[8,2,64,128]{3,2,1,0:T(8,128)S(1)}, f32[8,2,64,128]{3,2,1,0:T(8,128)S(1)}, u32[]{:S(2)}, u32[]{:S(2)}) collective-permute-start(f32[8,2,64,128]{3,2,1,0:T(8,128)S(1)} %pad_maximum_fusion.mine_ref), channel_id=1, source_target_pairs={{0,1},{1,0},{2,3},{3,2},{4,5},{5,4},{6,7},{7,6},{8,9},{9,8},{10,11... | collective-permute-start | bytes 1572872 | tf_op jit(solution)/shard_map/ppermute | solution.py:141
  27.6 0.1 collective-permute-start.6
  27.7 2.2 %setup.1 = (f32[12,8,32,128]{3,2,1,0:T(8,128)S(1)}, f32[4,9,32,128]{3,2,1,0:T(8,128)S(1)}, f32[4,8,32,128]{3,2,1,0:T(8,128)S(1)}, f32[8,8,32,128]{3,2,1,0:T(8,12...) custom-call(s32[2]{0:T(128)S(1)} %pad_add_fusion.place_ref, ...), custom_call_target="tpu_custom_call" | custom-call | tf_op jit(solution)/shard_map/setup/pallas_call | solution.py:641
  30.0 8.2 %solve.1 = (f32[2,64,128]{2,1,0:T(8,128)S(1)}, f32[2,32,128]{2,1,0:T(8,128)S(1)}, f32[2,96,128]{2,1,0:T(8,128)S(1)}, f32[1,2,2,32,128]{4,3,2,1,0:T(8,128)S(1)}) custom-call(s32[2]{0:T(128)S(1)} %pad_add_fusion.place_ref, f32[4]{0:T(128)S(1)} %copy-done.5, s32[2]{0:T(128)S(1)} %copy-done.3, f32[8,2,64,128]{3,2,1,0:T(8,128)S(1)} %pad_maximum_fusion.mine_ref, ...), custom_call_target="tpu_custom_call" | custom-call | tf_op jit(solution)/shard_map/solve/pallas_call | solution.py:651
  38.2 0.5 %collective-permute-start.10 = (f32[2,96,128]{2,1,0:T(8,128)S(1)}, f32[2,96,128]{2,1,0:T(8,128)S(1)}, u32[]{:S(2)}, u32[]{:S(2)}) collective-permute-start(f32[2,96,128]{2,1,0:T(8,128)S(1)} %get-tuple-element.43), channel_id=1, source_target_pairs={{0,1},{1,0},{2,3},{3,2},{4,5},{5,4},{6,7},{7,6},{8,9},{9,8},{10,11... | collective-permute-start | bytes 294920 | tf_op jit(solution)/shard_map/ppermute | solution.py:686
  38.8 1.8 %collective-permute-start.11 = (f32[2,32,128]{2,1,0:T(8,128)S(1)}, f32[2,32,128]{2,1,0:T(8,128)S(1)}, u32[]{:S(2)}, u32[]{:S(2)}) collective-permute-start(f32[2,32,128]{2,1,0:T(8,128)S(1)} %get-tuple-element.51), channel_id=1, source_target_pairs={{0,16},{1,17},{2,18},{3,19},{4,20},{5,21},{6,22},{7,23},{8,24},{9,... | collective-permute-start | bytes 98312 | tf_op jit(solution)/shard_map/ppermute | solution.py:695
  40.5 0.1 collective-permute-start.12
  40.6 0.7 %pad_maximum_fusion.3 = f32[2,2,64,128]{3,2,1,0:T(8,128)} fusion(f32[1,2,64,128]{3,2,1,0:T(8,128)S(1)} %get-tuple-element.49, f32[1,2,64,128]{3,2,1,0:T(8,128)S(1)} %get-tuple-element.48), kind=kLoop, calls=%fused_computation.3 | loop fusion | flops 32768 | bytes 262144 | tf_op jit(solution)/shard_map/stack | solution.py:698
  41.3 1.4 %collective-permute-done.11 = f32[2,32,128]{2,1,0:T(8,128)S(1)} collective-permute-done((f32[2,32,128]{2,1,0:T(8,128)S(1)}, f32[2,32,128]{2,1,0:T(8,128)S(1)}, u32[]{:S(2)}, u32[]{:S(2)}) %collective-permute-start.11) | collective-permute-done | bytes 32800 | tf_op jit(solution)/shard_map/ppermute | solution.py:695
  42.7 1.2 %collective-permute-done.12 = f32[2,32,128]{2,1,0:T(8,128)S(1)} collective-permute-done((f32[2,32,128]{2,1,0:T(8,128)S(1)}, f32[2,32,128]{2,1,0:T(8,128)S(1)}, u32[]{:S(2)}, u32[]{:S(2)}) %collective-permute-start.12) | collective-permute-done | bytes 32800 | tf_op jit(solution)/shard_map/ppermute | solution.py:695
  43.9 0.6 %add_add_fusion = f32[2,32,128]{2,1,0:T(8,128)} fusion(f32[2,32,128]{2,1,0:T(8,128)S(1)} %collective-permute-done.11, f32[2,32,128]{2,1,0:T(8,128)S(1)} %collective-permute-done.12, f32[2,32,128]{2,1,0:T(8,128)S(1)} %get-tuple-element.45, f32[2,96,128]{2,1,0:T(8,128)S(1)} %collective-permute-done.10), kind=kLoop, calls=%fused_computation.9 | loop fusion | flops 24576 | bytes 163840 | tf_op jit(solution)/shard_map/add | solution.py:702
  (25 shorter events, 0.2 us)
Async XLA Ops:
  0.6 7.4 %collective-permute-start = (f32[2,64,128]{2,1,0:T(8,128)}, f32[2,64,128]{2,1,0:T(8,128)S(1)}, u32[]{:S(2)}, u32[]{:S(2)}) collective-permute-start(f32[2,64,128]{2,1,0:T(8,128)} %kappa_ref.1), channel_id=1, source_target_pairs={{0,8},{1,3},{2,10},{3,1},{4,12},{5,7},{6,14},{7,5},{8,0},{9,11},{1... | collective-permute-start | bytes 196616 | tf_op jit(solution)/shard_map/ppermute | solution.py:122
  4.7 4.5 %collective-permute-start.1 = (f32[2,64,128]{2,1,0:T(8,128)}, f32[2,64,128]{2,1,0:T(8,128)S(1)}, u32[]{:S(2)}, u32[]{:S(2)}) collective-permute-start(f32[2,64,128]{2,1,0:T(8,128)} %misfit_ref.1), channel_id=1, source_target_pairs={{0,2},{1,9},{2,0},{3,11},{4,6},{5,13},{6,4},{7,15},{8,10},{9,1},{1... | collective-permute-start | bytes 196616 | tf_op jit(solution)/shard_map/ppermute | solution.py:122
  6.2 0.8 %copy-start.1 = (f32[2,64,128]{2,1,0:T(8,128)S(1)}, f32[2,64,128]{2,1,0:T(8,128)}, u32[]{:S(2)}) copy-start(f32[2,64,128]{2,1,0:T(8,128)} %kappa_ref.1) | copy-start | bytes 196612
  7.1 0.8 %copy-start.2 = (f32[2,64,128]{2,1,0:T(8,128)S(1)}, f32[2,64,128]{2,1,0:T(8,128)}, u32[]{:S(2)}) copy-start(f32[2,64,128]{2,1,0:T(8,128)} %misfit_ref.1) | copy-start | bytes 196612
  9.9 5.4 %collective-permute-start.7 = (f32[2,2,64,128]{3,2,1,0:T(8,128)S(1)}, f32[2,2,64,128]{3,2,1,0:T(8,128)S(1)}, u32[]{:S(2)}, u32[]{:S(2)}) collective-permute-start(f32[2,2,64,128]{3,2,1,0:T(8,128)S(1)} %get-tuple-element.32), channel_id=1, source_target_pairs={{0,4},{1,9},{2,6},{3,11},{4,0},{5,13},{6,2},{7,15},{8,12},{9,1},{1... | collective-permute-start | bytes 393224 | tf_op jit(solution)/shard_map/ppermute | solution.py:122
  11.5 5.1 %collective-permute-start.2 = (f32[2,2,64,128]{3,2,1,0:T(8,128)S(1)}, f32[2,2,64,128]{3,2,1,0:T(8,128)S(1)}, u32[]{:S(2)}, u32[]{:S(2)}) collective-permute-start(f32[2,2,64,128]{3,2,1,0:T(8,128)S(1)} %get-tuple-element.28), channel_id=1, source_target_pairs={{0,4},{1,3},{2,6},{3,1},{4,0},{5,7},{6,2},{7,5},{8,12},{9,11},{10,... | collective-permute-start | bytes 393224 | tf_op jit(solution)/shard_map/ppermute | solution.py:122
  12.9 14.7 %copy-start = (f32[2,2,64,128]{3,2,1,0:T(8,128)S(1)}, f32[2,2,64,128]{3,2,1,0:T(8,128)}, u32[]{:S(2)}) copy-start(f32[2,2,64,128]{3,2,1,0:T(8,128)} %state_ref.1) | copy-start | bytes 393220
  15.3 12.4 %copy-start.3 = (s32[2]{0:T(128)S(1)}, s32[2]{0:T(128)}, u32[]{:S(2)}) copy-start(s32[2]{0:T(128)} %order_ref.3) | copy-start | bytes 28
  15.3 12.4 %copy-start.4 = (f32[4]{0:T(128)S(1)}, f32[4]{0:T(128)}, u32[]{:S(2)}) copy-start(f32[4]{0:T(128)} %shifts_ref.1) | copy-start | bytes 52
  15.3 6.4 %collective-permute-start.8 = (f32[4,2,64,128]{3,2,1,0:T(8,128)S(1)}, f32[4,2,64,128]{3,2,1,0:T(8,128)S(1)}, u32[]{:S(2)}, u32[]{:S(2)}) collective-permute-start(f32[4,2,64,128]{3,2,1,0:T(8,128)S(1)} %pad_maximum_fusion.2), channel_id=1, source_target_pairs={{0,2},{1,5},{2,0},{3,7},{4,6},{5,1},{6,4},{7,3},{8,10},{9,13},{10,... | collective-permute-start | bytes 786440 | tf_op jit(solution)/shard_map/ppermute | solution.py:122
  16.7 9.5 %collective-permute-start.3 = (f32[4,2,64,128]{3,2,1,0:T(8,128)S(1)}, f32[4,2,64,128]{3,2,1,0:T(8,128)S(1)}, u32[]{:S(2)}, u32[]{:S(2)}) collective-permute-start(f32[4,2,64,128]{3,2,1,0:T(8,128)S(1)} %pad_maximum_fusion.1), channel_id=1, source_target_pairs={{0,8},{1,5},{2,10},{3,7},{4,12},{5,1},{6,14},{7,3},{8,0},{9,13},{1... | collective-permute-start | bytes 786440 | tf_op jit(solution)/shard_map/ppermute | solution.py:122
  19.8 6.4 %collective-permute-start.4 = (f32[2,1,64,128]{3,2,1,0:T(8,128)S(1)}, f32[2,1,64,128]{3,2,1,0:T(8,128)S(1)}, u32[]{:S(2)}, u32[]{:S(2)}) collective-permute-start(f32[2,1,64,128]{3,2,1,0:T(8,128)S(1)} %slice_select_fusion.1), channel_id=1, source_target_pairs={{1,2},{2,1},{3,4},{4,3},{5,6},{6,5},{7,8},{8,7},{9,10},{10,9},{11,... | collective-permute-start | bytes 196616 | tf_op jit(solution)/shard_map/ppermute | solution.py:137
  20.5 9.5 %copy-start.5 = (f32[4]{0:T(128)S(1)}, f32[4]{0:T(128)}, u32[]{:S(2)}) copy-start(f32[4]{0:T(128)} %weights_ref.1) | copy-start | bytes 52
  21.8 5.9 %collective-permute-start.9 = (f32[8,2,64,128]{3,2,1,0:T(8,128)S(1)}, f32[8,2,64,128]{3,2,1,0:T(8,128)S(1)}, u32[]{:S(2)}, u32[]{:S(2)}) collective-permute-start(f32[8,2,64,128]{3,2,1,0:T(8,128)S(1)} %constant_dynamic-update-slice_fusion.2.mine_ref), channel_id=1, source_target_pairs={{0,1},{1,0},{2,3},{3,2},{4,5},{5,4},{6,7},{7,6},{8,9},{9,8},{10,11... | collective-permute-start | bytes 1572872 | tf_op jit(solution)/shard_map/ppermute | solution.py:141
  26.2 3.8 %collective-permute-start.5 = (f32[8,2,64,128]{3,2,1,0:T(8,128)S(1)}, f32[8,2,64,128]{3,2,1,0:T(8,128)S(1)}, u32[]{:S(2)}, u32[]{:S(2)}) collective-permute-start(f32[8,2,64,128]{3,2,1,0:T(8,128)S(1)} %pad_maximum_fusion.mine_ref), channel_id=1, source_target_pairs={{0,1},{1,0},{2,3},{3,2},{4,5},{5,4},{6,7},{7,6},{8,9},{9,8},{10,11... | collective-permute-start | bytes 1572872 | tf_op jit(solution)/shard_map/ppermute | solution.py:141
  27.6 2.4 %collective-permute-start.6 = (f32[3,64,128]{2,1,0:T(8,128)S(1)}, f32[3,64,128]{2,1,0:T(8,128)S(1)}, u32[]{:S(2)}, u32[]{:S(2)}) collective-permute-start(f32[3,64,128]{2,1,0:T(8,128)S(1)} %fusion), channel_id=1, source_target_pairs={{0,1},{1,0},{2,3},{3,2},{4,5},{5,4},{6,7},{7,6},{8,9},{9,8},{10,11... | collective-permute-start | bytes 294920 | tf_op jit(solution)/shard_map/ppermute | solution.py:140
  38.2 2.4 %collective-permute-start.10 = (f32[2,96,128]{2,1,0:T(8,128)S(1)}, f32[2,96,128]{2,1,0:T(8,128)S(1)}, u32[]{:S(2)}, u32[]{:S(2)}) collective-permute-start(f32[2,96,128]{2,1,0:T(8,128)S(1)} %get-tuple-element.43), channel_id=1, source_target_pairs={{0,1},{1,0},{2,3},{3,2},{4,5},{5,4},{6,7},{7,6},{8,9},{9,8},{10,11... | collective-permute-start | bytes 294920 | tf_op jit(solution)/shard_map/ppermute | solution.py:686
  38.8 3.9 %collective-permute-start.11 = (f32[2,32,128]{2,1,0:T(8,128)S(1)}, f32[2,32,128]{2,1,0:T(8,128)S(1)}, u32[]{:S(2)}, u32[]{:S(2)}) collective-permute-start(f32[2,32,128]{2,1,0:T(8,128)S(1)} %get-tuple-element.51), channel_id=1, source_target_pairs={{0,16},{1,17},{2,18},{3,19},{4,20},{5,21},{6,22},{7,23},{8,24},{9,... | collective-permute-start | bytes 98312 | tf_op jit(solution)/shard_map/ppermute | solution.py:695
  40.5 3.4 %collective-permute-start.12 = (f32[2,32,128]{2,1,0:T(8,128)S(1)}, f32[2,32,128]{2,1,0:T(8,128)S(1)}, u32[]{:S(2)}, u32[]{:S(2)}) collective-permute-start(f32[2,32,128]{2,1,0:T(8,128)S(1)} %get-tuple-element.50), channel_id=1, source_target_pairs={{0,17},{1,16},{2,19},{3,18},{4,21},{5,20},{6,23},{7,22},{8,25},{9,... | collective-permute-start | bytes 98312 | tf_op jit(solution)/shard_map/ppermute | solution.py:695

commit v12 on v11

--- a/solution.py
+++ b/solution.py
@@ -12,7 +12,9 @@
 REPLICATED_CELLS = 32 * 64 * 128
 HALF = 64
 TILE = 8
-UNROLL = 2
+UNROLL = 8
+SETUP_FLOPS = 40 * REPLICATED_CELLS
+SETUP_BYTES = 10 * 1024 * 1024
 
 
 def extended(array, sides, width):
@@ -62,9 +64,8 @@
     while mask > 1:
         falling.append(mask)
         mask //= 2
-    if flip:
-        return falling[::-1], falling[:1] + falling[:0:-1]
-    return falling, falling[-1:] + falling[:-1]
+    rotated = falling[-1:] + falling[:-1]
+    return (rotated, falling) if flip else (falling, rotated)
 
 
 def block_pair(u, holder, peers, flip):
@@ -135,11 +136,9 @@
         )(place, *own, *arrived)
         held[1], states = lax.optimization_barrier((held[1], states))
         far = lax.ppermute(jnp.where(even, states[:, :1], states[:, -1:]), axis, over)
-    held[1], far = lax.optimization_barrier((held[1], far))
     given = jnp.concatenate([states, far], axis=1)
     near = lax.ppermute(jnp.where(even, given[1], given[0]), axis, swap)
-    other = [lax.ppermute(part, axis, swap) for part in held]
-    return held, other, far, near
+    return held, lambda part: lax.ppermute(part, axis, swap), far, near
 
 
 CLASSES = [(a, b, c) for a in (0, 1) for b in (0, 1) for c in (0, 1)]
@@ -321,7 +320,7 @@
             coarse_damped[i, tile(j)] = DAMPING * inverse(tree_sum(coarse_total) + 8.0 * shift)
         return carry
 
-    lax.fori_loop(0, half, plane, 0)
+    lax.fori_loop(0, half, plane, 0, unroll=UNROLL)
     for j in range(tiles):
         part = []
         for p, q in PAIRS:
@@ -614,7 +613,7 @@
     groups = lax.axis_size("pole")
     place = jnp.stack([lax.axis_index("space"), lax.axis_index("pole")]).astype(jnp.int32)
     peers = lax.axis_size("space")
-    mine, theirs, far, near = gather_blocks(
+    mine, fetch, far, near = gather_blocks(
         place, [conductivity, misfit], forward_states, "space"
     )
     half, rows = peers * own // 4, ny // 2
@@ -645,8 +644,12 @@
         out_specs=[vmem] * len(shapes),
         scratch_shapes=[held(*field(8, half + 2))],
         compiler_params=pltpu.CompilerParams(vmem_limit_bytes=6 * 1024 * 1024),
+        cost_estimate=pl.CostEstimate(
+            flops=SETUP_FLOPS, bytes_accessed=SETUP_BYTES, transcendentals=0
+        ),
         name="setup",
-    )(place, pole_shifts, pole_order, mine[0], theirs[0])
+    )(place, pole_shifts, pole_order, mine[0], fetch(mine[0]))
+    coefficients, source, far = lax.optimization_barrier((coefficients, mine[1], far))
     chunk = ny // groups
     adjoint, gradient, partner, send = pl.pallas_call(
         solve_kernel,
@@ -675,8 +678,8 @@
         place,
         pole_weights,
         pole_order,
-        mine[1],
-        theirs[1],
+        source,
+        fetch(source),
         forward_states,
         far,
         near,

time: 44.8 us -> 47.7 us (1.065)
  waiting for transfers between devices: 11 us -> 15.6 us
  Pallas kernels: 11.2 us -> 9.86 us
  other arithmetic: 2.35 us -> 1.47 us
  starting transfers between devices: 17.4 us -> 17.9 us
    ppermute x6, waiting for transfers between devices: 8.35 us -> 11.6 us  [gather_blocks(): arrived.append(lax.ppermute(held[at], axis, pairs))]
    ppermute x6, starting transfers between devices: 12 us -> 13.8 us  [gather_blocks(): arrived.append(lax.ppermute(held[at], axis, pairs))]
    ppermute x1, waiting for transfers between devices: 0.01 us -> 1.42 us  [gather_blocks(): near = lax.ppermute(jnp.where(even, given[1], given[0]), axis, swap)]
    ppermute x2, starting transfers between devices: 2.29 us -> 0.96 us  [gather_blocks(): return (held, lambda part: lax.ppermute(part, axis, swap), far, near)]
    pallas_call x1, Pallas kernels: 8.23 us -> 7.28 us  [whole_grid(): pl.pallas_call(solve_kernel, out_shape=[jax.ShapeDtypeStruct((own, ny, nz...]
    select_n x1, other arithmetic: 0.88 us -> 0.01 us  [gather_blocks(): jnp.where(even, states[:, :1], states[:, -1:])]
  transfers between devices with their start and end apart: 13 -> 13, of which waited for: 7 -> 8; matrix products, arithmetic and copies ran while one was open for 4% -> 2% of each run, Pallas kernels for 5% -> 4%
where the time goes in v12:
time: 47.7 us; the launch traced here: 47.4 us
  starting transfers between devices  17.9 us (38%)
  waiting for transfers between devices  15.6 us (33%)
  Pallas kernels  9.86 us (21%)
  local copies, waits for them, and re-layouts  1.76 us (4%)
  other arithmetic  1.47 us (3%)
  between operations  0.81 us (2%)
    ppermute x6, starting transfers between devices, gather_blocks(): arrived.append(lax.ppermute(held[at], axis, pairs))  13.8 us
    ppermute x6, waiting for transfers between devices, gather_blocks(): arrived.append(lax.ppermute(held[at], axis, pairs))  11.6 us
    pallas_call x1, Pallas kernels, whole_grid(): pl.pallas_call(solve_kernel, out_shape=[jax.ShapeDtypeStruct((own, ny, nz...  7.28 us
    ppermute x2, waiting for transfers between devices, whole_grid(): shares.append(lax.ppermute(send[k - 1, side], ('pole', 'space'), pairs))  2.55 us
    pallas_call x1, Pallas kernels, whole_grid(): pl.pallas_call(setup_kernel, out_shape=[jax.ShapeDtypeStruct(shape, jnp.f...  1.89 us
    unnamed x15, local copies, waits for them, and re-layouts  1.73 us
    ppermute x2, starting transfers between devices, whole_grid(): shares.append(lax.ppermute(send[k - 1, side], ('pole', 'space'), pairs))  1.73 us
    ppermute x1, waiting for transfers between devices, gather_blocks(): near = lax.ppermute(jnp.where(even, given[1], given[0]), axis, swap)  1.42 us
  transfers between devices with their start and end apart: 13, of which 8 were waited for; matrix products, arithmetic and copies ran while one was open for 2% of the time, Pallas kernels for 4%

profile of v12, /device:TPU:0, one launch (start us, length us, event | category | flops | bytes accessed | tf_op | source)
XLA Modules:
  0.0 47.4 jit_solution(3177425602693612146)
XLA Ops:
  0.6 4.1 %collective-permute-start = (f32[2,64,128]{2,1,0:T(8,128)}, f32[2,64,128]{2,1,0:T(8,128)S(1)}, u32[]{:S(2)}, u32[]{:S(2)}) collective-permute-start(f32[2,64,128]{2,1,0:T(8,128)} %kappa_ref.1), channel_id=1, source_target_pairs={{0,8},{1,3},{2,10},{3,1},{4,12},{5,7},{6,14},{7,5},{8,0},{9,11},{1... | collective-permute-start | bytes 196616 | tf_op jit(solution)/shard_map/ppermute | solution.py:123
  4.7 1.5 %collective-permute-start.1 = (f32[2,64,128]{2,1,0:T(8,128)}, f32[2,64,128]{2,1,0:T(8,128)S(1)}, u32[]{:S(2)}, u32[]{:S(2)}) collective-permute-start(f32[2,64,128]{2,1,0:T(8,128)} %misfit_ref.1), channel_id=1, source_target_pairs={{0,2},{1,9},{2,0},{3,11},{4,6},{5,13},{6,4},{7,15},{8,10},{9,1},{1... | collective-permute-start | bytes 196616 | tf_op jit(solution)/shard_map/ppermute | solution.py:123
  6.2 0.8 %copy-done.1 = f32[2,64,128]{2,1,0:T(8,128)S(1)} copy-done((f32[2,64,128]{2,1,0:T(8,128)S(1)}, f32[2,64,128]{2,1,0:T(8,128)}, u32[]{:S(2)}) %copy-start.1) | copy-done | bytes 65560
  7.1 0.8 %copy-done.2 = f32[2,64,128]{2,1,0:T(8,128)S(1)} copy-done((f32[2,64,128]{2,1,0:T(8,128)S(1)}, f32[2,64,128]{2,1,0:T(8,128)}, u32[]{:S(2)}) %copy-start.2) | copy-done | bytes 65560
  7.9 0.1 pad_add_fusion.place_ref
  8.0 1.2 %collective-permute-done.1.refs_3_ = f32[2,64,128]{2,1,0:T(8,128)S(1)} collective-permute-done((f32[2,64,128]{2,1,0:T(8,128)}, f32[2,64,128]{2,1,0:T(8,128)S(1)}, u32[]{:S(2)}, u32[]{:S(2)}) %collective-permute-start.1) | collective-permute-done | bytes 65568 | tf_op jit(solution)/shard_map/ppermute | solution.py:123
  9.2 0.7 %join.1 = (f32[2,2,64,128]{3,2,1,0:T(8,128)S(1)}, f32[2,2,64,128]{3,2,1,0:T(8,128)S(1)}) custom-call(s32[2]{0:T(128)S(1)} %pad_add_fusion.place_ref, f32[2,64,128]{2,1,0:T(8,128)S(1)} %get-tuple-element.34.refs_0_, f32[2,64,128]{2,1,0:T(8,128)S(1)} %get-tuple-element.35.refs_1_, f32[2,64,128]{2,1,0:T(8,128)S(1)} %collective-permute-done.refs_2_, ...), custom_call_target="tpu_custom_call" | custom-call | tf_op jit(solution)/shard_map/join/pallas_call | solution.py:129
  9.9 0.0 copy-start.3
  9.9 0.0 copy-start.4
  9.9 1.6 %collective-permute-start.2 = (f32[2,2,64,128]{3,2,1,0:T(8,128)S(1)}, f32[2,2,64,128]{3,2,1,0:T(8,128)S(1)}, u32[]{:S(2)}, u32[]{:S(2)}) collective-permute-start(f32[2,2,64,128]{3,2,1,0:T(8,128)S(1)} %get-tuple-element.36), channel_id=1, source_target_pairs={{0,4},{1,9},{2,6},{3,11},{4,0},{5,13},{6,2},{7,15},{8,12},{9,1},{1... | collective-permute-start | bytes 393224 | tf_op jit(solution)/shard_map/ppermute | solution.py:123
  11.6 3.7 %collective-permute-done.2 = f32[2,2,64,128]{3,2,1,0:T(8,128)S(1)} collective-permute-done((f32[2,2,64,128]{3,2,1,0:T(8,128)S(1)}, f32[2,2,64,128]{3,2,1,0:T(8,128)S(1)}, u32[]{:S(2)}, u32[]{:S(2)}) %collective-permute-start.2) | collective-permute-done | bytes 131104 | tf_op jit(solution)/shard_map/ppermute | solution.py:123
  15.3 1.2 %collective-permute-start.3 = (f32[4,2,64,128]{3,2,1,0:T(8,128)S(1)}, f32[4,2,64,128]{3,2,1,0:T(8,128)S(1)}, u32[]{:S(2)}, u32[]{:S(2)}) collective-permute-start(f32[4,2,64,128]{3,2,1,0:T(8,128)S(1)} %pad_maximum_fusion.1), channel_id=1, source_target_pairs={{0,2},{1,5},{2,0},{3,7},{4,6},{5,1},{6,4},{7,3},{8,10},{9,13},{10,... | collective-permute-start | bytes 786440 | tf_op jit(solution)/shard_map/ppermute | solution.py:123
  16.5 2.4 %collective-permute-start.5 = (f32[2,2,64,128]{3,2,1,0:T(8,128)S(1)}, f32[2,2,64,128]{3,2,1,0:T(8,128)S(1)}, u32[]{:S(2)}, u32[]{:S(2)}) collective-permute-start(f32[2,2,64,128]{3,2,1,0:T(8,128)S(1)} %get-tuple-element.47), channel_id=1, source_target_pairs={{0,8},{1,5},{2,10},{3,7},{4,12},{5,1},{6,14},{7,3},{8,0},{9,13},{1... | collective-permute-start | bytes 393224 | tf_op jit(solution)/shard_map/ppermute | solution.py:123
  18.9 2.8 %collective-permute-done.3 = f32[4,2,64,128]{3,2,1,0:T(8,128)S(1)} collective-permute-done((f32[4,2,64,128]{3,2,1,0:T(8,128)S(1)}, f32[4,2,64,128]{3,2,1,0:T(8,128)S(1)}, u32[]{:S(2)}, u32[]{:S(2)}) %collective-permute-start.3) | collective-permute-done | bytes 262176 | tf_op jit(solution)/shard_map/ppermute | solution.py:123
  21.8 0.9 %collective-permute-start.4 = (f32[8,2,64,128]{3,2,1,0:T(8,128)S(1)}, f32[8,2,64,128]{3,2,1,0:T(8,128)S(1)}, u32[]{:S(2)}, u32[]{:S(2)}) collective-permute-start(f32[8,2,64,128]{3,2,1,0:T(8,128)S(1)} %constant_dynamic-update-slice_fusion.mine_ref), channel_id=1, source_target_pairs={{0,1},{1,0},{2,3},{3,2},{4,5},{5,4},{6,7},{7,6},{8,9},{9,8},{10,11... | collective-permute-start | bytes 1572872 | tf_op jit(solution)/shard_map/ppermute | solution.py:141
  22.7 0.2 collective-permute-done.5
  22.9 0.0 copy-start.5
  22.9 3.0 %collective-permute-start.6 = (f32[4,2,64,128]{3,2,1,0:T(8,128)S(1)}, f32[4,2,64,128]{3,2,1,0:T(8,128)S(1)}, u32[]{:S(2)}, u32[]{:S(2)}) collective-permute-start(f32[4,2,64,128]{3,2,1,0:T(8,128)S(1)} %pad_maximum_fusion.2), channel_id=1, source_target_pairs={{0,4},{1,3},{2,6},{3,1},{4,0},{5,7},{6,2},{7,5},{8,12},{9,11},{10,... | collective-permute-start | bytes 786440 | tf_op jit(solution)/shard_map/ppermute | solution.py:123
  25.9 0.7 %collective-permute-start.7 = (f32[2,1,64,128]{3,2,1,0:T(8,128)S(1)}, f32[2,1,64,128]{3,2,1,0:T(8,128)S(1)}, u32[]{:S(2)}, u32[]{:S(2)}) collective-permute-start(f32[2,1,64,128]{3,2,1,0:T(8,128)S(1)} %slice_select_fusion.1), channel_id=1, source_target_pairs={{1,2},{2,1},{3,4},{4,3},{5,6},{6,5},{7,8},{8,7},{9,10},{10,9},{11,... | collective-permute-start | bytes 196616 | tf_op jit(solution)/shard_map/ppermute | solution.py:138
  26.6 3.7 %collective-permute-done.6 = f32[4,2,64,128]{3,2,1,0:T(8,128)S(1)} collective-permute-done((f32[4,2,64,128]{3,2,1,0:T(8,128)S(1)}, f32[4,2,64,128]{3,2,1,0:T(8,128)S(1)}, u32[]{:S(2)}, u32[]{:S(2)}) %collective-permute-start.6) | collective-permute-done | bytes 262176 | tf_op jit(solution)/shard_map/ppermute | solution.py:123
  30.3 1.9 %setup.1 = (f32[12,8,32,128]{3,2,1,0:T(8,128)S(1)}, f32[4,9,32,128]{3,2,1,0:T(8,128)S(1)}, f32[4,8,32,128]{3,2,1,0:T(8,128)S(1)}, f32[8,8,32,128]{3,2,1,0:T(8,12...) custom-call(s32[2]{0:T(128)S(1)} %pad_add_fusion.place_ref, ...), custom_call_target="tpu_custom_call" | custom-call | flops 10485760 | bytes 10485760 | tf_op jit(solution)/shard_map/setup/pallas_call | solution.py:640
  32.2 0.1 collective-permute-start.8
  32.4 0.6 %collective-permute-start.9 = (f32[3,64,128]{2,1,0:T(8,128)S(1)}, f32[3,64,128]{2,1,0:T(8,128)S(1)}, u32[]{:S(2)}, u32[]{:S(2)}) collective-permute-start(f32[3,64,128]{2,1,0:T(8,128)S(1)} %fusion), channel_id=1, source_target_pairs={{0,1},{1,0},{2,3},{3,2},{4,5},{5,4},{6,7},{7,6},{8,9},{9,8},{10,11... | collective-permute-start | bytes 294920 | tf_op jit(solution)/shard_map/ppermute | solution.py:140
  32.9 1.4 %collective-permute-done.9.near_ref = f32[3,64,128]{2,1,0:T(8,128)S(1)} collective-permute-done((f32[3,64,128]{2,1,0:T(8,128)S(1)}, f32[3,64,128]{2,1,0:T(8,128)S(1)}, u32[]{:S(2)}, u32[]{:S(2)}) %collective-permute-start.9) | collective-permute-done | bytes 98336 | tf_op jit(solution)/shard_map/ppermute | solution.py:140
  34.4 7.3 %solve.1 = (f32[2,64,128]{2,1,0:T(8,128)S(1)}, f32[2,32,128]{2,1,0:T(8,128)S(1)}, f32[2,96,128]{2,1,0:T(8,128)S(1)}, f32[1,2,2,32,128]{4,3,2,1,0:T(8,128)S(1)}) custom-call(s32[2]{0:T(128)S(1)} %pad_add_fusion.place_ref, f32[4]{0:T(128)S(1)} %copy-done.5, s32[2]{0:T(128)S(1)} %copy-done.3, f32[8,2,64,128]{3,2,1,0:T(8,128)S(1)} %pad_maximum_fusion.mine_ref, ...), custom_call_target="tpu_custom_call" | custom-call | tf_op jit(solution)/shard_map/solve/pallas_call | solution.py:654
  41.7 0.2 collective-permute-start.10
  41.9 1.5 %collective-permute-start.11 = (f32[2,32,128]{2,1,0:T(8,128)S(1)}, f32[2,32,128]{2,1,0:T(8,128)S(1)}, u32[]{:S(2)}, u32[]{:S(2)}) collective-permute-start(f32[2,32,128]{2,1,0:T(8,128)S(1)} %get-tuple-element.69), channel_id=1, source_target_pairs={{0,16},{1,17},{2,18},{3,19},{4,20},{5,21},{6,22},{7,23},{8,24},{9,... | collective-permute-start | bytes 98312 | tf_op jit(solution)/shard_map/ppermute | solution.py:698
  43.4 0.2 collective-permute-start.12
  43.6 0.7 %pad_maximum_fusion.3 = f32[2,2,64,128]{3,2,1,0:T(8,128)} fusion(f32[1,2,64,128]{3,2,1,0:T(8,128)S(1)} %get-tuple-element.67, f32[1,2,64,128]{3,2,1,0:T(8,128)S(1)} %get-tuple-element.66), kind=kLoop, calls=%fused_computation.3 | loop fusion | flops 32768 | bytes 262144 | tf_op jit(solution)/shard_map/stack | solution.py:701
  44.3 1.5 %collective-permute-done.11 = f32[2,32,128]{2,1,0:T(8,128)S(1)} collective-permute-done((f32[2,32,128]{2,1,0:T(8,128)S(1)}, f32[2,32,128]{2,1,0:T(8,128)S(1)}, u32[]{:S(2)}, u32[]{:S(2)}) %collective-permute-start.11) | collective-permute-done | bytes 32800 | tf_op jit(solution)/shard_map/ppermute | solution.py:698
  45.8 1.0 %collective-permute-done.12 = f32[2,32,128]{2,1,0:T(8,128)S(1)} collective-permute-done((f32[2,32,128]{2,1,0:T(8,128)S(1)}, f32[2,32,128]{2,1,0:T(8,128)S(1)}, u32[]{:S(2)}, u32[]{:S(2)}) %collective-permute-start.12) | collective-permute-done | bytes 32800 | tf_op jit(solution)/shard_map/ppermute | solution.py:698
  46.8 0.6 %add_add_fusion = f32[2,32,128]{2,1,0:T(8,128)} fusion(f32[2,32,128]{2,1,0:T(8,128)S(1)} %collective-permute-done.11, f32[2,32,128]{2,1,0:T(8,128)S(1)} %collective-permute-done.12, f32[2,32,128]{2,1,0:T(8,128)S(1)} %get-tuple-element.63, f32[2,96,128]{2,1,0:T(8,128)S(1)} %collective-permute-done.10), kind=kLoop, calls=%fused_computation.9 | loop fusion | flops 24576 | bytes 163840 | tf_op jit(solution)/shard_map/add | solution.py:705
  (25 shorter events, 0.2 us)
Async XLA Ops:
  0.6 25.3 %copy-start = (f32[2,2,64,128]{3,2,1,0:T(8,128)S(1)}, f32[2,2,64,128]{3,2,1,0:T(8,128)}, u32[]{:S(2)}) copy-start(f32[2,2,64,128]{3,2,1,0:T(8,128)} %state_ref.1) | copy-start | bytes 393220
  0.6 7.4 %collective-permute-start = (f32[2,64,128]{2,1,0:T(8,128)}, f32[2,64,128]{2,1,0:T(8,128)S(1)}, u32[]{:S(2)}, u32[]{:S(2)}) collective-permute-start(f32[2,64,128]{2,1,0:T(8,128)} %kappa_ref.1), channel_id=1, source_target_pairs={{0,8},{1,3},{2,10},{3,1},{4,12},{5,7},{6,14},{7,5},{8,0},{9,11},{1... | collective-permute-start | bytes 196616 | tf_op jit(solution)/shard_map/ppermute | solution.py:123
  4.7 4.5 %collective-permute-start.1 = (f32[2,64,128]{2,1,0:T(8,128)}, f32[2,64,128]{2,1,0:T(8,128)S(1)}, u32[]{:S(2)}, u32[]{:S(2)}) collective-permute-start(f32[2,64,128]{2,1,0:T(8,128)} %misfit_ref.1), channel_id=1, source_target_pairs={{0,2},{1,9},{2,0},{3,11},{4,6},{5,13},{6,4},{7,15},{8,10},{9,1},{1... | collective-permute-start | bytes 196616 | tf_op jit(solution)/shard_map/ppermute | solution.py:123
  6.2 0.8 %copy-start.1 = (f32[2,64,128]{2,1,0:T(8,128)S(1)}, f32[2,64,128]{2,1,0:T(8,128)}, u32[]{:S(2)}) copy-start(f32[2,64,128]{2,1,0:T(8,128)} %kappa_ref.1) | copy-start | bytes 196612
  7.1 0.8 %copy-start.2 = (f32[2,64,128]{2,1,0:T(8,128)S(1)}, f32[2,64,128]{2,1,0:T(8,128)}, u32[]{:S(2)}) copy-start(f32[2,64,128]{2,1,0:T(8,128)} %misfit_ref.1) | copy-start | bytes 196612
  9.9 20.4 %copy-start.3 = (s32[2]{0:T(128)S(1)}, s32[2]{0:T(128)}, u32[]{:S(2)}) copy-start(s32[2]{0:T(128)} %order_ref.3) | copy-start | bytes 28
  9.9 20.4 %copy-start.4 = (f32[4]{0:T(128)S(1)}, f32[4]{0:T(128)}, u32[]{:S(2)}) copy-start(f32[4]{0:T(128)} %shifts_ref.1) | copy-start | bytes 52
  9.9 5.4 %collective-permute-start.2 = (f32[2,2,64,128]{3,2,1,0:T(8,128)S(1)}, f32[2,2,64,128]{3,2,1,0:T(8,128)S(1)}, u32[]{:S(2)}, u32[]{:S(2)}) collective-permute-start(f32[2,2,64,128]{3,2,1,0:T(8,128)S(1)} %get-tuple-element.36), channel_id=1, source_target_pairs={{0,4},{1,9},{2,6},{3,11},{4,0},{5,13},{6,2},{7,15},{8,12},{9,1},{1... | collective-permute-start | bytes 393224 | tf_op jit(solution)/shard_map/ppermute | solution.py:123
  15.3 6.4 %collective-permute-start.3 = (f32[4,2,64,128]{3,2,1,0:T(8,128)S(1)}, f32[4,2,64,128]{3,2,1,0:T(8,128)S(1)}, u32[]{:S(2)}, u32[]{:S(2)}) collective-permute-start(f32[4,2,64,128]{3,2,1,0:T(8,128)S(1)} %pad_maximum_fusion.1), channel_id=1, source_target_pairs={{0,2},{1,5},{2,0},{3,7},{4,6},{5,1},{6,4},{7,3},{8,10},{9,13},{10,... | collective-permute-start | bytes 786440 | tf_op jit(solution)/shard_map/ppermute | solution.py:123
  16.5 6.3 %collective-permute-start.5 = (f32[2,2,64,128]{3,2,1,0:T(8,128)S(1)}, f32[2,2,64,128]{3,2,1,0:T(8,128)S(1)}, u32[]{:S(2)}, u32[]{:S(2)}) collective-permute-start(f32[2,2,64,128]{3,2,1,0:T(8,128)S(1)} %get-tuple-element.47), channel_id=1, source_target_pairs={{0,8},{1,5},{2,10},{3,7},{4,12},{5,1},{6,14},{7,3},{8,0},{9,13},{1... | collective-permute-start | bytes 393224 | tf_op jit(solution)/shard_map/ppermute | solution.py:123
  21.8 8.5 %collective-permute-start.4 = (f32[8,2,64,128]{3,2,1,0:T(8,128)S(1)}, f32[8,2,64,128]{3,2,1,0:T(8,128)S(1)}, u32[]{:S(2)}, u32[]{:S(2)}) collective-permute-start(f32[8,2,64,128]{3,2,1,0:T(8,128)S(1)} %constant_dynamic-update-slice_fusion.mine_ref), channel_id=1, source_target_pairs={{0,1},{1,0},{2,3},{3,2},{4,5},{5,4},{6,7},{7,6},{8,9},{9,8},{10,11... | collective-permute-start | bytes 1572872 | tf_op jit(solution)/shard_map/ppermute | solution.py:141
  22.9 11.5 %copy-start.5 = (f32[4]{0:T(128)S(1)}, f32[4]{0:T(128)}, u32[]{:S(2)}) copy-start(f32[4]{0:T(128)} %weights_ref.1) | copy-start | bytes 52
  22.9 7.4 %collective-permute-start.6 = (f32[4,2,64,128]{3,2,1,0:T(8,128)S(1)}, f32[4,2,64,128]{3,2,1,0:T(8,128)S(1)}, u32[]{:S(2)}, u32[]{:S(2)}) collective-permute-start(f32[4,2,64,128]{3,2,1,0:T(8,128)S(1)} %pad_maximum_fusion.2), channel_id=1, source_target_pairs={{0,4},{1,3},{2,6},{3,1},{4,0},{5,7},{6,2},{7,5},{8,12},{9,11},{10,... | collective-permute-start | bytes 786440 | tf_op jit(solution)/shard_map/ppermute | solution.py:123
  25.9 6.3 %collective-permute-start.7 = (f32[2,1,64,128]{3,2,1,0:T(8,128)S(1)}, f32[2,1,64,128]{3,2,1,0:T(8,128)S(1)}, u32[]{:S(2)}, u32[]{:S(2)}) collective-permute-start(f32[2,1,64,128]{3,2,1,0:T(8,128)S(1)} %slice_select_fusion.1), channel_id=1, source_target_pairs={{1,2},{2,1},{3,4},{4,3},{5,6},{6,5},{7,8},{8,7},{9,10},{10,9},{11,... | collective-permute-start | bytes 196616 | tf_op jit(solution)/shard_map/ppermute | solution.py:138
  32.2 2.1 %collective-permute-start.8 = (f32[8,2,64,128]{3,2,1,0:T(8,128)S(1)}, f32[8,2,64,128]{3,2,1,0:T(8,128)S(1)}, u32[]{:S(2)}, u32[]{:S(2)}) collective-permute-start(f32[8,2,64,128]{3,2,1,0:T(8,128)S(1)} %pad_maximum_fusion.mine_ref), channel_id=1, source_target_pairs={{0,1},{1,0},{2,3},{3,2},{4,5},{5,4},{6,7},{7,6},{8,9},{9,8},{10,11... | collective-permute-start | bytes 1572872 | tf_op jit(solution)/shard_map/ppermute | solution.py:141
  32.4 2.0 %collective-permute-start.9 = (f32[3,64,128]{2,1,0:T(8,128)S(1)}, f32[3,64,128]{2,1,0:T(8,128)S(1)}, u32[]{:S(2)}, u32[]{:S(2)}) collective-permute-start(f32[3,64,128]{2,1,0:T(8,128)S(1)} %fusion), channel_id=1, source_target_pairs={{0,1},{1,0},{2,3},{3,2},{4,5},{5,4},{6,7},{7,6},{8,9},{9,8},{10,11... | collective-permute-start | bytes 294920 | tf_op jit(solution)/shard_map/ppermute | solution.py:140
  41.7 1.9 %collective-permute-start.10 = (f32[2,96,128]{2,1,0:T(8,128)S(1)}, f32[2,96,128]{2,1,0:T(8,128)S(1)}, u32[]{:S(2)}, u32[]{:S(2)}) collective-permute-start(f32[2,96,128]{2,1,0:T(8,128)S(1)} %get-tuple-element.61), channel_id=1, source_target_pairs={{0,1},{1,0},{2,3},{3,2},{4,5},{5,4},{6,7},{7,6},{8,9},{9,8},{10,11... | collective-permute-start | bytes 294920 | tf_op jit(solution)/shard_map/ppermute | solution.py:689
  41.9 3.9 %collective-permute-start.11 = (f32[2,32,128]{2,1,0:T(8,128)S(1)}, f32[2,32,128]{2,1,0:T(8,128)S(1)}, u32[]{:S(2)}, u32[]{:S(2)}) collective-permute-start(f32[2,32,128]{2,1,0:T(8,128)S(1)} %get-tuple-element.69), channel_id=1, source_target_pairs={{0,16},{1,17},{2,18},{3,19},{4,20},{5,21},{6,22},{7,23},{8,24},{9,... | collective-permute-start | bytes 98312 | tf_op jit(solution)/shard_map/ppermute | solution.py:698
  43.4 3.4 %collective-permute-start.12 = (f32[2,32,128]{2,1,0:T(8,128)S(1)}, f32[2,32,128]{2,1,0:T(8,128)S(1)}, u32[]{:S(2)}, u32[]{:S(2)}) collective-permute-start(f32[2,32,128]{2,1,0:T(8,128)S(1)} %get-tuple-element.68), channel_id=1, source_target_pairs={{0,17},{1,16},{2,19},{3,18},{4,21},{5,20},{6,23},{7,22},{8,25},{9,... | collective-permute-start | bytes 98312 | tf_op jit(solution)/shard_map/ppermute | solution.py:698

commit v13 on v11

--- a/solution.py
+++ b/solution.py
@@ -9,10 +9,11 @@
 
 ITERS = 2
 DAMPING = 0.8
+KEPT = 2.0 - DAMPING
 REPLICATED_CELLS = 32 * 64 * 128
 HALF = 64
 TILE = 8
-UNROLL = 2
+UNROLL = 8
 
 
 def extended(array, sides, width):
@@ -83,9 +84,11 @@
     return first, second, home
 
 
-def prepare_kernel(kappa_ref, misfit_ref, kappa_out, misfit_out):
-    kappa_out[...] = kappa_ref[...]
-    misfit_out[...] = misfit_ref[...]
+def prepare_kernel(place_ref, kappa_ref, misfit_ref, kappa_out, misfit_out, *, peers):
+    at_ = Layout(kappa_ref.shape[1] // 2)
+    upper = jnp.where(place_ref[0] >= peers // 2, 1, 0)
+    at_.deal(kappa_ref, kappa_out, upper)
+    at_.deal(misfit_ref, misfit_out, upper)
 
 
 def join_kernel(place_ref, *refs, masks, peers):
@@ -93,8 +96,8 @@
     at_ = Layout(refs[0].shape[1] // 2)
     for at, (even, odd) in enumerate(masks):
         partner = place ^ jnp.where(place % 2 == 0, even, odd)
-        for t, (ref, holder) in enumerate(((refs[at], place), (refs[2 + at], partner))):
-            at_.deal(ref, refs[4 + at].at[t], jnp.where(holder >= peers // 2, 1, 0))
+        refs[4 + at][0] = refs[at][...]
+        at_.deal(refs[2 + at], refs[4 + at].at[1], jnp.where(partner >= peers // 2, 1, 0))
 
 
 def gather_blocks(place, blocks, states, axis):
@@ -106,13 +109,13 @@
     vmem = pl.BlockSpec(memory_space=pltpu.VMEM)
     swaps = [list(zip(*swap_masks(peers, flip))) for flip in (False, True)]
     own = pl.pallas_call(
-        prepare_kernel,
+        functools.partial(prepare_kernel, peers=peers),
         out_shape=[jax.ShapeDtypeStruct(block.shape, jnp.float32) for block in blocks],
-        in_specs=[vmem] * 2,
+        in_specs=[smem] + [vmem] * 2,
         out_specs=[vmem] * 2,
         compiler_params=pltpu.CompilerParams(vmem_limit_bytes=1024 * 1024),
         name="prepare",
-    )(*blocks)
+    )(place, *blocks)
     held = list(blocks)
     for step in range(len(swaps[0])):
         arrived = []
@@ -315,13 +318,13 @@
                 base = within + without + shift
                 diagonal[k, i, tile(j)] = base
                 coarse_total.append(without)
-                damped[k, i, tile(j)] = DAMPING * inverse(base)
+                damped[k, i, tile(j)] = (DAMPING / KEPT) * inverse(base)
             for at, part in enumerate(off):
                 coarse_off[at, i, tile(j)] = tree_sum(part)
             coarse_damped[i, tile(j)] = DAMPING * inverse(tree_sum(coarse_total) + 8.0 * shift)
         return carry
 
-    lax.fori_loop(0, half, plane, 0)
+    lax.fori_loop(0, half, plane, 0, unroll=UNROLL)
     for j in range(tiles):
         part = []
         for p, q in PAIRS:
@@ -371,7 +374,7 @@
     weight = weights_ref[order_ref[core]]
 
     def begin(k, spot, j, value):
-        res = weight * value
+        res = (KEPT * weight) * value
         residual[k, spot, tile(j)] = res
         scaled[k, spot + 1, tile(j)] = damped[k, spot, tile(j)] * res
 
@@ -438,14 +441,14 @@
             (roll(here, 1, 1), roll(here, -1, 1)),
         )
 
-    def precondition(result, other):
+    def precondition(result):
         def down(i, carry):
             for j, _, sums in stencil(scaled, i, True):
                 res = [residual[k, i, tile(j)] for k in range(8)]
-                parts = [(2.0 - DAMPING) * res[k] + sums[k] for k in range(8)]
+                parts = [res[k] + sums[k] for k in range(8)]
                 for k in range(8):
                     partial[k, i, tile(j)] = parts[k]
-                rhs = tree_sum(parts) - tree_sum(res)
+                rhs = tree_sum(parts) - (1.0 / KEPT) * tree_sum(res)
                 coarse_one[0, i + 1, tile(j)] = coarse_damped[i, tile(j)] * rhs
             return carry
 
@@ -461,7 +464,7 @@
                 more = more + coarse_off[2, i, tile(j)] * sides[1][1]
                 most = coarse_off[3, i, tile(j)] * sides[2][0]
                 most = most + coarse_off[4, i, tile(j)] * sides[2][1]
-                coarse_two[0, i + 1, tile(j)] = (2.0 - DAMPING) * here + coarse_damped[
+                coarse_two[0, i + 1, tile(j)] = KEPT * here + coarse_damped[
                     i, tile(j)
                 ] * (total + more + most)
             return carry
@@ -469,13 +472,12 @@
         lax.fori_loop(0, half, smooth, 0, unroll=UNROLL)
         at_.seam(coarse_two, [0], [0])
 
-        def up(i, carry):
-            gamma, cross = carry
+        def up(i, gamma):
             face_get, _, face_after = rows_of(outer_y, i)
             for j in range(tiles):
                 here, sides = coarse_sides(coarse_two, i, j)
-                kept = (1.0 - DAMPING) * here
-                dots, crosses = [], []
+                kept = ((1.0 - DAMPING) / KEPT) * here
+                dots = []
                 for a, b, c in CLASSES:
                     k = cls(a, b, c)
                     value = tree_sum(
@@ -490,18 +492,14 @@
                     new = kept + damped[k, i, tile(j)] * value
                     result[k, i + 1, tile(j)] = new
                     dots.append(residual[k, i, tile(j)] * new)
-                    if other is not None:
-                        crosses.append(other[k, i, tile(j)] * new)
                 gamma = gamma + tree_sum(dots)
-                if other is not None:
-                    cross = cross + tree_sum(crosses)
-            return gamma, cross
-
-        sums = lax.fori_loop(0, half, up, (zero, zero), unroll=UNROLL)
+            return gamma
+
+        gamma = lax.fori_loop(0, half, up, zero, unroll=UNROLL)
         at_.seam_fine(result)
-        return [grand_total(part) for part in sums]
-
-    gamma, _ = precondition(first_dir, None)
+        return grand_total(gamma)
+
+    gamma = precondition(first_dir)
 
     def apply(i, acc):
         for j, here, sums in stencil(first_dir, i, True):
@@ -527,7 +525,7 @@
     lax.fori_loop(0, half, update, 0, unroll=UNROLL)
     at_.seam_fine(scaled)
 
-    gamma_next, cross = precondition(second_dir, image)
+    gamma_next = precondition(second_dir)
 
     def bend(i, carry):
         own_part, face_part = carry
@@ -541,8 +539,9 @@
     own_part, face_part = lax.fori_loop(0, half, bend, (zero, zero), unroll=UNROLL)
     ratio = gamma_next / gamma
     curve_next = grand_total(own_part - 2.0 * face_part)
-    step_two = gamma_next / (curve_next + ratio * (2.0 * cross + ratio * curve))
-    step_first = step_one + step_two * ratio
+    step_two = gamma_next / (curve_next - ratio * ratio * curve)
+    step_first = (step_one + step_two * ratio) * (1.0 / KEPT)
+    step_two = step_two * (1.0 / KEPT)
 
     own, ny, nz = adjoint_ref.shape
     start = (place_ref[0] - core) * (own // 2)

time: 44.8 us -> 43.3 us (0.967)
  Pallas kernels: 11.2 us -> 10.3 us
  waiting for transfers between devices: 11 us -> 10.3 us
    pallas_call x1, Pallas kernels: 8.23 us -> 7.11 us  [whole_grid(): pl.pallas_call(solve_kernel, out_shape=[jax.ShapeDtypeStruct((own, ny, nz...]
    ppermute x6, waiting for transfers between devices: 8.35 us -> 7.72 us  [gather_blocks(): arrived.append(lax.ppermute(held[at], axis, pairs))]
    pallas_call x1, Pallas kernels: 0.01 us -> 0.64 us  [gather_blocks(): pl.pallas_call(functools.partial(prepare_kernel, peers=peers), out_shape=...]
  transfers between devices with their start and end apart: 13 -> 13, of which waited for: 7 -> 7; matrix products, arithmetic and copies ran while one was open for 4% -> 4% of each run, Pallas kernels for 5% -> 6%
where the time goes in v13:
time: 43.3 us; the launch traced here: 43 us
  starting transfers between devices  17.4 us (40%)
  Pallas kernels  10.3 us (24%)
  waiting for transfers between devices  10.3 us (24%)
  other arithmetic  2.35 us (5%)
  local copies, waits for them, and re-layouts  1.76 us (4%)
  between operations  0.82 us (2%)
    ppermute x6, starting transfers between devices, gather_blocks(): arrived.append(lax.ppermute(held[at], axis, pairs))  12 us
    ppermute x6, waiting for transfers between devices, gather_blocks(): arrived.append(lax.ppermute(held[at], axis, pairs))  7.72 us
    pallas_call x1, Pallas kernels, whole_grid(): pl.pallas_call(solve_kernel, out_shape=[jax.ShapeDtypeStruct((own, ny, nz...  7.11 us
    ppermute x2, waiting for transfers between devices, whole_grid(): shares.append(lax.ppermute(send[k - 1, side], ('pole', 'space'), pairs))  2.59 us
    ppermute x2, starting transfers between devices, gather_blocks(): other = [lax.ppermute(part, axis, swap) for part in held]  2.29 us
    pallas_call x1, Pallas kernels, whole_grid(): pl.pallas_call(setup_kernel, out_shape=[jax.ShapeDtypeStruct(shape, jnp.f...  1.9 us
    ppermute x2, starting transfers between devices, whole_grid(): shares.append(lax.ppermute(send[k - 1, side], ('pole', 'space'), pairs))  1.84 us
    unnamed x15, local copies, waits for them, and re-layouts  1.73 us
  transfers between devices with their start and end apart: 13, of which 7 were waited for; matrix products, arithmetic and copies ran while one was open for 4% of the time, Pallas kernels for 6%

profile of v13, /device:TPU:0, one launch (start us, length us, event | category | flops | bytes accessed | tf_op | source)
XLA Modules:
  0.0 43.0 jit_solution(18360588304259395181)
XLA Ops:
  0.6 4.1 %collective-permute-start = (f32[2,64,128]{2,1,0:T(8,128)}, f32[2,64,128]{2,1,0:T(8,128)S(1)}, u32[]{:S(2)}, u32[]{:S(2)}) collective-permute-start(f32[2,64,128]{2,1,0:T(8,128)} %kappa_ref.1), channel_id=1, source_target_pairs={{0,8},{1,3},{2,10},{3,1},{4,12},{5,7},{6,14},{7,5},{8,0},{9,11},{1... | collective-permute-start | bytes 196616 | tf_op jit(solution)/shard_map/ppermute | solution.py:125
  4.7 1.5 %collective-permute-start.1 = (f32[2,64,128]{2,1,0:T(8,128)}, f32[2,64,128]{2,1,0:T(8,128)S(1)}, u32[]{:S(2)}, u32[]{:S(2)}) collective-permute-start(f32[2,64,128]{2,1,0:T(8,128)} %misfit_ref.1), channel_id=1, source_target_pairs={{0,2},{1,9},{2,0},{3,11},{4,6},{5,13},{6,4},{7,15},{8,10},{9,1},{1... | collective-permute-start | bytes 196616 | tf_op jit(solution)/shard_map/ppermute | solution.py:125
  6.2 0.1 pad_add_fusion.place_ref
  6.3 0.8 %copy-done.1 = f32[2,64,128]{2,1,0:T(8,128)S(1)} copy-done((f32[2,64,128]{2,1,0:T(8,128)S(1)}, f32[2,64,128]{2,1,0:T(8,128)}, u32[]{:S(2)}) %copy-start.1) | copy-done | bytes 65560
  7.1 0.8 %copy-done.2 = f32[2,64,128]{2,1,0:T(8,128)S(1)} copy-done((f32[2,64,128]{2,1,0:T(8,128)S(1)}, f32[2,64,128]{2,1,0:T(8,128)}, u32[]{:S(2)}) %copy-start.2) | copy-done | bytes 65560
  8.0 0.6 %prepare.1 = (f32[2,64,128]{2,1,0:T(8,128)S(1)}, f32[2,64,128]{2,1,0:T(8,128)S(1)}) custom-call(s32[2]{0:T(128)S(1)} %pad_add_fusion.place_ref, f32[2,64,128]{2,1,0:T(8,128)S(1)} %copy-done.1, f32[2,64,128]{2,1,0:T(8,128)S(1)} %copy-done.2), custom_call_target="tpu_custom_call" | custom-call | tf_op jit(solution)/shard_map/prepare/pallas_call | solution.py:111
  8.6 0.6 %collective-permute-done.1.refs_3_ = f32[2,64,128]{2,1,0:T(8,128)S(1)} collective-permute-done((f32[2,64,128]{2,1,0:T(8,128)}, f32[2,64,128]{2,1,0:T(8,128)S(1)}, u32[]{:S(2)}, u32[]{:S(2)}) %collective-permute-start.1) | collective-permute-done | bytes 65568 | tf_op jit(solution)/shard_map/ppermute | solution.py:125
  9.2 0.6 %join.1 = (f32[2,2,64,128]{3,2,1,0:T(8,128)S(1)}, f32[2,2,64,128]{3,2,1,0:T(8,128)S(1)}) custom-call(s32[2]{0:T(128)S(1)} %pad_add_fusion.place_ref, f32[2,64,128]{2,1,0:T(8,128)S(1)} %get-tuple-element.25.refs_0_, f32[2,64,128]{2,1,0:T(8,128)S(1)} %get-tuple-element.26.refs_1_, f32[2,64,128]{2,1,0:T(8,128)S(1)} %collective-permute-done.refs_2_, ...), custom_call_target="tpu_custom_call" | custom-call | tf_op jit(solution)/shard_map/join/pallas_call | solution.py:131
  9.9 1.6 %collective-permute-start.7 = (f32[2,2,64,128]{3,2,1,0:T(8,128)S(1)}, f32[2,2,64,128]{3,2,1,0:T(8,128)S(1)}, u32[]{:S(2)}, u32[]{:S(2)}) collective-permute-start(f32[2,2,64,128]{3,2,1,0:T(8,128)S(1)} %get-tuple-element.32), channel_id=1, source_target_pairs={{0,4},{1,9},{2,6},{3,11},{4,0},{5,13},{6,2},{7,15},{8,12},{9,1},{1... | collective-permute-start | bytes 393224 | tf_op jit(solution)/shard_map/ppermute | solution.py:125
  11.5 0.4 %collective-permute-start.2 = (f32[2,2,64,128]{3,2,1,0:T(8,128)S(1)}, f32[2,2,64,128]{3,2,1,0:T(8,128)S(1)}, u32[]{:S(2)}, u32[]{:S(2)}) collective-permute-start(f32[2,2,64,128]{3,2,1,0:T(8,128)S(1)} %get-tuple-element.28), channel_id=1, source_target_pairs={{0,4},{1,3},{2,6},{3,1},{4,0},{5,7},{6,2},{7,5},{8,12},{9,11},{10,... | collective-permute-start | bytes 393224 | tf_op jit(solution)/shard_map/ppermute | solution.py:125
  12.0 0.9 %slice_select_fusion.1 = f32[2,1,64,128]{3,2,1,0:T(8,128)S(1)} fusion(f32[2,2,64,128]{3,2,1,0:T(8,128)} %state_ref.1, pred[]{:T(512)S(6)} %eq.7), kind=kLoop, calls=%fused_computation.8 | loop fusion | flops 16384 | bytes 196609 | tf_op jit(solution)/shard_map/jit(_where)/select_n | solution.py:140
  12.8 0.0 copy-start
  12.8 2.4 %collective-permute-done.7 = f32[2,2,64,128]{3,2,1,0:T(8,128)S(1)} collective-permute-done((f32[2,2,64,128]{3,2,1,0:T(8,128)S(1)}, f32[2,2,64,128]{3,2,1,0:T(8,128)S(1)}, u32[]{:S(2)}, u32[]{:S(2)}) %collective-permute-start.7) | collective-permute-done | bytes 131104 | tf_op jit(solution)/shard_map/ppermute | solution.py:125
  15.3 0.0 copy-start.4
  15.3 1.2 %collective-permute-start.8 = (f32[4,2,64,128]{3,2,1,0:T(8,128)S(1)}, f32[4,2,64,128]{3,2,1,0:T(8,128)S(1)}, u32[]{:S(2)}, u32[]{:S(2)}) collective-permute-start(f32[4,2,64,128]{3,2,1,0:T(8,128)S(1)} %pad_maximum_fusion.2), channel_id=1, source_target_pairs={{0,2},{1,5},{2,0},{3,7},{4,6},{5,1},{6,4},{7,3},{8,10},{9,13},{10,... | collective-permute-start | bytes 786440 | tf_op jit(solution)/shard_map/ppermute | solution.py:125
  16.5 0.1 collective-permute-done.2
  16.7 3.1 %collective-permute-start.3 = (f32[4,2,64,128]{3,2,1,0:T(8,128)S(1)}, f32[4,2,64,128]{3,2,1,0:T(8,128)S(1)}, u32[]{:S(2)}, u32[]{:S(2)}) collective-permute-start(f32[4,2,64,128]{3,2,1,0:T(8,128)S(1)} %pad_maximum_fusion.1), channel_id=1, source_target_pairs={{0,8},{1,5},{2,10},{3,7},{4,12},{5,1},{6,14},{7,3},{8,0},{9,13},{1... | collective-permute-start | bytes 786440 | tf_op jit(solution)/shard_map/ppermute | solution.py:125
  19.8 0.7 %collective-permute-start.4 = (f32[2,1,64,128]{3,2,1,0:T(8,128)S(1)}, f32[2,1,64,128]{3,2,1,0:T(8,128)S(1)}, u32[]{:S(2)}, u32[]{:S(2)}) collective-permute-start(f32[2,1,64,128]{3,2,1,0:T(8,128)S(1)} %slice_select_fusion.1), channel_id=1, source_target_pairs={{1,2},{2,1},{3,4},{4,3},{5,6},{6,5},{7,8},{8,7},{9,10},{10,9},{11,... | collective-permute-start | bytes 196616 | tf_op jit(solution)/shard_map/ppermute | solution.py:140
  20.5 1.2 %collective-permute-done.8 = f32[4,2,64,128]{3,2,1,0:T(8,128)S(1)} collective-permute-done((f32[4,2,64,128]{3,2,1,0:T(8,128)S(1)}, f32[4,2,64,128]{3,2,1,0:T(8,128)S(1)}, u32[]{:S(2)}, u32[]{:S(2)}) %collective-permute-start.8) | collective-permute-done | bytes 262176 | tf_op jit(solution)/shard_map/ppermute | solution.py:125
  21.7 1.0 %collective-permute-start.9 = (f32[8,2,64,128]{3,2,1,0:T(8,128)S(1)}, f32[8,2,64,128]{3,2,1,0:T(8,128)S(1)}, u32[]{:S(2)}, u32[]{:S(2)}) collective-permute-start(f32[8,2,64,128]{3,2,1,0:T(8,128)S(1)} %constant_dynamic-update-slice_fusion.2.mine_ref), channel_id=1, source_target_pairs={{0,1},{1,0},{2,3},{3,2},{4,5},{5,4},{6,7},{7,6},{8,9},{9,8},{10,11... | collective-permute-start | bytes 1572872 | tf_op jit(solution)/shard_map/ppermute | solution.py:144
  22.7 3.4 %collective-permute-done.3 = f32[4,2,64,128]{3,2,1,0:T(8,128)S(1)} collective-permute-done((f32[4,2,64,128]{3,2,1,0:T(8,128)S(1)}, f32[4,2,64,128]{3,2,1,0:T(8,128)S(1)}, u32[]{:S(2)}, u32[]{:S(2)}) %collective-permute-start.3) | collective-permute-done | bytes 262176 | tf_op jit(solution)/shard_map/ppermute | solution.py:125
  26.2 1.3 %collective-permute-start.5 = (f32[8,2,64,128]{3,2,1,0:T(8,128)S(1)}, f32[8,2,64,128]{3,2,1,0:T(8,128)S(1)}, u32[]{:S(2)}, u32[]{:S(2)}) collective-permute-start(f32[8,2,64,128]{3,2,1,0:T(8,128)S(1)} %pad_maximum_fusion.mine_ref), channel_id=1, source_target_pairs={{0,1},{1,0},{2,3},{3,2},{4,5},{5,4},{6,7},{7,6},{8,9},{9,8},{10,11... | collective-permute-start | bytes 1572872 | tf_op jit(solution)/shard_map/ppermute | solution.py:144
  27.6 0.1 collective-permute-start.6
  27.7 1.9 %setup.1 = (f32[12,8,32,128]{3,2,1,0:T(8,128)S(1)}, f32[4,9,32,128]{3,2,1,0:T(8,128)S(1)}, f32[4,8,32,128]{3,2,1,0:T(8,128)S(1)}, f32[8,8,32,128]{3,2,1,0:T(8,12...) custom-call(s32[2]{0:T(128)S(1)} %pad_add_fusion.place_ref, ...), custom_call_target="tpu_custom_call" | custom-call | tf_op jit(solution)/shard_map/setup/pallas_call | solution.py:640
  29.6 7.1 %solve.1 = (f32[2,64,128]{2,1,0:T(8,128)S(1)}, f32[2,32,128]{2,1,0:T(8,128)S(1)}, f32[2,96,128]{2,1,0:T(8,128)S(1)}, f32[1,2,2,32,128]{4,3,2,1,0:T(8,128)S(1)}) custom-call(s32[2]{0:T(128)S(1)} %pad_add_fusion.place_ref, f32[4]{0:T(128)S(1)} %copy-done.5, s32[2]{0:T(128)S(1)} %copy-done.3, f32[8,2,64,128]{3,2,1,0:T(8,128)S(1)} %pad_maximum_fusion.mine_ref, ...), custom_call_target="tpu_custom_call" | custom-call | tf_op jit(solution)/shard_map/solve/pallas_call | solution.py:650
  36.7 0.5 %collective-permute-start.10 = (f32[2,96,128]{2,1,0:T(8,128)S(1)}, f32[2,96,128]{2,1,0:T(8,128)S(1)}, u32[]{:S(2)}, u32[]{:S(2)}) collective-permute-start(f32[2,96,128]{2,1,0:T(8,128)S(1)} %get-tuple-element.43), channel_id=1, source_target_pairs={{0,1},{1,0},{2,3},{3,2},{4,5},{5,4},{6,7},{7,6},{8,9},{9,8},{10,11... | collective-permute-start | bytes 294920 | tf_op jit(solution)/shard_map/ppermute | solution.py:685
  37.3 1.8 %collective-permute-start.11 = (f32[2,32,128]{2,1,0:T(8,128)S(1)}, f32[2,32,128]{2,1,0:T(8,128)S(1)}, u32[]{:S(2)}, u32[]{:S(2)}) collective-permute-start(f32[2,32,128]{2,1,0:T(8,128)S(1)} %get-tuple-element.51), channel_id=1, source_target_pairs={{0,16},{1,17},{2,18},{3,19},{4,20},{5,21},{6,22},{7,23},{8,24},{9,... | collective-permute-start | bytes 98312 | tf_op jit(solution)/shard_map/ppermute | solution.py:694
  39.0 0.1 collective-permute-start.12
  39.1 0.7 %pad_maximum_fusion.3 = f32[2,2,64,128]{3,2,1,0:T(8,128)} fusion(f32[1,2,64,128]{3,2,1,0:T(8,128)S(1)} %get-tuple-element.49, f32[1,2,64,128]{3,2,1,0:T(8,128)S(1)} %get-tuple-element.48), kind=kLoop, calls=%fused_computation.3 | loop fusion | flops 32768 | bytes 262144 | tf_op jit(solution)/shard_map/stack | solution.py:697
  39.8 1.4 %collective-permute-done.11 = f32[2,32,128]{2,1,0:T(8,128)S(1)} collective-permute-done((f32[2,32,128]{2,1,0:T(8,128)S(1)}, f32[2,32,128]{2,1,0:T(8,128)S(1)}, u32[]{:S(2)}, u32[]{:S(2)}) %collective-permute-start.11) | collective-permute-done | bytes 32800 | tf_op jit(solution)/shard_map/ppermute | solution.py:694
  41.2 1.2 %collective-permute-done.12 = f32[2,32,128]{2,1,0:T(8,128)S(1)} collective-permute-done((f32[2,32,128]{2,1,0:T(8,128)S(1)}, f32[2,32,128]{2,1,0:T(8,128)S(1)}, u32[]{:S(2)}, u32[]{:S(2)}) %collective-permute-start.12) | collective-permute-done | bytes 32800 | tf_op jit(solution)/shard_map/ppermute | solution.py:694
  42.4 0.6 %add_add_fusion = f32[2,32,128]{2,1,0:T(8,128)} fusion(f32[2,32,128]{2,1,0:T(8,128)S(1)} %collective-permute-done.11, f32[2,32,128]{2,1,0:T(8,128)S(1)} %collective-permute-done.12, f32[2,32,128]{2,1,0:T(8,128)S(1)} %get-tuple-element.45, f32[2,96,128]{2,1,0:T(8,128)S(1)} %collective-permute-done.10), kind=kLoop, calls=%fused_computation.9 | loop fusion | flops 24576 | bytes 163840 | tf_op jit(solution)/shard_map/add | solution.py:701
  (25 shorter events, 0.2 us)
Async XLA Ops:
  0.6 8.0 %collective-permute-start = (f32[2,64,128]{2,1,0:T(8,128)}, f32[2,64,128]{2,1,0:T(8,128)S(1)}, u32[]{:S(2)}, u32[]{:S(2)}) collective-permute-start(f32[2,64,128]{2,1,0:T(8,128)} %kappa_ref.1), channel_id=1, source_target_pairs={{0,8},{1,3},{2,10},{3,1},{4,12},{5,7},{6,14},{7,5},{8,0},{9,11},{1... | collective-permute-start | bytes 196616 | tf_op jit(solution)/shard_map/ppermute | solution.py:125
  4.7 4.5 %collective-permute-start.1 = (f32[2,64,128]{2,1,0:T(8,128)}, f32[2,64,128]{2,1,0:T(8,128)S(1)}, u32[]{:S(2)}, u32[]{:S(2)}) collective-permute-start(f32[2,64,128]{2,1,0:T(8,128)} %misfit_ref.1), channel_id=1, source_target_pairs={{0,2},{1,9},{2,0},{3,11},{4,6},{5,13},{6,4},{7,15},{8,10},{9,1},{1... | collective-permute-start | bytes 196616 | tf_op jit(solution)/shard_map/ppermute | solution.py:125
  6.3 0.8 %copy-start.1 = (f32[2,64,128]{2,1,0:T(8,128)S(1)}, f32[2,64,128]{2,1,0:T(8,128)}, u32[]{:S(2)}) copy-start(f32[2,64,128]{2,1,0:T(8,128)} %kappa_ref.1) | copy-start | bytes 196612
  7.1 0.8 %copy-start.2 = (f32[2,64,128]{2,1,0:T(8,128)S(1)}, f32[2,64,128]{2,1,0:T(8,128)}, u32[]{:S(2)}) copy-start(f32[2,64,128]{2,1,0:T(8,128)} %misfit_ref.1) | copy-start | bytes 196612
  9.9 5.4 %collective-permute-start.7 = (f32[2,2,64,128]{3,2,1,0:T(8,128)S(1)}, f32[2,2,64,128]{3,2,1,0:T(8,128)S(1)}, u32[]{:S(2)}, u32[]{:S(2)}) collective-permute-start(f32[2,2,64,128]{3,2,1,0:T(8,128)S(1)} %get-tuple-element.32), channel_id=1, source_target_pairs={{0,4},{1,9},{2,6},{3,11},{4,0},{5,13},{6,2},{7,15},{8,12},{9,1},{1... | collective-permute-start | bytes 393224 | tf_op jit(solution)/shard_map/ppermute | solution.py:125
  11.5 5.1 %collective-permute-start.2 = (f32[2,2,64,128]{3,2,1,0:T(8,128)S(1)}, f32[2,2,64,128]{3,2,1,0:T(8,128)S(1)}, u32[]{:S(2)}, u32[]{:S(2)}) collective-permute-start(f32[2,2,64,128]{3,2,1,0:T(8,128)S(1)} %get-tuple-element.28), channel_id=1, source_target_pairs={{0,4},{1,3},{2,6},{3,1},{4,0},{5,7},{6,2},{7,5},{8,12},{9,11},{10,... | collective-permute-start | bytes 393224 | tf_op jit(solution)/shard_map/ppermute | solution.py:125
  12.8 14.7 %copy-start = (f32[2,2,64,128]{3,2,1,0:T(8,128)S(1)}, f32[2,2,64,128]{3,2,1,0:T(8,128)}, u32[]{:S(2)}) copy-start(f32[2,2,64,128]{3,2,1,0:T(8,128)} %state_ref.1) | copy-start | bytes 393220
  15.2 12.4 %copy-start.3 = (s32[2]{0:T(128)S(1)}, s32[2]{0:T(128)}, u32[]{:S(2)}) copy-start(s32[2]{0:T(128)} %order_ref.3) | copy-start | bytes 28
  15.3 12.4 %copy-start.4 = (f32[4]{0:T(128)S(1)}, f32[4]{0:T(128)}, u32[]{:S(2)}) copy-start(f32[4]{0:T(128)} %shifts_ref.1) | copy-start | bytes 52
  15.3 6.4 %collective-permute-start.8 = (f32[4,2,64,128]{3,2,1,0:T(8,128)S(1)}, f32[4,2,64,128]{3,2,1,0:T(8,128)S(1)}, u32[]{:S(2)}, u32[]{:S(2)}) collective-permute-start(f32[4,2,64,128]{3,2,1,0:T(8,128)S(1)} %pad_maximum_fusion.2), channel_id=1, source_target_pairs={{0,2},{1,5},{2,0},{3,7},{4,6},{5,1},{6,4},{7,3},{8,10},{9,13},{10,... | collective-permute-start | bytes 786440 | tf_op jit(solution)/shard_map/ppermute | solution.py:125
  16.7 9.5 %collective-permute-start.3 = (f32[4,2,64,128]{3,2,1,0:T(8,128)S(1)}, f32[4,2,64,128]{3,2,1,0:T(8,128)S(1)}, u32[]{:S(2)}, u32[]{:S(2)}) collective-permute-start(f32[4,2,64,128]{3,2,1,0:T(8,128)S(1)} %pad_maximum_fusion.1), channel_id=1, source_target_pairs={{0,8},{1,5},{2,10},{3,7},{4,12},{5,1},{6,14},{7,3},{8,0},{9,13},{1... | collective-permute-start | bytes 786440 | tf_op jit(solution)/shard_map/ppermute | solution.py:125
  19.8 6.4 %collective-permute-start.4 = (f32[2,1,64,128]{3,2,1,0:T(8,128)S(1)}, f32[2,1,64,128]{3,2,1,0:T(8,128)S(1)}, u32[]{:S(2)}, u32[]{:S(2)}) collective-permute-start(f32[2,1,64,128]{3,2,1,0:T(8,128)S(1)} %slice_select_fusion.1), channel_id=1, source_target_pairs={{1,2},{2,1},{3,4},{4,3},{5,6},{6,5},{7,8},{8,7},{9,10},{10,9},{11,... | collective-permute-start | bytes 196616 | tf_op jit(solution)/shard_map/ppermute | solution.py:140
  20.5 9.1 %copy-start.5 = (f32[4]{0:T(128)S(1)}, f32[4]{0:T(128)}, u32[]{:S(2)}) copy-start(f32[4]{0:T(128)} %weights_ref.1) | copy-start | bytes 52
  21.7 5.9 %collective-permute-start.9 = (f32[8,2,64,128]{3,2,1,0:T(8,128)S(1)}, f32[8,2,64,128]{3,2,1,0:T(8,128)S(1)}, u32[]{:S(2)}, u32[]{:S(2)}) collective-permute-start(f32[8,2,64,128]{3,2,1,0:T(8,128)S(1)} %constant_dynamic-update-slice_fusion.2.mine_ref), channel_id=1, source_target_pairs={{0,1},{1,0},{2,3},{3,2},{4,5},{5,4},{6,7},{7,6},{8,9},{9,8},{10,11... | collective-permute-start | bytes 1572872 | tf_op jit(solution)/shard_map/ppermute | solution.py:144
  26.2 3.4 %collective-permute-start.5 = (f32[8,2,64,128]{3,2,1,0:T(8,128)S(1)}, f32[8,2,64,128]{3,2,1,0:T(8,128)S(1)}, u32[]{:S(2)}, u32[]{:S(2)}) collective-permute-start(f32[8,2,64,128]{3,2,1,0:T(8,128)S(1)} %pad_maximum_fusion.mine_ref), channel_id=1, source_target_pairs={{0,1},{1,0},{2,3},{3,2},{4,5},{5,4},{6,7},{7,6},{8,9},{9,8},{10,11... | collective-permute-start | bytes 1572872 | tf_op jit(solution)/shard_map/ppermute | solution.py:144
  27.6 2.0 %collective-permute-start.6 = (f32[3,64,128]{2,1,0:T(8,128)S(1)}, f32[3,64,128]{2,1,0:T(8,128)S(1)}, u32[]{:S(2)}, u32[]{:S(2)}) collective-permute-start(f32[3,64,128]{2,1,0:T(8,128)S(1)} %fusion), channel_id=1, source_target_pairs={{0,1},{1,0},{2,3},{3,2},{4,5},{5,4},{6,7},{7,6},{8,9},{9,8},{10,11... | collective-permute-start | bytes 294920 | tf_op jit(solution)/shard_map/ppermute | solution.py:143
  36.7 2.4 %collective-permute-start.10 = (f32[2,96,128]{2,1,0:T(8,128)S(1)}, f32[2,96,128]{2,1,0:T(8,128)S(1)}, u32[]{:S(2)}, u32[]{:S(2)}) collective-permute-start(f32[2,96,128]{2,1,0:T(8,128)S(1)} %get-tuple-element.43), channel_id=1, source_target_pairs={{0,1},{1,0},{2,3},{3,2},{4,5},{5,4},{6,7},{7,6},{8,9},{9,8},{10,11... | collective-permute-start | bytes 294920 | tf_op jit(solution)/shard_map/ppermute | solution.py:685
  37.3 3.9 %collective-permute-start.11 = (f32[2,32,128]{2,1,0:T(8,128)S(1)}, f32[2,32,128]{2,1,0:T(8,128)S(1)}, u32[]{:S(2)}, u32[]{:S(2)}) collective-permute-start(f32[2,32,128]{2,1,0:T(8,128)S(1)} %get-tuple-element.51), channel_id=1, source_target_pairs={{0,16},{1,17},{2,18},{3,19},{4,20},{5,21},{6,22},{7,23},{8,24},{9,... | collective-permute-start | bytes 98312 | tf_op jit(solution)/shard_map/ppermute | solution.py:694
  39.0 3.4 %collective-permute-start.12 = (f32[2,32,128]{2,1,0:T(8,128)S(1)}, f32[2,32,128]{2,1,0:T(8,128)S(1)}, u32[]{:S(2)}, u32[]{:S(2)}) collective-permute-start(f32[2,32,128]{2,1,0:T(8,128)S(1)} %get-tuple-element.50), channel_id=1, source_target_pairs={{0,17},{1,16},{2,19},{3,18},{4,21},{5,20},{6,23},{7,22},{8,25},{9,... | collective-permute-start | bytes 98312 | tf_op jit(solution)/shard_map/ppermute | solution.py:694

commit v14 on v13

--- a/solution.py
+++ b/solution.py
@@ -84,15 +84,15 @@
     return first, second, home
 
 
-def prepare_kernel(place_ref, kappa_ref, misfit_ref, kappa_out, misfit_out, *, peers):
+def prepare_kernel(kappa_ref, misfit_ref, kappa_out, misfit_out, *, axis, peers):
     at_ = Layout(kappa_ref.shape[1] // 2)
-    upper = jnp.where(place_ref[0] >= peers // 2, 1, 0)
+    upper = jnp.where(lax.axis_index(axis) >= peers // 2, 1, 0)
     at_.deal(kappa_ref, kappa_out, upper)
     at_.deal(misfit_ref, misfit_out, upper)
 
 
-def join_kernel(place_ref, *refs, masks, peers):
-    place = place_ref[0]
+def join_kernel(*refs, masks, axis, peers):
+    place = lax.axis_index(axis)
     at_ = Layout(refs[0].shape[1] // 2)
     for at, (even, odd) in enumerate(masks):
         partner = place ^ jnp.where(place % 2 == 0, even, odd)
@@ -100,22 +100,21 @@
         at_.deal(refs[2 + at], refs[4 + at].at[1], jnp.where(partner >= peers // 2, 1, 0))
 
 
-def gather_blocks(place, blocks, states, axis):
+def gather_blocks(blocks, states, axis):
     peers = lax.axis_size(axis)
-    even = place[0] % 2 == 0
+    even = lax.axis_index(axis) % 2 == 0
     swap = [(i, i ^ 1) for i in range(peers)]
     over = [(i, i + 1 if i % 2 else i - 1) for i in range(1, peers - 1)]
-    smem = pl.BlockSpec(memory_space=pltpu.SMEM)
     vmem = pl.BlockSpec(memory_space=pltpu.VMEM)
     swaps = [list(zip(*swap_masks(peers, flip))) for flip in (False, True)]
     own = pl.pallas_call(
-        functools.partial(prepare_kernel, peers=peers),
+        functools.partial(prepare_kernel, axis=axis, peers=peers),
         out_shape=[jax.ShapeDtypeStruct(block.shape, jnp.float32) for block in blocks],
-        in_specs=[smem] + [vmem] * 2,
+        in_specs=[vmem] * 2,
         out_specs=[vmem] * 2,
         compiler_params=pltpu.CompilerParams(vmem_limit_bytes=1024 * 1024),
         name="prepare",
-    )(place, *blocks)
+    )(*blocks)
     held = list(blocks)
     for step in range(len(swaps[0])):
         arrived = []
@@ -129,13 +128,13 @@
         masks = [swaps[at][0] for at in (0, 1)]
         shape = jax.ShapeDtypeStruct((2, *blocks[0].shape), jnp.float32)
         held[:] = pl.pallas_call(
-            functools.partial(join_kernel, masks=masks, peers=peers),
+            functools.partial(join_kernel, masks=masks, axis=axis, peers=peers),
             out_shape=[shape] * 2,
-            in_specs=[smem] + [vmem] * 4,
+            in_specs=[vmem] * 4,
             out_specs=[vmem] * 2,
             compiler_params=pltpu.CompilerParams(vmem_limit_bytes=1024 * 1024),
             name="join",
-        )(place, *own, *arrived)
+        )(*own, *arrived)
         held[1], states = lax.optimization_barrier((held[1], states))
         far = lax.ppermute(jnp.where(even, states[:, :1], states[:, -1:]), axis, over)
     held[1], far = lax.optimization_barrier((held[1], far))
@@ -232,9 +231,7 @@
 
 
 def setup_kernel(
-    place_ref,
-    shifts_ref,
-    order_ref,
+    pole_ref,
     mine_ref,
     theirs_ref,
     inner,
@@ -251,12 +248,12 @@
     half = inner.shape[1]
     at_ = Layout(inner.shape[2])
     tile, tiles = at_.tile, at_.tiles
-    shift = shifts_ref[order_ref[place_ref[0] % 2]]
+    shift = pole_ref[0] + at_.zero
 
     def keep(k, spot, j, value):
         half_kappa[k, spot + 1, tile(j)] = 0.5 * value
 
-    at_.arrange(mine_ref, theirs_ref, place_ref[0], False, keep)
+    at_.arrange(mine_ref, theirs_ref, lax.axis_index("space"), False, keep)
     at_.seam_fine(half_kappa)
 
     z_low = jnp.where(at_.lane % HALF > 0, 1.0, 0.0)
@@ -336,9 +333,7 @@
 
 
 def solve_kernel(
-    place_ref,
-    weights_ref,
-    order_ref,
+    pole_ref,
     mine_ref,
     theirs_ref,
     state_ref,
@@ -370,15 +365,16 @@
     half, rows = inner.shape[1:3]
     at_ = Layout(rows)
     tile, tiles, zero = at_.tile, at_.tiles, at_.zero
-    core = place_ref[0] % 2
-    weight = weights_ref[order_ref[core]]
+    place = lax.axis_index("space")
+    core = place % 2
+    weight = KEPT * pole_ref[1] + zero
 
     def begin(k, spot, j, value):
-        res = (KEPT * weight) * value
+        res = weight * value
         residual[k, spot, tile(j)] = res
         scaled[k, spot + 1, tile(j)] = damped[k, spot, tile(j)] * res
 
-    at_.arrange(mine_ref, theirs_ref, place_ref[0], True, begin)
+    at_.arrange(mine_ref, theirs_ref, place, True, begin)
     at_.seam_fine(scaled)
 
     def rows_of(ref, i):
@@ -544,7 +540,7 @@
     step_two = step_two * (1.0 / KEPT)
 
     own, ny, nz = adjoint_ref.shape
-    start = (place_ref[0] - core) * (own // 2)
+    start = (place - core) * (own // 2)
     upper = jnp.where(start >= half, 1, 0)
     start = start - half * upper
     even = at_.lane % 2 == 0
@@ -597,7 +593,7 @@
         adjoint_ref[x] = planes[1 + mine]
         partner_ref[x, :ny] = planes[1 + other]
         for k in range(groups):
-            at = pl.multiple_of(lax.rem(place_ref[1] + k, groups) * chunk, chunk)
+            at = pl.multiple_of(lax.rem(lax.axis_index("pole") + k, groups) * chunk, chunk)
             for side, plane in enumerate((mine, other)):
                 share = planes[terms + plane, pl.ds(at, chunk), :]
                 if k:
@@ -611,11 +607,13 @@
 def whole_grid(conductivity, misfit, forward_states, pole_shifts, pole_weights, pole_order):
     members, own, ny, nz = forward_states.shape
     groups = lax.axis_size("pole")
-    place = jnp.stack([lax.axis_index("space"), lax.axis_index("pole")]).astype(jnp.int32)
     peers = lax.axis_size("space")
-    mine, theirs, far, near = gather_blocks(
-        place, [conductivity, misfit], forward_states, "space"
-    )
+    even = lax.axis_index("space") % 2 == 0
+    pole = jnp.where(even, pole_order[0], pole_order[1])
+    chosen = jnp.arange(pole_shifts.shape[0], dtype=jnp.int32) == pole
+    scalars = jnp.sum(jnp.where(chosen, jnp.stack([pole_shifts, pole_weights]), 0.0), axis=1)
+    scalars = jnp.broadcast_to(scalars[:, None, None], (2, 1, nz))
+    mine, theirs, far, near = gather_blocks([conductivity, misfit], forward_states, "space")
     half, rows = peers * own // 4, ny // 2
 
     def field(count, extent):
@@ -624,7 +622,6 @@
     def held(*shape):
         return pltpu.VMEM(shape, jnp.float32)
 
-    smem = pl.BlockSpec(memory_space=pltpu.SMEM)
     vmem = pl.BlockSpec(memory_space=pltpu.VMEM)
     shapes = [
         field(12, half),
@@ -640,12 +637,12 @@
     coefficients = pl.pallas_call(
         setup_kernel,
         out_shape=[jax.ShapeDtypeStruct(shape, jnp.float32) for shape in shapes],
-        in_specs=[smem] * 3 + [vmem] * 2,
+        in_specs=[vmem] * 3,
         out_specs=[vmem] * len(shapes),
         scratch_shapes=[held(*field(8, half + 2))],
         compiler_params=pltpu.CompilerParams(vmem_limit_bytes=6 * 1024 * 1024),
         name="setup",
-    )(place, pole_shifts, pole_order, mine[0], theirs[0])
+    )(scalars, mine[0], theirs[0])
     chunk = ny // groups
     adjoint, gradient, partner, send = pl.pallas_call(
         solve_kernel,
@@ -655,7 +652,7 @@
             jax.ShapeDtypeStruct((own, ny + chunk, nz), jnp.float32),
             jax.ShapeDtypeStruct((groups - 1, 2, own, chunk, nz), jnp.float32),
         ],
-        in_specs=[smem] * 3 + [vmem] * (5 + len(shapes)),
+        in_specs=[vmem] * (6 + len(shapes)),
         out_specs=[vmem] * 4,
         scratch_shapes=[
             held(*field(8, half)),
@@ -671,9 +668,7 @@
         compiler_params=pltpu.CompilerParams(vmem_limit_bytes=12 * 1024 * 1024),
         name="solve",
     )(
-        place,
-        pole_weights,
-        pole_order,
+        scalars,
         mine[1],
         theirs[1],
         forward_states,
@@ -692,7 +687,6 @@
                 for j in range(peers)
             ]
             shares.append(lax.ppermute(send[k - 1, side], ("pole", "space"), pairs))
-    even = place[0] % 2 == 0
     theirs = arrived[:, :ny]
     adjoint_states = jnp.stack(
         [jnp.where(even, adjoint, theirs), jnp.where(even, theirs, adjoint)]

time: 43.3 us -> 42.8 us (0.988)
  starting transfers between devices: 17.4 us -> 13.2 us
  waiting for transfers between devices: 10.3 us -> 13.5 us
  Pallas kernels: 10.3 us -> 8.05 us
  local copies, waits for them, and re-layouts: 1.76 us -> 3.14 us
  between operations: 0.82 us -> 2.15 us
    ppermute x6, waiting for transfers between devices: 7.72 us -> 11.1 us  [gather_blocks(): arrived.append(lax.ppermute(held[at], axis, pairs))]
    ppermute x2, starting transfers between devices: 2.29 us -> 0.14 us  [gather_blocks(): other = [lax.ppermute(part, axis, swap) for part in held]]
    ppermute x6, starting transfers between devices: 12 us -> 9.93 us  [gather_blocks(): arrived.append(lax.ppermute(held[at], axis, pairs))]
    slice x0 -> x1, local copies, waits for them, and re-layouts: none -> 1.31 us  [whole_grid(): pole = jnp.where(even, pole_order[0], pole_order[1])]
    pallas_call x2, Pallas kernels: 1.28 us -> 0.21 us  [the longest x1 0.11 us: gather_blocks(): pl.pallas_call(functools.partial(join_kernel, masks=masks, axis=axis, pee...]
    pallas_call x1, Pallas kernels: 7.11 us -> 6.39 us  [whole_grid(): pl.pallas_call(solve_kernel, out_shape=[jax.ShapeDtypeStruct((own, ny, nz...]
    pallas_call x1, Pallas kernels: 1.9 us -> 1.44 us  [whole_grid(): pl.pallas_call(setup_kernel, out_shape=[jax.ShapeDtypeStruct(shape, jnp.f...]
    ppermute x1, starting transfers between devices: 0.09 us -> 0.55 us  [gather_blocks(): near = lax.ppermute(jnp.where(even, given[1], given[0]), axis, swap)]
  transfers between devices with their start and end apart: 13 -> 13, of which waited for: 7 -> 6; matrix products, arithmetic and copies ran while one was open for 4% -> 8% of each run, Pallas kernels for 6% -> 4%
where the time goes in v14:
time: 42.8 us; the launch traced here: 42.5 us
  waiting for transfers between devices  13.5 us (32%)
  starting transfers between devices  13.2 us (31%)
  Pallas kernels  8.05 us (19%)
  local copies, waits for them, and re-layouts  3.14 us (7%)
  other arithmetic  2.4 us (6%)
  between operations  2.15 us (5%)
    ppermute x6, waiting for transfers between devices, gather_blocks(): arrived.append(lax.ppermute(held[at], axis, pairs))  11.1 us
    ppermute x6, starting transfers between devices, gather_blocks(): arrived.append(lax.ppermute(held[at], axis, pairs))  9.93 us
    pallas_call x1, Pallas kernels, whole_grid(): pl.pallas_call(solve_kernel, out_shape=[jax.ShapeDtypeStruct((own, ny, nz...  6.39 us
    ppermute x2, waiting for transfers between devices, whole_grid(): shares.append(lax.ppermute(send[k - 1, side], ('pole', 'space'), pairs))  2.4 us
    ppermute x2, starting transfers between devices, whole_grid(): shares.append(lax.ppermute(send[k - 1, side], ('pole', 'space'), pairs))  1.85 us
    unnamed x13, local copies, waits for them, and re-layouts  1.73 us
    pallas_call x1, Pallas kernels, whole_grid(): pl.pallas_call(setup_kernel, out_shape=[jax.ShapeDtypeStruct(shape, jnp.f...  1.44 us
    slice x1, local copies, waits for them, and re-layouts, whole_grid(): pole = jnp.where(even, pole_order[0], pole_order[1])  1.31 us
  transfers between devices with their start and end apart: 13, of which 6 were waited for; matrix products, arithmetic and copies ran while one was open for 8% of the time, Pallas kernels for 4%

profile of v14, /device:TPU:0, one launch (start us, length us, event | category | flops | bytes accessed | tf_op | source)
XLA Modules:
  0.0 42.5 jit_solution(10107009451843205350)
XLA Ops:
  0.6 4.1 %collective-permute-start = (f32[2,64,128]{2,1,0:T(8,128)}, f32[2,64,128]{2,1,0:T(8,128)S(1)}, u32[]{:S(2)}, u32[]{:S(2)}) collective-permute-start(f32[2,64,128]{2,1,0:T(8,128)} %kappa_ref.1), channel_id=1, source_target_pairs={{0,8},{1,3},{2,10},{3,1},{4,12},{5,7},{6,14},{7,5},{8,0},{9,11},{1... | collective-permute-start | bytes 196616 | tf_op jit(solution)/shard_map/ppermute | solution.py:124
  4.7 1.5 %collective-permute-start.1 = (f32[2,64,128]{2,1,0:T(8,128)}, f32[2,64,128]{2,1,0:T(8,128)S(1)}, u32[]{:S(2)}, u32[]{:S(2)}) collective-permute-start(f32[2,64,128]{2,1,0:T(8,128)} %misfit_ref.1), channel_id=1, source_target_pairs={{0,2},{1,9},{2,0},{3,11},{4,6},{5,13},{6,4},{7,15},{8,10},{9,1},{1... | collective-permute-start | bytes 196616 | tf_op jit(solution)/shard_map/ppermute | solution.py:124
  6.2 0.8 %copy-done.1 = f32[2,64,128]{2,1,0:T(8,128)S(1)} copy-done((f32[2,64,128]{2,1,0:T(8,128)S(1)}, f32[2,64,128]{2,1,0:T(8,128)}, u32[]{:S(2)}) %copy-start.1) | copy-done | bytes 65560
  7.1 0.8 %copy-done.2 = f32[2,64,128]{2,1,0:T(8,128)S(1)} copy-done((f32[2,64,128]{2,1,0:T(8,128)S(1)}, f32[2,64,128]{2,1,0:T(8,128)}, u32[]{:S(2)}) %copy-start.2) | copy-done | bytes 65560
  7.9 0.1 prepare.1
  8.0 1.3 %fusion.2 = (s32[1]{0:T(128)}, s32[1]{0:T(128)}) fusion(s32[2]{0:T(128)} %param.11), kind=kLoop, calls=%fused_computation.20 | loop fusion | bytes 16 | tf_op jit(solution)/shard_map/slice | solution.py:612
  10.7 0.1 join.1
  10.8 1.6 %collective-permute-start.7 = (f32[2,2,64,128]{3,2,1,0:T(8,128)S(1)}, f32[2,2,64,128]{3,2,1,0:T(8,128)S(1)}, u32[]{:S(2)}, u32[]{:S(2)}) collective-permute-start(f32[2,2,64,128]{3,2,1,0:T(8,128)S(1)} %get-tuple-element.32), channel_id=1, source_target_pairs={{0,4},{1,9},{2,6},{3,11},{4,0},{5,13},{6,2},{7,15},{8,12},{9,1},{1... | collective-permute-start | bytes 393224 | tf_op jit(solution)/shard_map/ppermute | solution.py:124
  12.4 0.4 %collective-permute-start.2 = (f32[2,2,64,128]{3,2,1,0:T(8,128)S(1)}, f32[2,2,64,128]{3,2,1,0:T(8,128)S(1)}, u32[]{:S(2)}, u32[]{:S(2)}) collective-permute-start(f32[2,2,64,128]{3,2,1,0:T(8,128)S(1)} %get-tuple-element.28), channel_id=1, source_target_pairs={{0,4},{1,3},{2,6},{3,1},{4,0},{5,7},{6,2},{7,5},{8,12},{9,11},{10,... | collective-permute-start | bytes 393224 | tf_op jit(solution)/shard_map/ppermute | solution.py:124
  12.9 0.9 %slice_select_fusion.1 = f32[2,1,64,128]{3,2,1,0:T(8,128)S(1)} fusion(f32[2,2,64,128]{3,2,1,0:T(8,128)} %state_ref.1, pred[]{:T(512)S(6)} %eq.13), kind=kLoop, calls=%fused_computation.8 | loop fusion | flops 16384 | bytes 196609 | tf_op jit(solution)/shard_map/jit(_where)/select_n | solution.py:139
  13.8 0.0 copy-start
  13.8 2.7 %collective-permute-done.7 = f32[2,2,64,128]{3,2,1,0:T(8,128)S(1)} collective-permute-done((f32[2,2,64,128]{3,2,1,0:T(8,128)S(1)}, f32[2,2,64,128]{3,2,1,0:T(8,128)S(1)}, u32[]{:S(2)}, u32[]{:S(2)}) %collective-permute-start.7) | collective-permute-done | bytes 131104 | tf_op jit(solution)/shard_map/ppermute | solution.py:124
  16.5 0.6 %collective-permute-start.8 = (f32[4,2,64,128]{3,2,1,0:T(8,128)S(1)}, f32[4,2,64,128]{3,2,1,0:T(8,128)S(1)}, u32[]{:S(2)}, u32[]{:S(2)}) collective-permute-start(f32[4,2,64,128]{3,2,1,0:T(8,128)S(1)} %pad_maximum_fusion.2), channel_id=1, source_target_pairs={{0,2},{1,5},{2,0},{3,7},{4,6},{5,1},{6,4},{7,3},{8,10},{9,13},{10,... | collective-permute-start | bytes 786440 | tf_op jit(solution)/shard_map/ppermute | solution.py:124
  17.1 0.8 %collective-permute-done.2 = f32[2,2,64,128]{3,2,1,0:T(8,128)S(1)} collective-permute-done((f32[2,2,64,128]{3,2,1,0:T(8,128)S(1)}, f32[2,2,64,128]{3,2,1,0:T(8,128)S(1)}, u32[]{:S(2)}, u32[]{:S(2)}) %collective-permute-start.2) | collective-permute-done | bytes 131104 | tf_op jit(solution)/shard_map/ppermute | solution.py:124
  17.9 1.6 %collective-permute-start.3 = (f32[4,2,64,128]{3,2,1,0:T(8,128)S(1)}, f32[4,2,64,128]{3,2,1,0:T(8,128)S(1)}, u32[]{:S(2)}, u32[]{:S(2)}) collective-permute-start(f32[4,2,64,128]{3,2,1,0:T(8,128)S(1)} %pad_maximum_fusion.1), channel_id=1, source_target_pairs={{0,8},{1,5},{2,10},{3,7},{4,12},{5,1},{6,14},{7,3},{8,0},{9,13},{1... | collective-permute-start | bytes 786440 | tf_op jit(solution)/shard_map/ppermute | solution.py:124
  19.5 0.7 %collective-permute-start.4 = (f32[2,1,64,128]{3,2,1,0:T(8,128)S(1)}, f32[2,1,64,128]{3,2,1,0:T(8,128)S(1)}, u32[]{:S(2)}, u32[]{:S(2)}) collective-permute-start(f32[2,1,64,128]{3,2,1,0:T(8,128)S(1)} %slice_select_fusion.1), channel_id=1, source_target_pairs={{1,2},{2,1},{3,4},{4,3},{5,6},{6,5},{7,8},{8,7},{9,10},{10,9},{11,... | collective-permute-start | bytes 196616 | tf_op jit(solution)/shard_map/ppermute | solution.py:139
  20.2 2.7 %collective-permute-done.8 = f32[4,2,64,128]{3,2,1,0:T(8,128)S(1)} collective-permute-done((f32[4,2,64,128]{3,2,1,0:T(8,128)S(1)}, f32[4,2,64,128]{3,2,1,0:T(8,128)S(1)}, u32[]{:S(2)}, u32[]{:S(2)}) %collective-permute-start.8) | collective-permute-done | bytes 262176 | tf_op jit(solution)/shard_map/ppermute | solution.py:124
  22.9 0.1 collective-permute-start.9
  23.0 5.0 %collective-permute-done.3 = f32[4,2,64,128]{3,2,1,0:T(8,128)S(1)} collective-permute-done((f32[4,2,64,128]{3,2,1,0:T(8,128)S(1)}, f32[4,2,64,128]{3,2,1,0:T(8,128)S(1)}, u32[]{:S(2)}, u32[]{:S(2)}) %collective-permute-start.3) | collective-permute-done | bytes 262176 | tf_op jit(solution)/shard_map/ppermute | solution.py:124
  28.1 0.1 collective-permute-start.5
  28.2 0.5 %collective-permute-start.6 = (f32[3,64,128]{2,1,0:T(8,128)S(1)}, f32[3,64,128]{2,1,0:T(8,128)S(1)}, u32[]{:S(2)}, u32[]{:S(2)}) collective-permute-start(f32[3,64,128]{2,1,0:T(8,128)S(1)} %fusion), channel_id=1, source_target_pairs={{0,1},{1,0},{2,3},{3,2},{4,5},{5,4},{6,7},{7,6},{8,9},{9,8},{10,11... | collective-permute-start | bytes 294920 | tf_op jit(solution)/shard_map/ppermute | solution.py:142
  28.8 0.1 fusion.1
  28.9 0.1 broadcast_in_dim.16.pole_ref
  29.0 1.4 %setup.1 = (f32[12,8,32,128]{3,2,1,0:T(8,128)S(1)}, f32[4,9,32,128]{3,2,1,0:T(8,128)S(1)}, f32[4,8,32,128]{3,2,1,0:T(8,128)S(1)}, f32[8,8,32,128]{3,2,1,0:T(8,12...) custom-call(f32[2,1,128]{2,1,0:T(1,128)S(1)} %broadcast_in_dim.16.po, ...), custom_call_target="tpu_custom_call" | custom-call | tf_op jit(solution)/shard_map/setup/pallas_call | solution.py:637
  30.4 6.4 %solve.1 = (f32[2,64,128]{2,1,0:T(8,128)S(1)}, f32[2,32,128]{2,1,0:T(8,128)S(1)}, f32[2,96,128]{2,1,0:T(8,128)S(1)}, f32[1,2,2,32,128]{4,3,2,1,0:T(8,128)S(1)}) custom-call(f32[2,1,128]{2,1,0:T(1,128)S(1)} %broadcast_in_dim.16.pole_ref, f32[8,2,64,128]{3,2,1,0:T(8,128)S(1)} %pad_maximum_fusion.mine_ref, ...), custom_call_target="tpu_custom_call" | custom-call | tf_op jit(solution)/shard_map/solve/pallas_call | solution.py:647
  36.8 0.1 collective-permute-start.10
  36.9 1.6 %collective-permute-start.11 = (f32[2,32,128]{2,1,0:T(8,128)S(1)}, f32[2,32,128]{2,1,0:T(8,128)S(1)}, u32[]{:S(2)}, u32[]{:S(2)}) collective-permute-start(f32[2,32,128]{2,1,0:T(8,128)S(1)} %get-tuple-element.51), channel_id=1, source_target_pairs={{0,16},{1,17},{2,18},{3,19},{4,20},{5,21},{6,22},{7,23},{8,24},{9,... | collective-permute-start | bytes 98312 | tf_op jit(solution)/shard_map/ppermute | solution.py:689
  38.5 0.3 collective-permute-start.12
  38.8 0.7 %pad_maximum_fusion.3 = f32[2,2,64,128]{3,2,1,0:T(8,128)} fusion(f32[1,2,64,128]{3,2,1,0:T(8,128)S(1)} %get-tuple-element.49, f32[1,2,64,128]{3,2,1,0:T(8,128)S(1)} %get-tuple-element.48), kind=kLoop, calls=%fused_computation.3 | loop fusion | flops 32768 | bytes 262144 | tf_op jit(solution)/shard_map/stack | solution.py:691
  39.5 1.4 %collective-permute-done.11 = f32[2,32,128]{2,1,0:T(8,128)S(1)} collective-permute-done((f32[2,32,128]{2,1,0:T(8,128)S(1)}, f32[2,32,128]{2,1,0:T(8,128)S(1)}, u32[]{:S(2)}, u32[]{:S(2)}) %collective-permute-start.11) | collective-permute-done | bytes 32800 | tf_op jit(solution)/shard_map/ppermute | solution.py:689
  40.9 1.0 %collective-permute-done.12 = f32[2,32,128]{2,1,0:T(8,128)S(1)} collective-permute-done((f32[2,32,128]{2,1,0:T(8,128)S(1)}, f32[2,32,128]{2,1,0:T(8,128)S(1)}, u32[]{:S(2)}, u32[]{:S(2)}) %collective-permute-start.12) | collective-permute-done | bytes 32800 | tf_op jit(solution)/shard_map/ppermute | solution.py:689
  41.9 0.6 %add_add_fusion = f32[2,32,128]{2,1,0:T(8,128)} fusion(f32[2,32,128]{2,1,0:T(8,128)S(1)} %collective-permute-done.11, f32[2,32,128]{2,1,0:T(8,128)S(1)} %collective-permute-done.12, f32[2,32,128]{2,1,0:T(8,128)S(1)} %get-tuple-element.45, f32[2,96,128]{2,1,0:T(8,128)S(1)} %collective-permute-done.10), kind=kLoop, calls=%fused_computation.9 | loop fusion | flops 24576 | bytes 163840 | tf_op jit(solution)/shard_map/add | solution.py:695
  (26 shorter events, 0.2 us)
Async XLA Ops:
  0.6 10.0 %collective-permute-start = (f32[2,64,128]{2,1,0:T(8,128)}, f32[2,64,128]{2,1,0:T(8,128)S(1)}, u32[]{:S(2)}, u32[]{:S(2)}) collective-permute-start(f32[2,64,128]{2,1,0:T(8,128)} %kappa_ref.1), channel_id=1, source_target_pairs={{0,8},{1,3},{2,10},{3,1},{4,12},{5,7},{6,14},{7,5},{8,0},{9,11},{1... | collective-permute-start | bytes 196616 | tf_op jit(solution)/shard_map/ppermute | solution.py:124
  4.7 5.9 %collective-permute-start.1 = (f32[2,64,128]{2,1,0:T(8,128)}, f32[2,64,128]{2,1,0:T(8,128)S(1)}, u32[]{:S(2)}, u32[]{:S(2)}) collective-permute-start(f32[2,64,128]{2,1,0:T(8,128)} %misfit_ref.1), channel_id=1, source_target_pairs={{0,2},{1,9},{2,0},{3,11},{4,6},{5,13},{6,4},{7,15},{8,10},{9,1},{1... | collective-permute-start | bytes 196616 | tf_op jit(solution)/shard_map/ppermute | solution.py:124
  6.2 0.8 %copy-start.1 = (f32[2,64,128]{2,1,0:T(8,128)S(1)}, f32[2,64,128]{2,1,0:T(8,128)}, u32[]{:S(2)}) copy-start(f32[2,64,128]{2,1,0:T(8,128)} %kappa_ref.1) | copy-start | bytes 196612
  7.1 0.8 %copy-start.2 = (f32[2,64,128]{2,1,0:T(8,128)S(1)}, f32[2,64,128]{2,1,0:T(8,128)}, u32[]{:S(2)}) copy-start(f32[2,64,128]{2,1,0:T(8,128)} %misfit_ref.1) | copy-start | bytes 196612
  10.8 5.6 %collective-permute-start.7 = (f32[2,2,64,128]{3,2,1,0:T(8,128)S(1)}, f32[2,2,64,128]{3,2,1,0:T(8,128)S(1)}, u32[]{:S(2)}, u32[]{:S(2)}) collective-permute-start(f32[2,2,64,128]{3,2,1,0:T(8,128)S(1)} %get-tuple-element.32), channel_id=1, source_target_pairs={{0,4},{1,9},{2,6},{3,11},{4,0},{5,13},{6,2},{7,15},{8,12},{9,1},{1... | collective-permute-start | bytes 393224 | tf_op jit(solution)/shard_map/ppermute | solution.py:124
  12.4 5.4 %collective-permute-start.2 = (f32[2,2,64,128]{3,2,1,0:T(8,128)S(1)}, f32[2,2,64,128]{3,2,1,0:T(8,128)S(1)}, u32[]{:S(2)}, u32[]{:S(2)}) collective-permute-start(f32[2,2,64,128]{3,2,1,0:T(8,128)S(1)} %get-tuple-element.28), channel_id=1, source_target_pairs={{0,4},{1,3},{2,6},{3,1},{4,0},{5,7},{6,2},{7,5},{8,12},{9,11},{10,... | collective-permute-start | bytes 393224 | tf_op jit(solution)/shard_map/ppermute | solution.py:124
  13.8 14.4 %copy-start = (f32[2,2,64,128]{3,2,1,0:T(8,128)S(1)}, f32[2,2,64,128]{3,2,1,0:T(8,128)}, u32[]{:S(2)}) copy-start(f32[2,2,64,128]{3,2,1,0:T(8,128)} %state_ref.1) | copy-start | bytes 393220
  16.5 12.3 %copy-start.3 = (f32[4]{0:T(128)S(1)}, f32[4]{0:T(128)}, u32[]{:S(2)}) copy-start(f32[4]{0:T(128)} %param.10) | copy-start | bytes 52
  16.5 12.3 %copy-start.4 = (f32[4]{0:T(128)S(1)}, f32[4]{0:T(128)}, u32[]{:S(2)}) copy-start(f32[4]{0:T(128)} %param.9) | copy-start | bytes 52
  16.5 6.4 %collective-permute-start.8 = (f32[4,2,64,128]{3,2,1,0:T(8,128)S(1)}, f32[4,2,64,128]{3,2,1,0:T(8,128)S(1)}, u32[]{:S(2)}, u32[]{:S(2)}) collective-permute-start(f32[4,2,64,128]{3,2,1,0:T(8,128)S(1)} %pad_maximum_fusion.2), channel_id=1, source_target_pairs={{0,2},{1,5},{2,0},{3,7},{4,6},{5,1},{6,4},{7,3},{8,10},{9,13},{10,... | collective-permute-start | bytes 786440 | tf_op jit(solution)/shard_map/ppermute | solution.py:124
  17.9 10.1 %collective-permute-start.3 = (f32[4,2,64,128]{3,2,1,0:T(8,128)S(1)}, f32[4,2,64,128]{3,2,1,0:T(8,128)S(1)}, u32[]{:S(2)}, u32[]{:S(2)}) collective-permute-start(f32[4,2,64,128]{3,2,1,0:T(8,128)S(1)} %pad_maximum_fusion.1), channel_id=1, source_target_pairs={{0,8},{1,5},{2,10},{3,7},{4,12},{5,1},{6,14},{7,3},{8,0},{9,13},{1... | collective-permute-start | bytes 786440 | tf_op jit(solution)/shard_map/ppermute | solution.py:124
  19.5 8.5 %collective-permute-start.4 = (f32[2,1,64,128]{3,2,1,0:T(8,128)S(1)}, f32[2,1,64,128]{3,2,1,0:T(8,128)S(1)}, u32[]{:S(2)}, u32[]{:S(2)}) collective-permute-start(f32[2,1,64,128]{3,2,1,0:T(8,128)S(1)} %slice_select_fusion.1), channel_id=1, source_target_pairs={{1,2},{2,1},{3,4},{4,3},{5,6},{6,5},{7,8},{8,7},{9,10},{10,9},{11,... | collective-permute-start | bytes 196616 | tf_op jit(solution)/shard_map/ppermute | solution.py:139
  22.9 5.9 %collective-permute-start.9 = (f32[8,2,64,128]{3,2,1,0:T(8,128)S(1)}, f32[8,2,64,128]{3,2,1,0:T(8,128)S(1)}, u32[]{:S(2)}, u32[]{:S(2)}) collective-permute-start(f32[8,2,64,128]{3,2,1,0:T(8,128)S(1)} %constant_dynamic-update-slice_fusion.2.mine_ref), channel_id=1, source_target_pairs={{0,1},{1,0},{2,3},{3,2},{4,5},{5,4},{6,7},{7,6},{8,9},{9,8},{10,11... | collective-permute-start | bytes 1572872 | tf_op jit(solution)/shard_map/ppermute | solution.py:143
  28.1 2.4 %collective-permute-start.5 = (f32[8,2,64,128]{3,2,1,0:T(8,128)S(1)}, f32[8,2,64,128]{3,2,1,0:T(8,128)S(1)}, u32[]{:S(2)}, u32[]{:S(2)}) collective-permute-start(f32[8,2,64,128]{3,2,1,0:T(8,128)S(1)} %pad_maximum_fusion.mine_ref), channel_id=1, source_target_pairs={{0,1},{1,0},{2,3},{3,2},{4,5},{5,4},{6,7},{7,6},{8,9},{9,8},{10,11... | collective-permute-start | bytes 1572872 | tf_op jit(solution)/shard_map/ppermute | solution.py:143
  28.2 2.2 %collective-permute-start.6 = (f32[3,64,128]{2,1,0:T(8,128)S(1)}, f32[3,64,128]{2,1,0:T(8,128)S(1)}, u32[]{:S(2)}, u32[]{:S(2)}) collective-permute-start(f32[3,64,128]{2,1,0:T(8,128)S(1)} %fusion), channel_id=1, source_target_pairs={{0,1},{1,0},{2,3},{3,2},{4,5},{5,4},{6,7},{7,6},{8,9},{9,8},{10,11... | collective-permute-start | bytes 294920 | tf_op jit(solution)/shard_map/ppermute | solution.py:142
  36.8 1.9 %collective-permute-start.10 = (f32[2,96,128]{2,1,0:T(8,128)S(1)}, f32[2,96,128]{2,1,0:T(8,128)S(1)}, u32[]{:S(2)}, u32[]{:S(2)}) collective-permute-start(f32[2,96,128]{2,1,0:T(8,128)S(1)} %get-tuple-element.43), channel_id=1, source_target_pairs={{0,1},{1,0},{2,3},{3,2},{4,5},{5,4},{6,7},{7,6},{8,9},{9,8},{10,11... | collective-permute-start | bytes 294920 | tf_op jit(solution)/shard_map/ppermute | solution.py:680
  36.9 4.0 %collective-permute-start.11 = (f32[2,32,128]{2,1,0:T(8,128)S(1)}, f32[2,32,128]{2,1,0:T(8,128)S(1)}, u32[]{:S(2)}, u32[]{:S(2)}) collective-permute-start(f32[2,32,128]{2,1,0:T(8,128)S(1)} %get-tuple-element.51), channel_id=1, source_target_pairs={{0,16},{1,17},{2,18},{3,19},{4,20},{5,21},{6,22},{7,23},{8,24},{9,... | collective-permute-start | bytes 98312 | tf_op jit(solution)/shard_map/ppermute | solution.py:689
  38.5 3.4 %collective-permute-start.12 = (f32[2,32,128]{2,1,0:T(8,128)S(1)}, f32[2,32,128]{2,1,0:T(8,128)S(1)}, u32[]{:S(2)}, u32[]{:S(2)}) collective-permute-start(f32[2,32,128]{2,1,0:T(8,128)S(1)} %get-tuple-element.50), channel_id=1, source_target_pairs={{0,17},{1,16},{2,19},{3,18},{4,21},{5,20},{6,23},{7,22},{8,25},{9,... | collective-permute-start | bytes 98312 | tf_op jit(solution)/shard_map/ppermute | solution.py:689

commit v15 on v14

--- a/solution.py
+++ b/solution.py
@@ -137,11 +137,14 @@
         )(*own, *arrived)
         held[1], states = lax.optimization_barrier((held[1], states))
         far = lax.ppermute(jnp.where(even, states[:, :1], states[:, -1:]), axis, over)
-    held[1], far = lax.optimization_barrier((held[1], far))
-    given = jnp.concatenate([states, far], axis=1)
-    near = lax.ppermute(jnp.where(even, given[1], given[0]), axis, swap)
     other = [lax.ppermute(part, axis, swap) for part in held]
-    return held, other, far, near
+
+    def fetch_near(after):
+        late, states_late, far_late = lax.optimization_barrier((after, states, far))
+        given = jnp.concatenate([states_late, far_late], axis=1)
+        return late, lax.ppermute(jnp.where(even, given[1], given[0]), axis, swap)
+
+    return held, other, far, fetch_near
 
 
 CLASSES = [(a, b, c) for a in (0, 1) for b in (0, 1) for c in (0, 1)]
@@ -231,7 +234,9 @@
 
 
 def setup_kernel(
-    pole_ref,
+    order_ref,
+    shifts_ref,
+    weights_ref,
     mine_ref,
     theirs_ref,
     inner,
@@ -243,17 +248,24 @@
     damped,
     coarse_off,
     coarse_damped,
+    chosen,
     half_kappa,
 ):
     half = inner.shape[1]
     at_ = Layout(inner.shape[2])
     tile, tiles = at_.tile, at_.tiles
-    shift = pole_ref[0] + at_.zero
+    place = lax.axis_index("space")
+    pole = jnp.where(place % 2 == 0, order_ref[:, 0:1], order_ref[:, 1:2])
+    taken = lane_index(shifts_ref.shape) == pole
+    shift = jnp.sum(jnp.where(taken, shifts_ref[...], 0.0), axis=1, keepdims=True)
+    weight = jnp.sum(jnp.where(taken, weights_ref[...], 0.0), axis=1, keepdims=True)
+    shift = jnp.broadcast_to(shift, at_.zero.shape)
+    chosen[...] = jnp.broadcast_to(weight, at_.zero.shape)
 
     def keep(k, spot, j, value):
         half_kappa[k, spot + 1, tile(j)] = 0.5 * value
 
-    at_.arrange(mine_ref, theirs_ref, lax.axis_index("space"), False, keep)
+    at_.arrange(mine_ref, theirs_ref, place, False, keep)
     at_.seam_fine(half_kappa)
 
     z_low = jnp.where(at_.lane % HALF > 0, 1.0, 0.0)
@@ -333,12 +345,8 @@
 
 
 def solve_kernel(
-    pole_ref,
     mine_ref,
     theirs_ref,
-    state_ref,
-    far_ref,
-    near_ref,
     inner,
     outer_x,
     outer_y,
@@ -348,10 +356,8 @@
     damped,
     coarse_off,
     coarse_damped,
-    adjoint_ref,
-    keep_ref,
-    partner_ref,
-    send_ref,
+    chosen,
+    planes,
     residual,
     scaled,
     partial,
@@ -360,14 +366,15 @@
     image,
     coarse_one,
     coarse_two,
-    planes,
+    *,
+    own,
 ):
     half, rows = inner.shape[1:3]
     at_ = Layout(rows)
     tile, tiles, zero = at_.tile, at_.tiles, at_.zero
     place = lax.axis_index("space")
     core = place % 2
-    weight = KEPT * pole_ref[1] + zero
+    weight = KEPT * chosen[...]
 
     def begin(k, spot, j, value):
         res = weight * value
@@ -539,7 +546,6 @@
     step_first = (step_one + step_two * ratio) * (1.0 / KEPT)
     step_two = step_two * (1.0 / KEPT)
 
-    own, ny, nz = adjoint_ref.shape
     start = (place - core) * (own // 2)
     upper = jnp.where(start >= half, 1, 0)
     start = start - half * upper
@@ -561,6 +567,10 @@
                     jnp.take_along_axis(both[1], source, axis=1),
                 )
 
+
+def finish_kernel(planes_ref, state_ref, far_ref, near_ref, adjoint_ref, keep_ref, partner_ref, send_ref, terms):
+    own, ny, nz = adjoint_ref.shape
+    core = lax.axis_index("space") % 2
     full = (ny, nz)
     y_at = row_index(full)
     z_at = lane_index(full)
@@ -576,26 +586,26 @@
     state += [jnp.where(is_even, state_ref[core, x], near_ref[x]) for x in range(own)]
     state += [jnp.where(is_even, near_ref[x], state_ref[core, x]) for x in range(own)]
     state += [jnp.where(is_even, near_ref[own], far_ref[core, 0])]
-    terms = 2 * own + 2
     for x in range(2 * own):
-        here, f = planes[x + 1], state[x + 1]
-        term = (here - planes[x + 2]) * (f - state[x + 2])
-        term = term + (here - planes[x]) * (f - state[x])
+        here, f = planes_ref[x + 1], state[x + 1]
+        term = (here - planes_ref[x + 2]) * (f - state[x + 2])
+        term = term + (here - planes_ref[x]) * (f - state[x])
         for axis in (0, 1):
             for up in (True, False):
                 term = term + drop(here, axis, up) * drop(f, axis, up)
-        planes[terms + x] = -0.5 * term
+        terms[x] = -0.5 * term
 
     groups = send_ref.shape[0] + 1
     chunk = keep_ref.shape[1]
     for x in range(own):
         mine, other = core * own + x, (1 - core) * own + x
-        adjoint_ref[x] = planes[1 + mine]
-        partner_ref[x, :ny] = planes[1 + other]
+        adjoint_ref[x] = planes_ref[1 + mine]
+        partner_ref[x, :ny] = planes_ref[1 + other]
         for k in range(groups):
-            at = pl.multiple_of(lax.rem(lax.axis_index("pole") + k, groups) * chunk, chunk)
+            at = lax.rem(lax.axis_index("pole") + k, groups) * chunk
+            at = pl.multiple_of(at, chunk)
             for side, plane in enumerate((mine, other)):
-                share = planes[terms + plane, pl.ds(at, chunk), :]
+                share = terms[plane, pl.ds(at, chunk), :]
                 if k:
                     send_ref[k - 1, side, x] = share
                 elif side:
@@ -609,11 +619,7 @@
     groups = lax.axis_size("pole")
     peers = lax.axis_size("space")
     even = lax.axis_index("space") % 2 == 0
-    pole = jnp.where(even, pole_order[0], pole_order[1])
-    chosen = jnp.arange(pole_shifts.shape[0], dtype=jnp.int32) == pole
-    scalars = jnp.sum(jnp.where(chosen, jnp.stack([pole_shifts, pole_weights]), 0.0), axis=1)
-    scalars = jnp.broadcast_to(scalars[:, None, None], (2, 1, nz))
-    mine, theirs, far, near = gather_blocks([conductivity, misfit], forward_states, "space")
+    mine, theirs, far, fetch_near = gather_blocks([conductivity, misfit], forward_states, "space")
     half, rows = peers * own // 4, ny // 2
 
     def field(count, extent):
@@ -633,27 +639,23 @@
         field(8, half),
         field(5, half + 1),
         (half, rows, 2 * HALF),
+        (TILE, 2 * HALF),
     ]
     coefficients = pl.pallas_call(
         setup_kernel,
         out_shape=[jax.ShapeDtypeStruct(shape, jnp.float32) for shape in shapes],
-        in_specs=[vmem] * 3,
+        in_specs=[vmem] * 5,
         out_specs=[vmem] * len(shapes),
         scratch_shapes=[held(*field(8, half + 2))],
         compiler_params=pltpu.CompilerParams(vmem_limit_bytes=6 * 1024 * 1024),
         name="setup",
-    )(scalars, mine[0], theirs[0])
-    chunk = ny // groups
-    adjoint, gradient, partner, send = pl.pallas_call(
-        solve_kernel,
-        out_shape=[
-            jax.ShapeDtypeStruct((own, ny, nz), jnp.float32),
-            jax.ShapeDtypeStruct((own, chunk, nz), jnp.float32),
-            jax.ShapeDtypeStruct((own, ny + chunk, nz), jnp.float32),
-            jax.ShapeDtypeStruct((groups - 1, 2, own, chunk, nz), jnp.float32),
-        ],
-        in_specs=[vmem] * (6 + len(shapes)),
-        out_specs=[vmem] * 4,
+    )(pole_order[None], pole_shifts[None], pole_weights[None], mine[0], theirs[0])
+    coefficients, near = fetch_near(coefficients)
+    planes = pl.pallas_call(
+        functools.partial(solve_kernel, own=own),
+        out_shape=jax.ShapeDtypeStruct((2 * own + 2, ny, nz), jnp.float32),
+        in_specs=[vmem] * (2 + len(shapes)),
+        out_specs=vmem,
         scratch_shapes=[
             held(*field(8, half)),
             held(*field(8, half + 2)),
@@ -663,19 +665,25 @@
             held(*field(8, half)),
             held(*field(1, half + 2)),
             held(*field(1, half + 2)),
-            held(4 * own + 2, ny, nz),
         ],
         compiler_params=pltpu.CompilerParams(vmem_limit_bytes=12 * 1024 * 1024),
         name="solve",
-    )(
-        scalars,
-        mine[1],
-        theirs[1],
-        forward_states,
-        far,
-        near,
-        *coefficients,
-    )
+    )(mine[1], theirs[1], *coefficients)
+    chunk = ny // groups
+    adjoint, gradient, partner, send = pl.pallas_call(
+        finish_kernel,
+        out_shape=[
+            jax.ShapeDtypeStruct((own, ny, nz), jnp.float32),
+            jax.ShapeDtypeStruct((own, chunk, nz), jnp.float32),
+            jax.ShapeDtypeStruct((own, ny + chunk, nz), jnp.float32),
+            jax.ShapeDtypeStruct((groups - 1, 2, own, chunk, nz), jnp.float32),
+        ],
+        in_specs=[vmem] * 4,
+        out_specs=[vmem] * 4,
+        scratch_shapes=[held(2 * own, ny, nz)],
+        compiler_params=pltpu.CompilerParams(vmem_limit_bytes=4 * 1024 * 1024),
+        name="finish",
+    )(planes, forward_states, far, near)
 
     arrived = lax.ppermute(partner, "space", [(i, i ^ 1) for i in range(peers)])
     shares = []

time: 42.8 us -> 41.1 us (0.960)
  starting transfers between devices: 13.2 us -> 16.6 us
  local copies, waits for them, and re-layouts: 3.14 us -> 1.79 us
  between operations: 2.15 us -> 0.82 us
  other arithmetic: 2.4 us -> 1.37 us
  waiting for transfers between devices: 13.5 us -> 12.6 us
    ppermute x6, starting transfers between devices: 9.93 us -> 12 us  [gather_blocks(): arrived.append(lax.ppermute(held[at], axis, pairs))]
    slice x1 -> x0, local copies, waits for them, and re-layouts: 1.31 us -> none  [whole_grid(): pole = jnp.where(even, pole_order[0], pole_order[1])]
    ppermute x6, waiting for transfers between devices: 11.1 us -> 10.1 us  [gather_blocks(): arrived.append(lax.ppermute(held[at], axis, pairs))]
    select_n x1, other arithmetic: 0.88 us -> 0.01 us  [gather_blocks(): jnp.where(even, states[:, :1], states[:, -1:])]
    ppermute x2, starting transfers between devices: 1.85 us -> 2.57 us  [whole_grid(): shares.append(lax.ppermute(send[k - 1, side], ('pole', 'space'), pairs))]
    ppermute x2, starting transfers between devices: 0.14 us -> 0.7 us  [gather_blocks(): other = [lax.ppermute(part, axis, swap) for part in held]]
    ppermute x1, starting transfers between devices: 0.55 us -> 0.09 us  [fetch_near(): return (late, lax.ppermute(jnp.where(even, given[1], given[0]), axis, swap))]
    ppermute x1, starting transfers between devices: 0.09 us -> 0.53 us  [whole_grid(): arrived = lax.ppermute(partner, 'space', [(i, i ^ 1) for i in range(peers)])]
  transfers between devices with their start and end apart: 13 -> 13, of which waited for: 6 -> 7; matrix products, arithmetic and copies ran while one was open for 8% -> 2% of each run, Pallas kernels for 4% -> 18%
where the time goes in v15:
time: 41.1 us; the launch traced here: 40.9 us
  starting transfers between devices  16.6 us (40%)
  waiting for transfers between devices  12.6 us (31%)
  Pallas kernels  7.72 us (19%)
  local copies, waits for them, and re-layouts  1.79 us (4%)
  other arithmetic  1.37 us (3%)
  between operations  0.82 us (2%)
    ppermute x6, starting transfers between devices, gather_blocks(): arrived.append(lax.ppermute(held[at], axis, pairs))  12 us
    ppermute x6, waiting for transfers between devices, gather_blocks(): arrived.append(lax.ppermute(held[at], axis, pairs))  10.1 us
    pallas_call x1, Pallas kernels, whole_grid(): pl.pallas_call(functools.partial(solve_kernel, own=own), out_shape=jax.Sh...  5.73 us
    ppermute x2, starting transfers between devices, whole_grid(): shares.append(lax.ppermute(send[k - 1, side], ('pole', 'space'), pairs))  2.57 us
    ppermute x2, waiting for transfers between devices, whole_grid(): shares.append(lax.ppermute(send[k - 1, side], ('pole', 'space'), pairs))  2.55 us
    unnamed x17, local copies, waits for them, and re-layouts  1.75 us
    pallas_call x1, Pallas kernels, whole_grid(): pl.pallas_call(setup_kernel, out_shape=[jax.ShapeDtypeStruct(shape, jnp.f...  1.53 us
  transfers between devices with their start and end apart: 13, of which 7 were waited for; matrix products, arithmetic and copies ran while one was open for 2% of the time, Pallas kernels for 18%

profile of v15, /device:TPU:0, one launch (start us, length us, event | category | flops | bytes accessed | tf_op | source)
XLA Modules:
  0.0 40.9 jit_solution(3524570409819159052)
XLA Ops:
  0.6 4.1 %collective-permute-start = (f32[2,64,128]{2,1,0:T(8,128)}, f32[2,64,128]{2,1,0:T(8,128)S(1)}, u32[]{:S(2)}, u32[]{:S(2)}) collective-permute-start(f32[2,64,128]{2,1,0:T(8,128)} %kappa_ref.1), channel_id=1, source_target_pairs={{0,8},{1,3},{2,10},{3,1},{4,12},{5,7},{6,14},{7,5},{8,0},{9,11},{1... | collective-permute-start | bytes 196616 | tf_op jit(solution)/shard_map/ppermute | solution.py:124
  4.7 1.5 %collective-permute-start.1 = (f32[2,64,128]{2,1,0:T(8,128)}, f32[2,64,128]{2,1,0:T(8,128)S(1)}, u32[]{:S(2)}, u32[]{:S(2)}) collective-permute-start(f32[2,64,128]{2,1,0:T(8,128)} %misfit_ref.1), channel_id=1, source_target_pairs={{0,2},{1,9},{2,0},{3,11},{4,6},{5,13},{6,4},{7,15},{8,10},{9,1},{1... | collective-permute-start | bytes 196616 | tf_op jit(solution)/shard_map/ppermute | solution.py:124
  6.2 0.8 %copy-done.1 = f32[2,64,128]{2,1,0:T(8,128)S(1)} copy-done((f32[2,64,128]{2,1,0:T(8,128)S(1)}, f32[2,64,128]{2,1,0:T(8,128)}, u32[]{:S(2)}) %copy-start.1) | copy-done | bytes 65560
  7.1 0.8 %copy-done.2 = f32[2,64,128]{2,1,0:T(8,128)S(1)} copy-done((f32[2,64,128]{2,1,0:T(8,128)S(1)}, f32[2,64,128]{2,1,0:T(8,128)}, u32[]{:S(2)}) %copy-start.2) | copy-done | bytes 65560
  7.9 0.1 prepare.1
  8.0 0.0 collective-permute-done.refs_2_
  8.0 1.2 %collective-permute-done.1.refs_3_ = f32[2,64,128]{2,1,0:T(8,128)S(1)} collective-permute-done((f32[2,64,128]{2,1,0:T(8,128)}, f32[2,64,128]{2,1,0:T(8,128)S(1)}, u32[]{:S(2)}, u32[]{:S(2)}) %collective-permute-start.1) | collective-permute-done | bytes 65568 | tf_op jit(solution)/shard_map/ppermute | solution.py:124
  9.2 0.1 join.1
  9.3 1.6 %collective-permute-start.5 = (f32[2,2,64,128]{3,2,1,0:T(8,128)S(1)}, f32[2,2,64,128]{3,2,1,0:T(8,128)S(1)}, u32[]{:S(2)}, u32[]{:S(2)}) collective-permute-start(f32[2,2,64,128]{3,2,1,0:T(8,128)S(1)} %get-tuple-element.40), channel_id=1, source_target_pairs={{0,4},{1,9},{2,6},{3,11},{4,0},{5,13},{6,2},{7,15},{8,12},{9,1},{1... | collective-permute-start | bytes 393224 | tf_op jit(solution)/shard_map/ppermute | solution.py:124
  11.0 0.4 %collective-permute-start.2 = (f32[2,2,64,128]{3,2,1,0:T(8,128)S(1)}, f32[2,2,64,128]{3,2,1,0:T(8,128)S(1)}, u32[]{:S(2)}, u32[]{:S(2)}) collective-permute-start(f32[2,2,64,128]{3,2,1,0:T(8,128)S(1)} %get-tuple-element.39), channel_id=1, source_target_pairs={{0,4},{1,3},{2,6},{3,1},{4,0},{5,7},{6,2},{7,5},{8,12},{9,11},{10,... | collective-permute-start | bytes 393224 | tf_op jit(solution)/shard_map/ppermute | solution.py:124
  11.4 3.3 %collective-permute-done.5 = f32[2,2,64,128]{3,2,1,0:T(8,128)S(1)} collective-permute-done((f32[2,2,64,128]{3,2,1,0:T(8,128)S(1)}, f32[2,2,64,128]{3,2,1,0:T(8,128)S(1)}, u32[]{:S(2)}, u32[]{:S(2)}) %collective-permute-start.5) | collective-permute-done | bytes 131104 | tf_op jit(solution)/shard_map/ppermute | solution.py:124
  14.7 1.2 %collective-permute-start.6 = (f32[4,2,64,128]{3,2,1,0:T(8,128)S(1)}, f32[4,2,64,128]{3,2,1,0:T(8,128)S(1)}, u32[]{:S(2)}, u32[]{:S(2)}) collective-permute-start(f32[4,2,64,128]{3,2,1,0:T(8,128)S(1)} %pad_maximum_fusion.1), channel_id=1, source_target_pairs={{0,2},{1,5},{2,0},{3,7},{4,6},{5,1},{6,4},{7,3},{8,10},{9,13},{10,... | collective-permute-start | bytes 786440 | tf_op jit(solution)/shard_map/ppermute | solution.py:124
  16.0 0.1 collective-permute-done.2
  16.1 3.1 %collective-permute-start.3 = (f32[4,2,64,128]{3,2,1,0:T(8,128)S(1)}, f32[4,2,64,128]{3,2,1,0:T(8,128)S(1)}, u32[]{:S(2)}, u32[]{:S(2)}) collective-permute-start(f32[4,2,64,128]{3,2,1,0:T(8,128)S(1)} %pad_maximum_fusion), channel_id=1, source_target_pairs={{0,8},{1,5},{2,10},{3,7},{4,12},{5,1},{6,14},{7,3},{8,0},{9,13},{1... | collective-permute-start | bytes 786440 | tf_op jit(solution)/shard_map/ppermute | solution.py:124
  19.3 1.9 %collective-permute-done.6 = f32[4,2,64,128]{3,2,1,0:T(8,128)S(1)} collective-permute-done((f32[4,2,64,128]{3,2,1,0:T(8,128)S(1)}, f32[4,2,64,128]{3,2,1,0:T(8,128)S(1)}, u32[]{:S(2)}, u32[]{:S(2)}) %collective-permute-start.6) | collective-permute-done | bytes 262176 | tf_op jit(solution)/shard_map/ppermute | solution.py:124
  21.2 0.1 collective-permute-start.7
  21.3 0.7 %collective-permute-start.8 = (f32[2,1,64,128]{3,2,1,0:T(8,128)S(1)}, f32[2,1,64,128]{3,2,1,0:T(8,128)S(1)}, u32[]{:S(2)}, u32[]{:S(2)}) collective-permute-start(f32[2,1,64,128]{3,2,1,0:T(8,128)S(1)} %slice_select_fusion.1), channel_id=1, source_target_pairs={{1,2},{2,1},{3,4},{4,3},{5,6},{6,5},{7,8},{8,7},{9,10},{10,9},{11,... | collective-permute-start | bytes 196616 | tf_op jit(solution)/shard_map/ppermute | solution.py:139
  22.0 3.6 %collective-permute-done.3 = f32[4,2,64,128]{3,2,1,0:T(8,128)S(1)} collective-permute-done((f32[4,2,64,128]{3,2,1,0:T(8,128)S(1)}, f32[4,2,64,128]{3,2,1,0:T(8,128)S(1)}, u32[]{:S(2)}, u32[]{:S(2)}) %collective-permute-start.3) | collective-permute-done | bytes 262176 | tf_op jit(solution)/shard_map/ppermute | solution.py:124
  25.6 0.6 %collective-permute-start.4 = (f32[8,2,64,128]{3,2,1,0:T(8,128)S(1)}, f32[8,2,64,128]{3,2,1,0:T(8,128)S(1)}, u32[]{:S(2)}, u32[]{:S(2)}) collective-permute-start(f32[8,2,64,128]{3,2,1,0:T(8,128)S(1)} %constant_dynamic-update-slice_fusion.mine_ref), channel_id=1, source_target_pairs={{0,1},{1,0},{2,3},{3,2},{4,5},{5,4},{6,7},{7,6},{8,9},{9,8},{10,11... | collective-permute-start | bytes 1572872 | tf_op jit(solution)/shard_map/ppermute | solution.py:140
  26.2 1.5 %setup.1 = (f32[12,8,32,128]{3,2,1,0:T(8,128)S(1)}, f32[4,9,32,128]{3,2,1,0:T(8,128)S(1)}, f32[4,8,32,128]{3,2,1,0:T(8,128)S(1)}, f32[8,8,32,128]{3,2,1,0:T(8,12...) custom-call(s32[1,2]{1,0:T(1,128)S(1)} %bitcast.13, ...), custom_call_target="tpu_custom_call" | custom-call | tf_op jit(solution)/shard_map/setup/pallas_call | solution.py:644
  27.8 0.0 collective-permute-done.8.far_ref
  27.8 0.1 collective-permute-start.9
  27.9 5.7 %solve.1.planes_ref = f32[6,64,128]{2,1,0:T(8,128)S(1)} custom-call(f32[8,2,64,128]{3,2,1,0:T(8,128)S(1)} %constant_dynamic-update-slice_fusion.mine_ref, f32[8,2,64,128]{3,2,1,0:T(8,128)S(1)} %collective-permute-done.4.theirs_ref, f32[12,8,32,128]{3,2,1,0:T(8,128)S(1)} %get-tuple-element.52.inner, f32[4,9,32,128]{3,2,1,0:T(8,128)S(1)} %get-tuple-element.53.outer_x, ...), custom_call_target="tpu_custom_call" | custom-call | tf_op jit(solution)/shard_map/solve/pallas_call | solution.py:654
  33.7 0.0 collective-permute-done.9.near_ref
  33.7 0.2 finish.1
  33.9 0.5 %collective-permute-start.10 = (f32[2,96,128]{2,1,0:T(8,128)S(1)}, f32[2,96,128]{2,1,0:T(8,128)S(1)}, u32[]{:S(2)}, u32[]{:S(2)}) collective-permute-start(f32[2,96,128]{2,1,0:T(8,128)S(1)} %get-tuple-element.65), channel_id=1, source_target_pairs={{0,1},{1,0},{2,3},{3,2},{4,5},{5,4},{6,7},{7,6},{8,9},{9,8},{10,11... | collective-permute-start | bytes 294920 | tf_op jit(solution)/shard_map/ppermute | solution.py:688
  34.5 2.5 %collective-permute-start.11 = (f32[2,32,128]{2,1,0:T(8,128)S(1)}, f32[2,32,128]{2,1,0:T(8,128)S(1)}, u32[]{:S(2)}, u32[]{:S(2)}) collective-permute-start(f32[2,32,128]{2,1,0:T(8,128)S(1)} %get-tuple-element.73), channel_id=1, source_target_pairs={{0,16},{1,17},{2,18},{3,19},{4,20},{5,21},{6,22},{7,23},{8,24},{9,... | collective-permute-start | bytes 98312 | tf_op jit(solution)/shard_map/ppermute | solution.py:697
  36.9 0.1 collective-permute-start.12
  37.1 0.7 %pad_maximum_fusion.2 = f32[2,2,64,128]{3,2,1,0:T(8,128)} fusion(f32[1,2,64,128]{3,2,1,0:T(8,128)S(1)} %get-tuple-element.71, f32[1,2,64,128]{3,2,1,0:T(8,128)S(1)} %get-tuple-element.70), kind=kLoop, calls=%fused_computation.2 | loop fusion | flops 32768 | bytes 262144 | tf_op jit(solution)/shard_map/stack | solution.py:699
  37.7 1.2 %collective-permute-done.11 = f32[2,32,128]{2,1,0:T(8,128)S(1)} collective-permute-done((f32[2,32,128]{2,1,0:T(8,128)S(1)}, f32[2,32,128]{2,1,0:T(8,128)S(1)}, u32[]{:S(2)}, u32[]{:S(2)}) %collective-permute-start.11) | collective-permute-done | bytes 32800 | tf_op jit(solution)/shard_map/ppermute | solution.py:697
  38.9 1.4 %collective-permute-done.12 = f32[2,32,128]{2,1,0:T(8,128)S(1)} collective-permute-done((f32[2,32,128]{2,1,0:T(8,128)S(1)}, f32[2,32,128]{2,1,0:T(8,128)S(1)}, u32[]{:S(2)}, u32[]{:S(2)}) %collective-permute-start.12) | collective-permute-done | bytes 32800 | tf_op jit(solution)/shard_map/ppermute | solution.py:697
  40.3 0.6 %add_add_fusion = f32[2,32,128]{2,1,0:T(8,128)} fusion(f32[2,32,128]{2,1,0:T(8,128)S(1)} %collective-permute-done.11, f32[2,32,128]{2,1,0:T(8,128)S(1)} %collective-permute-done.12, f32[2,32,128]{2,1,0:T(8,128)S(1)} %get-tuple-element.67, f32[2,96,128]{2,1,0:T(8,128)S(1)} %collective-permute-done.10), kind=kLoop, calls=%fused_computation.8 | loop fusion | flops 24576 | bytes 163840 | tf_op jit(solution)/shard_map/add | solution.py:703
  (27 shorter events, 0.2 us)
Async XLA Ops:
  0.6 20.6 %copy-start = (f32[2,2,64,128]{3,2,1,0:T(8,128)S(1)}, f32[2,2,64,128]{3,2,1,0:T(8,128)}, u32[]{:S(2)}) copy-start(f32[2,2,64,128]{3,2,1,0:T(8,128)} %state_ref.1) | copy-start | bytes 393220
  0.6 7.4 %collective-permute-start = (f32[2,64,128]{2,1,0:T(8,128)}, f32[2,64,128]{2,1,0:T(8,128)S(1)}, u32[]{:S(2)}, u32[]{:S(2)}) collective-permute-start(f32[2,64,128]{2,1,0:T(8,128)} %kappa_ref.1), channel_id=1, source_target_pairs={{0,8},{1,3},{2,10},{3,1},{4,12},{5,7},{6,14},{7,5},{8,0},{9,11},{1... | collective-permute-start | bytes 196616 | tf_op jit(solution)/shard_map/ppermute | solution.py:124
  4.7 4.5 %collective-permute-start.1 = (f32[2,64,128]{2,1,0:T(8,128)}, f32[2,64,128]{2,1,0:T(8,128)S(1)}, u32[]{:S(2)}, u32[]{:S(2)}) collective-permute-start(f32[2,64,128]{2,1,0:T(8,128)} %misfit_ref.1), channel_id=1, source_target_pairs={{0,2},{1,9},{2,0},{3,11},{4,6},{5,13},{6,4},{7,15},{8,10},{9,1},{1... | collective-permute-start | bytes 196616 | tf_op jit(solution)/shard_map/ppermute | solution.py:124
  6.2 0.8 %copy-start.1 = (f32[2,64,128]{2,1,0:T(8,128)S(1)}, f32[2,64,128]{2,1,0:T(8,128)}, u32[]{:S(2)}) copy-start(f32[2,64,128]{2,1,0:T(8,128)} %kappa_ref.1) | copy-start | bytes 196612
  7.1 0.8 %copy-start.2 = (f32[2,64,128]{2,1,0:T(8,128)S(1)}, f32[2,64,128]{2,1,0:T(8,128)}, u32[]{:S(2)}) copy-start(f32[2,64,128]{2,1,0:T(8,128)} %misfit_ref.1) | copy-start | bytes 196612
  9.3 5.4 %collective-permute-start.5 = (f32[2,2,64,128]{3,2,1,0:T(8,128)S(1)}, f32[2,2,64,128]{3,2,1,0:T(8,128)S(1)}, u32[]{:S(2)}, u32[]{:S(2)}) collective-permute-start(f32[2,2,64,128]{3,2,1,0:T(8,128)S(1)} %get-tuple-element.40), channel_id=1, source_target_pairs={{0,4},{1,9},{2,6},{3,11},{4,0},{5,13},{6,2},{7,15},{8,12},{9,1},{1... | collective-permute-start | bytes 393224 | tf_op jit(solution)/shard_map/ppermute | solution.py:124
  11.0 15.2 %copy-start.3 = (s32[2]{0:T(128)S(1)}, s32[2]{0:T(128)}, u32[]{:S(2)}) copy-start(s32[2]{0:T(128)} %param.11) | copy-start | bytes 28
  11.0 15.2 %copy-start.4 = (f32[4]{0:T(128)S(1)}, f32[4]{0:T(128)}, u32[]{:S(2)}) copy-start(f32[4]{0:T(128)} %param.9) | copy-start | bytes 52
  11.0 15.2 %copy-start.5 = (f32[4]{0:T(128)S(1)}, f32[4]{0:T(128)}, u32[]{:S(2)}) copy-start(f32[4]{0:T(128)} %param.10) | copy-start | bytes 52
  11.0 5.1 %collective-permute-start.2 = (f32[2,2,64,128]{3,2,1,0:T(8,128)S(1)}, f32[2,2,64,128]{3,2,1,0:T(8,128)S(1)}, u32[]{:S(2)}, u32[]{:S(2)}) collective-permute-start(f32[2,2,64,128]{3,2,1,0:T(8,128)S(1)} %get-tuple-element.39), channel_id=1, source_target_pairs={{0,4},{1,3},{2,6},{3,1},{4,0},{5,7},{6,2},{7,5},{8,12},{9,11},{10,... | collective-permute-start | bytes 393224 | tf_op jit(solution)/shard_map/ppermute | solution.py:124
  14.7 6.4 %collective-permute-start.6 = (f32[4,2,64,128]{3,2,1,0:T(8,128)S(1)}, f32[4,2,64,128]{3,2,1,0:T(8,128)S(1)}, u32[]{:S(2)}, u32[]{:S(2)}) collective-permute-start(f32[4,2,64,128]{3,2,1,0:T(8,128)S(1)} %pad_maximum_fusion.1), channel_id=1, source_target_pairs={{0,2},{1,5},{2,0},{3,7},{4,6},{5,1},{6,4},{7,3},{8,10},{9,13},{10,... | collective-permute-start | bytes 786440 | tf_op jit(solution)/shard_map/ppermute | solution.py:124
  16.1 9.4 %collective-permute-start.3 = (f32[4,2,64,128]{3,2,1,0:T(8,128)S(1)}, f32[4,2,64,128]{3,2,1,0:T(8,128)S(1)}, u32[]{:S(2)}, u32[]{:S(2)}) collective-permute-start(f32[4,2,64,128]{3,2,1,0:T(8,128)S(1)} %pad_maximum_fusion), channel_id=1, source_target_pairs={{0,8},{1,5},{2,10},{3,7},{4,12},{5,1},{6,14},{7,3},{8,0},{9,13},{1... | collective-permute-start | bytes 786440 | tf_op jit(solution)/shard_map/ppermute | solution.py:124
  21.2 5.0 %collective-permute-start.7 = (f32[8,2,64,128]{3,2,1,0:T(8,128)S(1)}, f32[8,2,64,128]{3,2,1,0:T(8,128)S(1)}, u32[]{:S(2)}, u32[]{:S(2)}) collective-permute-start(f32[8,2,64,128]{3,2,1,0:T(8,128)S(1)} %constant_dynamic-update-slice_fusion.3.mine_ref), channel_id=1, source_target_pairs={{0,1},{1,0},{2,3},{3,2},{4,5},{5,4},{6,7},{7,6},{8,9},{9,8},{10,11... | collective-permute-start | bytes 1572872 | tf_op jit(solution)/shard_map/ppermute | solution.py:140
  21.3 6.5 %collective-permute-start.8 = (f32[2,1,64,128]{3,2,1,0:T(8,128)S(1)}, f32[2,1,64,128]{3,2,1,0:T(8,128)S(1)}, u32[]{:S(2)}, u32[]{:S(2)}) collective-permute-start(f32[2,1,64,128]{3,2,1,0:T(8,128)S(1)} %slice_select_fusion.1), channel_id=1, source_target_pairs={{1,2},{2,1},{3,4},{4,3},{5,6},{6,5},{7,8},{8,7},{9,10},{10,9},{11,... | collective-permute-start | bytes 196616 | tf_op jit(solution)/shard_map/ppermute | solution.py:139
  25.6 2.4 %collective-permute-start.4 = (f32[8,2,64,128]{3,2,1,0:T(8,128)S(1)}, f32[8,2,64,128]{3,2,1,0:T(8,128)S(1)}, u32[]{:S(2)}, u32[]{:S(2)}) collective-permute-start(f32[8,2,64,128]{3,2,1,0:T(8,128)S(1)} %constant_dynamic-update-slice_fusion.mine_ref), channel_id=1, source_target_pairs={{0,1},{1,0},{2,3},{3,2},{4,5},{5,4},{6,7},{7,6},{8,9},{9,8},{10,11... | collective-permute-start | bytes 1572872 | tf_op jit(solution)/shard_map/ppermute | solution.py:140
  27.8 5.8 %collective-permute-start.9 = (f32[3,64,128]{2,1,0:T(8,128)S(1)}, f32[3,64,128]{2,1,0:T(8,128)S(1)}, u32[]{:S(2)}, u32[]{:S(2)}) collective-permute-start(f32[3,64,128]{2,1,0:T(8,128)S(1)} %fusion), channel_id=1, source_target_pairs={{0,1},{1,0},{2,3},{3,2},{4,5},{5,4},{6,7},{7,6},{8,9},{9,8},{10,11... | collective-permute-start | bytes 294920 | tf_op jit(solution)/shard_map/ppermute | solution.py:145
  33.9 3.1 %collective-permute-start.10 = (f32[2,96,128]{2,1,0:T(8,128)S(1)}, f32[2,96,128]{2,1,0:T(8,128)S(1)}, u32[]{:S(2)}, u32[]{:S(2)}) collective-permute-start(f32[2,96,128]{2,1,0:T(8,128)S(1)} %get-tuple-element.65), channel_id=1, source_target_pairs={{0,1},{1,0},{2,3},{3,2},{4,5},{5,4},{6,7},{7,6},{8,9},{9,8},{10,11... | collective-permute-start | bytes 294920 | tf_op jit(solution)/shard_map/ppermute | solution.py:688
  34.5 4.4 %collective-permute-start.11 = (f32[2,32,128]{2,1,0:T(8,128)S(1)}, f32[2,32,128]{2,1,0:T(8,128)S(1)}, u32[]{:S(2)}, u32[]{:S(2)}) collective-permute-start(f32[2,32,128]{2,1,0:T(8,128)S(1)} %get-tuple-element.73), channel_id=1, source_target_pairs={{0,16},{1,17},{2,18},{3,19},{4,20},{5,21},{6,22},{7,23},{8,24},{9,... | collective-permute-start | bytes 98312 | tf_op jit(solution)/shard_map/ppermute | solution.py:697
  36.9 3.4 %collective-permute-start.12 = (f32[2,32,128]{2,1,0:T(8,128)S(1)}, f32[2,32,128]{2,1,0:T(8,128)S(1)}, u32[]{:S(2)}, u32[]{:S(2)}) collective-permute-start(f32[2,32,128]{2,1,0:T(8,128)S(1)} %get-tuple-element.72), channel_id=1, source_target_pairs={{0,17},{1,16},{2,19},{3,18},{4,21},{5,20},{6,23},{7,22},{8,25},{9,... | collective-permute-start | bytes 98312 | tf_op jit(solution)/shard_map/ppermute | solution.py:697

commit v16 on v15

--- a/solution.py
+++ b/solution.py
@@ -63,9 +63,8 @@
     while mask > 1:
         falling.append(mask)
         mask //= 2
-    if flip:
-        return falling[::-1], falling[:1] + falling[:0:-1]
-    return falling, falling[-1:] + falling[:-1]
+    rotated = falling[-1:] + falling[:-1]
+    return (rotated, falling) if flip else (falling, rotated)
 
 
 def block_pair(u, holder, peers, flip):

time: 41.1 us -> 45.3 us (1.10)
  starting transfers between devices: 16.6 us -> 24.6 us
  waiting for transfers between devices: 12.6 us -> 8.77 us
    ppermute x6, waiting for transfers between devices: 10.1 us -> 6.21 us  [gather_blocks(): arrived.append(lax.ppermute(held[at], axis, pairs))]
    ppermute x6, starting transfers between devices: 12 us -> 15.2 us  [gather_blocks(): arrived.append(lax.ppermute(held[at], axis, pairs))]
    ppermute x2, starting transfers between devices: 2.57 us -> 5.46 us  [whole_grid(): shares.append(lax.ppermute(send[k - 1, side], ('pole', 'space'), pairs))]
    ppermute x2, starting transfers between devices: 0.7 us -> 2.64 us  [gather_blocks(): other = [lax.ppermute(part, axis, swap) for part in held]]
  transfers between devices with their start and end apart: 13 -> 13, of which waited for: 7 -> 7; matrix products, arithmetic and copies ran while one was open for 2% -> 2% of each run, Pallas kernels for 18% -> 16%
where the time goes in v16:
time: 45.3 us; the launch traced here: 45.1 us
  starting transfers between devices  24.6 us (54%)
  waiting for transfers between devices  8.77 us (19%)
  Pallas kernels  7.71 us (17%)
  local copies, waits for them, and re-layouts  1.79 us (4%)
  other arithmetic  1.37 us (3%)
  between operations  0.82 us (2%)
    ppermute x6, starting transfers between devices, gather_blocks(): arrived.append(lax.ppermute(held[at], axis, pairs))  15.2 us
    ppermute x6, waiting for transfers between devices, gather_blocks(): arrived.append(lax.ppermute(held[at], axis, pairs))  6.21 us
    pallas_call x1, Pallas kernels, whole_grid(): pl.pallas_call(functools.partial(solve_kernel, own=own), out_shape=jax.Sh...  5.72 us
    ppermute x2, starting transfers between devices, whole_grid(): shares.append(lax.ppermute(send[k - 1, side], ('pole', 'space'), pairs))  5.46 us
    ppermute x2, starting transfers between devices, gather_blocks(): other = [lax.ppermute(part, axis, swap) for part in held]  2.64 us
    ppermute x2, waiting for transfers between devices, whole_grid(): shares.append(lax.ppermute(send[k - 1, side], ('pole', 'space'), pairs))  2.55 us
    unnamed x17, local copies, waits for them, and re-layouts  1.75 us
    pallas_call x1, Pallas kernels, whole_grid(): pl.pallas_call(setup_kernel, out_shape=[jax.ShapeDtypeStruct(shape, jnp.f...  1.53 us
  transfers between devices with their start and end apart: 13, of which 7 were waited for; matrix products, arithmetic and copies ran while one was open for 2% of the time, Pallas kernels for 16%

profile of v16, /device:TPU:0, one launch (start us, length us, event | category | flops | bytes accessed | tf_op | source)
XLA Modules:
  0.0 45.1 jit_solution(8149950806869000847)
XLA Ops:
  0.6 4.1 %collective-permute-start = (f32[2,64,128]{2,1,0:T(8,128)}, f32[2,64,128]{2,1,0:T(8,128)S(1)}, u32[]{:S(2)}, u32[]{:S(2)}) collective-permute-start(f32[2,64,128]{2,1,0:T(8,128)} %kappa_ref.1), channel_id=1, source_target_pairs={{0,8},{1,3},{2,10},{3,1},{4,12},{5,7},{6,14},{7,5},{8,0},{9,11},{1... | collective-permute-start | bytes 196616 | tf_op jit(solution)/shard_map/ppermute | solution.py:123
  4.7 1.5 %collective-permute-start.1 = (f32[2,64,128]{2,1,0:T(8,128)}, f32[2,64,128]{2,1,0:T(8,128)S(1)}, u32[]{:S(2)}, u32[]{:S(2)}) collective-permute-start(f32[2,64,128]{2,1,0:T(8,128)} %misfit_ref.1), channel_id=1, source_target_pairs={{0,2},{1,9},{2,0},{3,11},{4,6},{5,13},{6,4},{7,15},{8,10},{9,1},{1... | collective-permute-start | bytes 196616 | tf_op jit(solution)/shard_map/ppermute | solution.py:123
  6.2 0.8 %copy-done.1 = f32[2,64,128]{2,1,0:T(8,128)S(1)} copy-done((f32[2,64,128]{2,1,0:T(8,128)S(1)}, f32[2,64,128]{2,1,0:T(8,128)}, u32[]{:S(2)}) %copy-start.1) | copy-done | bytes 65560
  7.1 0.8 %copy-done.2 = f32[2,64,128]{2,1,0:T(8,128)S(1)} copy-done((f32[2,64,128]{2,1,0:T(8,128)S(1)}, f32[2,64,128]{2,1,0:T(8,128)}, u32[]{:S(2)}) %copy-start.2) | copy-done | bytes 65560
  7.9 0.1 prepare.1
  8.0 0.0 collective-permute-done.refs_2_
  8.0 1.2 %collective-permute-done.1.refs_3_ = f32[2,64,128]{2,1,0:T(8,128)S(1)} collective-permute-done((f32[2,64,128]{2,1,0:T(8,128)}, f32[2,64,128]{2,1,0:T(8,128)S(1)}, u32[]{:S(2)}, u32[]{:S(2)}) %collective-permute-start.1) | collective-permute-done | bytes 65568 | tf_op jit(solution)/shard_map/ppermute | solution.py:123
  9.2 0.1 join.1
  9.3 1.6 %collective-permute-start.5 = (f32[2,2,64,128]{3,2,1,0:T(8,128)S(1)}, f32[2,2,64,128]{3,2,1,0:T(8,128)S(1)}, u32[]{:S(2)}, u32[]{:S(2)}) collective-permute-start(f32[2,2,64,128]{3,2,1,0:T(8,128)S(1)} %get-tuple-element.40), channel_id=1, source_target_pairs={{0,4},{1,9},{2,6},{3,11},{4,0},{5,13},{6,2},{7,15},{8,12},{9,1},{1... | collective-permute-start | bytes 393224 | tf_op jit(solution)/shard_map/ppermute | solution.py:123
  11.0 2.9 %collective-permute-start.2 = (f32[2,2,64,128]{3,2,1,0:T(8,128)S(1)}, f32[2,2,64,128]{3,2,1,0:T(8,128)S(1)}, u32[]{:S(2)}, u32[]{:S(2)}) collective-permute-start(f32[2,2,64,128]{3,2,1,0:T(8,128)S(1)} %get-tuple-element.39), channel_id=1, source_target_pairs={{0,8},{1,5},{2,10},{3,7},{4,12},{5,1},{6,14},{7,3},{8,0},{9,13},{1... | collective-permute-start | bytes 393224 | tf_op jit(solution)/shard_map/ppermute | solution.py:123
  13.9 0.9 %collective-permute-done.5 = f32[2,2,64,128]{3,2,1,0:T(8,128)S(1)} collective-permute-done((f32[2,2,64,128]{3,2,1,0:T(8,128)S(1)}, f32[2,2,64,128]{3,2,1,0:T(8,128)S(1)}, u32[]{:S(2)}, u32[]{:S(2)}) %collective-permute-start.5) | collective-permute-done | bytes 131104 | tf_op jit(solution)/shard_map/ppermute | solution.py:123
  14.8 2.1 %collective-permute-start.6 = (f32[4,2,64,128]{3,2,1,0:T(8,128)S(1)}, f32[4,2,64,128]{3,2,1,0:T(8,128)S(1)}, u32[]{:S(2)}, u32[]{:S(2)}) collective-permute-start(f32[4,2,64,128]{3,2,1,0:T(8,128)S(1)} %pad_maximum_fusion.1), channel_id=1, source_target_pairs={{0,2},{1,5},{2,0},{3,7},{4,6},{5,1},{6,4},{7,3},{8,10},{9,13},{10,... | collective-permute-start | bytes 786440 | tf_op jit(solution)/shard_map/ppermute | solution.py:123
  16.9 0.6 %collective-permute-done.2 = f32[2,2,64,128]{3,2,1,0:T(8,128)S(1)} collective-permute-done((f32[2,2,64,128]{3,2,1,0:T(8,128)S(1)}, f32[2,2,64,128]{3,2,1,0:T(8,128)S(1)}, u32[]{:S(2)}, u32[]{:S(2)}) %collective-permute-start.2) | collective-permute-done | bytes 131104 | tf_op jit(solution)/shard_map/ppermute | solution.py:123
  17.5 3.0 %collective-permute-start.3 = (f32[4,2,64,128]{3,2,1,0:T(8,128)S(1)}, f32[4,2,64,128]{3,2,1,0:T(8,128)S(1)}, u32[]{:S(2)}, u32[]{:S(2)}) collective-permute-start(f32[4,2,64,128]{3,2,1,0:T(8,128)S(1)} %pad_maximum_fusion), channel_id=1, source_target_pairs={{0,4},{1,3},{2,6},{3,1},{4,0},{5,7},{6,2},{7,5},{8,12},{9,11},{10,... | collective-permute-start | bytes 786440 | tf_op jit(solution)/shard_map/ppermute | solution.py:123
  20.6 2.2 %collective-permute-done.6 = f32[4,2,64,128]{3,2,1,0:T(8,128)S(1)} collective-permute-done((f32[4,2,64,128]{3,2,1,0:T(8,128)S(1)}, f32[4,2,64,128]{3,2,1,0:T(8,128)S(1)}, u32[]{:S(2)}, u32[]{:S(2)}) %collective-permute-start.6) | collective-permute-done | bytes 262176 | tf_op jit(solution)/shard_map/ppermute | solution.py:123
  22.7 0.1 collective-permute-start.7
  22.8 0.7 %collective-permute-start.8 = (f32[2,1,64,128]{3,2,1,0:T(8,128)S(1)}, f32[2,1,64,128]{3,2,1,0:T(8,128)S(1)}, u32[]{:S(2)}, u32[]{:S(2)}) collective-permute-start(f32[2,1,64,128]{3,2,1,0:T(8,128)S(1)} %slice_select_fusion.1), channel_id=1, source_target_pairs={{1,2},{2,1},{3,4},{4,3},{5,6},{6,5},{7,8},{8,7},{9,10},{10,9},{11,... | collective-permute-start | bytes 196616 | tf_op jit(solution)/shard_map/ppermute | solution.py:138
  23.5 1.3 %collective-permute-done.3 = f32[4,2,64,128]{3,2,1,0:T(8,128)S(1)} collective-permute-done((f32[4,2,64,128]{3,2,1,0:T(8,128)S(1)}, f32[4,2,64,128]{3,2,1,0:T(8,128)S(1)}, u32[]{:S(2)}, u32[]{:S(2)}) %collective-permute-start.3) | collective-permute-done | bytes 262176 | tf_op jit(solution)/shard_map/ppermute | solution.py:123
  24.9 2.6 %collective-permute-start.4 = (f32[8,2,64,128]{3,2,1,0:T(8,128)S(1)}, f32[8,2,64,128]{3,2,1,0:T(8,128)S(1)}, u32[]{:S(2)}, u32[]{:S(2)}) collective-permute-start(f32[8,2,64,128]{3,2,1,0:T(8,128)S(1)} %constant_dynamic-update-slice_fusion.mine_ref), channel_id=1, source_target_pairs={{0,1},{1,0},{2,3},{3,2},{4,5},{5,4},{6,7},{7,6},{8,9},{9,8},{10,11... | collective-permute-start | bytes 1572872 | tf_op jit(solution)/shard_map/ppermute | solution.py:139
  27.5 1.5 %setup.1 = (f32[12,8,32,128]{3,2,1,0:T(8,128)S(1)}, f32[4,9,32,128]{3,2,1,0:T(8,128)S(1)}, f32[4,8,32,128]{3,2,1,0:T(8,128)S(1)}, f32[8,8,32,128]{3,2,1,0:T(8,12...) custom-call(s32[1,2]{1,0:T(1,128)S(1)} %bitcast.13, ...), custom_call_target="tpu_custom_call" | custom-call | tf_op jit(solution)/shard_map/setup/pallas_call | solution.py:643
  29.1 0.3 collective-permute-start.9
  29.4 0.0 collective-permute-done.4.theirs_ref
  29.4 5.7 %solve.1.planes_ref = f32[6,64,128]{2,1,0:T(8,128)S(1)} custom-call(f32[8,2,64,128]{3,2,1,0:T(8,128)S(1)} %constant_dynamic-update-slice_fusion.mine_ref, f32[8,2,64,128]{3,2,1,0:T(8,128)S(1)} %collective-permute-done.4.theirs_ref, f32[12,8,32,128]{3,2,1,0:T(8,128)S(1)} %get-tuple-element.52.inner, f32[4,9,32,128]{3,2,1,0:T(8,128)S(1)} %get-tuple-element.53.outer_x, ...), custom_call_target="tpu_custom_call" | custom-call | tf_op jit(solution)/shard_map/solve/pallas_call | solution.py:653
  35.1 0.0 collective-permute-done.9.near_ref
  35.1 0.2 finish.1
  35.4 0.4 collective-permute-start.10
  35.7 5.3 %collective-permute-start.11 = (f32[2,32,128]{2,1,0:T(8,128)S(1)}, f32[2,32,128]{2,1,0:T(8,128)S(1)}, u32[]{:S(2)}, u32[]{:S(2)}) collective-permute-start(f32[2,32,128]{2,1,0:T(8,128)S(1)} %get-tuple-element.73), channel_id=1, source_target_pairs={{0,16},{1,17},{2,18},{3,19},{4,20},{5,21},{6,22},{7,23},{8,24},{9,... | collective-permute-start | bytes 98312 | tf_op jit(solution)/shard_map/ppermute | solution.py:696
  41.1 0.1 collective-permute-start.12
  41.2 0.7 %pad_maximum_fusion.2 = f32[2,2,64,128]{3,2,1,0:T(8,128)} fusion(f32[1,2,64,128]{3,2,1,0:T(8,128)S(1)} %get-tuple-element.71, f32[1,2,64,128]{3,2,1,0:T(8,128)S(1)} %get-tuple-element.70), kind=kLoop, calls=%fused_computation.2 | loop fusion | flops 32768 | bytes 262144 | tf_op jit(solution)/shard_map/stack | solution.py:698
  41.9 1.2 %collective-permute-done.11 = f32[2,32,128]{2,1,0:T(8,128)S(1)} collective-permute-done((f32[2,32,128]{2,1,0:T(8,128)S(1)}, f32[2,32,128]{2,1,0:T(8,128)S(1)}, u32[]{:S(2)}, u32[]{:S(2)}) %collective-permute-start.11) | collective-permute-done | bytes 32800 | tf_op jit(solution)/shard_map/ppermute | solution.py:696
  43.1 1.4 %collective-permute-done.12 = f32[2,32,128]{2,1,0:T(8,128)S(1)} collective-permute-done((f32[2,32,128]{2,1,0:T(8,128)S(1)}, f32[2,32,128]{2,1,0:T(8,128)S(1)}, u32[]{:S(2)}, u32[]{:S(2)}) %collective-permute-start.12) | collective-permute-done | bytes 32800 | tf_op jit(solution)/shard_map/ppermute | solution.py:696
  44.4 0.6 %add_add_fusion = f32[2,32,128]{2,1,0:T(8,128)} fusion(f32[2,32,128]{2,1,0:T(8,128)S(1)} %collective-permute-done.11, f32[2,32,128]{2,1,0:T(8,128)S(1)} %collective-permute-done.12, f32[2,32,128]{2,1,0:T(8,128)S(1)} %get-tuple-element.67, f32[2,96,128]{2,1,0:T(8,128)S(1)} %collective-permute-done.10), kind=kLoop, calls=%fused_computation.8 | loop fusion | flops 24576 | bytes 163840 | tf_op jit(solution)/shard_map/add | solution.py:702
  (27 shorter events, 0.2 us)
Async XLA Ops:
  0.6 22.2 %copy-start = (f32[2,2,64,128]{3,2,1,0:T(8,128)S(1)}, f32[2,2,64,128]{3,2,1,0:T(8,128)}, u32[]{:S(2)}) copy-start(f32[2,2,64,128]{3,2,1,0:T(8,128)} %state_ref.1) | copy-start | bytes 393220
  0.6 7.4 %collective-permute-start = (f32[2,64,128]{2,1,0:T(8,128)}, f32[2,64,128]{2,1,0:T(8,128)S(1)}, u32[]{:S(2)}, u32[]{:S(2)}) collective-permute-start(f32[2,64,128]{2,1,0:T(8,128)} %kappa_ref.1), channel_id=1, source_target_pairs={{0,8},{1,3},{2,10},{3,1},{4,12},{5,7},{6,14},{7,5},{8,0},{9,11},{1... | collective-permute-start | bytes 196616 | tf_op jit(solution)/shard_map/ppermute | solution.py:123
  4.7 4.5 %collective-permute-start.1 = (f32[2,64,128]{2,1,0:T(8,128)}, f32[2,64,128]{2,1,0:T(8,128)S(1)}, u32[]{:S(2)}, u32[]{:S(2)}) collective-permute-start(f32[2,64,128]{2,1,0:T(8,128)} %misfit_ref.1), channel_id=1, source_target_pairs={{0,2},{1,9},{2,0},{3,11},{4,6},{5,13},{6,4},{7,15},{8,10},{9,1},{1... | collective-permute-start | bytes 196616 | tf_op jit(solution)/shard_map/ppermute | solution.py:123
  6.2 0.8 %copy-start.1 = (f32[2,64,128]{2,1,0:T(8,128)S(1)}, f32[2,64,128]{2,1,0:T(8,128)}, u32[]{:S(2)}) copy-start(f32[2,64,128]{2,1,0:T(8,128)} %kappa_ref.1) | copy-start | bytes 196612
  7.1 0.8 %copy-start.2 = (f32[2,64,128]{2,1,0:T(8,128)S(1)}, f32[2,64,128]{2,1,0:T(8,128)}, u32[]{:S(2)}) copy-start(f32[2,64,128]{2,1,0:T(8,128)} %misfit_ref.1) | copy-start | bytes 196612
  9.3 5.4 %collective-permute-start.5 = (f32[2,2,64,128]{3,2,1,0:T(8,128)S(1)}, f32[2,2,64,128]{3,2,1,0:T(8,128)S(1)}, u32[]{:S(2)}, u32[]{:S(2)}) collective-permute-start(f32[2,2,64,128]{3,2,1,0:T(8,128)S(1)} %get-tuple-element.40), channel_id=1, source_target_pairs={{0,4},{1,9},{2,6},{3,11},{4,0},{5,13},{6,2},{7,15},{8,12},{9,1},{1... | collective-permute-start | bytes 393224 | tf_op jit(solution)/shard_map/ppermute | solution.py:123
  11.0 16.5 %copy-start.3 = (s32[2]{0:T(128)S(1)}, s32[2]{0:T(128)}, u32[]{:S(2)}) copy-start(s32[2]{0:T(128)} %param.11) | copy-start | bytes 28
  11.0 16.5 %copy-start.4 = (f32[4]{0:T(128)S(1)}, f32[4]{0:T(128)}, u32[]{:S(2)}) copy-start(f32[4]{0:T(128)} %param.9) | copy-start | bytes 52
  11.0 16.5 %copy-start.5 = (f32[4]{0:T(128)S(1)}, f32[4]{0:T(128)}, u32[]{:S(2)}) copy-start(f32[4]{0:T(128)} %param.10) | copy-start | bytes 52
  11.0 6.5 %collective-permute-start.2 = (f32[2,2,64,128]{3,2,1,0:T(8,128)S(1)}, f32[2,2,64,128]{3,2,1,0:T(8,128)S(1)}, u32[]{:S(2)}, u32[]{:S(2)}) collective-permute-start(f32[2,2,64,128]{3,2,1,0:T(8,128)S(1)} %get-tuple-element.39), channel_id=1, source_target_pairs={{0,8},{1,5},{2,10},{3,7},{4,12},{5,1},{6,14},{7,3},{8,0},{9,13},{1... | collective-permute-start | bytes 393224 | tf_op jit(solution)/shard_map/ppermute | solution.py:123
  14.8 7.9 %collective-permute-start.6 = (f32[4,2,64,128]{3,2,1,0:T(8,128)S(1)}, f32[4,2,64,128]{3,2,1,0:T(8,128)S(1)}, u32[]{:S(2)}, u32[]{:S(2)}) collective-permute-start(f32[4,2,64,128]{3,2,1,0:T(8,128)S(1)} %pad_maximum_fusion.1), channel_id=1, source_target_pairs={{0,2},{1,5},{2,0},{3,7},{4,6},{5,1},{6,4},{7,3},{8,10},{9,13},{10,... | collective-permute-start | bytes 786440 | tf_op jit(solution)/shard_map/ppermute | solution.py:123
  17.5 7.4 %collective-permute-start.3 = (f32[4,2,64,128]{3,2,1,0:T(8,128)S(1)}, f32[4,2,64,128]{3,2,1,0:T(8,128)S(1)}, u32[]{:S(2)}, u32[]{:S(2)}) collective-permute-start(f32[4,2,64,128]{3,2,1,0:T(8,128)S(1)} %pad_maximum_fusion), channel_id=1, source_target_pairs={{0,4},{1,3},{2,6},{3,1},{4,0},{5,7},{6,2},{7,5},{8,12},{9,11},{10,... | collective-permute-start | bytes 786440 | tf_op jit(solution)/shard_map/ppermute | solution.py:123
  22.7 4.8 %collective-permute-start.7 = (f32[8,2,64,128]{3,2,1,0:T(8,128)S(1)}, f32[8,2,64,128]{3,2,1,0:T(8,128)S(1)}, u32[]{:S(2)}, u32[]{:S(2)}) collective-permute-start(f32[8,2,64,128]{3,2,1,0:T(8,128)S(1)} %constant_dynamic-update-slice_fusion.3.mine_ref), channel_id=1, source_target_pairs={{0,1},{1,0},{2,3},{3,2},{4,5},{5,4},{6,7},{7,6},{8,9},{9,8},{10,11... | collective-permute-start | bytes 1572872 | tf_op jit(solution)/shard_map/ppermute | solution.py:139
  22.8 6.2 %collective-permute-start.8 = (f32[2,1,64,128]{3,2,1,0:T(8,128)S(1)}, f32[2,1,64,128]{3,2,1,0:T(8,128)S(1)}, u32[]{:S(2)}, u32[]{:S(2)}) collective-permute-start(f32[2,1,64,128]{3,2,1,0:T(8,128)S(1)} %slice_select_fusion.1), channel_id=1, source_target_pairs={{1,2},{2,1},{3,4},{4,3},{5,6},{6,5},{7,8},{8,7},{9,10},{10,9},{11,... | collective-permute-start | bytes 196616 | tf_op jit(solution)/shard_map/ppermute | solution.py:138
  24.9 4.5 %collective-permute-start.4 = (f32[8,2,64,128]{3,2,1,0:T(8,128)S(1)}, f32[8,2,64,128]{3,2,1,0:T(8,128)S(1)}, u32[]{:S(2)}, u32[]{:S(2)}) collective-permute-start(f32[8,2,64,128]{3,2,1,0:T(8,128)S(1)} %constant_dynamic-update-slice_fusion.mine_ref), channel_id=1, source_target_pairs={{0,1},{1,0},{2,3},{3,2},{4,5},{5,4},{6,7},{7,6},{8,9},{9,8},{10,11... | collective-permute-start | bytes 1572872 | tf_op jit(solution)/shard_map/ppermute | solution.py:139
  29.1 6.0 %collective-permute-start.9 = (f32[3,64,128]{2,1,0:T(8,128)S(1)}, f32[3,64,128]{2,1,0:T(8,128)S(1)}, u32[]{:S(2)}, u32[]{:S(2)}) collective-permute-start(f32[3,64,128]{2,1,0:T(8,128)S(1)} %fusion), channel_id=1, source_target_pairs={{0,1},{1,0},{2,3},{3,2},{4,5},{5,4},{6,7},{7,6},{8,9},{9,8},{10,11... | collective-permute-start | bytes 294920 | tf_op jit(solution)/shard_map/ppermute | solution.py:144
  35.4 5.8 %collective-permute-start.10 = (f32[2,96,128]{2,1,0:T(8,128)S(1)}, f32[2,96,128]{2,1,0:T(8,128)S(1)}, u32[]{:S(2)}, u32[]{:S(2)}) collective-permute-start(f32[2,96,128]{2,1,0:T(8,128)S(1)} %get-tuple-element.65), channel_id=1, source_target_pairs={{0,1},{1,0},{2,3},{3,2},{4,5},{5,4},{6,7},{7,6},{8,9},{9,8},{10,11... | collective-permute-start | bytes 294920 | tf_op jit(solution)/shard_map/ppermute | solution.py:687
  35.7 7.3 %collective-permute-start.11 = (f32[2,32,128]{2,1,0:T(8,128)S(1)}, f32[2,32,128]{2,1,0:T(8,128)S(1)}, u32[]{:S(2)}, u32[]{:S(2)}) collective-permute-start(f32[2,32,128]{2,1,0:T(8,128)S(1)} %get-tuple-element.73), channel_id=1, source_target_pairs={{0,16},{1,17},{2,18},{3,19},{4,20},{5,21},{6,22},{7,23},{8,24},{9,... | collective-permute-start | bytes 98312 | tf_op jit(solution)/shard_map/ppermute | solution.py:696
  41.1 3.4 %collective-permute-start.12 = (f32[2,32,128]{2,1,0:T(8,128)S(1)}, f32[2,32,128]{2,1,0:T(8,128)S(1)}, u32[]{:S(2)}, u32[]{:S(2)}) collective-permute-start(f32[2,32,128]{2,1,0:T(8,128)S(1)} %get-tuple-element.72), channel_id=1, source_target_pairs={{0,17},{1,16},{2,19},{3,18},{4,21},{5,20},{6,23},{7,22},{8,25},{9,... | collective-permute-start | bytes 98312 | tf_op jit(solution)/shard_map/ppermute | solution.py:696

commit v17 on v15

--- a/solution.py
+++ b/solution.py
@@ -64,8 +64,8 @@
         falling.append(mask)
         mask //= 2
     if flip:
-        return falling[::-1], falling[:1] + falling[:0:-1]
-    return falling, falling[-1:] + falling[:-1]
+        return falling, falling[-1:] + falling[:-1]
+    return falling[::-1], falling[:1] + falling[:0:-1]
 
 
 def block_pair(u, holder, peers, flip):

time: 41.1 us -> 44.6 us (1.085)
  the two profiles are of different devices: /device:TPU:0 before, /device:TPU:25 now
where the time goes in v17:
time: 44.6 us; the launch traced here: 44.3 us
  waiting for transfers between devices  16.8 us (38%)
  starting transfers between devices  15.9 us (36%)
  Pallas kernels  7.69 us (17%)
  local copies, waits for them, and re-layouts  1.8 us (4%)
  other arithmetic  1.37 us (3%)
  between operations  0.82 us (2%)
    ppermute x6, waiting for transfers between devices, gather_blocks(): arrived.append(lax.ppermute(held[at], axis, pairs))  11.7 us
    ppermute x2, starting transfers between devices, gather_blocks(): other = [lax.ppermute(part, axis, swap) for part in held]  7.43 us
    pallas_call x1, Pallas kernels, whole_grid(): pl.pallas_call(functools.partial(solve_kernel, own=own), out_shape=jax.Sh...  5.72 us
    ppermute x6, starting transfers between devices, gather_blocks(): arrived.append(lax.ppermute(held[at], axis, pairs))  3.94 us
    ppermute x1, waiting for transfers between devices, gather_blocks(): lax.ppermute(jnp.where(even, states[:, :1], states[:, -1:]), axis, over)  2.63 us
    ppermute x2, waiting for transfers between devices, whole_grid(): shares.append(lax.ppermute(send[k - 1, side], ('pole', 'space'), pairs))  2.42 us
    ppermute x2, starting transfers between devices, whole_grid(): shares.append(lax.ppermute(send[k - 1, side], ('pole', 'space'), pairs))  1.96 us
    ppermute x1, starting transfers between devices, gather_blocks(): lax.ppermute(jnp.where(even, states[:, :1], states[:, -1:]), axis, over)  1.92 us
  transfers between devices with their start and end apart: 13, of which 7 were waited for; matrix products, arithmetic and copies ran while one was open for 2% of the time, Pallas kernels for 17%

profile of v17, /device:TPU:25, one launch (start us, length us, event | category | flops | bytes accessed | tf_op | source)
XLA Modules:
  0.0 44.3 jit_solution(16357773091035826971)
XLA Ops:
  0.6 0.1 collective-permute-start
  0.8 1.2 %collective-permute-start.1 = (f32[2,64,128]{2,1,0:T(8,128)}, f32[2,64,128]{2,1,0:T(8,128)S(1)}, u32[]{:S(2)}, u32[]{:S(2)}) collective-permute-start(f32[2,64,128]{2,1,0:T(8,128)} %misfit_ref.1), channel_id=1, source_target_pairs={{0,8},{1,3},{2,10},{3,1},{4,12},{5,7},{6,14},{7,5},{8,0},{9,11},{1... | collective-permute-start | bytes 196616 | tf_op jit(solution)/shard_map/ppermute | solution.py:124
  2.0 0.8 %copy-done.1 = f32[2,64,128]{2,1,0:T(8,128)S(1)} copy-done((f32[2,64,128]{2,1,0:T(8,128)S(1)}, f32[2,64,128]{2,1,0:T(8,128)}, u32[]{:S(2)}) %copy-start.1) | copy-done | bytes 65560
  2.8 0.8 %copy-done.2 = f32[2,64,128]{2,1,0:T(8,128)S(1)} copy-done((f32[2,64,128]{2,1,0:T(8,128)S(1)}, f32[2,64,128]{2,1,0:T(8,128)}, u32[]{:S(2)}) %copy-start.2) | copy-done | bytes 65560
  3.7 0.1 prepare.1
  3.8 1.7 %collective-permute-done.refs_2_ = f32[2,64,128]{2,1,0:T(8,128)S(1)} collective-permute-done((f32[2,64,128]{2,1,0:T(8,128)}, f32[2,64,128]{2,1,0:T(8,128)S(1)}, u32[]{:S(2)}, u32[]{:S(2)}) %collective-permute-start) | collective-permute-done | bytes 65568 | tf_op jit(solution)/shard_map/ppermute | solution.py:124
  5.5 0.1 join.1
  5.6 1.3 %collective-permute-start.5 = (f32[2,2,64,128]{3,2,1,0:T(8,128)S(1)}, f32[2,2,64,128]{3,2,1,0:T(8,128)S(1)}, u32[]{:S(2)}, u32[]{:S(2)}) collective-permute-start(f32[2,2,64,128]{3,2,1,0:T(8,128)S(1)} %get-tuple-element.40), channel_id=1, source_target_pairs={{0,4},{1,3},{2,6},{3,1},{4,0},{5,7},{6,2},{7,5},{8,12},{9,11},{10,... | collective-permute-start | bytes 393224 | tf_op jit(solution)/shard_map/ppermute | solution.py:124
  6.9 1.2 %collective-permute-start.2 = (f32[2,2,64,128]{3,2,1,0:T(8,128)S(1)}, f32[2,2,64,128]{3,2,1,0:T(8,128)S(1)}, u32[]{:S(2)}, u32[]{:S(2)}) collective-permute-start(f32[2,2,64,128]{3,2,1,0:T(8,128)S(1)} %get-tuple-element.39), channel_id=1, source_target_pairs={{0,4},{1,9},{2,6},{3,11},{4,0},{5,13},{6,2},{7,15},{8,12},{9,1},{1... | collective-permute-start | bytes 393224 | tf_op jit(solution)/shard_map/ppermute | solution.py:124
  8.1 1.4 %collective-permute-done.5 = f32[2,2,64,128]{3,2,1,0:T(8,128)S(1)} collective-permute-done((f32[2,2,64,128]{3,2,1,0:T(8,128)S(1)}, f32[2,2,64,128]{3,2,1,0:T(8,128)S(1)}, u32[]{:S(2)}, u32[]{:S(2)}) %collective-permute-start.5) | collective-permute-done | bytes 131104 | tf_op jit(solution)/shard_map/ppermute | solution.py:124
  9.5 0.1 collective-permute-start.6
  9.6 2.8 %collective-permute-done.2 = f32[2,2,64,128]{3,2,1,0:T(8,128)S(1)} collective-permute-done((f32[2,2,64,128]{3,2,1,0:T(8,128)S(1)}, f32[2,2,64,128]{3,2,1,0:T(8,128)S(1)}, u32[]{:S(2)}, u32[]{:S(2)}) %collective-permute-start.2) | collective-permute-done | bytes 131104 | tf_op jit(solution)/shard_map/ppermute | solution.py:124
  12.5 0.1 collective-permute-start.3
  12.6 5.7 %collective-permute-done.6 = f32[4,2,64,128]{3,2,1,0:T(8,128)S(1)} collective-permute-done((f32[4,2,64,128]{3,2,1,0:T(8,128)S(1)}, f32[4,2,64,128]{3,2,1,0:T(8,128)S(1)}, u32[]{:S(2)}, u32[]{:S(2)}) %collective-permute-start.6) | collective-permute-done | bytes 262176 | tf_op jit(solution)/shard_map/ppermute | solution.py:124
  18.3 7.3 %collective-permute-start.7 = (f32[8,2,64,128]{3,2,1,0:T(8,128)S(1)}, f32[8,2,64,128]{3,2,1,0:T(8,128)S(1)}, u32[]{:S(2)}, u32[]{:S(2)}) collective-permute-start(f32[8,2,64,128]{3,2,1,0:T(8,128)S(1)} %constant_dynamic-update-slice_fusion.3.mine_ref), channel_id=1, source_target_pairs={{0,1},{1,0},{2,3},{3,2},{4,5},{5,4},{6,7},{7,6},{8,9},{9,8},{10,11... | collective-permute-start | bytes 1572872 | tf_op jit(solution)/shard_map/ppermute | solution.py:140
  25.7 1.9 %collective-permute-start.8 = (f32[2,1,64,128]{3,2,1,0:T(8,128)S(1)}, f32[2,1,64,128]{3,2,1,0:T(8,128)S(1)}, u32[]{:S(2)}, u32[]{:S(2)}) collective-permute-start(f32[2,1,64,128]{3,2,1,0:T(8,128)S(1)} %slice_select_fusion.1), channel_id=1, source_target_pairs={{1,2},{2,1},{3,4},{4,3},{5,6},{6,5},{7,8},{8,7},{9,10},{10,9},{11,... | collective-permute-start | bytes 196616 | tf_op jit(solution)/shard_map/ppermute | solution.py:139
  27.6 0.0 collective-permute-done.3
  27.7 0.1 collective-permute-start.4
  27.8 0.0 collective-permute-done.7.theirs_ref
  27.8 1.5 %setup.1 = (f32[12,8,32,128]{3,2,1,0:T(8,128)S(1)}, f32[4,9,32,128]{3,2,1,0:T(8,128)S(1)}, f32[4,8,32,128]{3,2,1,0:T(8,128)S(1)}, f32[8,8,32,128]{3,2,1,0:T(8,12...) custom-call(s32[1,2]{1,0:T(1,128)S(1)} %bitcast.13, ...), custom_call_target="tpu_custom_call" | custom-call | tf_op jit(solution)/shard_map/setup/pallas_call | solution.py:644
  29.3 2.6 %collective-permute-done.8.far_ref = f32[2,1,64,128]{3,2,1,0:T(8,128)S(1)} collective-permute-done((f32[2,1,64,128]{3,2,1,0:T(8,128)S(1)}, f32[2,1,64,128]{3,2,1,0:T(8,128)S(1)}, u32[]{:S(2)}, u32[]{:S(2)}) %collective-permute-start.8) | collective-permute-done | bytes 65568 | tf_op jit(solution)/shard_map/ppermute | solution.py:139
  32.0 0.4 collective-permute-start.9
  32.4 5.7 %solve.1.planes_ref = f32[6,64,128]{2,1,0:T(8,128)S(1)} custom-call(f32[8,2,64,128]{3,2,1,0:T(8,128)S(1)} %constant_dynamic-update-slice_fusion.mine_ref, f32[8,2,64,128]{3,2,1,0:T(8,128)S(1)} %collective-permute-done.4.theirs_ref, f32[12,8,32,128]{3,2,1,0:T(8,128)S(1)} %get-tuple-element.52.inner, f32[4,9,32,128]{3,2,1,0:T(8,128)S(1)} %get-tuple-element.53.outer_x, ...), custom_call_target="tpu_custom_call" | custom-call | tf_op jit(solution)/shard_map/solve/pallas_call | solution.py:654
  38.2 0.2 finish.1
  38.4 0.2 collective-permute-start.10
  38.7 1.2 %collective-permute-start.11 = (f32[2,32,128]{2,1,0:T(8,128)S(1)}, f32[2,32,128]{2,1,0:T(8,128)S(1)}, u32[]{:S(2)}, u32[]{:S(2)}) collective-permute-start(f32[2,32,128]{2,1,0:T(8,128)S(1)} %get-tuple-element.73), channel_id=1, source_target_pairs={{0,16},{1,17},{2,18},{3,19},{4,20},{5,21},{6,22},{7,23},{8,24},{9,... | collective-permute-start | bytes 98312 | tf_op jit(solution)/shard_map/ppermute | solution.py:697
  39.9 0.7 %collective-permute-start.12 = (f32[2,32,128]{2,1,0:T(8,128)S(1)}, f32[2,32,128]{2,1,0:T(8,128)S(1)}, u32[]{:S(2)}, u32[]{:S(2)}) collective-permute-start(f32[2,32,128]{2,1,0:T(8,128)S(1)} %get-tuple-element.72), channel_id=1, source_target_pairs={{0,17},{1,16},{2,19},{3,18},{4,21},{5,20},{6,23},{7,22},{8,25},{9,... | collective-permute-start | bytes 98312 | tf_op jit(solution)/shard_map/ppermute | solution.py:697
  40.6 0.0 collective-permute-done.10
  40.6 0.7 %pad_maximum_fusion.2 = f32[2,2,64,128]{3,2,1,0:T(8,128)} fusion(f32[1,2,64,128]{3,2,1,0:T(8,128)S(1)} %get-tuple-element.71, f32[1,2,64,128]{3,2,1,0:T(8,128)S(1)} %get-tuple-element.70), kind=kLoop, calls=%fused_computation.2 | loop fusion | flops 32768 | bytes 262144 | tf_op jit(solution)/shard_map/stack | solution.py:699
  41.3 0.1 collective-permute-done.11
  41.4 2.3 %collective-permute-done.12 = f32[2,32,128]{2,1,0:T(8,128)S(1)} collective-permute-done((f32[2,32,128]{2,1,0:T(8,128)S(1)}, f32[2,32,128]{2,1,0:T(8,128)S(1)}, u32[]{:S(2)}, u32[]{:S(2)}) %collective-permute-start.12) | collective-permute-done | bytes 32800 | tf_op jit(solution)/shard_map/ppermute | solution.py:697
  43.7 0.6 %add_add_fusion = f32[2,32,128]{2,1,0:T(8,128)} fusion(f32[2,32,128]{2,1,0:T(8,128)S(1)} %collective-permute-done.11, f32[2,32,128]{2,1,0:T(8,128)S(1)} %collective-permute-done.12, f32[2,32,128]{2,1,0:T(8,128)S(1)} %get-tuple-element.67, f32[2,96,128]{2,1,0:T(8,128)S(1)} %collective-permute-done.10), kind=kLoop, calls=%fused_computation.8 | loop fusion | flops 24576 | bytes 163840 | tf_op jit(solution)/shard_map/add | solution.py:703
  (27 shorter events, 0.2 us)
Async XLA Ops:
  0.6 25.0 %copy-start = (f32[2,2,64,128]{3,2,1,0:T(8,128)S(1)}, f32[2,2,64,128]{3,2,1,0:T(8,128)}, u32[]{:S(2)}) copy-start(f32[2,2,64,128]{3,2,1,0:T(8,128)} %state_ref.1) | copy-start | bytes 393220
  0.6 4.9 %collective-permute-start = (f32[2,64,128]{2,1,0:T(8,128)}, f32[2,64,128]{2,1,0:T(8,128)S(1)}, u32[]{:S(2)}, u32[]{:S(2)}) collective-permute-start(f32[2,64,128]{2,1,0:T(8,128)} %kappa_ref.1), channel_id=1, source_target_pairs={{0,2},{1,9},{2,0},{3,11},{4,6},{5,13},{6,4},{7,15},{8,10},{9,1},{1... | collective-permute-start | bytes 196616 | tf_op jit(solution)/shard_map/ppermute | solution.py:124
  0.8 4.8 %collective-permute-start.1 = (f32[2,64,128]{2,1,0:T(8,128)}, f32[2,64,128]{2,1,0:T(8,128)S(1)}, u32[]{:S(2)}, u32[]{:S(2)}) collective-permute-start(f32[2,64,128]{2,1,0:T(8,128)} %misfit_ref.1), channel_id=1, source_target_pairs={{0,8},{1,3},{2,10},{3,1},{4,12},{5,7},{6,14},{7,5},{8,0},{9,11},{1... | collective-permute-start | bytes 196616 | tf_op jit(solution)/shard_map/ppermute | solution.py:124
  2.0 0.8 %copy-start.1 = (f32[2,64,128]{2,1,0:T(8,128)S(1)}, f32[2,64,128]{2,1,0:T(8,128)}, u32[]{:S(2)}) copy-start(f32[2,64,128]{2,1,0:T(8,128)} %kappa_ref.1) | copy-start | bytes 196612
  2.8 0.8 %copy-start.2 = (f32[2,64,128]{2,1,0:T(8,128)S(1)}, f32[2,64,128]{2,1,0:T(8,128)}, u32[]{:S(2)}) copy-start(f32[2,64,128]{2,1,0:T(8,128)} %misfit_ref.1) | copy-start | bytes 196612
  5.6 3.9 %collective-permute-start.5 = (f32[2,2,64,128]{3,2,1,0:T(8,128)S(1)}, f32[2,2,64,128]{3,2,1,0:T(8,128)S(1)}, u32[]{:S(2)}, u32[]{:S(2)}) collective-permute-start(f32[2,2,64,128]{3,2,1,0:T(8,128)S(1)} %get-tuple-element.40), channel_id=1, source_target_pairs={{0,4},{1,3},{2,6},{3,1},{4,0},{5,7},{6,2},{7,5},{8,12},{9,11},{10,... | collective-permute-start | bytes 393224 | tf_op jit(solution)/shard_map/ppermute | solution.py:124
  6.9 20.9 %copy-start.3 = (s32[2]{0:T(128)S(1)}, s32[2]{0:T(128)}, u32[]{:S(2)}) copy-start(s32[2]{0:T(128)} %param.11) | copy-start | bytes 28
  6.9 20.9 %copy-start.4 = (f32[4]{0:T(128)S(1)}, f32[4]{0:T(128)}, u32[]{:S(2)}) copy-start(f32[4]{0:T(128)} %param.9) | copy-start | bytes 52
  6.9 20.9 %copy-start.5 = (f32[4]{0:T(128)S(1)}, f32[4]{0:T(128)}, u32[]{:S(2)}) copy-start(f32[4]{0:T(128)} %param.10) | copy-start | bytes 52
  6.9 5.5 %collective-permute-start.2 = (f32[2,2,64,128]{3,2,1,0:T(8,128)S(1)}, f32[2,2,64,128]{3,2,1,0:T(8,128)S(1)}, u32[]{:S(2)}, u32[]{:S(2)}) collective-permute-start(f32[2,2,64,128]{3,2,1,0:T(8,128)S(1)} %get-tuple-element.39), channel_id=1, source_target_pairs={{0,4},{1,9},{2,6},{3,11},{4,0},{5,13},{6,2},{7,15},{8,12},{9,1},{1... | collective-permute-start | bytes 393224 | tf_op jit(solution)/shard_map/ppermute | solution.py:124
  9.5 8.8 %collective-permute-start.6 = (f32[4,2,64,128]{3,2,1,0:T(8,128)S(1)}, f32[4,2,64,128]{3,2,1,0:T(8,128)S(1)}, u32[]{:S(2)}, u32[]{:S(2)}) collective-permute-start(f32[4,2,64,128]{3,2,1,0:T(8,128)S(1)} %pad_maximum_fusion.1), channel_id=1, source_target_pairs={{0,8},{1,5},{2,10},{3,7},{4,12},{5,1},{6,14},{7,3},{8,0},{9,13},{1... | collective-permute-start | bytes 786440 | tf_op jit(solution)/shard_map/ppermute | solution.py:124
  12.5 15.2 %collective-permute-start.3 = (f32[4,2,64,128]{3,2,1,0:T(8,128)S(1)}, f32[4,2,64,128]{3,2,1,0:T(8,128)S(1)}, u32[]{:S(2)}, u32[]{:S(2)}) collective-permute-start(f32[4,2,64,128]{3,2,1,0:T(8,128)S(1)} %pad_maximum_fusion), channel_id=1, source_target_pairs={{0,2},{1,5},{2,0},{3,7},{4,6},{5,1},{6,4},{7,3},{8,10},{9,13},{10,... | collective-permute-start | bytes 786440 | tf_op jit(solution)/shard_map/ppermute | solution.py:124
  18.3 9.5 %collective-permute-start.7 = (f32[8,2,64,128]{3,2,1,0:T(8,128)S(1)}, f32[8,2,64,128]{3,2,1,0:T(8,128)S(1)}, u32[]{:S(2)}, u32[]{:S(2)}) collective-permute-start(f32[8,2,64,128]{3,2,1,0:T(8,128)S(1)} %constant_dynamic-update-slice_fusion.3.mine_ref), channel_id=1, source_target_pairs={{0,1},{1,0},{2,3},{3,2},{4,5},{5,4},{6,7},{7,6},{8,9},{9,8},{10,11... | collective-permute-start | bytes 1572872 | tf_op jit(solution)/shard_map/ppermute | solution.py:140
  25.7 6.3 %collective-permute-start.8 = (f32[2,1,64,128]{3,2,1,0:T(8,128)S(1)}, f32[2,1,64,128]{3,2,1,0:T(8,128)S(1)}, u32[]{:S(2)}, u32[]{:S(2)}) collective-permute-start(f32[2,1,64,128]{3,2,1,0:T(8,128)S(1)} %slice_select_fusion.1), channel_id=1, source_target_pairs={{1,2},{2,1},{3,4},{4,3},{5,6},{6,5},{7,8},{8,7},{9,10},{10,9},{11,... | collective-permute-start | bytes 196616 | tf_op jit(solution)/shard_map/ppermute | solution.py:139
  27.7 4.7 %collective-permute-start.4 = (f32[8,2,64,128]{3,2,1,0:T(8,128)S(1)}, f32[8,2,64,128]{3,2,1,0:T(8,128)S(1)}, u32[]{:S(2)}, u32[]{:S(2)}) collective-permute-start(f32[8,2,64,128]{3,2,1,0:T(8,128)S(1)} %constant_dynamic-update-slice_fusion.mine_ref), channel_id=1, source_target_pairs={{0,1},{1,0},{2,3},{3,2},{4,5},{5,4},{6,7},{7,6},{8,9},{9,8},{10,11... | collective-permute-start | bytes 1572872 | tf_op jit(solution)/shard_map/ppermute | solution.py:140
  32.0 6.1 %collective-permute-start.9 = (f32[3,64,128]{2,1,0:T(8,128)S(1)}, f32[3,64,128]{2,1,0:T(8,128)S(1)}, u32[]{:S(2)}, u32[]{:S(2)}) collective-permute-start(f32[3,64,128]{2,1,0:T(8,128)S(1)} %fusion), channel_id=1, source_target_pairs={{0,1},{1,0},{2,3},{3,2},{4,5},{5,4},{6,7},{7,6},{8,9},{9,8},{10,11... | collective-permute-start | bytes 294920 | tf_op jit(solution)/shard_map/ppermute | solution.py:145
  38.4 2.2 %collective-permute-start.10 = (f32[2,96,128]{2,1,0:T(8,128)S(1)}, f32[2,96,128]{2,1,0:T(8,128)S(1)}, u32[]{:S(2)}, u32[]{:S(2)}) collective-permute-start(f32[2,96,128]{2,1,0:T(8,128)S(1)} %get-tuple-element.65), channel_id=1, source_target_pairs={{0,1},{1,0},{2,3},{3,2},{4,5},{5,4},{6,7},{7,6},{8,9},{9,8},{10,11... | collective-permute-start | bytes 294920 | tf_op jit(solution)/shard_map/ppermute | solution.py:688
  38.7 2.8 %collective-permute-start.11 = (f32[2,32,128]{2,1,0:T(8,128)S(1)}, f32[2,32,128]{2,1,0:T(8,128)S(1)}, u32[]{:S(2)}, u32[]{:S(2)}) collective-permute-start(f32[2,32,128]{2,1,0:T(8,128)S(1)} %get-tuple-element.73), channel_id=1, source_target_pairs={{0,16},{1,17},{2,18},{3,19},{4,20},{5,21},{6,22},{7,23},{8,24},{9,... | collective-permute-start | bytes 98312 | tf_op jit(solution)/shard_map/ppermute | solution.py:697
  39.9 3.8 %collective-permute-start.12 = (f32[2,32,128]{2,1,0:T(8,128)S(1)}, f32[2,32,128]{2,1,0:T(8,128)S(1)}, u32[]{:S(2)}, u32[]{:S(2)}) collective-permute-start(f32[2,32,128]{2,1,0:T(8,128)S(1)} %get-tuple-element.72), channel_id=1, source_target_pairs={{0,17},{1,16},{2,19},{3,18},{4,21},{5,20},{6,23},{7,22},{8,25},{9,... | collective-permute-start | bytes 98312 | tf_op jit(solution)/shard_map/ppermute | solution.py:697

commit v18 on v15

--- a/solution.py
+++ b/solution.py
@@ -64,7 +64,7 @@
         falling.append(mask)
         mask //= 2
     if flip:
-        return falling[::-1], falling[:1] + falling[:0:-1]
+        return falling[:1] + falling[:0:-1], falling
     return falling, falling[-1:] + falling[:-1]
 
 

time: 41.1 us -> 44 us (1.071)
  starting transfers between devices: 16.6 us -> 18.9 us
  waiting for transfers between devices: 12.6 us -> 13.2 us
    ppermute x2, starting transfers between devices: 0.7 us -> 3.02 us  [gather_blocks(): other = [lax.ppermute(part, axis, swap) for part in held]]
    ppermute x1, starting transfers between devices: 0.09 us -> 0.86 us  [fetch_near(): return (late, lax.ppermute(jnp.where(even, given[1], given[0]), axis, swap))]
    ppermute x6, waiting for transfers between devices: 10.1 us -> 10.6 us  [gather_blocks(): arrived.append(lax.ppermute(held[at], axis, pairs))]
  transfers between devices with their start and end apart: 13 -> 13, of which waited for: 7 -> 6; matrix products, arithmetic and copies ran while one was open for 2% -> 2% of each run, Pallas kernels for 18% -> 17%
where the time goes in v18:
time: 44 us; the launch traced here: 43.8 us
  starting transfers between devices  18.9 us (43%)
  waiting for transfers between devices  13.2 us (30%)
  Pallas kernels  7.68 us (17%)
  local copies, waits for them, and re-layouts  1.8 us (4%)
  other arithmetic  1.37 us (3%)
  between operations  0.83 us (2%)
    ppermute x6, starting transfers between devices, gather_blocks(): arrived.append(lax.ppermute(held[at], axis, pairs))  11.8 us
    ppermute x6, waiting for transfers between devices, gather_blocks(): arrived.append(lax.ppermute(held[at], axis, pairs))  10.6 us
    pallas_call x1, Pallas kernels, whole_grid(): pl.pallas_call(functools.partial(solve_kernel, own=own), out_shape=jax.Sh...  5.69 us
    ppermute x2, starting transfers between devices, gather_blocks(): other = [lax.ppermute(part, axis, swap) for part in held]  3.02 us
    ppermute x2, waiting for transfers between devices, whole_grid(): shares.append(lax.ppermute(send[k - 1, side], ('pole', 'space'), pairs))  2.55 us
    ppermute x2, starting transfers between devices, whole_grid(): shares.append(lax.ppermute(send[k - 1, side], ('pole', 'space'), pairs))  2.46 us
    unnamed x17, local copies, waits for them, and re-layouts  1.75 us
    pallas_call x1, Pallas kernels, whole_grid(): pl.pallas_call(setup_kernel, out_shape=[jax.ShapeDtypeStruct(shape, jnp.f...  1.53 us
  transfers between devices with their start and end apart: 13, of which 6 were waited for; matrix products, arithmetic and copies ran while one was open for 2% of the time, Pallas kernels for 17%

profile of v18, /device:TPU:0, one launch (start us, length us, event | category | flops | bytes accessed | tf_op | source)
XLA Modules:
  0.0 43.8 jit_solution(15841333527401806129)
XLA Ops:
  0.6 4.1 %collective-permute-start = (f32[2,64,128]{2,1,0:T(8,128)}, f32[2,64,128]{2,1,0:T(8,128)S(1)}, u32[]{:S(2)}, u32[]{:S(2)}) collective-permute-start(f32[2,64,128]{2,1,0:T(8,128)} %kappa_ref.1), channel_id=1, source_target_pairs={{0,8},{1,3},{2,10},{3,1},{4,12},{5,7},{6,14},{7,5},{8,0},{9,11},{1... | collective-permute-start | bytes 196616 | tf_op jit(solution)/shard_map/ppermute | solution.py:124
  4.7 0.1 collective-permute-start.1
  4.8 0.8 %copy-done.1 = f32[2,64,128]{2,1,0:T(8,128)S(1)} copy-done((f32[2,64,128]{2,1,0:T(8,128)S(1)}, f32[2,64,128]{2,1,0:T(8,128)}, u32[]{:S(2)}) %copy-start.1) | copy-done | bytes 65560
  5.7 0.8 %copy-done.2 = f32[2,64,128]{2,1,0:T(8,128)S(1)} copy-done((f32[2,64,128]{2,1,0:T(8,128)S(1)}, f32[2,64,128]{2,1,0:T(8,128)}, u32[]{:S(2)}) %copy-start.2) | copy-done | bytes 65560
  6.5 0.1 prepare.1
  6.6 1.0 %collective-permute-done.refs_2_ = f32[2,64,128]{2,1,0:T(8,128)S(1)} collective-permute-done((f32[2,64,128]{2,1,0:T(8,128)}, f32[2,64,128]{2,1,0:T(8,128)S(1)}, u32[]{:S(2)}, u32[]{:S(2)}) %collective-permute-start) | collective-permute-done | bytes 65568 | tf_op jit(solution)/shard_map/ppermute | solution.py:124
  7.6 2.5 %collective-permute-done.1.refs_3_ = f32[2,64,128]{2,1,0:T(8,128)S(1)} collective-permute-done((f32[2,64,128]{2,1,0:T(8,128)}, f32[2,64,128]{2,1,0:T(8,128)S(1)}, u32[]{:S(2)}, u32[]{:S(2)}) %collective-permute-start.1) | collective-permute-done | bytes 65568 | tf_op jit(solution)/shard_map/ppermute | solution.py:124
  10.1 0.1 join.1
  10.2 1.8 %collective-permute-start.5 = (f32[2,2,64,128]{3,2,1,0:T(8,128)S(1)}, f32[2,2,64,128]{3,2,1,0:T(8,128)S(1)}, u32[]{:S(2)}, u32[]{:S(2)}) collective-permute-start(f32[2,2,64,128]{3,2,1,0:T(8,128)S(1)} %get-tuple-element.40), channel_id=1, source_target_pairs={{0,4},{1,9},{2,6},{3,11},{4,0},{5,13},{6,2},{7,15},{8,12},{9,1},{1... | collective-permute-start | bytes 393224 | tf_op jit(solution)/shard_map/ppermute | solution.py:124
  12.0 1.5 %collective-permute-start.2 = (f32[2,2,64,128]{3,2,1,0:T(8,128)S(1)}, f32[2,2,64,128]{3,2,1,0:T(8,128)S(1)}, u32[]{:S(2)}, u32[]{:S(2)}) collective-permute-start(f32[2,2,64,128]{3,2,1,0:T(8,128)S(1)} %get-tuple-element.39), channel_id=1, source_target_pairs={{0,2},{1,5},{2,0},{3,7},{4,6},{5,1},{6,4},{7,3},{8,10},{9,13},{10,... | collective-permute-start | bytes 393224 | tf_op jit(solution)/shard_map/ppermute | solution.py:124
  13.5 1.8 %collective-permute-done.5 = f32[2,2,64,128]{3,2,1,0:T(8,128)S(1)} collective-permute-done((f32[2,2,64,128]{3,2,1,0:T(8,128)S(1)}, f32[2,2,64,128]{3,2,1,0:T(8,128)S(1)}, u32[]{:S(2)}, u32[]{:S(2)}) %collective-permute-start.5) | collective-permute-done | bytes 131104 | tf_op jit(solution)/shard_map/ppermute | solution.py:124
  15.3 2.6 %collective-permute-start.6 = (f32[4,2,64,128]{3,2,1,0:T(8,128)S(1)}, f32[4,2,64,128]{3,2,1,0:T(8,128)S(1)}, u32[]{:S(2)}, u32[]{:S(2)}) collective-permute-start(f32[4,2,64,128]{3,2,1,0:T(8,128)S(1)} %pad_maximum_fusion.1), channel_id=1, source_target_pairs={{0,2},{1,5},{2,0},{3,7},{4,6},{5,1},{6,4},{7,3},{8,10},{9,13},{10,... | collective-permute-start | bytes 786440 | tf_op jit(solution)/shard_map/ppermute | solution.py:124
  17.9 0.0 collective-permute-done.2
  18.0 1.8 %collective-permute-start.3 = (f32[4,2,64,128]{3,2,1,0:T(8,128)S(1)}, f32[4,2,64,128]{3,2,1,0:T(8,128)S(1)}, u32[]{:S(2)}, u32[]{:S(2)}) collective-permute-start(f32[4,2,64,128]{3,2,1,0:T(8,128)S(1)} %pad_maximum_fusion), channel_id=1, source_target_pairs={{0,4},{1,3},{2,6},{3,1},{4,0},{5,7},{6,2},{7,5},{8,12},{9,11},{10,... | collective-permute-start | bytes 786440 | tf_op jit(solution)/shard_map/ppermute | solution.py:124
  19.7 5.3 %collective-permute-done.6 = f32[4,2,64,128]{3,2,1,0:T(8,128)S(1)} collective-permute-done((f32[4,2,64,128]{3,2,1,0:T(8,128)S(1)}, f32[4,2,64,128]{3,2,1,0:T(8,128)S(1)}, u32[]{:S(2)}, u32[]{:S(2)}) %collective-permute-start.6) | collective-permute-done | bytes 262176 | tf_op jit(solution)/shard_map/ppermute | solution.py:124
  25.1 0.1 collective-permute-start.7
  25.2 0.7 %collective-permute-start.8 = (f32[2,1,64,128]{3,2,1,0:T(8,128)S(1)}, f32[2,1,64,128]{3,2,1,0:T(8,128)S(1)}, u32[]{:S(2)}, u32[]{:S(2)}) collective-permute-start(f32[2,1,64,128]{3,2,1,0:T(8,128)S(1)} %slice_select_fusion.1), channel_id=1, source_target_pairs={{1,2},{2,1},{3,4},{4,3},{5,6},{6,5},{7,8},{8,7},{9,10},{10,9},{11,... | collective-permute-start | bytes 196616 | tf_op jit(solution)/shard_map/ppermute | solution.py:139
  25.9 2.9 %collective-permute-start.4 = (f32[8,2,64,128]{3,2,1,0:T(8,128)S(1)}, f32[8,2,64,128]{3,2,1,0:T(8,128)S(1)}, u32[]{:S(2)}, u32[]{:S(2)}) collective-permute-start(f32[8,2,64,128]{3,2,1,0:T(8,128)S(1)} %constant_dynamic-update-slice_fusion.mine_ref), channel_id=1, source_target_pairs={{0,1},{1,0},{2,3},{3,2},{4,5},{5,4},{6,7},{7,6},{8,9},{9,8},{10,11... | collective-permute-start | bytes 1572872 | tf_op jit(solution)/shard_map/ppermute | solution.py:140
  28.9 0.0 collective-permute-done.7.theirs_ref
  28.9 1.5 %setup.1 = (f32[12,8,32,128]{3,2,1,0:T(8,128)S(1)}, f32[4,9,32,128]{3,2,1,0:T(8,128)S(1)}, f32[4,8,32,128]{3,2,1,0:T(8,128)S(1)}, f32[8,8,32,128]{3,2,1,0:T(8,12...) custom-call(s32[1,2]{1,0:T(1,128)S(1)} %bitcast.13, ...), custom_call_target="tpu_custom_call" | custom-call | tf_op jit(solution)/shard_map/setup/pallas_call | solution.py:644
  30.4 0.0 collective-permute-done.8.far_ref
  30.5 0.9 %collective-permute-start.9 = (f32[3,64,128]{2,1,0:T(8,128)S(1)}, f32[3,64,128]{2,1,0:T(8,128)S(1)}, u32[]{:S(2)}, u32[]{:S(2)}) collective-permute-start(f32[3,64,128]{2,1,0:T(8,128)S(1)} %fusion), channel_id=1, source_target_pairs={{0,1},{1,0},{2,3},{3,2},{4,5},{5,4},{6,7},{7,6},{8,9},{9,8},{10,11... | collective-permute-start | bytes 294920 | tf_op jit(solution)/shard_map/ppermute | solution.py:145
  31.4 5.7 %solve.1.planes_ref = f32[6,64,128]{2,1,0:T(8,128)S(1)} custom-call(f32[8,2,64,128]{3,2,1,0:T(8,128)S(1)} %constant_dynamic-update-slice_fusion.mine_ref, f32[8,2,64,128]{3,2,1,0:T(8,128)S(1)} %collective-permute-done.4.theirs_ref, f32[12,8,32,128]{3,2,1,0:T(8,128)S(1)} %get-tuple-element.52.inner, f32[4,9,32,128]{3,2,1,0:T(8,128)S(1)} %get-tuple-element.53.outer_x, ...), custom_call_target="tpu_custom_call" | custom-call | tf_op jit(solution)/shard_map/solve/pallas_call | solution.py:654
  37.1 0.0 collective-permute-done.9.near_ref
  37.1 0.2 finish.1
  37.3 0.1 collective-permute-start.10
  37.4 2.3 %collective-permute-start.11 = (f32[2,32,128]{2,1,0:T(8,128)S(1)}, f32[2,32,128]{2,1,0:T(8,128)S(1)}, u32[]{:S(2)}, u32[]{:S(2)}) collective-permute-start(f32[2,32,128]{2,1,0:T(8,128)S(1)} %get-tuple-element.73), channel_id=1, source_target_pairs={{0,16},{1,17},{2,18},{3,19},{4,20},{5,21},{6,22},{7,23},{8,24},{9,... | collective-permute-start | bytes 98312 | tf_op jit(solution)/shard_map/ppermute | solution.py:697
  39.8 0.1 collective-permute-start.12
  39.9 0.7 %pad_maximum_fusion.2 = f32[2,2,64,128]{3,2,1,0:T(8,128)} fusion(f32[1,2,64,128]{3,2,1,0:T(8,128)S(1)} %get-tuple-element.71, f32[1,2,64,128]{3,2,1,0:T(8,128)S(1)} %get-tuple-element.70), kind=kLoop, calls=%fused_computation.2 | loop fusion | flops 32768 | bytes 262144 | tf_op jit(solution)/shard_map/stack | solution.py:699
  40.6 1.2 %collective-permute-done.11 = f32[2,32,128]{2,1,0:T(8,128)S(1)} collective-permute-done((f32[2,32,128]{2,1,0:T(8,128)S(1)}, f32[2,32,128]{2,1,0:T(8,128)S(1)}, u32[]{:S(2)}, u32[]{:S(2)}) %collective-permute-start.11) | collective-permute-done | bytes 32800 | tf_op jit(solution)/shard_map/ppermute | solution.py:697
  41.8 1.4 %collective-permute-done.12 = f32[2,32,128]{2,1,0:T(8,128)S(1)} collective-permute-done((f32[2,32,128]{2,1,0:T(8,128)S(1)}, f32[2,32,128]{2,1,0:T(8,128)S(1)}, u32[]{:S(2)}, u32[]{:S(2)}) %collective-permute-start.12) | collective-permute-done | bytes 32800 | tf_op jit(solution)/shard_map/ppermute | solution.py:697
  43.1 0.6 %add_add_fusion = f32[2,32,128]{2,1,0:T(8,128)} fusion(f32[2,32,128]{2,1,0:T(8,128)S(1)} %collective-permute-done.11, f32[2,32,128]{2,1,0:T(8,128)S(1)} %collective-permute-done.12, f32[2,32,128]{2,1,0:T(8,128)S(1)} %get-tuple-element.67, f32[2,96,128]{2,1,0:T(8,128)S(1)} %collective-permute-done.10), kind=kLoop, calls=%fused_computation.8 | loop fusion | flops 24576 | bytes 163840 | tf_op jit(solution)/shard_map/add | solution.py:703
  (27 shorter events, 0.2 us)
Async XLA Ops:
  0.6 24.5 %copy-start = (f32[2,2,64,128]{3,2,1,0:T(8,128)S(1)}, f32[2,2,64,128]{3,2,1,0:T(8,128)}, u32[]{:S(2)}) copy-start(f32[2,2,64,128]{3,2,1,0:T(8,128)} %state_ref.1) | copy-start | bytes 393220
  0.6 6.9 %collective-permute-start = (f32[2,64,128]{2,1,0:T(8,128)}, f32[2,64,128]{2,1,0:T(8,128)S(1)}, u32[]{:S(2)}, u32[]{:S(2)}) collective-permute-start(f32[2,64,128]{2,1,0:T(8,128)} %kappa_ref.1), channel_id=1, source_target_pairs={{0,8},{1,3},{2,10},{3,1},{4,12},{5,7},{6,14},{7,5},{8,0},{9,11},{1... | collective-permute-start | bytes 196616 | tf_op jit(solution)/shard_map/ppermute | solution.py:124
  4.7 5.4 %collective-permute-start.1 = (f32[2,64,128]{2,1,0:T(8,128)}, f32[2,64,128]{2,1,0:T(8,128)S(1)}, u32[]{:S(2)}, u32[]{:S(2)}) collective-permute-start(f32[2,64,128]{2,1,0:T(8,128)} %misfit_ref.1), channel_id=1, source_target_pairs={{0,8},{1,9},{2,10},{3,11},{4,12},{5,13},{6,14},{7,15},{8,0},{9,1},... | collective-permute-start | bytes 196616 | tf_op jit(solution)/shard_map/ppermute | solution.py:124
  4.8 0.8 %copy-start.1 = (f32[2,64,128]{2,1,0:T(8,128)S(1)}, f32[2,64,128]{2,1,0:T(8,128)}, u32[]{:S(2)}) copy-start(f32[2,64,128]{2,1,0:T(8,128)} %kappa_ref.1) | copy-start | bytes 196612
  5.7 0.8 %copy-start.2 = (f32[2,64,128]{2,1,0:T(8,128)S(1)}, f32[2,64,128]{2,1,0:T(8,128)}, u32[]{:S(2)}) copy-start(f32[2,64,128]{2,1,0:T(8,128)} %misfit_ref.1) | copy-start | bytes 196612
  10.2 5.0 %collective-permute-start.5 = (f32[2,2,64,128]{3,2,1,0:T(8,128)S(1)}, f32[2,2,64,128]{3,2,1,0:T(8,128)S(1)}, u32[]{:S(2)}, u32[]{:S(2)}) collective-permute-start(f32[2,2,64,128]{3,2,1,0:T(8,128)S(1)} %get-tuple-element.40), channel_id=1, source_target_pairs={{0,4},{1,9},{2,6},{3,11},{4,0},{5,13},{6,2},{7,15},{8,12},{9,1},{1... | collective-permute-start | bytes 393224 | tf_op jit(solution)/shard_map/ppermute | solution.py:124
  12.0 16.9 %copy-start.3 = (s32[2]{0:T(128)S(1)}, s32[2]{0:T(128)}, u32[]{:S(2)}) copy-start(s32[2]{0:T(128)} %param.11) | copy-start | bytes 28
  12.0 16.9 %copy-start.4 = (f32[4]{0:T(128)S(1)}, f32[4]{0:T(128)}, u32[]{:S(2)}) copy-start(f32[4]{0:T(128)} %param.9) | copy-start | bytes 52
  12.0 16.9 %copy-start.5 = (f32[4]{0:T(128)S(1)}, f32[4]{0:T(128)}, u32[]{:S(2)}) copy-start(f32[4]{0:T(128)} %param.10) | copy-start | bytes 52
  12.0 5.9 %collective-permute-start.2 = (f32[2,2,64,128]{3,2,1,0:T(8,128)S(1)}, f32[2,2,64,128]{3,2,1,0:T(8,128)S(1)}, u32[]{:S(2)}, u32[]{:S(2)}) collective-permute-start(f32[2,2,64,128]{3,2,1,0:T(8,128)S(1)} %get-tuple-element.39), channel_id=1, source_target_pairs={{0,2},{1,5},{2,0},{3,7},{4,6},{5,1},{6,4},{7,3},{8,10},{9,13},{10,... | collective-permute-start | bytes 393224 | tf_op jit(solution)/shard_map/ppermute | solution.py:124
  15.3 9.8 %collective-permute-start.6 = (f32[4,2,64,128]{3,2,1,0:T(8,128)S(1)}, f32[4,2,64,128]{3,2,1,0:T(8,128)S(1)}, u32[]{:S(2)}, u32[]{:S(2)}) collective-permute-start(f32[4,2,64,128]{3,2,1,0:T(8,128)S(1)} %pad_maximum_fusion.1), channel_id=1, source_target_pairs={{0,2},{1,5},{2,0},{3,7},{4,6},{5,1},{6,4},{7,3},{8,10},{9,13},{10,... | collective-permute-start | bytes 786440 | tf_op jit(solution)/shard_map/ppermute | solution.py:124
  18.0 7.9 %collective-permute-start.3 = (f32[4,2,64,128]{3,2,1,0:T(8,128)S(1)}, f32[4,2,64,128]{3,2,1,0:T(8,128)S(1)}, u32[]{:S(2)}, u32[]{:S(2)}) collective-permute-start(f32[4,2,64,128]{3,2,1,0:T(8,128)S(1)} %pad_maximum_fusion), channel_id=1, source_target_pairs={{0,4},{1,3},{2,6},{3,1},{4,0},{5,7},{6,2},{7,5},{8,12},{9,11},{10,... | collective-permute-start | bytes 786440 | tf_op jit(solution)/shard_map/ppermute | solution.py:124
  25.1 3.8 %collective-permute-start.7 = (f32[8,2,64,128]{3,2,1,0:T(8,128)S(1)}, f32[8,2,64,128]{3,2,1,0:T(8,128)S(1)}, u32[]{:S(2)}, u32[]{:S(2)}) collective-permute-start(f32[8,2,64,128]{3,2,1,0:T(8,128)S(1)} %constant_dynamic-update-slice_fusion.3.mine_ref), channel_id=1, source_target_pairs={{0,1},{1,0},{2,3},{3,2},{4,5},{5,4},{6,7},{7,6},{8,9},{9,8},{10,11... | collective-permute-start | bytes 1572872 | tf_op jit(solution)/shard_map/ppermute | solution.py:140
  25.2 5.3 %collective-permute-start.8 = (f32[2,1,64,128]{3,2,1,0:T(8,128)S(1)}, f32[2,1,64,128]{3,2,1,0:T(8,128)S(1)}, u32[]{:S(2)}, u32[]{:S(2)}) collective-permute-start(f32[2,1,64,128]{3,2,1,0:T(8,128)S(1)} %slice_select_fusion.1), channel_id=1, source_target_pairs={{1,2},{2,1},{3,4},{4,3},{5,6},{6,5},{7,8},{8,7},{9,10},{10,9},{11,... | collective-permute-start | bytes 196616 | tf_op jit(solution)/shard_map/ppermute | solution.py:139
  25.9 5.4 %collective-permute-start.4 = (f32[8,2,64,128]{3,2,1,0:T(8,128)S(1)}, f32[8,2,64,128]{3,2,1,0:T(8,128)S(1)}, u32[]{:S(2)}, u32[]{:S(2)}) collective-permute-start(f32[8,2,64,128]{3,2,1,0:T(8,128)S(1)} %constant_dynamic-update-slice_fusion.mine_ref), channel_id=1, source_target_pairs={{0,1},{1,0},{2,3},{3,2},{4,5},{5,4},{6,7},{7,6},{8,9},{9,8},{10,11... | collective-permute-start | bytes 1572872 | tf_op jit(solution)/shard_map/ppermute | solution.py:140
  30.5 6.6 %collective-permute-start.9 = (f32[3,64,128]{2,1,0:T(8,128)S(1)}, f32[3,64,128]{2,1,0:T(8,128)S(1)}, u32[]{:S(2)}, u32[]{:S(2)}) collective-permute-start(f32[3,64,128]{2,1,0:T(8,128)S(1)} %fusion), channel_id=1, source_target_pairs={{0,1},{1,0},{2,3},{3,2},{4,5},{5,4},{6,7},{7,6},{8,9},{9,8},{10,11... | collective-permute-start | bytes 294920 | tf_op jit(solution)/shard_map/ppermute | solution.py:145
  37.3 2.6 %collective-permute-start.10 = (f32[2,96,128]{2,1,0:T(8,128)S(1)}, f32[2,96,128]{2,1,0:T(8,128)S(1)}, u32[]{:S(2)}, u32[]{:S(2)}) collective-permute-start(f32[2,96,128]{2,1,0:T(8,128)S(1)} %get-tuple-element.65), channel_id=1, source_target_pairs={{0,1},{1,0},{2,3},{3,2},{4,5},{5,4},{6,7},{7,6},{8,9},{9,8},{10,11... | collective-permute-start | bytes 294920 | tf_op jit(solution)/shard_map/ppermute | solution.py:688
  37.4 4.3 %collective-permute-start.11 = (f32[2,32,128]{2,1,0:T(8,128)S(1)}, f32[2,32,128]{2,1,0:T(8,128)S(1)}, u32[]{:S(2)}, u32[]{:S(2)}) collective-permute-start(f32[2,32,128]{2,1,0:T(8,128)S(1)} %get-tuple-element.73), channel_id=1, source_target_pairs={{0,16},{1,17},{2,18},{3,19},{4,20},{5,21},{6,22},{7,23},{8,24},{9,... | collective-permute-start | bytes 98312 | tf_op jit(solution)/shard_map/ppermute | solution.py:697
  39.8 3.4 %collective-permute-start.12 = (f32[2,32,128]{2,1,0:T(8,128)S(1)}, f32[2,32,128]{2,1,0:T(8,128)S(1)}, u32[]{:S(2)}, u32[]{:S(2)}) collective-permute-start(f32[2,32,128]{2,1,0:T(8,128)S(1)} %get-tuple-element.72), channel_id=1, source_target_pairs={{0,17},{1,16},{2,19},{3,18},{4,21},{5,20},{6,23},{7,22},{8,25},{9,... | collective-permute-start | bytes 98312 | tf_op jit(solution)/shard_map/ppermute | solution.py:697

commit v19 on v15

--- a/solution.py
+++ b/solution.py
@@ -137,14 +137,11 @@
         )(*own, *arrived)
         held[1], states = lax.optimization_barrier((held[1], states))
         far = lax.ppermute(jnp.where(even, states[:, :1], states[:, -1:]), axis, over)
+    held[1], far = lax.optimization_barrier((held[1], far))
+    given = jnp.concatenate([states, far], axis=1)
+    near = lax.ppermute(jnp.where(even, given[1], given[0]), axis, swap)
     other = [lax.ppermute(part, axis, swap) for part in held]
-
-    def fetch_near(after):
-        late, states_late, far_late = lax.optimization_barrier((after, states, far))
-        given = jnp.concatenate([states_late, far_late], axis=1)
-        return late, lax.ppermute(jnp.where(even, given[1], given[0]), axis, swap)
-
-    return held, other, far, fetch_near
+    return held, other, far, near
 
 
 CLASSES = [(a, b, c) for a in (0, 1) for b in (0, 1) for c in (0, 1)]
@@ -230,7 +227,7 @@
                             store(cls(x % 2, b, 1), spot, j, odd)
             return carry
 
-        lax.fori_loop(0, blocks // 2, pair, 0)
+        lax.fori_loop(0, blocks // 2, pair, 0, unroll=True)
 
 
 def setup_kernel(
@@ -374,12 +371,10 @@
     tile, tiles, zero = at_.tile, at_.tiles, at_.zero
     place = lax.axis_index("space")
     core = place % 2
-    weight = KEPT * chosen[...]
 
     def begin(k, spot, j, value):
-        res = weight * value
-        residual[k, spot, tile(j)] = res
-        scaled[k, spot + 1, tile(j)] = damped[k, spot, tile(j)] * res
+        residual[k, spot, tile(j)] = value
+        scaled[k, spot + 1, tile(j)] = damped[k, spot, tile(j)] * value
 
     at_.arrange(mine_ref, theirs_ref, place, True, begin)
     at_.seam_fine(scaled)
@@ -543,8 +538,9 @@
     ratio = gamma_next / gamma
     curve_next = grand_total(own_part - 2.0 * face_part)
     step_two = gamma_next / (curve_next - ratio * ratio * curve)
-    step_first = (step_one + step_two * ratio) * (1.0 / KEPT)
-    step_two = step_two * (1.0 / KEPT)
+    weight = chosen[...]
+    step_first = (step_one + step_two * ratio) * weight
+    step_two = step_two * weight
 
     start = (place - core) * (own // 2)
     upper = jnp.where(start >= half, 1, 0)
@@ -619,7 +615,7 @@
     groups = lax.axis_size("pole")
     peers = lax.axis_size("space")
     even = lax.axis_index("space") % 2 == 0
-    mine, theirs, far, fetch_near = gather_blocks([conductivity, misfit], forward_states, "space")
+    mine, theirs, far, near = gather_blocks([conductivity, misfit], forward_states, "space")
     half, rows = peers * own // 4, ny // 2
 
     def field(count, extent):
@@ -650,7 +646,6 @@
         compiler_params=pltpu.CompilerParams(vmem_limit_bytes=6 * 1024 * 1024),
         name="setup",
     )(pole_order[None], pole_shifts[None], pole_weights[None], mine[0], theirs[0])
-    coefficients, near = fetch_near(coefficients)
     planes = pl.pallas_call(
         functools.partial(solve_kernel, own=own),
         out_shape=jax.ShapeDtypeStruct((2 * own + 2, ny, nz), jnp.float32),

time: 41.1 us -> 41.4 us (level)
  other arithmetic: 1.37 us -> 2.28 us
  Pallas kernels: 7.72 us -> 7.09 us
    ppermute x6, waiting for transfers between devices: 10.1 us -> 8.23 us  [gather_blocks(): arrived.append(lax.ppermute(held[at], axis, pairs))]
    ppermute x2, waiting for transfers between devices: 0.01 us -> 1.57 us  [gather_blocks(): other = [lax.ppermute(part, axis, swap) for part in held]]
    select_n x1, other arithmetic: 0.01 us -> 0.88 us  [gather_blocks(): jnp.where(even, states[:, :1], states[:, -1:])]
    ppermute x6, starting transfers between devices: 12 us -> 11.4 us  [gather_blocks(): arrived.append(lax.ppermute(held[at], axis, pairs))]
    ppermute x2, starting transfers between devices: 0.7 us -> 1.18 us  [gather_blocks(): other = [lax.ppermute(part, axis, swap) for part in held]]
    unnamed x17 -> x15, local copies, waits for them, and re-layouts: 1.75 us -> 1.73 us
  transfers between devices with their start and end apart: 13 -> 13, of which waited for: 7 -> 6; matrix products, arithmetic and copies ran while one was open for 2% -> 4% of each run, Pallas kernels for 18% -> 16%
where the time goes in v19:
time: 41.4 us; the launch traced here: 41.1 us
  starting transfers between devices  16.7 us (40%)
  waiting for transfers between devices  12.5 us (30%)
  Pallas kernels  7.09 us (17%)
  other arithmetic  2.28 us (6%)
  local copies, waits for them, and re-layouts  1.76 us (4%)
  between operations  0.81 us (2%)
    ppermute x6, starting transfers between devices, gather_blocks(): arrived.append(lax.ppermute(held[at], axis, pairs))  11.4 us
    ppermute x6, waiting for transfers between devices, gather_blocks(): arrived.append(lax.ppermute(held[at], axis, pairs))  8.23 us
    pallas_call x1, Pallas kernels, whole_grid(): pl.pallas_call(functools.partial(solve_kernel, own=own), out_shape=jax.Sh...  5.49 us
    ppermute x2, waiting for transfers between devices, whole_grid(): shares.append(lax.ppermute(send[k - 1, side], ('pole', 'space'), pairs))  2.7 us
    ppermute x2, starting transfers between devices, whole_grid(): shares.append(lax.ppermute(send[k - 1, side], ('pole', 'space'), pairs))  2.54 us
    unnamed x15, local copies, waits for them, and re-layouts  1.73 us
    ppermute x2, waiting for transfers between devices, gather_blocks(): other = [lax.ppermute(part, axis, swap) for part in held]  1.57 us
    ppermute x2, starting transfers between devices, gather_blocks(): other = [lax.ppermute(part, axis, swap) for part in held]  1.18 us
  transfers between devices with their start and end apart: 13, of which 6 were waited for; matrix products, arithmetic and copies ran while one was open for 4% of the time, Pallas kernels for 16%

profile of v19, /device:TPU:0, one launch (start us, length us, event | category | flops | bytes accessed | tf_op | source)
XLA Modules:
  0.0 41.1 jit_solution(745912324546667957)
XLA Ops:
  0.6 4.1 %collective-permute-start = (f32[2,64,128]{2,1,0:T(8,128)}, f32[2,64,128]{2,1,0:T(8,128)S(1)}, u32[]{:S(2)}, u32[]{:S(2)}) collective-permute-start(f32[2,64,128]{2,1,0:T(8,128)} %kappa_ref.1), channel_id=1, source_target_pairs={{0,8},{1,3},{2,10},{3,1},{4,12},{5,7},{6,14},{7,5},{8,0},{9,11},{1... | collective-permute-start | bytes 196616 | tf_op jit(solution)/shard_map/ppermute | solution.py:124
  4.7 1.5 %collective-permute-start.1 = (f32[2,64,128]{2,1,0:T(8,128)}, f32[2,64,128]{2,1,0:T(8,128)S(1)}, u32[]{:S(2)}, u32[]{:S(2)}) collective-permute-start(f32[2,64,128]{2,1,0:T(8,128)} %misfit_ref.1), channel_id=1, source_target_pairs={{0,2},{1,9},{2,0},{3,11},{4,6},{5,13},{6,4},{7,15},{8,10},{9,1},{1... | collective-permute-start | bytes 196616 | tf_op jit(solution)/shard_map/ppermute | solution.py:124
  6.2 0.8 %copy-done.1 = f32[2,64,128]{2,1,0:T(8,128)S(1)} copy-done((f32[2,64,128]{2,1,0:T(8,128)S(1)}, f32[2,64,128]{2,1,0:T(8,128)}, u32[]{:S(2)}) %copy-start.1) | copy-done | bytes 65560
  7.1 0.8 %copy-done.2 = f32[2,64,128]{2,1,0:T(8,128)S(1)} copy-done((f32[2,64,128]{2,1,0:T(8,128)S(1)}, f32[2,64,128]{2,1,0:T(8,128)}, u32[]{:S(2)}) %copy-start.2) | copy-done | bytes 65560
  7.9 0.1 prepare.1
  8.0 1.2 %collective-permute-done.1.refs_3_ = f32[2,64,128]{2,1,0:T(8,128)S(1)} collective-permute-done((f32[2,64,128]{2,1,0:T(8,128)}, f32[2,64,128]{2,1,0:T(8,128)S(1)}, u32[]{:S(2)}, u32[]{:S(2)}) %collective-permute-start.1) | collective-permute-done | bytes 65568 | tf_op jit(solution)/shard_map/ppermute | solution.py:124
  9.2 0.1 join.1
  9.3 1.6 %collective-permute-start.2 = (f32[2,2,64,128]{3,2,1,0:T(8,128)S(1)}, f32[2,2,64,128]{3,2,1,0:T(8,128)S(1)}, u32[]{:S(2)}, u32[]{:S(2)}) collective-permute-start(f32[2,2,64,128]{3,2,1,0:T(8,128)S(1)} %get-tuple-element.29), channel_id=1, source_target_pairs={{0,4},{1,3},{2,6},{3,1},{4,0},{5,7},{6,2},{7,5},{8,12},{9,11},{10,... | collective-permute-start | bytes 393224 | tf_op jit(solution)/shard_map/ppermute | solution.py:124
  11.0 0.4 %collective-permute-start.6 = (f32[2,2,64,128]{3,2,1,0:T(8,128)S(1)}, f32[2,2,64,128]{3,2,1,0:T(8,128)S(1)}, u32[]{:S(2)}, u32[]{:S(2)}) collective-permute-start(f32[2,2,64,128]{3,2,1,0:T(8,128)S(1)} %get-tuple-element.32), channel_id=1, source_target_pairs={{0,4},{1,9},{2,6},{3,11},{4,0},{5,13},{6,2},{7,15},{8,12},{9,1},{1... | collective-permute-start | bytes 393224 | tf_op jit(solution)/shard_map/ppermute | solution.py:124
  11.4 0.9 %slice_select_fusion.1 = f32[2,1,64,128]{3,2,1,0:T(8,128)S(1)} fusion(f32[2,2,64,128]{3,2,1,0:T(8,128)} %state_ref.1, pred[]{:T(512)S(6)} %eq.7), kind=kLoop, calls=%fused_computation.8 | loop fusion | flops 16384 | bytes 196609 | tf_op jit(solution)/shard_map/jit(_where)/select_n | solution.py:139
  12.3 0.0 copy-start
  12.3 2.5 %collective-permute-done.2 = f32[2,2,64,128]{3,2,1,0:T(8,128)S(1)} collective-permute-done((f32[2,2,64,128]{3,2,1,0:T(8,128)S(1)}, f32[2,2,64,128]{3,2,1,0:T(8,128)S(1)}, u32[]{:S(2)}, u32[]{:S(2)}) %collective-permute-start.2) | collective-permute-done | bytes 131104 | tf_op jit(solution)/shard_map/ppermute | solution.py:124
  14.8 0.0 copy-start.3
  14.8 0.0 copy-start.4
  14.8 3.1 %collective-permute-start.3 = (f32[4,2,64,128]{3,2,1,0:T(8,128)S(1)}, f32[4,2,64,128]{3,2,1,0:T(8,128)S(1)}, u32[]{:S(2)}, u32[]{:S(2)}) collective-permute-start(f32[4,2,64,128]{3,2,1,0:T(8,128)S(1)} %pad_maximum_fusion.1), channel_id=1, source_target_pairs={{0,8},{1,5},{2,10},{3,7},{4,12},{5,1},{6,14},{7,3},{8,0},{9,13},{1... | collective-permute-start | bytes 786440 | tf_op jit(solution)/shard_map/ppermute | solution.py:124
  17.9 0.6 %collective-permute-start.7 = (f32[4,2,64,128]{3,2,1,0:T(8,128)S(1)}, f32[4,2,64,128]{3,2,1,0:T(8,128)S(1)}, u32[]{:S(2)}, u32[]{:S(2)}) collective-permute-start(f32[4,2,64,128]{3,2,1,0:T(8,128)S(1)} %pad_maximum_fusion.2), channel_id=1, source_target_pairs={{0,2},{1,5},{2,0},{3,7},{4,6},{5,1},{6,4},{7,3},{8,10},{9,13},{10,... | collective-permute-start | bytes 786440 | tf_op jit(solution)/shard_map/ppermute | solution.py:124
  18.6 0.7 %collective-permute-start.4 = (f32[2,1,64,128]{3,2,1,0:T(8,128)S(1)}, f32[2,1,64,128]{3,2,1,0:T(8,128)S(1)}, u32[]{:S(2)}, u32[]{:S(2)}) collective-permute-start(f32[2,1,64,128]{3,2,1,0:T(8,128)S(1)} %slice_select_fusion.1), channel_id=1, source_target_pairs={{1,2},{2,1},{3,4},{4,3},{5,6},{6,5},{7,8},{8,7},{9,10},{10,9},{11,... | collective-permute-start | bytes 196616 | tf_op jit(solution)/shard_map/ppermute | solution.py:139
  19.3 4.6 %collective-permute-done.3 = f32[4,2,64,128]{3,2,1,0:T(8,128)S(1)} collective-permute-done((f32[4,2,64,128]{3,2,1,0:T(8,128)S(1)}, f32[4,2,64,128]{3,2,1,0:T(8,128)S(1)}, u32[]{:S(2)}, u32[]{:S(2)}) %collective-permute-start.3) | collective-permute-done | bytes 262176 | tf_op jit(solution)/shard_map/ppermute | solution.py:124
  23.9 1.0 %collective-permute-start.5 = (f32[8,2,64,128]{3,2,1,0:T(8,128)S(1)}, f32[8,2,64,128]{3,2,1,0:T(8,128)S(1)}, u32[]{:S(2)}, u32[]{:S(2)}) collective-permute-start(f32[8,2,64,128]{3,2,1,0:T(8,128)S(1)} %pad_maximum_fusion.mine_ref), channel_id=1, source_target_pairs={{0,1},{1,0},{2,3},{3,2},{4,5},{5,4},{6,7},{7,6},{8,9},{9,8},{10,11... | collective-permute-start | bytes 1572872 | tf_op jit(solution)/shard_map/ppermute | solution.py:143
  24.9 0.2 collective-permute-start.8
  25.2 0.4 %collective-permute-start.9 = (f32[3,64,128]{2,1,0:T(8,128)S(1)}, f32[3,64,128]{2,1,0:T(8,128)S(1)}, u32[]{:S(2)}, u32[]{:S(2)}) collective-permute-start(f32[3,64,128]{2,1,0:T(8,128)S(1)} %fusion), channel_id=1, source_target_pairs={{0,1},{1,0},{2,3},{3,2},{4,5},{5,4},{6,7},{7,6},{8,9},{9,8},{10,11... | collective-permute-start | bytes 294920 | tf_op jit(solution)/shard_map/ppermute | solution.py:142
  25.6 1.6 %collective-permute-done.8.theirs_ref = f32[8,2,64,128]{3,2,1,0:T(8,128)S(1)} collective-permute-done((f32[8,2,64,128]{3,2,1,0:T(8,128)S(1)}, f32[8,2,64,128]{3,2,1,0:T(8,128)S(1)}, u32[]{:S(2)}, u32[]{:S(2)}) %collective-permute-start.8) | collective-permute-done | bytes 524320 | tf_op jit(solution)/shard_map/ppermute | solution.py:143
  27.2 1.1 %setup.1 = (f32[12,8,32,128]{3,2,1,0:T(8,128)S(1)}, f32[4,9,32,128]{3,2,1,0:T(8,128)S(1)}, f32[4,8,32,128]{3,2,1,0:T(8,128)S(1)}, f32[8,8,32,128]{3,2,1,0:T(8,12...) custom-call(s32[1,2]{1,0:T(1,128)S(1)} %bitcast.13, ...), custom_call_target="tpu_custom_call" | custom-call | tf_op jit(solution)/shard_map/setup/pallas_call | solution.py:640
  28.3 5.5 %solve.1.planes_ref = f32[6,64,128]{2,1,0:T(8,128)S(1)} custom-call(f32[8,2,64,128]{3,2,1,0:T(8,128)S(1)} %pad_maximum_fusion.mine_ref, f32[8,2,64,128]{3,2,1,0:T(8,128)S(1)} %collective-permute-done.5.theirs_ref, f32[12,8,32,128]{3,2,1,0:T(8,128)S(1)} %get-tuple-element.33.inner, f32[4,9,32,128]{3,2,1,0:T(8,128)S(1)} %get-tuple-element.34.outer_x, ...), custom_call_target="tpu_custom_call" | custom-call | tf_op jit(solution)/shard_map/solve/pallas_call | solution.py:649
  33.9 0.2 finish.1
  34.1 0.4 %collective-permute-start.10 = (f32[2,96,128]{2,1,0:T(8,128)S(1)}, f32[2,96,128]{2,1,0:T(8,128)S(1)}, u32[]{:S(2)}, u32[]{:S(2)}) collective-permute-start(f32[2,96,128]{2,1,0:T(8,128)S(1)} %get-tuple-element.45), channel_id=1, source_target_pairs={{0,1},{1,0},{2,3},{3,2},{4,5},{5,4},{6,7},{7,6},{8,9},{9,8},{10,11... | collective-permute-start | bytes 294920 | tf_op jit(solution)/shard_map/ppermute | solution.py:683
  34.6 2.5 %collective-permute-start.11 = (f32[2,32,128]{2,1,0:T(8,128)S(1)}, f32[2,32,128]{2,1,0:T(8,128)S(1)}, u32[]{:S(2)}, u32[]{:S(2)}) collective-permute-start(f32[2,32,128]{2,1,0:T(8,128)S(1)} %get-tuple-element.53), channel_id=1, source_target_pairs={{0,16},{1,17},{2,18},{3,19},{4,20},{5,21},{6,22},{7,23},{8,24},{9,... | collective-permute-start | bytes 98312 | tf_op jit(solution)/shard_map/ppermute | solution.py:692
  37.1 0.0 collective-permute-start.12
  37.1 0.7 %pad_maximum_fusion.3 = f32[2,2,64,128]{3,2,1,0:T(8,128)} fusion(f32[1,2,64,128]{3,2,1,0:T(8,128)S(1)} %get-tuple-element.51, f32[1,2,64,128]{3,2,1,0:T(8,128)S(1)} %get-tuple-element.50), kind=kLoop, calls=%fused_computation.3 | loop fusion | flops 32768 | bytes 262144 | tf_op jit(solution)/shard_map/stack | solution.py:694
  37.8 1.2 %collective-permute-done.11 = f32[2,32,128]{2,1,0:T(8,128)S(1)} collective-permute-done((f32[2,32,128]{2,1,0:T(8,128)S(1)}, f32[2,32,128]{2,1,0:T(8,128)S(1)}, u32[]{:S(2)}, u32[]{:S(2)}) %collective-permute-start.11) | collective-permute-done | bytes 32800 | tf_op jit(solution)/shard_map/ppermute | solution.py:692
  39.0 1.5 %collective-permute-done.12 = f32[2,32,128]{2,1,0:T(8,128)S(1)} collective-permute-done((f32[2,32,128]{2,1,0:T(8,128)S(1)}, f32[2,32,128]{2,1,0:T(8,128)S(1)}, u32[]{:S(2)}, u32[]{:S(2)}) %collective-permute-start.12) | collective-permute-done | bytes 32800 | tf_op jit(solution)/shard_map/ppermute | solution.py:692
  40.5 0.6 %add_add_fusion = f32[2,32,128]{2,1,0:T(8,128)} fusion(f32[2,32,128]{2,1,0:T(8,128)S(1)} %collective-permute-done.11, f32[2,32,128]{2,1,0:T(8,128)S(1)} %collective-permute-done.12, f32[2,32,128]{2,1,0:T(8,128)S(1)} %get-tuple-element.47, f32[2,96,128]{2,1,0:T(8,128)S(1)} %collective-permute-done.10), kind=kLoop, calls=%fused_computation.9 | loop fusion | flops 24576 | bytes 163840 | tf_op jit(solution)/shard_map/add | solution.py:698
  (25 shorter events, 0.2 us)
Async XLA Ops:
  0.6 7.4 %collective-permute-start = (f32[2,64,128]{2,1,0:T(8,128)}, f32[2,64,128]{2,1,0:T(8,128)S(1)}, u32[]{:S(2)}, u32[]{:S(2)}) collective-permute-start(f32[2,64,128]{2,1,0:T(8,128)} %kappa_ref.1), channel_id=1, source_target_pairs={{0,8},{1,3},{2,10},{3,1},{4,12},{5,7},{6,14},{7,5},{8,0},{9,11},{1... | collective-permute-start | bytes 196616 | tf_op jit(solution)/shard_map/ppermute | solution.py:124
  4.7 4.5 %collective-permute-start.1 = (f32[2,64,128]{2,1,0:T(8,128)}, f32[2,64,128]{2,1,0:T(8,128)S(1)}, u32[]{:S(2)}, u32[]{:S(2)}) collective-permute-start(f32[2,64,128]{2,1,0:T(8,128)} %misfit_ref.1), channel_id=1, source_target_pairs={{0,2},{1,9},{2,0},{3,11},{4,6},{5,13},{6,4},{7,15},{8,10},{9,1},{1... | collective-permute-start | bytes 196616 | tf_op jit(solution)/shard_map/ppermute | solution.py:124
  6.2 0.8 %copy-start.1 = (f32[2,64,128]{2,1,0:T(8,128)S(1)}, f32[2,64,128]{2,1,0:T(8,128)}, u32[]{:S(2)}) copy-start(f32[2,64,128]{2,1,0:T(8,128)} %kappa_ref.1) | copy-start | bytes 196612
  7.1 0.8 %copy-start.2 = (f32[2,64,128]{2,1,0:T(8,128)S(1)}, f32[2,64,128]{2,1,0:T(8,128)}, u32[]{:S(2)}) copy-start(f32[2,64,128]{2,1,0:T(8,128)} %misfit_ref.1) | copy-start | bytes 196612
  9.3 5.4 %collective-permute-start.2 = (f32[2,2,64,128]{3,2,1,0:T(8,128)S(1)}, f32[2,2,64,128]{3,2,1,0:T(8,128)S(1)}, u32[]{:S(2)}, u32[]{:S(2)}) collective-permute-start(f32[2,2,64,128]{3,2,1,0:T(8,128)S(1)} %get-tuple-element.29), channel_id=1, source_target_pairs={{0,4},{1,3},{2,6},{3,1},{4,0},{5,7},{6,2},{7,5},{8,12},{9,11},{10,... | collective-permute-start | bytes 393224 | tf_op jit(solution)/shard_map/ppermute | solution.py:124
  11.0 6.9 %collective-permute-start.6 = (f32[2,2,64,128]{3,2,1,0:T(8,128)S(1)}, f32[2,2,64,128]{3,2,1,0:T(8,128)S(1)}, u32[]{:S(2)}, u32[]{:S(2)}) collective-permute-start(f32[2,2,64,128]{3,2,1,0:T(8,128)S(1)} %get-tuple-element.32), channel_id=1, source_target_pairs={{0,4},{1,9},{2,6},{3,11},{4,0},{5,13},{6,2},{7,15},{8,12},{9,1},{1... | collective-permute-start | bytes 393224 | tf_op jit(solution)/shard_map/ppermute | solution.py:124
  12.3 12.8 %copy-start = (f32[2,2,64,128]{3,2,1,0:T(8,128)S(1)}, f32[2,2,64,128]{3,2,1,0:T(8,128)}, u32[]{:S(2)}) copy-start(f32[2,2,64,128]{3,2,1,0:T(8,128)} %state_ref.1) | copy-start | bytes 393220
  14.8 12.4 %copy-start.3 = (s32[2]{0:T(128)S(1)}, s32[2]{0:T(128)}, u32[]{:S(2)}) copy-start(s32[2]{0:T(128)} %param.11) | copy-start | bytes 28
  14.8 12.4 %copy-start.4 = (f32[4]{0:T(128)S(1)}, f32[4]{0:T(128)}, u32[]{:S(2)}) copy-start(f32[4]{0:T(128)} %param.9) | copy-start | bytes 52
  14.8 12.4 %copy-start.5 = (f32[4]{0:T(128)S(1)}, f32[4]{0:T(128)}, u32[]{:S(2)}) copy-start(f32[4]{0:T(128)} %param.10) | copy-start | bytes 52
  14.8 9.0 %collective-permute-start.3 = (f32[4,2,64,128]{3,2,1,0:T(8,128)S(1)}, f32[4,2,64,128]{3,2,1,0:T(8,128)S(1)}, u32[]{:S(2)}, u32[]{:S(2)}) collective-permute-start(f32[4,2,64,128]{3,2,1,0:T(8,128)S(1)} %pad_maximum_fusion.1), channel_id=1, source_target_pairs={{0,8},{1,5},{2,10},{3,7},{4,12},{5,1},{6,14},{7,3},{8,0},{9,13},{1... | collective-permute-start | bytes 786440 | tf_op jit(solution)/shard_map/ppermute | solution.py:124
  17.9 7.0 %collective-permute-start.7 = (f32[4,2,64,128]{3,2,1,0:T(8,128)S(1)}, f32[4,2,64,128]{3,2,1,0:T(8,128)S(1)}, u32[]{:S(2)}, u32[]{:S(2)}) collective-permute-start(f32[4,2,64,128]{3,2,1,0:T(8,128)S(1)} %pad_maximum_fusion.2), channel_id=1, source_target_pairs={{0,2},{1,5},{2,0},{3,7},{4,6},{5,1},{6,4},{7,3},{8,10},{9,13},{10,... | collective-permute-start | bytes 786440 | tf_op jit(solution)/shard_map/ppermute | solution.py:124
  18.6 5.3 %collective-permute-start.4 = (f32[2,1,64,128]{3,2,1,0:T(8,128)S(1)}, f32[2,1,64,128]{3,2,1,0:T(8,128)S(1)}, u32[]{:S(2)}, u32[]{:S(2)}) collective-permute-start(f32[2,1,64,128]{3,2,1,0:T(8,128)S(1)} %slice_select_fusion.1), channel_id=1, source_target_pairs={{1,2},{2,1},{3,4},{4,3},{5,6},{6,5},{7,8},{8,7},{9,10},{10,9},{11,... | collective-permute-start | bytes 196616 | tf_op jit(solution)/shard_map/ppermute | solution.py:139
  23.9 4.4 %collective-permute-start.5 = (f32[8,2,64,128]{3,2,1,0:T(8,128)S(1)}, f32[8,2,64,128]{3,2,1,0:T(8,128)S(1)}, u32[]{:S(2)}, u32[]{:S(2)}) collective-permute-start(f32[8,2,64,128]{3,2,1,0:T(8,128)S(1)} %pad_maximum_fusion.mine_ref), channel_id=1, source_target_pairs={{0,1},{1,0},{2,3},{3,2},{4,5},{5,4},{6,7},{7,6},{8,9},{9,8},{10,11... | collective-permute-start | bytes 1572872 | tf_op jit(solution)/shard_map/ppermute | solution.py:143
  24.9 2.3 %collective-permute-start.8 = (f32[8,2,64,128]{3,2,1,0:T(8,128)S(1)}, f32[8,2,64,128]{3,2,1,0:T(8,128)S(1)}, u32[]{:S(2)}, u32[]{:S(2)}) collective-permute-start(f32[8,2,64,128]{3,2,1,0:T(8,128)S(1)} %constant_dynamic-update-slice_fusion.mine_ref), channel_id=1, source_target_pairs={{0,1},{1,0},{2,3},{3,2},{4,5},{5,4},{6,7},{7,6},{8,9},{9,8},{10,11... | collective-permute-start | bytes 1572872 | tf_op jit(solution)/shard_map/ppermute | solution.py:143
  25.2 8.7 %collective-permute-start.9 = (f32[3,64,128]{2,1,0:T(8,128)S(1)}, f32[3,64,128]{2,1,0:T(8,128)S(1)}, u32[]{:S(2)}, u32[]{:S(2)}) collective-permute-start(f32[3,64,128]{2,1,0:T(8,128)S(1)} %fusion), channel_id=1, source_target_pairs={{0,1},{1,0},{2,3},{3,2},{4,5},{5,4},{6,7},{7,6},{8,9},{9,8},{10,11... | collective-permute-start | bytes 294920 | tf_op jit(solution)/shard_map/ppermute | solution.py:142
  34.1 3.0 %collective-permute-start.10 = (f32[2,96,128]{2,1,0:T(8,128)S(1)}, f32[2,96,128]{2,1,0:T(8,128)S(1)}, u32[]{:S(2)}, u32[]{:S(2)}) collective-permute-start(f32[2,96,128]{2,1,0:T(8,128)S(1)} %get-tuple-element.45), channel_id=1, source_target_pairs={{0,1},{1,0},{2,3},{3,2},{4,5},{5,4},{6,7},{7,6},{8,9},{9,8},{10,11... | collective-permute-start | bytes 294920 | tf_op jit(solution)/shard_map/ppermute | solution.py:683
  34.6 4.4 %collective-permute-start.11 = (f32[2,32,128]{2,1,0:T(8,128)S(1)}, f32[2,32,128]{2,1,0:T(8,128)S(1)}, u32[]{:S(2)}, u32[]{:S(2)}) collective-permute-start(f32[2,32,128]{2,1,0:T(8,128)S(1)} %get-tuple-element.53), channel_id=1, source_target_pairs={{0,16},{1,17},{2,18},{3,19},{4,20},{5,21},{6,22},{7,23},{8,24},{9,... | collective-permute-start | bytes 98312 | tf_op jit(solution)/shard_map/ppermute | solution.py:692
  37.1 3.4 %collective-permute-start.12 = (f32[2,32,128]{2,1,0:T(8,128)S(1)}, f32[2,32,128]{2,1,0:T(8,128)S(1)}, u32[]{:S(2)}, u32[]{:S(2)}) collective-permute-start(f32[2,32,128]{2,1,0:T(8,128)S(1)} %get-tuple-element.52), channel_id=1, source_target_pairs={{0,17},{1,16},{2,19},{3,18},{4,21},{5,20},{6,23},{7,22},{8,25},{9,... | collective-permute-start | bytes 98312 | tf_op jit(solution)/shard_map/ppermute | solution.py:692

commit v20 on v19

--- a/solution.py
+++ b/solution.py
@@ -137,11 +137,14 @@
         )(*own, *arrived)
         held[1], states = lax.optimization_barrier((held[1], states))
         far = lax.ppermute(jnp.where(even, states[:, :1], states[:, -1:]), axis, over)
-    held[1], far = lax.optimization_barrier((held[1], far))
-    given = jnp.concatenate([states, far], axis=1)
-    near = lax.ppermute(jnp.where(even, given[1], given[0]), axis, swap)
     other = [lax.ppermute(part, axis, swap) for part in held]
-    return held, other, far, near
+
+    def fetch_near(after):
+        late, states_late, far_late = lax.optimization_barrier((after, states, far))
+        given = jnp.concatenate([states_late, far_late], axis=1)
+        return late, lax.ppermute(jnp.where(even, given[1], given[0]), axis, swap)
+
+    return held, other, far, fetch_near
 
 
 CLASSES = [(a, b, c) for a in (0, 1) for b in (0, 1) for c in (0, 1)]
@@ -615,7 +618,7 @@
     groups = lax.axis_size("pole")
     peers = lax.axis_size("space")
     even = lax.axis_index("space") % 2 == 0
-    mine, theirs, far, near = gather_blocks([conductivity, misfit], forward_states, "space")
+    mine, theirs, far, fetch_near = gather_blocks([conductivity, misfit], forward_states, "space")
     half, rows = peers * own // 4, ny // 2
 
     def field(count, extent):
@@ -646,6 +649,7 @@
         compiler_params=pltpu.CompilerParams(vmem_limit_bytes=6 * 1024 * 1024),
         name="setup",
     )(pole_order[None], pole_shifts[None], pole_weights[None], mine[0], theirs[0])
+    coefficients, near = fetch_near(coefficients)
     planes = pl.pallas_call(
         functools.partial(solve_kernel, own=own),
         out_shape=jax.ShapeDtypeStruct((2 * own + 2, ny, nz), jnp.float32),

time: 41.4 us -> 40.8 us (0.986)
  other arithmetic: 2.28 us -> 1.37 us
  waiting for transfers between devices: 12.5 us -> 13 us
    ppermute x6, waiting for transfers between devices: 8.23 us -> 10.1 us  [gather_blocks(): arrived.append(lax.ppermute(held[at], axis, pairs))]
    ppermute x2, waiting for transfers between devices: 1.57 us -> 0.21 us  [gather_blocks(): other = [lax.ppermute(part, axis, swap) for part in held]]
    select_n x1, other arithmetic: 0.88 us -> 0.01 us  [gather_blocks(): jnp.where(even, states[:, :1], states[:, -1:])]
    ppermute x6, starting transfers between devices: 11.4 us -> 12 us  [gather_blocks(): arrived.append(lax.ppermute(held[at], axis, pairs))]
    ppermute x2, starting transfers between devices: 1.18 us -> 0.7 us  [gather_blocks(): other = [lax.ppermute(part, axis, swap) for part in held]]
    unnamed x15 -> x17, local copies, waits for them, and re-layouts: 1.73 us -> 1.75 us
  transfers between devices with their start and end apart: 13 -> 13, of which waited for: 6 -> 8; matrix products, arithmetic and copies ran while one was open for 4% -> 2% of each run, Pallas kernels for 16% -> 17%
where the time goes in v20:
time: 40.8 us; the launch traced here: 40.6 us
  starting transfers between devices  16.5 us (40%)
  waiting for transfers between devices  13 us (32%)
  Pallas kernels  7.11 us (17%)
  local copies, waits for them, and re-layouts  1.79 us (4%)
  other arithmetic  1.37 us (3%)
  between operations  0.82 us (2%)
    ppermute x6, starting transfers between devices, gather_blocks(): arrived.append(lax.ppermute(held[at], axis, pairs))  12 us
    ppermute x6, waiting for transfers between devices, gather_blocks(): arrived.append(lax.ppermute(held[at], axis, pairs))  10.1 us
    pallas_call x1, Pallas kernels, whole_grid(): pl.pallas_call(functools.partial(solve_kernel, own=own), out_shape=jax.Sh...  5.51 us
    ppermute x2, waiting for transfers between devices, whole_grid(): shares.append(lax.ppermute(send[k - 1, side], ('pole', 'space'), pairs))  2.71 us
    ppermute x2, starting transfers between devices, whole_grid(): shares.append(lax.ppermute(send[k - 1, side], ('pole', 'space'), pairs))  2.55 us
    unnamed x17, local copies, waits for them, and re-layouts  1.75 us
    pallas_call x1, Pallas kernels, whole_grid(): pl.pallas_call(setup_kernel, out_shape=[jax.ShapeDtypeStruct(shape, jnp.f...  1.14 us
  transfers between devices with their start and end apart: 13, of which 8 were waited for; matrix products, arithmetic and copies ran while one was open for 2% of the time, Pallas kernels for 17%

profile of v20, /device:TPU:0, one launch (start us, length us, event | category | flops | bytes accessed | tf_op | source)
XLA Modules:
  0.0 40.6 jit_solution(11772172961405706437)
XLA Ops:
  0.6 4.1 %collective-permute-start = (f32[2,64,128]{2,1,0:T(8,128)}, f32[2,64,128]{2,1,0:T(8,128)S(1)}, u32[]{:S(2)}, u32[]{:S(2)}) collective-permute-start(f32[2,64,128]{2,1,0:T(8,128)} %kappa_ref.1), channel_id=1, source_target_pairs={{0,8},{1,3},{2,10},{3,1},{4,12},{5,7},{6,14},{7,5},{8,0},{9,11},{1... | collective-permute-start | bytes 196616 | tf_op jit(solution)/shard_map/ppermute | solution.py:124
  4.7 1.5 %collective-permute-start.1 = (f32[2,64,128]{2,1,0:T(8,128)}, f32[2,64,128]{2,1,0:T(8,128)S(1)}, u32[]{:S(2)}, u32[]{:S(2)}) collective-permute-start(f32[2,64,128]{2,1,0:T(8,128)} %misfit_ref.1), channel_id=1, source_target_pairs={{0,2},{1,9},{2,0},{3,11},{4,6},{5,13},{6,4},{7,15},{8,10},{9,1},{1... | collective-permute-start | bytes 196616 | tf_op jit(solution)/shard_map/ppermute | solution.py:124
  6.2 0.8 %copy-done.1 = f32[2,64,128]{2,1,0:T(8,128)S(1)} copy-done((f32[2,64,128]{2,1,0:T(8,128)S(1)}, f32[2,64,128]{2,1,0:T(8,128)}, u32[]{:S(2)}) %copy-start.1) | copy-done | bytes 65560
  7.1 0.8 %copy-done.2 = f32[2,64,128]{2,1,0:T(8,128)S(1)} copy-done((f32[2,64,128]{2,1,0:T(8,128)S(1)}, f32[2,64,128]{2,1,0:T(8,128)}, u32[]{:S(2)}) %copy-start.2) | copy-done | bytes 65560
  7.9 0.1 prepare.1
  8.0 0.0 collective-permute-done.refs_2_
  8.0 1.2 %collective-permute-done.1.refs_3_ = f32[2,64,128]{2,1,0:T(8,128)S(1)} collective-permute-done((f32[2,64,128]{2,1,0:T(8,128)}, f32[2,64,128]{2,1,0:T(8,128)S(1)}, u32[]{:S(2)}, u32[]{:S(2)}) %collective-permute-start.1) | collective-permute-done | bytes 65568 | tf_op jit(solution)/shard_map/ppermute | solution.py:124
  9.2 0.1 join.1
  9.3 1.6 %collective-permute-start.5 = (f32[2,2,64,128]{3,2,1,0:T(8,128)S(1)}, f32[2,2,64,128]{3,2,1,0:T(8,128)S(1)}, u32[]{:S(2)}, u32[]{:S(2)}) collective-permute-start(f32[2,2,64,128]{3,2,1,0:T(8,128)S(1)} %get-tuple-element.40), channel_id=1, source_target_pairs={{0,4},{1,9},{2,6},{3,11},{4,0},{5,13},{6,2},{7,15},{8,12},{9,1},{1... | collective-permute-start | bytes 393224 | tf_op jit(solution)/shard_map/ppermute | solution.py:124
  11.0 0.4 %collective-permute-start.2 = (f32[2,2,64,128]{3,2,1,0:T(8,128)S(1)}, f32[2,2,64,128]{3,2,1,0:T(8,128)S(1)}, u32[]{:S(2)}, u32[]{:S(2)}) collective-permute-start(f32[2,2,64,128]{3,2,1,0:T(8,128)S(1)} %get-tuple-element.39), channel_id=1, source_target_pairs={{0,4},{1,3},{2,6},{3,1},{4,0},{5,7},{6,2},{7,5},{8,12},{9,11},{10,... | collective-permute-start | bytes 393224 | tf_op jit(solution)/shard_map/ppermute | solution.py:124
  11.4 3.3 %collective-permute-done.5 = f32[2,2,64,128]{3,2,1,0:T(8,128)S(1)} collective-permute-done((f32[2,2,64,128]{3,2,1,0:T(8,128)S(1)}, f32[2,2,64,128]{3,2,1,0:T(8,128)S(1)}, u32[]{:S(2)}, u32[]{:S(2)}) %collective-permute-start.5) | collective-permute-done | bytes 131104 | tf_op jit(solution)/shard_map/ppermute | solution.py:124
  14.7 1.2 %collective-permute-start.6 = (f32[4,2,64,128]{3,2,1,0:T(8,128)S(1)}, f32[4,2,64,128]{3,2,1,0:T(8,128)S(1)}, u32[]{:S(2)}, u32[]{:S(2)}) collective-permute-start(f32[4,2,64,128]{3,2,1,0:T(8,128)S(1)} %pad_maximum_fusion.1), channel_id=1, source_target_pairs={{0,2},{1,5},{2,0},{3,7},{4,6},{5,1},{6,4},{7,3},{8,10},{9,13},{10,... | collective-permute-start | bytes 786440 | tf_op jit(solution)/shard_map/ppermute | solution.py:124
  16.0 0.1 collective-permute-done.2
  16.1 3.1 %collective-permute-start.3 = (f32[4,2,64,128]{3,2,1,0:T(8,128)S(1)}, f32[4,2,64,128]{3,2,1,0:T(8,128)S(1)}, u32[]{:S(2)}, u32[]{:S(2)}) collective-permute-start(f32[4,2,64,128]{3,2,1,0:T(8,128)S(1)} %pad_maximum_fusion), channel_id=1, source_target_pairs={{0,8},{1,5},{2,10},{3,7},{4,12},{5,1},{6,14},{7,3},{8,0},{9,13},{1... | collective-permute-start | bytes 786440 | tf_op jit(solution)/shard_map/ppermute | solution.py:124
  19.3 1.9 %collective-permute-done.6 = f32[4,2,64,128]{3,2,1,0:T(8,128)S(1)} collective-permute-done((f32[4,2,64,128]{3,2,1,0:T(8,128)S(1)}, f32[4,2,64,128]{3,2,1,0:T(8,128)S(1)}, u32[]{:S(2)}, u32[]{:S(2)}) %collective-permute-start.6) | collective-permute-done | bytes 262176 | tf_op jit(solution)/shard_map/ppermute | solution.py:124
  21.2 0.1 collective-permute-start.7
  21.3 0.7 %collective-permute-start.8 = (f32[2,1,64,128]{3,2,1,0:T(8,128)S(1)}, f32[2,1,64,128]{3,2,1,0:T(8,128)S(1)}, u32[]{:S(2)}, u32[]{:S(2)}) collective-permute-start(f32[2,1,64,128]{3,2,1,0:T(8,128)S(1)} %slice_select_fusion.1), channel_id=1, source_target_pairs={{1,2},{2,1},{3,4},{4,3},{5,6},{6,5},{7,8},{8,7},{9,10},{10,9},{11,... | collective-permute-start | bytes 196616 | tf_op jit(solution)/shard_map/ppermute | solution.py:139
  22.0 3.6 %collective-permute-done.3 = f32[4,2,64,128]{3,2,1,0:T(8,128)S(1)} collective-permute-done((f32[4,2,64,128]{3,2,1,0:T(8,128)S(1)}, f32[4,2,64,128]{3,2,1,0:T(8,128)S(1)}, u32[]{:S(2)}, u32[]{:S(2)}) %collective-permute-start.3) | collective-permute-done | bytes 262176 | tf_op jit(solution)/shard_map/ppermute | solution.py:124
  25.6 0.6 %collective-permute-start.4 = (f32[8,2,64,128]{3,2,1,0:T(8,128)S(1)}, f32[8,2,64,128]{3,2,1,0:T(8,128)S(1)}, u32[]{:S(2)}, u32[]{:S(2)}) collective-permute-start(f32[8,2,64,128]{3,2,1,0:T(8,128)S(1)} %constant_dynamic-update-slice_fusion.mine_ref), channel_id=1, source_target_pairs={{0,1},{1,0},{2,3},{3,2},{4,5},{5,4},{6,7},{7,6},{8,9},{9,8},{10,11... | collective-permute-start | bytes 1572872 | tf_op jit(solution)/shard_map/ppermute | solution.py:140
  26.2 0.0 collective-permute-done.7.theirs_ref
  26.2 1.1 %setup.1 = (f32[12,8,32,128]{3,2,1,0:T(8,128)S(1)}, f32[4,9,32,128]{3,2,1,0:T(8,128)S(1)}, f32[4,8,32,128]{3,2,1,0:T(8,128)S(1)}, f32[8,8,32,128]{3,2,1,0:T(8,12...) custom-call(s32[1,2]{1,0:T(1,128)S(1)} %bitcast.13, ...), custom_call_target="tpu_custom_call" | custom-call | tf_op jit(solution)/shard_map/setup/pallas_call | solution.py:643
  27.4 0.1 collective-permute-start.9
  27.5 0.2 collective-permute-done.4.theirs_ref
  27.8 5.5 %solve.1.planes_ref = f32[6,64,128]{2,1,0:T(8,128)S(1)} custom-call(f32[8,2,64,128]{3,2,1,0:T(8,128)S(1)} %constant_dynamic-update-slice_fusion.mine_ref, f32[8,2,64,128]{3,2,1,0:T(8,128)S(1)} %collective-permute-done.4.theirs_ref, f32[12,8,32,128]{3,2,1,0:T(8,128)S(1)} %get-tuple-element.52.inner, f32[4,9,32,128]{3,2,1,0:T(8,128)S(1)} %get-tuple-element.53.outer_x, ...), custom_call_target="tpu_custom_call" | custom-call | tf_op jit(solution)/shard_map/solve/pallas_call | solution.py:653
  33.3 0.2 finish.1
  33.5 0.4 %collective-permute-start.10 = (f32[2,96,128]{2,1,0:T(8,128)S(1)}, f32[2,96,128]{2,1,0:T(8,128)S(1)}, u32[]{:S(2)}, u32[]{:S(2)}) collective-permute-start(f32[2,96,128]{2,1,0:T(8,128)S(1)} %get-tuple-element.65), channel_id=1, source_target_pairs={{0,1},{1,0},{2,3},{3,2},{4,5},{5,4},{6,7},{7,6},{8,9},{9,8},{10,11... | collective-permute-start | bytes 294920 | tf_op jit(solution)/shard_map/ppermute | solution.py:687
  34.0 2.5 %collective-permute-start.11 = (f32[2,32,128]{2,1,0:T(8,128)S(1)}, f32[2,32,128]{2,1,0:T(8,128)S(1)}, u32[]{:S(2)}, u32[]{:S(2)}) collective-permute-start(f32[2,32,128]{2,1,0:T(8,128)S(1)} %get-tuple-element.73), channel_id=1, source_target_pairs={{0,16},{1,17},{2,18},{3,19},{4,20},{5,21},{6,22},{7,23},{8,24},{9,... | collective-permute-start | bytes 98312 | tf_op jit(solution)/shard_map/ppermute | solution.py:696
  36.5 0.0 collective-permute-start.12
  36.6 0.7 %pad_maximum_fusion.2 = f32[2,2,64,128]{3,2,1,0:T(8,128)} fusion(f32[1,2,64,128]{3,2,1,0:T(8,128)S(1)} %get-tuple-element.71, f32[1,2,64,128]{3,2,1,0:T(8,128)S(1)} %get-tuple-element.70), kind=kLoop, calls=%fused_computation.2 | loop fusion | flops 32768 | bytes 262144 | tf_op jit(solution)/shard_map/stack | solution.py:698
  37.2 1.2 %collective-permute-done.11 = f32[2,32,128]{2,1,0:T(8,128)S(1)} collective-permute-done((f32[2,32,128]{2,1,0:T(8,128)S(1)}, f32[2,32,128]{2,1,0:T(8,128)S(1)}, u32[]{:S(2)}, u32[]{:S(2)}) %collective-permute-start.11) | collective-permute-done | bytes 32800 | tf_op jit(solution)/shard_map/ppermute | solution.py:696
  38.4 1.5 %collective-permute-done.12 = f32[2,32,128]{2,1,0:T(8,128)S(1)} collective-permute-done((f32[2,32,128]{2,1,0:T(8,128)S(1)}, f32[2,32,128]{2,1,0:T(8,128)S(1)}, u32[]{:S(2)}, u32[]{:S(2)}) %collective-permute-start.12) | collective-permute-done | bytes 32800 | tf_op jit(solution)/shard_map/ppermute | solution.py:696
  39.9 0.6 %add_add_fusion = f32[2,32,128]{2,1,0:T(8,128)} fusion(f32[2,32,128]{2,1,0:T(8,128)S(1)} %collective-permute-done.11, f32[2,32,128]{2,1,0:T(8,128)S(1)} %collective-permute-done.12, f32[2,32,128]{2,1,0:T(8,128)S(1)} %get-tuple-element.67, f32[2,96,128]{2,1,0:T(8,128)S(1)} %collective-permute-done.10), kind=kLoop, calls=%fused_computation.8 | loop fusion | flops 24576 | bytes 163840 | tf_op jit(solution)/shard_map/add | solution.py:702
  (27 shorter events, 0.2 us)
Async XLA Ops:
  0.6 20.6 %copy-start = (f32[2,2,64,128]{3,2,1,0:T(8,128)S(1)}, f32[2,2,64,128]{3,2,1,0:T(8,128)}, u32[]{:S(2)}) copy-start(f32[2,2,64,128]{3,2,1,0:T(8,128)} %state_ref.1) | copy-start | bytes 393220
  0.6 7.4 %collective-permute-start = (f32[2,64,128]{2,1,0:T(8,128)}, f32[2,64,128]{2,1,0:T(8,128)S(1)}, u32[]{:S(2)}, u32[]{:S(2)}) collective-permute-start(f32[2,64,128]{2,1,0:T(8,128)} %kappa_ref.1), channel_id=1, source_target_pairs={{0,8},{1,3},{2,10},{3,1},{4,12},{5,7},{6,14},{7,5},{8,0},{9,11},{1... | collective-permute-start | bytes 196616 | tf_op jit(solution)/shard_map/ppermute | solution.py:124
  4.7 4.5 %collective-permute-start.1 = (f32[2,64,128]{2,1,0:T(8,128)}, f32[2,64,128]{2,1,0:T(8,128)S(1)}, u32[]{:S(2)}, u32[]{:S(2)}) collective-permute-start(f32[2,64,128]{2,1,0:T(8,128)} %misfit_ref.1), channel_id=1, source_target_pairs={{0,2},{1,9},{2,0},{3,11},{4,6},{5,13},{6,4},{7,15},{8,10},{9,1},{1... | collective-permute-start | bytes 196616 | tf_op jit(solution)/shard_map/ppermute | solution.py:124
  6.2 0.8 %copy-start.1 = (f32[2,64,128]{2,1,0:T(8,128)S(1)}, f32[2,64,128]{2,1,0:T(8,128)}, u32[]{:S(2)}) copy-start(f32[2,64,128]{2,1,0:T(8,128)} %kappa_ref.1) | copy-start | bytes 196612
  7.1 0.8 %copy-start.2 = (f32[2,64,128]{2,1,0:T(8,128)S(1)}, f32[2,64,128]{2,1,0:T(8,128)}, u32[]{:S(2)}) copy-start(f32[2,64,128]{2,1,0:T(8,128)} %misfit_ref.1) | copy-start | bytes 196612
  9.3 5.4 %collective-permute-start.5 = (f32[2,2,64,128]{3,2,1,0:T(8,128)S(1)}, f32[2,2,64,128]{3,2,1,0:T(8,128)S(1)}, u32[]{:S(2)}, u32[]{:S(2)}) collective-permute-start(f32[2,2,64,128]{3,2,1,0:T(8,128)S(1)} %get-tuple-element.40), channel_id=1, source_target_pairs={{0,4},{1,9},{2,6},{3,11},{4,0},{5,13},{6,2},{7,15},{8,12},{9,1},{1... | collective-permute-start | bytes 393224 | tf_op jit(solution)/shard_map/ppermute | solution.py:124
  11.0 15.2 %copy-start.3 = (s32[2]{0:T(128)S(1)}, s32[2]{0:T(128)}, u32[]{:S(2)}) copy-start(s32[2]{0:T(128)} %param.11) | copy-start | bytes 28
  11.0 15.2 %copy-start.4 = (f32[4]{0:T(128)S(1)}, f32[4]{0:T(128)}, u32[]{:S(2)}) copy-start(f32[4]{0:T(128)} %param.9) | copy-start | bytes 52
  11.0 15.2 %copy-start.5 = (f32[4]{0:T(128)S(1)}, f32[4]{0:T(128)}, u32[]{:S(2)}) copy-start(f32[4]{0:T(128)} %param.10) | copy-start | bytes 52
  11.0 5.1 %collective-permute-start.2 = (f32[2,2,64,128]{3,2,1,0:T(8,128)S(1)}, f32[2,2,64,128]{3,2,1,0:T(8,128)S(1)}, u32[]{:S(2)}, u32[]{:S(2)}) collective-permute-start(f32[2,2,64,128]{3,2,1,0:T(8,128)S(1)} %get-tuple-element.39), channel_id=1, source_target_pairs={{0,4},{1,3},{2,6},{3,1},{4,0},{5,7},{6,2},{7,5},{8,12},{9,11},{10,... | collective-permute-start | bytes 393224 | tf_op jit(solution)/shard_map/ppermute | solution.py:124
  14.7 6.4 %collective-permute-start.6 = (f32[4,2,64,128]{3,2,1,0:T(8,128)S(1)}, f32[4,2,64,128]{3,2,1,0:T(8,128)S(1)}, u32[]{:S(2)}, u32[]{:S(2)}) collective-permute-start(f32[4,2,64,128]{3,2,1,0:T(8,128)S(1)} %pad_maximum_fusion.1), channel_id=1, source_target_pairs={{0,2},{1,5},{2,0},{3,7},{4,6},{5,1},{6,4},{7,3},{8,10},{9,13},{10,... | collective-permute-start | bytes 786440 | tf_op jit(solution)/shard_map/ppermute | solution.py:124
  16.1 9.4 %collective-permute-start.3 = (f32[4,2,64,128]{3,2,1,0:T(8,128)S(1)}, f32[4,2,64,128]{3,2,1,0:T(8,128)S(1)}, u32[]{:S(2)}, u32[]{:S(2)}) collective-permute-start(f32[4,2,64,128]{3,2,1,0:T(8,128)S(1)} %pad_maximum_fusion), channel_id=1, source_target_pairs={{0,8},{1,5},{2,10},{3,7},{4,12},{5,1},{6,14},{7,3},{8,0},{9,13},{1... | collective-permute-start | bytes 786440 | tf_op jit(solution)/shard_map/ppermute | solution.py:124
  21.2 5.0 %collective-permute-start.7 = (f32[8,2,64,128]{3,2,1,0:T(8,128)S(1)}, f32[8,2,64,128]{3,2,1,0:T(8,128)S(1)}, u32[]{:S(2)}, u32[]{:S(2)}) collective-permute-start(f32[8,2,64,128]{3,2,1,0:T(8,128)S(1)} %constant_dynamic-update-slice_fusion.3.mine_ref), channel_id=1, source_target_pairs={{0,1},{1,0},{2,3},{3,2},{4,5},{5,4},{6,7},{7,6},{8,9},{9,8},{10,11... | collective-permute-start | bytes 1572872 | tf_op jit(solution)/shard_map/ppermute | solution.py:140
  21.3 6.1 %collective-permute-start.8 = (f32[2,1,64,128]{3,2,1,0:T(8,128)S(1)}, f32[2,1,64,128]{3,2,1,0:T(8,128)S(1)}, u32[]{:S(2)}, u32[]{:S(2)}) collective-permute-start(f32[2,1,64,128]{3,2,1,0:T(8,128)S(1)} %slice_select_fusion.1), channel_id=1, source_target_pairs={{1,2},{2,1},{3,4},{4,3},{5,6},{6,5},{7,8},{8,7},{9,10},{10,9},{11,... | collective-permute-start | bytes 196616 | tf_op jit(solution)/shard_map/ppermute | solution.py:139
  25.6 2.2 %collective-permute-start.4 = (f32[8,2,64,128]{3,2,1,0:T(8,128)S(1)}, f32[8,2,64,128]{3,2,1,0:T(8,128)S(1)}, u32[]{:S(2)}, u32[]{:S(2)}) collective-permute-start(f32[8,2,64,128]{3,2,1,0:T(8,128)S(1)} %constant_dynamic-update-slice_fusion.mine_ref), channel_id=1, source_target_pairs={{0,1},{1,0},{2,3},{3,2},{4,5},{5,4},{6,7},{7,6},{8,9},{9,8},{10,11... | collective-permute-start | bytes 1572872 | tf_op jit(solution)/shard_map/ppermute | solution.py:140
  27.4 5.8 %collective-permute-start.9 = (f32[3,64,128]{2,1,0:T(8,128)S(1)}, f32[3,64,128]{2,1,0:T(8,128)S(1)}, u32[]{:S(2)}, u32[]{:S(2)}) collective-permute-start(f32[3,64,128]{2,1,0:T(8,128)S(1)} %fusion), channel_id=1, source_target_pairs={{0,1},{1,0},{2,3},{3,2},{4,5},{5,4},{6,7},{7,6},{8,9},{9,8},{10,11... | collective-permute-start | bytes 294920 | tf_op jit(solution)/shard_map/ppermute | solution.py:145
  33.5 3.0 %collective-permute-start.10 = (f32[2,96,128]{2,1,0:T(8,128)S(1)}, f32[2,96,128]{2,1,0:T(8,128)S(1)}, u32[]{:S(2)}, u32[]{:S(2)}) collective-permute-start(f32[2,96,128]{2,1,0:T(8,128)S(1)} %get-tuple-element.65), channel_id=1, source_target_pairs={{0,1},{1,0},{2,3},{3,2},{4,5},{5,4},{6,7},{7,6},{8,9},{9,8},{10,11... | collective-permute-start | bytes 294920 | tf_op jit(solution)/shard_map/ppermute | solution.py:687
  34.0 4.4 %collective-permute-start.11 = (f32[2,32,128]{2,1,0:T(8,128)S(1)}, f32[2,32,128]{2,1,0:T(8,128)S(1)}, u32[]{:S(2)}, u32[]{:S(2)}) collective-permute-start(f32[2,32,128]{2,1,0:T(8,128)S(1)} %get-tuple-element.73), channel_id=1, source_target_pairs={{0,16},{1,17},{2,18},{3,19},{4,20},{5,21},{6,22},{7,23},{8,24},{9,... | collective-permute-start | bytes 98312 | tf_op jit(solution)/shard_map/ppermute | solution.py:696
  36.5 3.4 %collective-permute-start.12 = (f32[2,32,128]{2,1,0:T(8,128)S(1)}, f32[2,32,128]{2,1,0:T(8,128)S(1)}, u32[]{:S(2)}, u32[]{:S(2)}) collective-permute-start(f32[2,32,128]{2,1,0:T(8,128)S(1)} %get-tuple-element.72), channel_id=1, source_target_pairs={{0,17},{1,16},{2,19},{3,18},{4,21},{5,20},{6,23},{7,22},{8,25},{9,... | collective-permute-start | bytes 98312 | tf_op jit(solution)/shard_map/ppermute | solution.py:696

commit v21 on v20

--- a/solution.py
+++ b/solution.py
@@ -64,7 +64,7 @@
         falling.append(mask)
         mask //= 2
     if flip:
-        return falling[::-1], falling[:1] + falling[:0:-1]
+        return falling[:1] + falling[:0:-1], falling[::-1]
     return falling, falling[-1:] + falling[:-1]
 
 
@@ -323,8 +323,8 @@
             coarse_total = []
             for k in range(8):
                 within, without = tree_sum(inside[k]), tree_sum(outside[k])
-                inner_sum[k, i, tile(j)] = within
                 base = within + without + shift
+                inner_sum[k, i, tile(j)] = within + ((1.0 - DAMPING) / DAMPING) * base
                 diagonal[k, i, tile(j)] = base
                 coarse_total.append(without)
                 damped[k, i, tile(j)] = (DAMPING / KEPT) * inverse(base)
@@ -477,7 +477,6 @@
             face_get, _, face_after = rows_of(outer_y, i)
             for j in range(tiles):
                 here, sides = coarse_sides(coarse_two, i, j)
-                kept = ((1.0 - DAMPING) / KEPT) * here
                 dots = []
                 for a, b, c in CLASSES:
                     k = cls(a, b, c)
@@ -490,7 +489,7 @@
                             outer_z[4 * c + 2 * a + b, i, tile(j)] * sides[2][c],
                         ]
                     )
-                    new = kept + damped[k, i, tile(j)] * value
+                    new = damped[k, i, tile(j)] * value
                     result[k, i + 1, tile(j)] = new
                     dots.append(residual[k, i, tile(j)] * new)
                 gamma = gamma + tree_sum(dots)

time: 40.8 us -> 45.8 us (1.12)
  starting transfers between devices: 16.5 us -> 21.4 us
    ppermute x6, starting transfers between devices: 12 us -> 15.9 us  [gather_blocks(): arrived.append(lax.ppermute(held[at], axis, pairs))]
    ppermute x2, starting transfers between devices: 0.7 us -> 2.24 us  [gather_blocks(): other = [lax.ppermute(part, axis, swap) for part in held]]
    ppermute x2, starting transfers between devices: 2.55 us -> 1.83 us  [whole_grid(): shares.append(lax.ppermute(send[k - 1, side], ('pole', 'space'), pairs))]
    ppermute x1, starting transfers between devices: 0.1 us -> 0.68 us  [fetch_near(): return (late, lax.ppermute(jnp.where(even, given[1], given[0]), axis, swap))]
  transfers between devices with their start and end apart: 13 -> 13, of which waited for: 8 -> 7; matrix products, arithmetic and copies ran while one was open for 2% -> 2% of each run, Pallas kernels for 17% -> 15%
where the time goes in v21:
time: 45.8 us; the launch traced here: 45.2 us
  starting transfers between devices  21.4 us (47%)
  waiting for transfers between devices  12.7 us (28%)
  Pallas kernels  7.08 us (15%)
  local copies, waits for them, and re-layouts  1.8 us (4%)
  other arithmetic  1.37 us (3%)
  between operations  0.83 us (2%)
    ppermute x6, starting transfers between devices, gather_blocks(): arrived.append(lax.ppermute(held[at], axis, pairs))  15.9 us
    ppermute x6, waiting for transfers between devices, gather_blocks(): arrived.append(lax.ppermute(held[at], axis, pairs))  10.3 us
    pallas_call x1, Pallas kernels, whole_grid(): pl.pallas_call(functools.partial(solve_kernel, own=own), out_shape=jax.Sh...  5.41 us
    ppermute x2, waiting for transfers between devices, whole_grid(): shares.append(lax.ppermute(send[k - 1, side], ('pole', 'space'), pairs))  2.4 us
    ppermute x2, starting transfers between devices, gather_blocks(): other = [lax.ppermute(part, axis, swap) for part in held]  2.24 us
    ppermute x2, starting transfers between devices, whole_grid(): shares.append(lax.ppermute(send[k - 1, side], ('pole', 'space'), pairs))  1.83 us
    unnamed x17, local copies, waits for them, and re-layouts  1.75 us
    pallas_call x1, Pallas kernels, whole_grid(): pl.pallas_call(setup_kernel, out_shape=[jax.ShapeDtypeStruct(shape, jnp.f...  1.22 us
  transfers between devices with their start and end apart: 13, of which 7 were waited for; matrix products, arithmetic and copies ran while one was open for 2% of the time, Pallas kernels for 15%

profile of v21, /device:TPU:0, one launch (start us, length us, event | category | flops | bytes accessed | tf_op | source)
XLA Modules:
  0.0 45.2 jit_solution(13472414422018650710)
XLA Ops:
  0.6 4.1 %collective-permute-start = (f32[2,64,128]{2,1,0:T(8,128)}, f32[2,64,128]{2,1,0:T(8,128)S(1)}, u32[]{:S(2)}, u32[]{:S(2)}) collective-permute-start(f32[2,64,128]{2,1,0:T(8,128)} %kappa_ref.1), channel_id=1, source_target_pairs={{0,8},{1,3},{2,10},{3,1},{4,12},{5,7},{6,14},{7,5},{8,0},{9,11},{1... | collective-permute-start | bytes 196616 | tf_op jit(solution)/shard_map/ppermute | solution.py:124
  4.7 0.1 collective-permute-start.1
  4.8 0.8 %copy-done.1 = f32[2,64,128]{2,1,0:T(8,128)S(1)} copy-done((f32[2,64,128]{2,1,0:T(8,128)S(1)}, f32[2,64,128]{2,1,0:T(8,128)}, u32[]{:S(2)}) %copy-start.1) | copy-done | bytes 65560
  5.7 0.8 %copy-done.2 = f32[2,64,128]{2,1,0:T(8,128)S(1)} copy-done((f32[2,64,128]{2,1,0:T(8,128)S(1)}, f32[2,64,128]{2,1,0:T(8,128)}, u32[]{:S(2)}) %copy-start.2) | copy-done | bytes 65560
  6.5 0.1 prepare.1
  6.6 0.6 %collective-permute-done.refs_2_ = f32[2,64,128]{2,1,0:T(8,128)S(1)} collective-permute-done((f32[2,64,128]{2,1,0:T(8,128)}, f32[2,64,128]{2,1,0:T(8,128)S(1)}, u32[]{:S(2)}, u32[]{:S(2)}) %collective-permute-start) | collective-permute-done | bytes 65568 | tf_op jit(solution)/shard_map/ppermute | solution.py:124
  7.2 2.9 %collective-permute-done.1.refs_3_ = f32[2,64,128]{2,1,0:T(8,128)S(1)} collective-permute-done((f32[2,64,128]{2,1,0:T(8,128)}, f32[2,64,128]{2,1,0:T(8,128)S(1)}, u32[]{:S(2)}, u32[]{:S(2)}) %collective-permute-start.1) | collective-permute-done | bytes 65568 | tf_op jit(solution)/shard_map/ppermute | solution.py:124
  10.1 0.1 join.1
  10.2 1.7 %collective-permute-start.5 = (f32[2,2,64,128]{3,2,1,0:T(8,128)S(1)}, f32[2,2,64,128]{3,2,1,0:T(8,128)S(1)}, u32[]{:S(2)}, u32[]{:S(2)}) collective-permute-start(f32[2,2,64,128]{3,2,1,0:T(8,128)S(1)} %get-tuple-element.40), channel_id=1, source_target_pairs={{0,4},{1,9},{2,6},{3,11},{4,0},{5,13},{6,2},{7,15},{8,12},{9,1},{1... | collective-permute-start | bytes 393224 | tf_op jit(solution)/shard_map/ppermute | solution.py:124
  11.9 2.5 %collective-permute-start.2 = (f32[2,2,64,128]{3,2,1,0:T(8,128)S(1)}, f32[2,2,64,128]{3,2,1,0:T(8,128)S(1)}, u32[]{:S(2)}, u32[]{:S(2)}) collective-permute-start(f32[2,2,64,128]{3,2,1,0:T(8,128)S(1)} %get-tuple-element.39), channel_id=1, source_target_pairs={{0,2},{1,5},{2,0},{3,7},{4,6},{5,1},{6,4},{7,3},{8,10},{9,13},{10,... | collective-permute-start | bytes 393224 | tf_op jit(solution)/shard_map/ppermute | solution.py:124
  14.4 1.3 %collective-permute-done.5 = f32[2,2,64,128]{3,2,1,0:T(8,128)S(1)} collective-permute-done((f32[2,2,64,128]{3,2,1,0:T(8,128)S(1)}, f32[2,2,64,128]{3,2,1,0:T(8,128)S(1)}, u32[]{:S(2)}, u32[]{:S(2)}) %collective-permute-start.5) | collective-permute-done | bytes 131104 | tf_op jit(solution)/shard_map/ppermute | solution.py:124
  15.8 7.5 %collective-permute-start.6 = (f32[4,2,64,128]{3,2,1,0:T(8,128)S(1)}, f32[4,2,64,128]{3,2,1,0:T(8,128)S(1)}, u32[]{:S(2)}, u32[]{:S(2)}) collective-permute-start(f32[4,2,64,128]{3,2,1,0:T(8,128)S(1)} %pad_maximum_fusion.1), channel_id=1, source_target_pairs={{0,2},{1,5},{2,0},{3,7},{4,6},{5,1},{6,4},{7,3},{8,10},{9,13},{10,... | collective-permute-start | bytes 786440 | tf_op jit(solution)/shard_map/ppermute | solution.py:124
  23.2 0.0 collective-permute-done.2
  23.3 0.1 collective-permute-start.3
  23.4 4.2 %collective-permute-done.6 = f32[4,2,64,128]{3,2,1,0:T(8,128)S(1)} collective-permute-done((f32[4,2,64,128]{3,2,1,0:T(8,128)S(1)}, f32[4,2,64,128]{3,2,1,0:T(8,128)S(1)}, u32[]{:S(2)}, u32[]{:S(2)}) %collective-permute-start.6) | collective-permute-done | bytes 262176 | tf_op jit(solution)/shard_map/ppermute | solution.py:124
  27.6 0.1 collective-permute-start.7
  27.7 0.7 %collective-permute-start.8 = (f32[2,1,64,128]{3,2,1,0:T(8,128)S(1)}, f32[2,1,64,128]{3,2,1,0:T(8,128)S(1)}, u32[]{:S(2)}, u32[]{:S(2)}) collective-permute-start(f32[2,1,64,128]{3,2,1,0:T(8,128)S(1)} %slice_select_fusion.1), channel_id=1, source_target_pairs={{1,2},{2,1},{3,4},{4,3},{5,6},{6,5},{7,8},{8,7},{9,10},{10,9},{11,... | collective-permute-start | bytes 196616 | tf_op jit(solution)/shard_map/ppermute | solution.py:139
  28.4 1.3 %collective-permute-done.3 = f32[4,2,64,128]{3,2,1,0:T(8,128)S(1)} collective-permute-done((f32[4,2,64,128]{3,2,1,0:T(8,128)S(1)}, f32[4,2,64,128]{3,2,1,0:T(8,128)S(1)}, u32[]{:S(2)}, u32[]{:S(2)}) %collective-permute-start.3) | collective-permute-done | bytes 262176 | tf_op jit(solution)/shard_map/ppermute | solution.py:124
  29.7 2.2 %collective-permute-start.4 = (f32[8,2,64,128]{3,2,1,0:T(8,128)S(1)}, f32[8,2,64,128]{3,2,1,0:T(8,128)S(1)}, u32[]{:S(2)}, u32[]{:S(2)}) collective-permute-start(f32[8,2,64,128]{3,2,1,0:T(8,128)S(1)} %constant_dynamic-update-slice_fusion.mine_ref), channel_id=1, source_target_pairs={{0,1},{1,0},{2,3},{3,2},{4,5},{5,4},{6,7},{7,6},{8,9},{9,8},{10,11... | collective-permute-start | bytes 1572872 | tf_op jit(solution)/shard_map/ppermute | solution.py:140
  31.9 1.2 %setup.1 = (f32[12,8,32,128]{3,2,1,0:T(8,128)S(1)}, f32[4,9,32,128]{3,2,1,0:T(8,128)S(1)}, f32[4,8,32,128]{3,2,1,0:T(8,128)S(1)}, f32[8,8,32,128]{3,2,1,0:T(8,12...) custom-call(s32[1,2]{1,0:T(1,128)S(1)} %bitcast.13, ...), custom_call_target="tpu_custom_call" | custom-call | tf_op jit(solution)/shard_map/setup/pallas_call | solution.py:642
  33.1 0.0 collective-permute-done.8.far_ref
  33.2 0.7 %collective-permute-start.9 = (f32[3,64,128]{2,1,0:T(8,128)S(1)}, f32[3,64,128]{2,1,0:T(8,128)S(1)}, u32[]{:S(2)}, u32[]{:S(2)}) collective-permute-start(f32[3,64,128]{2,1,0:T(8,128)S(1)} %fusion), channel_id=1, source_target_pairs={{0,1},{1,0},{2,3},{3,2},{4,5},{5,4},{6,7},{7,6},{8,9},{9,8},{10,11... | collective-permute-start | bytes 294920 | tf_op jit(solution)/shard_map/ppermute | solution.py:145
  33.9 5.4 %solve.1.planes_ref = f32[6,64,128]{2,1,0:T(8,128)S(1)} custom-call(f32[8,2,64,128]{3,2,1,0:T(8,128)S(1)} %constant_dynamic-update-slice_fusion.mine_ref, f32[8,2,64,128]{3,2,1,0:T(8,128)S(1)} %collective-permute-done.4.theirs_ref, f32[12,8,32,128]{3,2,1,0:T(8,128)S(1)} %get-tuple-element.52.inner, f32[4,9,32,128]{3,2,1,0:T(8,128)S(1)} %get-tuple-element.53.outer_x, ...), custom_call_target="tpu_custom_call" | custom-call | tf_op jit(solution)/shard_map/solve/pallas_call | solution.py:652
  39.3 0.0 collective-permute-done.9.near_ref
  39.3 0.2 finish.1
  39.6 0.1 collective-permute-start.10
  39.7 1.6 %collective-permute-start.11 = (f32[2,32,128]{2,1,0:T(8,128)S(1)}, f32[2,32,128]{2,1,0:T(8,128)S(1)}, u32[]{:S(2)}, u32[]{:S(2)}) collective-permute-start(f32[2,32,128]{2,1,0:T(8,128)S(1)} %get-tuple-element.73), channel_id=1, source_target_pairs={{0,16},{1,17},{2,18},{3,19},{4,20},{5,21},{6,22},{7,23},{8,24},{9,... | collective-permute-start | bytes 98312 | tf_op jit(solution)/shard_map/ppermute | solution.py:695
  41.3 0.3 collective-permute-start.12
  41.5 0.7 %pad_maximum_fusion.2 = f32[2,2,64,128]{3,2,1,0:T(8,128)} fusion(f32[1,2,64,128]{3,2,1,0:T(8,128)S(1)} %get-tuple-element.71, f32[1,2,64,128]{3,2,1,0:T(8,128)S(1)} %get-tuple-element.70), kind=kLoop, calls=%fused_computation.2 | loop fusion | flops 32768 | bytes 262144 | tf_op jit(solution)/shard_map/stack | solution.py:697
  42.2 1.4 %collective-permute-done.11 = f32[2,32,128]{2,1,0:T(8,128)S(1)} collective-permute-done((f32[2,32,128]{2,1,0:T(8,128)S(1)}, f32[2,32,128]{2,1,0:T(8,128)S(1)}, u32[]{:S(2)}, u32[]{:S(2)}) %collective-permute-start.11) | collective-permute-done | bytes 32800 | tf_op jit(solution)/shard_map/ppermute | solution.py:695
  43.6 1.0 %collective-permute-done.12 = f32[2,32,128]{2,1,0:T(8,128)S(1)} collective-permute-done((f32[2,32,128]{2,1,0:T(8,128)S(1)}, f32[2,32,128]{2,1,0:T(8,128)S(1)}, u32[]{:S(2)}, u32[]{:S(2)}) %collective-permute-start.12) | collective-permute-done | bytes 32800 | tf_op jit(solution)/shard_map/ppermute | solution.py:695
  44.6 0.6 %add_add_fusion = f32[2,32,128]{2,1,0:T(8,128)} fusion(f32[2,32,128]{2,1,0:T(8,128)S(1)} %collective-permute-done.11, f32[2,32,128]{2,1,0:T(8,128)S(1)} %collective-permute-done.12, f32[2,32,128]{2,1,0:T(8,128)S(1)} %get-tuple-element.67, f32[2,96,128]{2,1,0:T(8,128)S(1)} %collective-permute-done.10), kind=kLoop, calls=%fused_computation.8 | loop fusion | flops 24576 | bytes 163840 | tf_op jit(solution)/shard_map/add | solution.py:701
  (27 shorter events, 0.2 us)
Async XLA Ops:
  0.6 27.0 %copy-start = (f32[2,2,64,128]{3,2,1,0:T(8,128)S(1)}, f32[2,2,64,128]{3,2,1,0:T(8,128)}, u32[]{:S(2)}) copy-start(f32[2,2,64,128]{3,2,1,0:T(8,128)} %state_ref.1) | copy-start | bytes 393220
  0.6 6.6 %collective-permute-start = (f32[2,64,128]{2,1,0:T(8,128)}, f32[2,64,128]{2,1,0:T(8,128)S(1)}, u32[]{:S(2)}, u32[]{:S(2)}) collective-permute-start(f32[2,64,128]{2,1,0:T(8,128)} %kappa_ref.1), channel_id=1, source_target_pairs={{0,8},{1,3},{2,10},{3,1},{4,12},{5,7},{6,14},{7,5},{8,0},{9,11},{1... | collective-permute-start | bytes 196616 | tf_op jit(solution)/shard_map/ppermute | solution.py:124
  4.7 5.4 %collective-permute-start.1 = (f32[2,64,128]{2,1,0:T(8,128)}, f32[2,64,128]{2,1,0:T(8,128)S(1)}, u32[]{:S(2)}, u32[]{:S(2)}) collective-permute-start(f32[2,64,128]{2,1,0:T(8,128)} %misfit_ref.1), channel_id=1, source_target_pairs={{0,8},{1,3},{2,10},{3,1},{4,12},{5,7},{6,14},{7,5},{8,0},{9,11},{1... | collective-permute-start | bytes 196616 | tf_op jit(solution)/shard_map/ppermute | solution.py:124
  4.8 0.8 %copy-start.1 = (f32[2,64,128]{2,1,0:T(8,128)S(1)}, f32[2,64,128]{2,1,0:T(8,128)}, u32[]{:S(2)}) copy-start(f32[2,64,128]{2,1,0:T(8,128)} %kappa_ref.1) | copy-start | bytes 196612
  5.7 0.8 %copy-start.2 = (f32[2,64,128]{2,1,0:T(8,128)S(1)}, f32[2,64,128]{2,1,0:T(8,128)}, u32[]{:S(2)}) copy-start(f32[2,64,128]{2,1,0:T(8,128)} %misfit_ref.1) | copy-start | bytes 196612
  10.2 5.5 %collective-permute-start.5 = (f32[2,2,64,128]{3,2,1,0:T(8,128)S(1)}, f32[2,2,64,128]{3,2,1,0:T(8,128)S(1)}, u32[]{:S(2)}, u32[]{:S(2)}) collective-permute-start(f32[2,2,64,128]{3,2,1,0:T(8,128)S(1)} %get-tuple-element.40), channel_id=1, source_target_pairs={{0,4},{1,9},{2,6},{3,11},{4,0},{5,13},{6,2},{7,15},{8,12},{9,1},{1... | collective-permute-start | bytes 393224 | tf_op jit(solution)/shard_map/ppermute | solution.py:124
  11.9 20.0 %copy-start.3 = (s32[2]{0:T(128)S(1)}, s32[2]{0:T(128)}, u32[]{:S(2)}) copy-start(s32[2]{0:T(128)} %param.11) | copy-start | bytes 28
  11.9 20.0 %copy-start.4 = (f32[4]{0:T(128)S(1)}, f32[4]{0:T(128)}, u32[]{:S(2)}) copy-start(f32[4]{0:T(128)} %param.9) | copy-start | bytes 52
  11.9 20.0 %copy-start.5 = (f32[4]{0:T(128)S(1)}, f32[4]{0:T(128)}, u32[]{:S(2)}) copy-start(f32[4]{0:T(128)} %param.10) | copy-start | bytes 52
  11.9 11.3 %collective-permute-start.2 = (f32[2,2,64,128]{3,2,1,0:T(8,128)S(1)}, f32[2,2,64,128]{3,2,1,0:T(8,128)S(1)}, u32[]{:S(2)}, u32[]{:S(2)}) collective-permute-start(f32[2,2,64,128]{3,2,1,0:T(8,128)S(1)} %get-tuple-element.39), channel_id=1, source_target_pairs={{0,2},{1,5},{2,0},{3,7},{4,6},{5,1},{6,4},{7,3},{8,10},{9,13},{10,... | collective-permute-start | bytes 393224 | tf_op jit(solution)/shard_map/ppermute | solution.py:124
  15.8 11.8 %collective-permute-start.6 = (f32[4,2,64,128]{3,2,1,0:T(8,128)S(1)}, f32[4,2,64,128]{3,2,1,0:T(8,128)S(1)}, u32[]{:S(2)}, u32[]{:S(2)}) collective-permute-start(f32[4,2,64,128]{3,2,1,0:T(8,128)S(1)} %pad_maximum_fusion.1), channel_id=1, source_target_pairs={{0,2},{1,5},{2,0},{3,7},{4,6},{5,1},{6,4},{7,3},{8,10},{9,13},{10,... | collective-permute-start | bytes 786440 | tf_op jit(solution)/shard_map/ppermute | solution.py:124
  23.3 6.4 %collective-permute-start.3 = (f32[4,2,64,128]{3,2,1,0:T(8,128)S(1)}, f32[4,2,64,128]{3,2,1,0:T(8,128)S(1)}, u32[]{:S(2)}, u32[]{:S(2)}) collective-permute-start(f32[4,2,64,128]{3,2,1,0:T(8,128)S(1)} %pad_maximum_fusion), channel_id=1, source_target_pairs={{0,4},{1,9},{2,6},{3,11},{4,0},{5,13},{6,2},{7,15},{8,12},{9,1},{1... | collective-permute-start | bytes 786440 | tf_op jit(solution)/shard_map/ppermute | solution.py:124
  27.6 4.3 %collective-permute-start.7 = (f32[8,2,64,128]{3,2,1,0:T(8,128)S(1)}, f32[8,2,64,128]{3,2,1,0:T(8,128)S(1)}, u32[]{:S(2)}, u32[]{:S(2)}) collective-permute-start(f32[8,2,64,128]{3,2,1,0:T(8,128)S(1)} %constant_dynamic-update-slice_fusion.3.mine_ref), channel_id=1, source_target_pairs={{0,1},{1,0},{2,3},{3,2},{4,5},{5,4},{6,7},{7,6},{8,9},{9,8},{10,11... | collective-permute-start | bytes 1572872 | tf_op jit(solution)/shard_map/ppermute | solution.py:140
  27.7 5.4 %collective-permute-start.8 = (f32[2,1,64,128]{3,2,1,0:T(8,128)S(1)}, f32[2,1,64,128]{3,2,1,0:T(8,128)S(1)}, u32[]{:S(2)}, u32[]{:S(2)}) collective-permute-start(f32[2,1,64,128]{3,2,1,0:T(8,128)S(1)} %slice_select_fusion.1), channel_id=1, source_target_pairs={{1,2},{2,1},{3,4},{4,3},{5,6},{6,5},{7,8},{8,7},{9,10},{10,9},{11,... | collective-permute-start | bytes 196616 | tf_op jit(solution)/shard_map/ppermute | solution.py:139
  29.7 4.2 %collective-permute-start.4 = (f32[8,2,64,128]{3,2,1,0:T(8,128)S(1)}, f32[8,2,64,128]{3,2,1,0:T(8,128)S(1)}, u32[]{:S(2)}, u32[]{:S(2)}) collective-permute-start(f32[8,2,64,128]{3,2,1,0:T(8,128)S(1)} %constant_dynamic-update-slice_fusion.mine_ref), channel_id=1, source_target_pairs={{0,1},{1,0},{2,3},{3,2},{4,5},{5,4},{6,7},{7,6},{8,9},{9,8},{10,11... | collective-permute-start | bytes 1572872 | tf_op jit(solution)/shard_map/ppermute | solution.py:140
  33.2 6.1 %collective-permute-start.9 = (f32[3,64,128]{2,1,0:T(8,128)S(1)}, f32[3,64,128]{2,1,0:T(8,128)S(1)}, u32[]{:S(2)}, u32[]{:S(2)}) collective-permute-start(f32[3,64,128]{2,1,0:T(8,128)S(1)} %fusion), channel_id=1, source_target_pairs={{0,1},{1,0},{2,3},{3,2},{4,5},{5,4},{6,7},{7,6},{8,9},{9,8},{10,11... | collective-permute-start | bytes 294920 | tf_op jit(solution)/shard_map/ppermute | solution.py:145
  39.6 1.9 %collective-permute-start.10 = (f32[2,96,128]{2,1,0:T(8,128)S(1)}, f32[2,96,128]{2,1,0:T(8,128)S(1)}, u32[]{:S(2)}, u32[]{:S(2)}) collective-permute-start(f32[2,96,128]{2,1,0:T(8,128)S(1)} %get-tuple-element.65), channel_id=1, source_target_pairs={{0,1},{1,0},{2,3},{3,2},{4,5},{5,4},{6,7},{7,6},{8,9},{9,8},{10,11... | collective-permute-start | bytes 294920 | tf_op jit(solution)/shard_map/ppermute | solution.py:686
  39.7 4.0 %collective-permute-start.11 = (f32[2,32,128]{2,1,0:T(8,128)S(1)}, f32[2,32,128]{2,1,0:T(8,128)S(1)}, u32[]{:S(2)}, u32[]{:S(2)}) collective-permute-start(f32[2,32,128]{2,1,0:T(8,128)S(1)} %get-tuple-element.73), channel_id=1, source_target_pairs={{0,16},{1,17},{2,18},{3,19},{4,20},{5,21},{6,22},{7,23},{8,24},{9,... | collective-permute-start | bytes 98312 | tf_op jit(solution)/shard_map/ppermute | solution.py:695
  41.3 3.4 %collective-permute-start.12 = (f32[2,32,128]{2,1,0:T(8,128)S(1)}, f32[2,32,128]{2,1,0:T(8,128)S(1)}, u32[]{:S(2)}, u32[]{:S(2)}) collective-permute-start(f32[2,32,128]{2,1,0:T(8,128)S(1)} %get-tuple-element.72), channel_id=1, source_target_pairs={{0,17},{1,16},{2,19},{3,18},{4,21},{5,20},{6,23},{7,22},{8,25},{9,... | collective-permute-start | bytes 98312 | tf_op jit(solution)/shard_map/ppermute | solution.py:695

commit v22 on v21

--- a/solution.py
+++ b/solution.py
@@ -64,7 +64,7 @@
         falling.append(mask)
         mask //= 2
     if flip:
-        return falling[:1] + falling[:0:-1], falling[::-1]
+        return falling[::-1], falling[:1] + falling[:0:-1]
     return falling, falling[-1:] + falling[:-1]
 
 

time: 45.8 us -> 40.7 us (0.89)
  starting transfers between devices: 21.4 us -> 16.5 us
    ppermute x6, starting transfers between devices: 15.9 us -> 12 us  [gather_blocks(): arrived.append(lax.ppermute(held[at], axis, pairs))]
    ppermute x2, starting transfers between devices: 2.24 us -> 0.7 us  [gather_blocks(): other = [lax.ppermute(part, axis, swap) for part in held]]
    ppermute x2, starting transfers between devices: 1.83 us -> 2.55 us  [whole_grid(): shares.append(lax.ppermute(send[k - 1, side], ('pole', 'space'), pairs))]
    ppermute x1, starting transfers between devices: 0.68 us -> 0.1 us  [fetch_near(): return (late, lax.ppermute(jnp.where(even, given[1], given[0]), axis, swap))]
  transfers between devices with their start and end apart: 13 -> 13, of which waited for: 7 -> 8; matrix products, arithmetic and copies ran while one was open for 2% -> 2% of each run, Pallas kernels for 15% -> 17%
where the time goes in v22:
time: 40.7 us; the launch traced here: 40.5 us
  starting transfers between devices  16.5 us (41%)
  waiting for transfers between devices  12.9 us (32%)
  Pallas kernels  7.08 us (17%)
  local copies, waits for them, and re-layouts  1.79 us (4%)
  other arithmetic  1.37 us (3%)
  between operations  0.82 us (2%)
    ppermute x6, starting transfers between devices, gather_blocks(): arrived.append(lax.ppermute(held[at], axis, pairs))  12 us
    ppermute x6, waiting for transfers between devices, gather_blocks(): arrived.append(lax.ppermute(held[at], axis, pairs))  10.1 us
    pallas_call x1, Pallas kernels, whole_grid(): pl.pallas_call(functools.partial(solve_kernel, own=own), out_shape=jax.Sh...  5.41 us
    ppermute x2, waiting for transfers between devices, whole_grid(): shares.append(lax.ppermute(send[k - 1, side], ('pole', 'space'), pairs))  2.71 us
    ppermute x2, starting transfers between devices, whole_grid(): shares.append(lax.ppermute(send[k - 1, side], ('pole', 'space'), pairs))  2.55 us
    unnamed x17, local copies, waits for them, and re-layouts  1.75 us
    pallas_call x1, Pallas kernels, whole_grid(): pl.pallas_call(setup_kernel, out_shape=[jax.ShapeDtypeStruct(shape, jnp.f...  1.22 us
  transfers between devices with their start and end apart: 13, of which 8 were waited for; matrix products, arithmetic and copies ran while one was open for 2% of the time, Pallas kernels for 17%

profile of v22, /device:TPU:0, one launch (start us, length us, event | category | flops | bytes accessed | tf_op | source)
XLA Modules:
  0.0 40.5 jit_solution(1742260549928792246)
XLA Ops:
  0.6 4.1 %collective-permute-start = (f32[2,64,128]{2,1,0:T(8,128)}, f32[2,64,128]{2,1,0:T(8,128)S(1)}, u32[]{:S(2)}, u32[]{:S(2)}) collective-permute-start(f32[2,64,128]{2,1,0:T(8,128)} %kappa_ref.1), channel_id=1, source_target_pairs={{0,8},{1,3},{2,10},{3,1},{4,12},{5,7},{6,14},{7,5},{8,0},{9,11},{1... | collective-permute-start | bytes 196616 | tf_op jit(solution)/shard_map/ppermute | solution.py:124
  4.7 1.5 %collective-permute-start.1 = (f32[2,64,128]{2,1,0:T(8,128)}, f32[2,64,128]{2,1,0:T(8,128)S(1)}, u32[]{:S(2)}, u32[]{:S(2)}) collective-permute-start(f32[2,64,128]{2,1,0:T(8,128)} %misfit_ref.1), channel_id=1, source_target_pairs={{0,2},{1,9},{2,0},{3,11},{4,6},{5,13},{6,4},{7,15},{8,10},{9,1},{1... | collective-permute-start | bytes 196616 | tf_op jit(solution)/shard_map/ppermute | solution.py:124
  6.2 0.8 %copy-done.1 = f32[2,64,128]{2,1,0:T(8,128)S(1)} copy-done((f32[2,64,128]{2,1,0:T(8,128)S(1)}, f32[2,64,128]{2,1,0:T(8,128)}, u32[]{:S(2)}) %copy-start.1) | copy-done | bytes 65560
  7.1 0.8 %copy-done.2 = f32[2,64,128]{2,1,0:T(8,128)S(1)} copy-done((f32[2,64,128]{2,1,0:T(8,128)S(1)}, f32[2,64,128]{2,1,0:T(8,128)}, u32[]{:S(2)}) %copy-start.2) | copy-done | bytes 65560
  7.9 0.1 prepare.1
  8.0 0.0 collective-permute-done.refs_2_
  8.0 1.2 %collective-permute-done.1.refs_3_ = f32[2,64,128]{2,1,0:T(8,128)S(1)} collective-permute-done((f32[2,64,128]{2,1,0:T(8,128)}, f32[2,64,128]{2,1,0:T(8,128)S(1)}, u32[]{:S(2)}, u32[]{:S(2)}) %collective-permute-start.1) | collective-permute-done | bytes 65568 | tf_op jit(solution)/shard_map/ppermute | solution.py:124
  9.2 0.1 join.1
  9.3 1.6 %collective-permute-start.5 = (f32[2,2,64,128]{3,2,1,0:T(8,128)S(1)}, f32[2,2,64,128]{3,2,1,0:T(8,128)S(1)}, u32[]{:S(2)}, u32[]{:S(2)}) collective-permute-start(f32[2,2,64,128]{3,2,1,0:T(8,128)S(1)} %get-tuple-element.40), channel_id=1, source_target_pairs={{0,4},{1,9},{2,6},{3,11},{4,0},{5,13},{6,2},{7,15},{8,12},{9,1},{1... | collective-permute-start | bytes 393224 | tf_op jit(solution)/shard_map/ppermute | solution.py:124
  11.0 0.4 %collective-permute-start.2 = (f32[2,2,64,128]{3,2,1,0:T(8,128)S(1)}, f32[2,2,64,128]{3,2,1,0:T(8,128)S(1)}, u32[]{:S(2)}, u32[]{:S(2)}) collective-permute-start(f32[2,2,64,128]{3,2,1,0:T(8,128)S(1)} %get-tuple-element.39), channel_id=1, source_target_pairs={{0,4},{1,3},{2,6},{3,1},{4,0},{5,7},{6,2},{7,5},{8,12},{9,11},{10,... | collective-permute-start | bytes 393224 | tf_op jit(solution)/shard_map/ppermute | solution.py:124
  11.4 3.3 %collective-permute-done.5 = f32[2,2,64,128]{3,2,1,0:T(8,128)S(1)} collective-permute-done((f32[2,2,64,128]{3,2,1,0:T(8,128)S(1)}, f32[2,2,64,128]{3,2,1,0:T(8,128)S(1)}, u32[]{:S(2)}, u32[]{:S(2)}) %collective-permute-start.5) | collective-permute-done | bytes 131104 | tf_op jit(solution)/shard_map/ppermute | solution.py:124
  14.7 1.2 %collective-permute-start.6 = (f32[4,2,64,128]{3,2,1,0:T(8,128)S(1)}, f32[4,2,64,128]{3,2,1,0:T(8,128)S(1)}, u32[]{:S(2)}, u32[]{:S(2)}) collective-permute-start(f32[4,2,64,128]{3,2,1,0:T(8,128)S(1)} %pad_maximum_fusion.1), channel_id=1, source_target_pairs={{0,2},{1,5},{2,0},{3,7},{4,6},{5,1},{6,4},{7,3},{8,10},{9,13},{10,... | collective-permute-start | bytes 786440 | tf_op jit(solution)/shard_map/ppermute | solution.py:124
  16.0 0.1 collective-permute-done.2
  16.1 3.1 %collective-permute-start.3 = (f32[4,2,64,128]{3,2,1,0:T(8,128)S(1)}, f32[4,2,64,128]{3,2,1,0:T(8,128)S(1)}, u32[]{:S(2)}, u32[]{:S(2)}) collective-permute-start(f32[4,2,64,128]{3,2,1,0:T(8,128)S(1)} %pad_maximum_fusion), channel_id=1, source_target_pairs={{0,8},{1,5},{2,10},{3,7},{4,12},{5,1},{6,14},{7,3},{8,0},{9,13},{1... | collective-permute-start | bytes 786440 | tf_op jit(solution)/shard_map/ppermute | solution.py:124
  19.3 1.9 %collective-permute-done.6 = f32[4,2,64,128]{3,2,1,0:T(8,128)S(1)} collective-permute-done((f32[4,2,64,128]{3,2,1,0:T(8,128)S(1)}, f32[4,2,64,128]{3,2,1,0:T(8,128)S(1)}, u32[]{:S(2)}, u32[]{:S(2)}) %collective-permute-start.6) | collective-permute-done | bytes 262176 | tf_op jit(solution)/shard_map/ppermute | solution.py:124
  21.2 0.1 collective-permute-start.7
  21.3 0.7 %collective-permute-start.8 = (f32[2,1,64,128]{3,2,1,0:T(8,128)S(1)}, f32[2,1,64,128]{3,2,1,0:T(8,128)S(1)}, u32[]{:S(2)}, u32[]{:S(2)}) collective-permute-start(f32[2,1,64,128]{3,2,1,0:T(8,128)S(1)} %slice_select_fusion.1), channel_id=1, source_target_pairs={{1,2},{2,1},{3,4},{4,3},{5,6},{6,5},{7,8},{8,7},{9,10},{10,9},{11,... | collective-permute-start | bytes 196616 | tf_op jit(solution)/shard_map/ppermute | solution.py:139
  22.0 3.6 %collective-permute-done.3 = f32[4,2,64,128]{3,2,1,0:T(8,128)S(1)} collective-permute-done((f32[4,2,64,128]{3,2,1,0:T(8,128)S(1)}, f32[4,2,64,128]{3,2,1,0:T(8,128)S(1)}, u32[]{:S(2)}, u32[]{:S(2)}) %collective-permute-start.3) | collective-permute-done | bytes 262176 | tf_op jit(solution)/shard_map/ppermute | solution.py:124
  25.6 0.6 %collective-permute-start.4 = (f32[8,2,64,128]{3,2,1,0:T(8,128)S(1)}, f32[8,2,64,128]{3,2,1,0:T(8,128)S(1)}, u32[]{:S(2)}, u32[]{:S(2)}) collective-permute-start(f32[8,2,64,128]{3,2,1,0:T(8,128)S(1)} %constant_dynamic-update-slice_fusion.mine_ref), channel_id=1, source_target_pairs={{0,1},{1,0},{2,3},{3,2},{4,5},{5,4},{6,7},{7,6},{8,9},{9,8},{10,11... | collective-permute-start | bytes 1572872 | tf_op jit(solution)/shard_map/ppermute | solution.py:140
  26.2 0.0 collective-permute-done.7.theirs_ref
  26.2 1.2 %setup.1 = (f32[12,8,32,128]{3,2,1,0:T(8,128)S(1)}, f32[4,9,32,128]{3,2,1,0:T(8,128)S(1)}, f32[4,8,32,128]{3,2,1,0:T(8,128)S(1)}, f32[8,8,32,128]{3,2,1,0:T(8,12...) custom-call(s32[1,2]{1,0:T(1,128)S(1)} %bitcast.13, ...), custom_call_target="tpu_custom_call" | custom-call | tf_op jit(solution)/shard_map/setup/pallas_call | solution.py:642
  27.5 0.1 collective-permute-start.9
  27.6 0.1 collective-permute-done.4.theirs_ref
  27.8 5.4 %solve.1.planes_ref = f32[6,64,128]{2,1,0:T(8,128)S(1)} custom-call(f32[8,2,64,128]{3,2,1,0:T(8,128)S(1)} %constant_dynamic-update-slice_fusion.mine_ref, f32[8,2,64,128]{3,2,1,0:T(8,128)S(1)} %collective-permute-done.4.theirs_ref, f32[12,8,32,128]{3,2,1,0:T(8,128)S(1)} %get-tuple-element.52.inner, f32[4,9,32,128]{3,2,1,0:T(8,128)S(1)} %get-tuple-element.53.outer_x, ...), custom_call_target="tpu_custom_call" | custom-call | tf_op jit(solution)/shard_map/solve/pallas_call | solution.py:652
  33.2 0.2 finish.1
  33.4 0.4 %collective-permute-start.10 = (f32[2,96,128]{2,1,0:T(8,128)S(1)}, f32[2,96,128]{2,1,0:T(8,128)S(1)}, u32[]{:S(2)}, u32[]{:S(2)}) collective-permute-start(f32[2,96,128]{2,1,0:T(8,128)S(1)} %get-tuple-element.65), channel_id=1, source_target_pairs={{0,1},{1,0},{2,3},{3,2},{4,5},{5,4},{6,7},{7,6},{8,9},{9,8},{10,11... | collective-permute-start | bytes 294920 | tf_op jit(solution)/shard_map/ppermute | solution.py:686
  33.9 2.5 %collective-permute-start.11 = (f32[2,32,128]{2,1,0:T(8,128)S(1)}, f32[2,32,128]{2,1,0:T(8,128)S(1)}, u32[]{:S(2)}, u32[]{:S(2)}) collective-permute-start(f32[2,32,128]{2,1,0:T(8,128)S(1)} %get-tuple-element.73), channel_id=1, source_target_pairs={{0,16},{1,17},{2,18},{3,19},{4,20},{5,21},{6,22},{7,23},{8,24},{9,... | collective-permute-start | bytes 98312 | tf_op jit(solution)/shard_map/ppermute | solution.py:695
  36.4 0.0 collective-permute-start.12
  36.5 0.7 %pad_maximum_fusion.2 = f32[2,2,64,128]{3,2,1,0:T(8,128)} fusion(f32[1,2,64,128]{3,2,1,0:T(8,128)S(1)} %get-tuple-element.71, f32[1,2,64,128]{3,2,1,0:T(8,128)S(1)} %get-tuple-element.70), kind=kLoop, calls=%fused_computation.2 | loop fusion | flops 32768 | bytes 262144 | tf_op jit(solution)/shard_map/stack | solution.py:697
  37.1 1.2 %collective-permute-done.11 = f32[2,32,128]{2,1,0:T(8,128)S(1)} collective-permute-done((f32[2,32,128]{2,1,0:T(8,128)S(1)}, f32[2,32,128]{2,1,0:T(8,128)S(1)}, u32[]{:S(2)}, u32[]{:S(2)}) %collective-permute-start.11) | collective-permute-done | bytes 32800 | tf_op jit(solution)/shard_map/ppermute | solution.py:695
  38.3 1.5 %collective-permute-done.12 = f32[2,32,128]{2,1,0:T(8,128)S(1)} collective-permute-done((f32[2,32,128]{2,1,0:T(8,128)S(1)}, f32[2,32,128]{2,1,0:T(8,128)S(1)}, u32[]{:S(2)}, u32[]{:S(2)}) %collective-permute-start.12) | collective-permute-done | bytes 32800 | tf_op jit(solution)/shard_map/ppermute | solution.py:695
  39.8 0.6 %add_add_fusion = f32[2,32,128]{2,1,0:T(8,128)} fusion(f32[2,32,128]{2,1,0:T(8,128)S(1)} %collective-permute-done.11, f32[2,32,128]{2,1,0:T(8,128)S(1)} %collective-permute-done.12, f32[2,32,128]{2,1,0:T(8,128)S(1)} %get-tuple-element.67, f32[2,96,128]{2,1,0:T(8,128)S(1)} %collective-permute-done.10), kind=kLoop, calls=%fused_computation.8 | loop fusion | flops 24576 | bytes 163840 | tf_op jit(solution)/shard_map/add | solution.py:701
  (27 shorter events, 0.2 us)
Async XLA Ops:
  0.6 20.6 %copy-start = (f32[2,2,64,128]{3,2,1,0:T(8,128)S(1)}, f32[2,2,64,128]{3,2,1,0:T(8,128)}, u32[]{:S(2)}) copy-start(f32[2,2,64,128]{3,2,1,0:T(8,128)} %state_ref.1) | copy-start | bytes 393220
  0.6 7.4 %collective-permute-start = (f32[2,64,128]{2,1,0:T(8,128)}, f32[2,64,128]{2,1,0:T(8,128)S(1)}, u32[]{:S(2)}, u32[]{:S(2)}) collective-permute-start(f32[2,64,128]{2,1,0:T(8,128)} %kappa_ref.1), channel_id=1, source_target_pairs={{0,8},{1,3},{2,10},{3,1},{4,12},{5,7},{6,14},{7,5},{8,0},{9,11},{1... | collective-permute-start | bytes 196616 | tf_op jit(solution)/shard_map/ppermute | solution.py:124
  4.7 4.5 %collective-permute-start.1 = (f32[2,64,128]{2,1,0:T(8,128)}, f32[2,64,128]{2,1,0:T(8,128)S(1)}, u32[]{:S(2)}, u32[]{:S(2)}) collective-permute-start(f32[2,64,128]{2,1,0:T(8,128)} %misfit_ref.1), channel_id=1, source_target_pairs={{0,2},{1,9},{2,0},{3,11},{4,6},{5,13},{6,4},{7,15},{8,10},{9,1},{1... | collective-permute-start | bytes 196616 | tf_op jit(solution)/shard_map/ppermute | solution.py:124
  6.2 0.8 %copy-start.1 = (f32[2,64,128]{2,1,0:T(8,128)S(1)}, f32[2,64,128]{2,1,0:T(8,128)}, u32[]{:S(2)}) copy-start(f32[2,64,128]{2,1,0:T(8,128)} %kappa_ref.1) | copy-start | bytes 196612
  7.1 0.8 %copy-start.2 = (f32[2,64,128]{2,1,0:T(8,128)S(1)}, f32[2,64,128]{2,1,0:T(8,128)}, u32[]{:S(2)}) copy-start(f32[2,64,128]{2,1,0:T(8,128)} %misfit_ref.1) | copy-start | bytes 196612
  9.3 5.4 %collective-permute-start.5 = (f32[2,2,64,128]{3,2,1,0:T(8,128)S(1)}, f32[2,2,64,128]{3,2,1,0:T(8,128)S(1)}, u32[]{:S(2)}, u32[]{:S(2)}) collective-permute-start(f32[2,2,64,128]{3,2,1,0:T(8,128)S(1)} %get-tuple-element.40), channel_id=1, source_target_pairs={{0,4},{1,9},{2,6},{3,11},{4,0},{5,13},{6,2},{7,15},{8,12},{9,1},{1... | collective-permute-start | bytes 393224 | tf_op jit(solution)/shard_map/ppermute | solution.py:124
  11.0 15.2 %copy-start.3 = (s32[2]{0:T(128)S(1)}, s32[2]{0:T(128)}, u32[]{:S(2)}) copy-start(s32[2]{0:T(128)} %param.11) | copy-start | bytes 28
  11.0 15.2 %copy-start.4 = (f32[4]{0:T(128)S(1)}, f32[4]{0:T(128)}, u32[]{:S(2)}) copy-start(f32[4]{0:T(128)} %param.9) | copy-start | bytes 52
  11.0 15.2 %copy-start.5 = (f32[4]{0:T(128)S(1)}, f32[4]{0:T(128)}, u32[]{:S(2)}) copy-start(f32[4]{0:T(128)} %param.10) | copy-start | bytes 52
  11.0 5.1 %collective-permute-start.2 = (f32[2,2,64,128]{3,2,1,0:T(8,128)S(1)}, f32[2,2,64,128]{3,2,1,0:T(8,128)S(1)}, u32[]{:S(2)}, u32[]{:S(2)}) collective-permute-start(f32[2,2,64,128]{3,2,1,0:T(8,128)S(1)} %get-tuple-element.39), channel_id=1, source_target_pairs={{0,4},{1,3},{2,6},{3,1},{4,0},{5,7},{6,2},{7,5},{8,12},{9,11},{10,... | collective-permute-start | bytes 393224 | tf_op jit(solution)/shard_map/ppermute | solution.py:124
  14.7 6.4 %collective-permute-start.6 = (f32[4,2,64,128]{3,2,1,0:T(8,128)S(1)}, f32[4,2,64,128]{3,2,1,0:T(8,128)S(1)}, u32[]{:S(2)}, u32[]{:S(2)}) collective-permute-start(f32[4,2,64,128]{3,2,1,0:T(8,128)S(1)} %pad_maximum_fusion.1), channel_id=1, source_target_pairs={{0,2},{1,5},{2,0},{3,7},{4,6},{5,1},{6,4},{7,3},{8,10},{9,13},{10,... | collective-permute-start | bytes 786440 | tf_op jit(solution)/shard_map/ppermute | solution.py:124
  16.1 9.4 %collective-permute-start.3 = (f32[4,2,64,128]{3,2,1,0:T(8,128)S(1)}, f32[4,2,64,128]{3,2,1,0:T(8,128)S(1)}, u32[]{:S(2)}, u32[]{:S(2)}) collective-permute-start(f32[4,2,64,128]{3,2,1,0:T(8,128)S(1)} %pad_maximum_fusion), channel_id=1, source_target_pairs={{0,8},{1,5},{2,10},{3,7},{4,12},{5,1},{6,14},{7,3},{8,0},{9,13},{1... | collective-permute-start | bytes 786440 | tf_op jit(solution)/shard_map/ppermute | solution.py:124
  21.2 5.0 %collective-permute-start.7 = (f32[8,2,64,128]{3,2,1,0:T(8,128)S(1)}, f32[8,2,64,128]{3,2,1,0:T(8,128)S(1)}, u32[]{:S(2)}, u32[]{:S(2)}) collective-permute-start(f32[8,2,64,128]{3,2,1,0:T(8,128)S(1)} %constant_dynamic-update-slice_fusion.3.mine_ref), channel_id=1, source_target_pairs={{0,1},{1,0},{2,3},{3,2},{4,5},{5,4},{6,7},{7,6},{8,9},{9,8},{10,11... | collective-permute-start | bytes 1572872 | tf_op jit(solution)/shard_map/ppermute | solution.py:140
  21.3 6.2 %collective-permute-start.8 = (f32[2,1,64,128]{3,2,1,0:T(8,128)S(1)}, f32[2,1,64,128]{3,2,1,0:T(8,128)S(1)}, u32[]{:S(2)}, u32[]{:S(2)}) collective-permute-start(f32[2,1,64,128]{3,2,1,0:T(8,128)S(1)} %slice_select_fusion.1), channel_id=1, source_target_pairs={{1,2},{2,1},{3,4},{4,3},{5,6},{6,5},{7,8},{8,7},{9,10},{10,9},{11,... | collective-permute-start | bytes 196616 | tf_op jit(solution)/shard_map/ppermute | solution.py:139
  25.6 2.2 %collective-permute-start.4 = (f32[8,2,64,128]{3,2,1,0:T(8,128)S(1)}, f32[8,2,64,128]{3,2,1,0:T(8,128)S(1)}, u32[]{:S(2)}, u32[]{:S(2)}) collective-permute-start(f32[8,2,64,128]{3,2,1,0:T(8,128)S(1)} %constant_dynamic-update-slice_fusion.mine_ref), channel_id=1, source_target_pairs={{0,1},{1,0},{2,3},{3,2},{4,5},{5,4},{6,7},{7,6},{8,9},{9,8},{10,11... | collective-permute-start | bytes 1572872 | tf_op jit(solution)/shard_map/ppermute | solution.py:140
  27.5 5.6 %collective-permute-start.9 = (f32[3,64,128]{2,1,0:T(8,128)S(1)}, f32[3,64,128]{2,1,0:T(8,128)S(1)}, u32[]{:S(2)}, u32[]{:S(2)}) collective-permute-start(f32[3,64,128]{2,1,0:T(8,128)S(1)} %fusion), channel_id=1, source_target_pairs={{0,1},{1,0},{2,3},{3,2},{4,5},{5,4},{6,7},{7,6},{8,9},{9,8},{10,11... | collective-permute-start | bytes 294920 | tf_op jit(solution)/shard_map/ppermute | solution.py:145
  33.4 3.0 %collective-permute-start.10 = (f32[2,96,128]{2,1,0:T(8,128)S(1)}, f32[2,96,128]{2,1,0:T(8,128)S(1)}, u32[]{:S(2)}, u32[]{:S(2)}) collective-permute-start(f32[2,96,128]{2,1,0:T(8,128)S(1)} %get-tuple-element.65), channel_id=1, source_target_pairs={{0,1},{1,0},{2,3},{3,2},{4,5},{5,4},{6,7},{7,6},{8,9},{9,8},{10,11... | collective-permute-start | bytes 294920 | tf_op jit(solution)/shard_map/ppermute | solution.py:686
  33.9 4.4 %collective-permute-start.11 = (f32[2,32,128]{2,1,0:T(8,128)S(1)}, f32[2,32,128]{2,1,0:T(8,128)S(1)}, u32[]{:S(2)}, u32[]{:S(2)}) collective-permute-start(f32[2,32,128]{2,1,0:T(8,128)S(1)} %get-tuple-element.73), channel_id=1, source_target_pairs={{0,16},{1,17},{2,18},{3,19},{4,20},{5,21},{6,22},{7,23},{8,24},{9,... | collective-permute-start | bytes 98312 | tf_op jit(solution)/shard_map/ppermute | solution.py:695
  36.4 3.4 %collective-permute-start.12 = (f32[2,32,128]{2,1,0:T(8,128)S(1)}, f32[2,32,128]{2,1,0:T(8,128)S(1)}, u32[]{:S(2)}, u32[]{:S(2)}) collective-permute-start(f32[2,32,128]{2,1,0:T(8,128)S(1)} %get-tuple-element.72), channel_id=1, source_target_pairs={{0,17},{1,16},{2,19},{3,18},{4,21},{5,20},{6,23},{7,22},{8,25},{9,... | collective-permute-start | bytes 98312 | tf_op jit(solution)/shard_map/ppermute | solution.py:695

commit v23 on v22

--- a/solution.py
+++ b/solution.py
@@ -249,7 +249,7 @@
     coarse_off,
     coarse_damped,
     chosen,
-    half_kappa,
+    kappa,
 ):
     half = inner.shape[1]
     at_ = Layout(inner.shape[2])
@@ -259,14 +259,14 @@
     taken = lane_index(shifts_ref.shape) == pole
     shift = jnp.sum(jnp.where(taken, shifts_ref[...], 0.0), axis=1, keepdims=True)
     weight = jnp.sum(jnp.where(taken, weights_ref[...], 0.0), axis=1, keepdims=True)
-    shift = jnp.broadcast_to(shift, at_.zero.shape)
-    chosen[...] = jnp.broadcast_to(weight, at_.zero.shape)
+    shift = jnp.broadcast_to(2.0 * shift, at_.zero.shape)
+    chosen[...] = jnp.broadcast_to(2.0 * weight, at_.zero.shape)
 
     def keep(k, spot, j, value):
-        half_kappa[k, spot + 1, tile(j)] = 0.5 * value
+        kappa[k, spot + 1, tile(j)] = value
 
     at_.arrange(mine_ref, theirs_ref, place, False, keep)
-    at_.seam_fine(half_kappa)
+    at_.seam_fine(kappa)
 
     z_low = jnp.where(at_.lane % HALF > 0, 1.0, 0.0)
     z_high = jnp.where(at_.lane % HALF < HALF - 1, 1.0, 0.0)
@@ -278,7 +278,7 @@
 
     def plane(i, carry):
         for j in range(tiles):
-            kap = [half_kappa[k, i + 1, tile(j)] for k in range(8)]
+            kap = [kappa[k, i + 1, tile(j)] for k in range(8)]
             inside = [[] for _ in range(8)]
             outside = [[] for _ in range(8)]
             off = [[] for _ in range(5)]
@@ -291,17 +291,17 @@
                 at = 2 * p + q
 
                 low, high = cls(0, p, q), cls(1, p, q)
-                minus = kap[low] + half_kappa[high, i, tile(j)]
-                plus = kap[high] + half_kappa[low, i + 2, tile(j)]
+                minus = kap[low] + kappa[high, i, tile(j)]
+                plus = kap[high] + kappa[low, i + 2, tile(j)]
                 outside[low].append(minus)
                 outside[high].append(plus)
                 outer_x[at, i, tile(j)] = minus
                 off[0].append(minus)
 
                 low, high = cls(p, 0, q), cls(p, 1, q)
-                side = at_.row_before(lambda r: half_kappa[high, i + 1, tile(r)], j)
+                side = at_.row_before(lambda r: kappa[high, i + 1, tile(r)], j)
                 minus = kap[low] + masked(y_low[j], side)
-                side = at_.row_after(lambda r: half_kappa[low, i + 1, tile(r)], j)
+                side = at_.row_after(lambda r: kappa[low, i + 1, tile(r)], j)
                 plus = kap[high] + masked(y_high[j], side)
                 outside[low].append(minus)
                 outside[high].append(plus)
@@ -337,8 +337,8 @@
     for j in range(tiles):
         part = []
         for p, q in PAIRS:
-            face = half_kappa[cls(0, p, q), half + 1, tile(j)]
-            face = face + half_kappa[cls(1, p, q), half, tile(j)]
+            face = kappa[cls(0, p, q), half + 1, tile(j)]
+            face = face + kappa[cls(1, p, q), half, tile(j)]
             outer_x[2 * p + q, half, tile(j)] = face
             part.append(face)
         coarse_off[0, half, tile(j)] = tree_sum(part)

time: 40.7 us -> 40.7 us (level)
  no operation moved by 1% of the time
where the time goes in v23:
time: 40.7 us; the launch traced here: 40.5 us
  starting transfers between devices  16.5 us (41%)
  waiting for transfers between devices  12.9 us (32%)
  Pallas kernels  7.09 us (17%)
  local copies, waits for them, and re-layouts  1.79 us (4%)
  other arithmetic  1.37 us (3%)
  between operations  0.82 us (2%)
    ppermute x6, starting transfers between devices, gather_blocks(): arrived.append(lax.ppermute(held[at], axis, pairs))  12 us
    ppermute x6, waiting for transfers between devices, gather_blocks(): arrived.append(lax.ppermute(held[at], axis, pairs))  10.1 us
    pallas_call x1, Pallas kernels, whole_grid(): pl.pallas_call(functools.partial(solve_kernel, own=own), out_shape=jax.Sh...  5.41 us
    ppermute x2, waiting for transfers between devices, whole_grid(): shares.append(lax.ppermute(send[k - 1, side], ('pole', 'space'), pairs))  2.71 us
    ppermute x2, starting transfers between devices, whole_grid(): shares.append(lax.ppermute(send[k - 1, side], ('pole', 'space'), pairs))  2.55 us
    unnamed x17, local copies, waits for them, and re-layouts  1.75 us
    pallas_call x1, Pallas kernels, whole_grid(): pl.pallas_call(setup_kernel, out_shape=[jax.ShapeDtypeStruct(shape, jnp.f...  1.22 us
  transfers between devices with their start and end apart: 13, of which 8 were waited for; matrix products, arithmetic and copies ran while one was open for 2% of the time, Pallas kernels for 17%

profile of v23, /device:TPU:0, one launch (start us, length us, event | category | flops | bytes accessed | tf_op | source)
XLA Modules:
  0.0 40.5 jit_solution(6891678275331978808)
XLA Ops:
  0.6 4.1 %collective-permute-start = (f32[2,64,128]{2,1,0:T(8,128)}, f32[2,64,128]{2,1,0:T(8,128)S(1)}, u32[]{:S(2)}, u32[]{:S(2)}) collective-permute-start(f32[2,64,128]{2,1,0:T(8,128)} %kappa_ref.1), channel_id=1, source_target_pairs={{0,8},{1,3},{2,10},{3,1},{4,12},{5,7},{6,14},{7,5},{8,0},{9,11},{1... | collective-permute-start | bytes 196616 | tf_op jit(solution)/shard_map/ppermute | solution.py:124
  4.7 1.5 %collective-permute-start.1 = (f32[2,64,128]{2,1,0:T(8,128)}, f32[2,64,128]{2,1,0:T(8,128)S(1)}, u32[]{:S(2)}, u32[]{:S(2)}) collective-permute-start(f32[2,64,128]{2,1,0:T(8,128)} %misfit_ref.1), channel_id=1, source_target_pairs={{0,2},{1,9},{2,0},{3,11},{4,6},{5,13},{6,4},{7,15},{8,10},{9,1},{1... | collective-permute-start | bytes 196616 | tf_op jit(solution)/shard_map/ppermute | solution.py:124
  6.2 0.8 %copy-done.1 = f32[2,64,128]{2,1,0:T(8,128)S(1)} copy-done((f32[2,64,128]{2,1,0:T(8,128)S(1)}, f32[2,64,128]{2,1,0:T(8,128)}, u32[]{:S(2)}) %copy-start.1) | copy-done | bytes 65560
  7.1 0.8 %copy-done.2 = f32[2,64,128]{2,1,0:T(8,128)S(1)} copy-done((f32[2,64,128]{2,1,0:T(8,128)S(1)}, f32[2,64,128]{2,1,0:T(8,128)}, u32[]{:S(2)}) %copy-start.2) | copy-done | bytes 65560
  7.9 0.1 prepare.1
  8.0 0.0 collective-permute-done.refs_2_
  8.0 1.2 %collective-permute-done.1.refs_3_ = f32[2,64,128]{2,1,0:T(8,128)S(1)} collective-permute-done((f32[2,64,128]{2,1,0:T(8,128)}, f32[2,64,128]{2,1,0:T(8,128)S(1)}, u32[]{:S(2)}, u32[]{:S(2)}) %collective-permute-start.1) | collective-permute-done | bytes 65568 | tf_op jit(solution)/shard_map/ppermute | solution.py:124
  9.2 0.1 join.1
  9.3 1.6 %collective-permute-start.5 = (f32[2,2,64,128]{3,2,1,0:T(8,128)S(1)}, f32[2,2,64,128]{3,2,1,0:T(8,128)S(1)}, u32[]{:S(2)}, u32[]{:S(2)}) collective-permute-start(f32[2,2,64,128]{3,2,1,0:T(8,128)S(1)} %get-tuple-element.40), channel_id=1, source_target_pairs={{0,4},{1,9},{2,6},{3,11},{4,0},{5,13},{6,2},{7,15},{8,12},{9,1},{1... | collective-permute-start | bytes 393224 | tf_op jit(solution)/shard_map/ppermute | solution.py:124
  11.0 0.4 %collective-permute-start.2 = (f32[2,2,64,128]{3,2,1,0:T(8,128)S(1)}, f32[2,2,64,128]{3,2,1,0:T(8,128)S(1)}, u32[]{:S(2)}, u32[]{:S(2)}) collective-permute-start(f32[2,2,64,128]{3,2,1,0:T(8,128)S(1)} %get-tuple-element.39), channel_id=1, source_target_pairs={{0,4},{1,3},{2,6},{3,1},{4,0},{5,7},{6,2},{7,5},{8,12},{9,11},{10,... | collective-permute-start | bytes 393224 | tf_op jit(solution)/shard_map/ppermute | solution.py:124
  11.4 3.3 %collective-permute-done.5 = f32[2,2,64,128]{3,2,1,0:T(8,128)S(1)} collective-permute-done((f32[2,2,64,128]{3,2,1,0:T(8,128)S(1)}, f32[2,2,64,128]{3,2,1,0:T(8,128)S(1)}, u32[]{:S(2)}, u32[]{:S(2)}) %collective-permute-start.5) | collective-permute-done | bytes 131104 | tf_op jit(solution)/shard_map/ppermute | solution.py:124
  14.7 1.2 %collective-permute-start.6 = (f32[4,2,64,128]{3,2,1,0:T(8,128)S(1)}, f32[4,2,64,128]{3,2,1,0:T(8,128)S(1)}, u32[]{:S(2)}, u32[]{:S(2)}) collective-permute-start(f32[4,2,64,128]{3,2,1,0:T(8,128)S(1)} %pad_maximum_fusion.1), channel_id=1, source_target_pairs={{0,2},{1,5},{2,0},{3,7},{4,6},{5,1},{6,4},{7,3},{8,10},{9,13},{10,... | collective-permute-start | bytes 786440 | tf_op jit(solution)/shard_map/ppermute | solution.py:124
  16.0 0.1 collective-permute-done.2
  16.1 3.1 %collective-permute-start.3 = (f32[4,2,64,128]{3,2,1,0:T(8,128)S(1)}, f32[4,2,64,128]{3,2,1,0:T(8,128)S(1)}, u32[]{:S(2)}, u32[]{:S(2)}) collective-permute-start(f32[4,2,64,128]{3,2,1,0:T(8,128)S(1)} %pad_maximum_fusion), channel_id=1, source_target_pairs={{0,8},{1,5},{2,10},{3,7},{4,12},{5,1},{6,14},{7,3},{8,0},{9,13},{1... | collective-permute-start | bytes 786440 | tf_op jit(solution)/shard_map/ppermute | solution.py:124
  19.3 1.9 %collective-permute-done.6 = f32[4,2,64,128]{3,2,1,0:T(8,128)S(1)} collective-permute-done((f32[4,2,64,128]{3,2,1,0:T(8,128)S(1)}, f32[4,2,64,128]{3,2,1,0:T(8,128)S(1)}, u32[]{:S(2)}, u32[]{:S(2)}) %collective-permute-start.6) | collective-permute-done | bytes 262176 | tf_op jit(solution)/shard_map/ppermute | solution.py:124
  21.2 0.1 collective-permute-start.7
  21.3 0.7 %collective-permute-start.8 = (f32[2,1,64,128]{3,2,1,0:T(8,128)S(1)}, f32[2,1,64,128]{3,2,1,0:T(8,128)S(1)}, u32[]{:S(2)}, u32[]{:S(2)}) collective-permute-start(f32[2,1,64,128]{3,2,1,0:T(8,128)S(1)} %slice_select_fusion.1), channel_id=1, source_target_pairs={{1,2},{2,1},{3,4},{4,3},{5,6},{6,5},{7,8},{8,7},{9,10},{10,9},{11,... | collective-permute-start | bytes 196616 | tf_op jit(solution)/shard_map/ppermute | solution.py:139
  22.0 3.6 %collective-permute-done.3 = f32[4,2,64,128]{3,2,1,0:T(8,128)S(1)} collective-permute-done((f32[4,2,64,128]{3,2,1,0:T(8,128)S(1)}, f32[4,2,64,128]{3,2,1,0:T(8,128)S(1)}, u32[]{:S(2)}, u32[]{:S(2)}) %collective-permute-start.3) | collective-permute-done | bytes 262176 | tf_op jit(solution)/shard_map/ppermute | solution.py:124
  25.6 0.6 %collective-permute-start.4 = (f32[8,2,64,128]{3,2,1,0:T(8,128)S(1)}, f32[8,2,64,128]{3,2,1,0:T(8,128)S(1)}, u32[]{:S(2)}, u32[]{:S(2)}) collective-permute-start(f32[8,2,64,128]{3,2,1,0:T(8,128)S(1)} %constant_dynamic-update-slice_fusion.mine_ref), channel_id=1, source_target_pairs={{0,1},{1,0},{2,3},{3,2},{4,5},{5,4},{6,7},{7,6},{8,9},{9,8},{10,11... | collective-permute-start | bytes 1572872 | tf_op jit(solution)/shard_map/ppermute | solution.py:140
  26.2 0.0 collective-permute-done.7.theirs_ref
  26.2 1.2 %setup.1 = (f32[12,8,32,128]{3,2,1,0:T(8,128)S(1)}, f32[4,9,32,128]{3,2,1,0:T(8,128)S(1)}, f32[4,8,32,128]{3,2,1,0:T(8,128)S(1)}, f32[8,8,32,128]{3,2,1,0:T(8,12...) custom-call(s32[1,2]{1,0:T(1,128)S(1)} %bitcast.13, ...), custom_call_target="tpu_custom_call" | custom-call | tf_op jit(solution)/shard_map/setup/pallas_call | solution.py:642
  27.5 0.1 collective-permute-start.9
  27.6 0.1 collective-permute-done.4.theirs_ref
  27.8 5.4 %solve.1.planes_ref = f32[6,64,128]{2,1,0:T(8,128)S(1)} custom-call(f32[8,2,64,128]{3,2,1,0:T(8,128)S(1)} %constant_dynamic-update-slice_fusion.mine_ref, f32[8,2,64,128]{3,2,1,0:T(8,128)S(1)} %collective-permute-done.4.theirs_ref, f32[12,8,32,128]{3,2,1,0:T(8,128)S(1)} %get-tuple-element.52.inner, f32[4,9,32,128]{3,2,1,0:T(8,128)S(1)} %get-tuple-element.53.outer_x, ...), custom_call_target="tpu_custom_call" | custom-call | tf_op jit(solution)/shard_map/solve/pallas_call | solution.py:652
  33.2 0.2 finish.1
  33.4 0.4 %collective-permute-start.10 = (f32[2,96,128]{2,1,0:T(8,128)S(1)}, f32[2,96,128]{2,1,0:T(8,128)S(1)}, u32[]{:S(2)}, u32[]{:S(2)}) collective-permute-start(f32[2,96,128]{2,1,0:T(8,128)S(1)} %get-tuple-element.65), channel_id=1, source_target_pairs={{0,1},{1,0},{2,3},{3,2},{4,5},{5,4},{6,7},{7,6},{8,9},{9,8},{10,11... | collective-permute-start | bytes 294920 | tf_op jit(solution)/shard_map/ppermute | solution.py:686
  33.9 2.5 %collective-permute-start.11 = (f32[2,32,128]{2,1,0:T(8,128)S(1)}, f32[2,32,128]{2,1,0:T(8,128)S(1)}, u32[]{:S(2)}, u32[]{:S(2)}) collective-permute-start(f32[2,32,128]{2,1,0:T(8,128)S(1)} %get-tuple-element.73), channel_id=1, source_target_pairs={{0,16},{1,17},{2,18},{3,19},{4,20},{5,21},{6,22},{7,23},{8,24},{9,... | collective-permute-start | bytes 98312 | tf_op jit(solution)/shard_map/ppermute | solution.py:695
  36.4 0.0 collective-permute-start.12
  36.5 0.7 %pad_maximum_fusion.2 = f32[2,2,64,128]{3,2,1,0:T(8,128)} fusion(f32[1,2,64,128]{3,2,1,0:T(8,128)S(1)} %get-tuple-element.71, f32[1,2,64,128]{3,2,1,0:T(8,128)S(1)} %get-tuple-element.70), kind=kLoop, calls=%fused_computation.2 | loop fusion | flops 32768 | bytes 262144 | tf_op jit(solution)/shard_map/stack | solution.py:697
  37.1 1.2 %collective-permute-done.11 = f32[2,32,128]{2,1,0:T(8,128)S(1)} collective-permute-done((f32[2,32,128]{2,1,0:T(8,128)S(1)}, f32[2,32,128]{2,1,0:T(8,128)S(1)}, u32[]{:S(2)}, u32[]{:S(2)}) %collective-permute-start.11) | collective-permute-done | bytes 32800 | tf_op jit(solution)/shard_map/ppermute | solution.py:695
  38.3 1.5 %collective-permute-done.12 = f32[2,32,128]{2,1,0:T(8,128)S(1)} collective-permute-done((f32[2,32,128]{2,1,0:T(8,128)S(1)}, f32[2,32,128]{2,1,0:T(8,128)S(1)}, u32[]{:S(2)}, u32[]{:S(2)}) %collective-permute-start.12) | collective-permute-done | bytes 32800 | tf_op jit(solution)/shard_map/ppermute | solution.py:695
  39.8 0.6 %add_add_fusion = f32[2,32,128]{2,1,0:T(8,128)} fusion(f32[2,32,128]{2,1,0:T(8,128)S(1)} %collective-permute-done.11, f32[2,32,128]{2,1,0:T(8,128)S(1)} %collective-permute-done.12, f32[2,32,128]{2,1,0:T(8,128)S(1)} %get-tuple-element.67, f32[2,96,128]{2,1,0:T(8,128)S(1)} %collective-permute-done.10), kind=kLoop, calls=%fused_computation.8 | loop fusion | flops 24576 | bytes 163840 | tf_op jit(solution)/shard_map/add | solution.py:701
  (27 shorter events, 0.2 us)
Async XLA Ops:
  0.6 20.6 %copy-start = (f32[2,2,64,128]{3,2,1,0:T(8,128)S(1)}, f32[2,2,64,128]{3,2,1,0:T(8,128)}, u32[]{:S(2)}) copy-start(f32[2,2,64,128]{3,2,1,0:T(8,128)} %state_ref.1) | copy-start | bytes 393220
  0.6 7.4 %collective-permute-start = (f32[2,64,128]{2,1,0:T(8,128)}, f32[2,64,128]{2,1,0:T(8,128)S(1)}, u32[]{:S(2)}, u32[]{:S(2)}) collective-permute-start(f32[2,64,128]{2,1,0:T(8,128)} %kappa_ref.1), channel_id=1, source_target_pairs={{0,8},{1,3},{2,10},{3,1},{4,12},{5,7},{6,14},{7,5},{8,0},{9,11},{1... | collective-permute-start | bytes 196616 | tf_op jit(solution)/shard_map/ppermute | solution.py:124
  4.7 4.5 %collective-permute-start.1 = (f32[2,64,128]{2,1,0:T(8,128)}, f32[2,64,128]{2,1,0:T(8,128)S(1)}, u32[]{:S(2)}, u32[]{:S(2)}) collective-permute-start(f32[2,64,128]{2,1,0:T(8,128)} %misfit_ref.1), channel_id=1, source_target_pairs={{0,2},{1,9},{2,0},{3,11},{4,6},{5,13},{6,4},{7,15},{8,10},{9,1},{1... | collective-permute-start | bytes 196616 | tf_op jit(solution)/shard_map/ppermute | solution.py:124
  6.2 0.8 %copy-start.1 = (f32[2,64,128]{2,1,0:T(8,128)S(1)}, f32[2,64,128]{2,1,0:T(8,128)}, u32[]{:S(2)}) copy-start(f32[2,64,128]{2,1,0:T(8,128)} %kappa_ref.1) | copy-start | bytes 196612
  7.1 0.8 %copy-start.2 = (f32[2,64,128]{2,1,0:T(8,128)S(1)}, f32[2,64,128]{2,1,0:T(8,128)}, u32[]{:S(2)}) copy-start(f32[2,64,128]{2,1,0:T(8,128)} %misfit_ref.1) | copy-start | bytes 196612
  9.3 5.4 %collective-permute-start.5 = (f32[2,2,64,128]{3,2,1,0:T(8,128)S(1)}, f32[2,2,64,128]{3,2,1,0:T(8,128)S(1)}, u32[]{:S(2)}, u32[]{:S(2)}) collective-permute-start(f32[2,2,64,128]{3,2,1,0:T(8,128)S(1)} %get-tuple-element.40), channel_id=1, source_target_pairs={{0,4},{1,9},{2,6},{3,11},{4,0},{5,13},{6,2},{7,15},{8,12},{9,1},{1... | collective-permute-start | bytes 393224 | tf_op jit(solution)/shard_map/ppermute | solution.py:124
  11.0 15.2 %copy-start.3 = (s32[2]{0:T(128)S(1)}, s32[2]{0:T(128)}, u32[]{:S(2)}) copy-start(s32[2]{0:T(128)} %param.11) | copy-start | bytes 28
  11.0 15.2 %copy-start.4 = (f32[4]{0:T(128)S(1)}, f32[4]{0:T(128)}, u32[]{:S(2)}) copy-start(f32[4]{0:T(128)} %param.9) | copy-start | bytes 52
  11.0 15.2 %copy-start.5 = (f32[4]{0:T(128)S(1)}, f32[4]{0:T(128)}, u32[]{:S(2)}) copy-start(f32[4]{0:T(128)} %param.10) | copy-start | bytes 52
  11.0 5.1 %collective-permute-start.2 = (f32[2,2,64,128]{3,2,1,0:T(8,128)S(1)}, f32[2,2,64,128]{3,2,1,0:T(8,128)S(1)}, u32[]{:S(2)}, u32[]{:S(2)}) collective-permute-start(f32[2,2,64,128]{3,2,1,0:T(8,128)S(1)} %get-tuple-element.39), channel_id=1, source_target_pairs={{0,4},{1,3},{2,6},{3,1},{4,0},{5,7},{6,2},{7,5},{8,12},{9,11},{10,... | collective-permute-start | bytes 393224 | tf_op jit(solution)/shard_map/ppermute | solution.py:124
  14.7 6.4 %collective-permute-start.6 = (f32[4,2,64,128]{3,2,1,0:T(8,128)S(1)}, f32[4,2,64,128]{3,2,1,0:T(8,128)S(1)}, u32[]{:S(2)}, u32[]{:S(2)}) collective-permute-start(f32[4,2,64,128]{3,2,1,0:T(8,128)S(1)} %pad_maximum_fusion.1), channel_id=1, source_target_pairs={{0,2},{1,5},{2,0},{3,7},{4,6},{5,1},{6,4},{7,3},{8,10},{9,13},{10,... | collective-permute-start | bytes 786440 | tf_op jit(solution)/shard_map/ppermute | solution.py:124
  16.1 9.4 %collective-permute-start.3 = (f32[4,2,64,128]{3,2,1,0:T(8,128)S(1)}, f32[4,2,64,128]{3,2,1,0:T(8,128)S(1)}, u32[]{:S(2)}, u32[]{:S(2)}) collective-permute-start(f32[4,2,64,128]{3,2,1,0:T(8,128)S(1)} %pad_maximum_fusion), channel_id=1, source_target_pairs={{0,8},{1,5},{2,10},{3,7},{4,12},{5,1},{6,14},{7,3},{8,0},{9,13},{1... | collective-permute-start | bytes 786440 | tf_op jit(solution)/shard_map/ppermute | solution.py:124
  21.2 5.0 %collective-permute-start.7 = (f32[8,2,64,128]{3,2,1,0:T(8,128)S(1)}, f32[8,2,64,128]{3,2,1,0:T(8,128)S(1)}, u32[]{:S(2)}, u32[]{:S(2)}) collective-permute-start(f32[8,2,64,128]{3,2,1,0:T(8,128)S(1)} %constant_dynamic-update-slice_fusion.3.mine_ref), channel_id=1, source_target_pairs={{0,1},{1,0},{2,3},{3,2},{4,5},{5,4},{6,7},{7,6},{8,9},{9,8},{10,11... | collective-permute-start | bytes 1572872 | tf_op jit(solution)/shard_map/ppermute | solution.py:140
  21.3 6.2 %collective-permute-start.8 = (f32[2,1,64,128]{3,2,1,0:T(8,128)S(1)}, f32[2,1,64,128]{3,2,1,0:T(8,128)S(1)}, u32[]{:S(2)}, u32[]{:S(2)}) collective-permute-start(f32[2,1,64,128]{3,2,1,0:T(8,128)S(1)} %slice_select_fusion.1), channel_id=1, source_target_pairs={{1,2},{2,1},{3,4},{4,3},{5,6},{6,5},{7,8},{8,7},{9,10},{10,9},{11,... | collective-permute-start | bytes 196616 | tf_op jit(solution)/shard_map/ppermute | solution.py:139
  25.6 2.2 %collective-permute-start.4 = (f32[8,2,64,128]{3,2,1,0:T(8,128)S(1)}, f32[8,2,64,128]{3,2,1,0:T(8,128)S(1)}, u32[]{:S(2)}, u32[]{:S(2)}) collective-permute-start(f32[8,2,64,128]{3,2,1,0:T(8,128)S(1)} %constant_dynamic-update-slice_fusion.mine_ref), channel_id=1, source_target_pairs={{0,1},{1,0},{2,3},{3,2},{4,5},{5,4},{6,7},{7,6},{8,9},{9,8},{10,11... | collective-permute-start | bytes 1572872 | tf_op jit(solution)/shard_map/ppermute | solution.py:140
  27.5 5.6 %collective-permute-start.9 = (f32[3,64,128]{2,1,0:T(8,128)S(1)}, f32[3,64,128]{2,1,0:T(8,128)S(1)}, u32[]{:S(2)}, u32[]{:S(2)}) collective-permute-start(f32[3,64,128]{2,1,0:T(8,128)S(1)} %fusion), channel_id=1, source_target_pairs={{0,1},{1,0},{2,3},{3,2},{4,5},{5,4},{6,7},{7,6},{8,9},{9,8},{10,11... | collective-permute-start | bytes 294920 | tf_op jit(solution)/shard_map/ppermute | solution.py:145
  33.4 3.0 %collective-permute-start.10 = (f32[2,96,128]{2,1,0:T(8,128)S(1)}, f32[2,96,128]{2,1,0:T(8,128)S(1)}, u32[]{:S(2)}, u32[]{:S(2)}) collective-permute-start(f32[2,96,128]{2,1,0:T(8,128)S(1)} %get-tuple-element.65), channel_id=1, source_target_pairs={{0,1},{1,0},{2,3},{3,2},{4,5},{5,4},{6,7},{7,6},{8,9},{9,8},{10,11... | collective-permute-start | bytes 294920 | tf_op jit(solution)/shard_map/ppermute | solution.py:686
  33.9 4.4 %collective-permute-start.11 = (f32[2,32,128]{2,1,0:T(8,128)S(1)}, f32[2,32,128]{2,1,0:T(8,128)S(1)}, u32[]{:S(2)}, u32[]{:S(2)}) collective-permute-start(f32[2,32,128]{2,1,0:T(8,128)S(1)} %get-tuple-element.73), channel_id=1, source_target_pairs={{0,16},{1,17},{2,18},{3,19},{4,20},{5,21},{6,22},{7,23},{8,24},{9,... | collective-permute-start | bytes 98312 | tf_op jit(solution)/shard_map/ppermute | solution.py:695
  36.4 3.4 %collective-permute-start.12 = (f32[2,32,128]{2,1,0:T(8,128)S(1)}, f32[2,32,128]{2,1,0:T(8,128)S(1)}, u32[]{:S(2)}, u32[]{:S(2)}) collective-permute-start(f32[2,32,128]{2,1,0:T(8,128)S(1)} %get-tuple-element.72), channel_id=1, source_target_pairs={{0,17},{1,16},{2,19},{3,18},{4,21},{5,20},{6,23},{7,22},{8,25},{9,... | collective-permute-start | bytes 98312 | tf_op jit(solution)/shard_map/ppermute | solution.py:695
